TPU v7x, 32 devices: a whole 2x2x4 slice. The times are simulated.
32 devices in a mesh: dp: 4 (over y, core), seq: 2 (over x), mp: 4 (over z).
Axes of the slice: x: 2, y: 2, z: 4, core: 2. Of those that a mesh axis runs over, the one named last changes fastest.
Arguments:
- tokens: bfloat16 [8, 4096, 768], P('dp', 'seq'), may hold values from -6 to 6
- places: int32 [8, 4096], P('dp', 'seq'), may hold values from 0 to 4095, as said below
- w_qkv: bfloat16 [3, 768, 768], P(None, ('dp', 'seq'), 'mp'), may hold values from -0.21875 to 0.21875
- b_qkv: bfloat16 [3, 12, 64], P(None, 'mp', ('dp', 'seq')), may hold values from -3 to 3
- w_dense: bfloat16 [768, 768], P('mp', ('dp', 'seq')), may hold values from -6 to 6
- b_dense: bfloat16 [768], P(('dp', 'seq')), may hold values from -3 to 3
- w_up: bfloat16 [768, 3072], P(('dp', 'seq'), 'mp'), may hold values from -0.21875 to 0.21875
- b_up: bfloat16 [24, 128], P('mp', ('dp', 'seq')), may hold values from -3 to 3
- w_down: bfloat16 [3072, 768], P('mp', ('dp', 'seq')), may hold values from -0.109375 to 0.109375
- b_down: bfloat16 [768], P(('dp', 'seq')), may hold values from -3 to 3
- norm1_gain: bfloat16 [768], P(('dp', 'seq')), may hold values from 0.5 to 1.5
- norm1_bias: bfloat16 [768], P(('dp', 'seq')), may hold values from -2 to 2
- norm2_gain: bfloat16 [768], P(('dp', 'seq')), may hold values from 0.5 to 1.5
- norm2_bias: bfloat16 [768], P(('dp', 'seq')), may hold values from -2 to 2
- out_grad: bfloat16 [8, 4096, 768], P('dp', 'seq'), may hold values from -6 to 6
Outputs:
- mixed: bfloat16 [8, 4096, 768], P('dp', 'seq')
- grad_tokens: bfloat16 [8, 4096, 768], P('dp', 'seq')
- grad_w_qkv: float32 [3, 768, 768], P(None, ('dp', 'seq'), 'mp')
- grad_b_qkv: float32 [3, 12, 64], P(None, 'mp', ('dp', 'seq'))
- grad_w_dense: float32 [768, 768], P('mp', ('dp', 'seq'))
- grad_b_dense: float32 [768], P(('dp', 'seq'))
- grad_w_up: float32 [768, 3072], P(('dp', 'seq'), 'mp')
- grad_b_up: float32 [24, 128], P('mp', ('dp', 'seq'))
- grad_w_down: float32 [3072, 768], P('mp', ('dp', 'seq'))
- grad_b_down: float32 [768], P(('dp', 'seq'))
- grad_norm1_gain: float32 [768], P(('dp', 'seq'))
- grad_norm1_bias: float32 [768], P(('dp', 'seq'))
- grad_norm2_gain: float32 [768], P(('dp', 'seq'))
- grad_norm2_bias: float32 [768], P(('dp', 'seq'))
Inputs may be any that keep to these rules, and one draw needn't show every extreme that they name: Each row places[s] is a permutation of the positions of one sequence. The 2048 stored tokens of a sequence on one index of seq are two runs of 1024 consecutive positions in increasing order: run t and run 2 * 2 - 1 - t of the sequence, with t different for every index of seq and drawn per sequence.
All inputs are finite; a program needn't handle non-finite values.
Results may differ from a plain program's by a relative error of at most 0.011.
Values may be sent and summed in bfloat16 or wider, within the bound.
No kernel may reach another device: no remote copies, remote signals or barrier semaphores. Data moves between devices by JAX's collectives and lax.ppermute only.
A program may use at most 512 MiB of HBM per device.

v0:
```python
from functools import partial

import jax
import jax.numpy as jnp
from jax import lax
from jax.sharding import PartitionSpec as P

HD = 64
ROT = 16


norm_eps = 1e-05
masked_value = -1e30


def layer_norm(values, gain, shift):
    centre = jnp.mean(values, axis=-1, keepdims=True)
    deviate = values - centre
    spread = jnp.mean(deviate * deviate, axis=-1, keepdims=True)
    return deviate * lax.rsqrt(spread + norm_eps) * gain + shift


def rotate(values, positions):
    half_dims = ROT // 2
    frequency = jnp.power(
        jnp.float32(10000.0), -2.0 * jnp.arange(half_dims, dtype=jnp.float32) / ROT
    )
    angles = positions.astype(jnp.float32)[:, None] * frequency[None, :]
    cosines = jnp.concatenate([jnp.cos(angles), jnp.cos(angles)], axis=-1)[:, None, :]
    sine_part = jnp.concatenate([jnp.sin(angles), jnp.sin(angles)], axis=-1)[:, None, :]
    leading = values[..., :ROT]
    turned = jnp.concatenate([-leading[..., half_dims:], leading[..., :half_dims]], axis=-1)
    return jnp.concatenate([leading * cosines + turned * sine_part, values[..., ROT:]], axis=-1)


def masked_scores(queries, keys_all, query_places, key_places):
    scores = jnp.einsum(
        "qhd,khd->hqk", queries, keys_all, preferred_element_type=jnp.float32
    ) * HD ** (-0.5)
    visible = key_places[None, None, :] <= query_places[None, :, None]
    return jnp.where(visible, scores, masked_value)


def attend(queries, keys_all, values_all, query_places, key_places):
    scores = masked_scores(queries, keys_all, query_places, key_places)
    row_max = jnp.max(scores, axis=-1, keepdims=True)
    log_total = row_max + jnp.log(jnp.sum(jnp.exp(scores - row_max), axis=-1, keepdims=True))
    soft_low = jnp.exp(scores - log_total).astype(jnp.bfloat16)
    attended = jnp.einsum("hqk,khd->qhd", soft_low, values_all, preferred_element_type=jnp.float32)
    return (attended, log_total)


def score_grads(queries, keys_all, values_all, query_places, key_places, log_total, grad_out):
    soft_full = jnp.exp(masked_scores(queries, keys_all, query_places, key_places) - log_total)
    grad_soft = jnp.einsum("qhd,khd->hqk", grad_out, values_all, preferred_element_type=jnp.float32)
    row_terms = jnp.sum(soft_full * grad_soft, axis=-1, keepdims=True)
    grad_scores = (soft_full * (grad_soft - row_terms)).astype(jnp.bfloat16)
    return (soft_full.astype(jnp.bfloat16), grad_scores, row_terms)


def body(
    tokens,
    places,
    w_qkv,
    b_qkv,
    w_dense,
    b_dense,
    w_up,
    b_up,
    w_down,
    b_down,
    norm1_gain,
    norm1_bias,
    norm2_gain,
    norm2_bias,
    out_grad,
):
    micro_count, seg_rows, width = tokens.shape
    all_places = lax.all_gather(places, "seq", axis=1, tiled=True)
    grad_sums = None
    mixed_rows = []
    input_grads = []
    for micro_index in range(micro_count):
        forward_weights = (
            lax.all_gather(w_qkv, ("dp", "seq"), axis=1, tiled=True),
            lax.all_gather(b_qkv, ("dp", "seq"), axis=2, tiled=True),
            lax.all_gather(w_dense, ("dp", "seq"), axis=1, tiled=True),
            lax.all_gather(b_dense, ("dp", "seq"), axis=0, tiled=True),
            lax.all_gather(w_up, ("dp", "seq"), axis=0, tiled=True),
            lax.all_gather(b_up, ("dp", "seq"), axis=1, tiled=True),
            lax.all_gather(w_down, ("dp", "seq"), axis=1, tiled=True),
            lax.all_gather(b_down, ("dp", "seq"), axis=0, tiled=True),
            lax.all_gather(norm1_gain, ("dp", "seq"), axis=0, tiled=True),
            lax.all_gather(norm1_bias, ("dp", "seq"), axis=0, tiled=True),
            lax.all_gather(norm2_gain, ("dp", "seq"), axis=0, tiled=True),
            lax.all_gather(norm2_bias, ("dp", "seq"), axis=0, tiled=True),
        )
        if grad_sums is None:
            grad_sums = tuple((jnp.zeros(param.shape, jnp.float32) for param in forward_weights))
        (
            qkv_w,
            qkv_b,
            dense_w,
            dense_b,
            up_w,
            up_b,
            down_w,
            down_b,
            gain_one,
            shift_one,
            gain_two,
            shift_two,
        ) = forward_weights
        heads_local = qkv_b.shape[1]
        x_rows = tokens[micro_index].astype(jnp.float32)
        my_places = places[micro_index]
        seq_places = all_places[micro_index]
        norm_one_full, norm_one_back = jax.vjp(
            layer_norm, x_rows, gain_one.astype(jnp.float32), shift_one.astype(jnp.float32)
        )
        norm_two_full, norm_two_back = jax.vjp(
            layer_norm, x_rows, gain_two.astype(jnp.float32), shift_two.astype(jnp.float32)
        )
        norm_one = norm_one_full.astype(jnp.bfloat16)
        norm_two = norm_two_full.astype(jnp.bfloat16)
        projected = jnp.einsum(
            "td,ide->ite", norm_one, qkv_w, preferred_element_type=jnp.float32
        ) + qkv_b.astype(jnp.float32).reshape(3, 1, heads_local * HD)
        query_pre = projected[0].reshape(seg_rows, heads_local, HD)
        queries = rotate(query_pre, my_places).astype(jnp.bfloat16)
        keys = rotate(projected[1].reshape(seg_rows, heads_local, HD), my_places).astype(
            jnp.bfloat16
        )
        values = projected[2].reshape(seg_rows, heads_local, HD).astype(jnp.bfloat16)
        keys_all, values_all = (
            lax.all_gather(keys, "seq", axis=0, tiled=True),
            lax.all_gather(values, "seq", axis=0, tiled=True),
        )
        attended, log_total = attend(queries, keys_all, values_all, my_places, seq_places)
        attended_low = attended.reshape(seg_rows, heads_local * HD).astype(jnp.bfloat16)
        hidden_pre = jnp.dot(norm_two, up_w, preferred_element_type=jnp.float32) + up_b.astype(
            jnp.float32
        ).reshape(-1)
        activated = jax.nn.gelu(hidden_pre, approximate=False).astype(jnp.bfloat16)
        summed = lax.psum(
            jnp.dot(attended_low, dense_w, preferred_element_type=jnp.float32)
            + jnp.dot(activated, down_w, preferred_element_type=jnp.float32),
            "mp",
        )
        mixed_rows.append(
            (x_rows + summed + dense_b.astype(jnp.float32) + down_b.astype(jnp.float32)).astype(
                jnp.bfloat16
            )
        )
        backward_weights = (
            lax.all_gather(w_qkv, ("dp", "seq"), axis=1, tiled=True),
            lax.all_gather(b_qkv, ("dp", "seq"), axis=2, tiled=True),
            lax.all_gather(w_dense, ("dp", "seq"), axis=1, tiled=True),
            lax.all_gather(b_dense, ("dp", "seq"), axis=0, tiled=True),
            lax.all_gather(w_up, ("dp", "seq"), axis=0, tiled=True),
            lax.all_gather(b_up, ("dp", "seq"), axis=1, tiled=True),
            lax.all_gather(w_down, ("dp", "seq"), axis=1, tiled=True),
            lax.all_gather(b_down, ("dp", "seq"), axis=0, tiled=True),
            lax.all_gather(norm1_gain, ("dp", "seq"), axis=0, tiled=True),
            lax.all_gather(norm1_bias, ("dp", "seq"), axis=0, tiled=True),
            lax.all_gather(norm2_gain, ("dp", "seq"), axis=0, tiled=True),
            lax.all_gather(norm2_bias, ("dp", "seq"), axis=0, tiled=True),
        )
        (
            qkv_w,
            qkv_b,
            dense_w,
            dense_b,
            up_w,
            up_b,
            down_w,
            down_b,
            gain_one,
            shift_one,
            gain_two,
            shift_two,
        ) = backward_weights
        grad_rows = out_grad[micro_index]
        grad_rows_full = grad_rows.astype(jnp.float32)
        column_sums = jnp.sum(grad_rows_full, axis=0)
        grad_dense_w = jnp.einsum(
            "te,td->ed", attended_low, grad_rows, preferred_element_type=jnp.float32
        )
        grad_down_w = jnp.einsum(
            "tf,td->fd", activated, grad_rows, preferred_element_type=jnp.float32
        )
        grad_attended = jnp.einsum(
            "td,ed->te", grad_rows, dense_w, preferred_element_type=jnp.float32
        ).astype(jnp.bfloat16)
        grad_act = jnp.einsum("td,fd->tf", grad_rows, down_w, preferred_element_type=jnp.float32)
        gelu_out, gelu_back = jax.vjp(partial(jax.nn.gelu, approximate=False), hidden_pre)
        grad_pre = gelu_back(grad_act)[0].astype(jnp.bfloat16)
        grad_up_w = jnp.einsum("td,tf->df", norm_two, grad_pre, preferred_element_type=jnp.float32)
        grad_up_b = jnp.sum(grad_pre.astype(jnp.float32), axis=0).reshape(up_b.shape)
        grad_out = grad_attended.reshape(seg_rows, heads_local, HD)
        soft_low, grad_scores, row_terms = score_grads(
            queries, keys_all, values_all, my_places, seq_places, log_total, grad_out
        )
        query_grad = jnp.einsum(
            "hqk,khd->qhd", grad_scores, keys_all, preferred_element_type=jnp.float32
        ) * HD ** (-0.5)
        key_terms = jnp.einsum(
            "hqk,qhd->khd", grad_scores, queries, preferred_element_type=jnp.float32
        ) * HD ** (-0.5)
        value_terms = jnp.einsum(
            "hqk,qhd->khd", soft_low, grad_out, preferred_element_type=jnp.float32
        )
        key_grad, value_grad = (
            lax.psum_scatter(
                key_terms.reshape(-1, heads_local * HD), "seq", scatter_dimension=0, tiled=True
            ),
            lax.psum_scatter(
                value_terms.reshape(-1, heads_local * HD), "seq", scatter_dimension=0, tiled=True
            ),
        )
        rotated_out, turn_back = jax.vjp(partial(rotate, positions=my_places), query_pre)
        query_back = turn_back(query_grad)[0].reshape(seg_rows, heads_local * HD)
        key_back = turn_back(key_grad.reshape(seg_rows, heads_local, HD))[0].reshape(
            seg_rows, heads_local * HD
        )
        grad_proj = jnp.stack([query_back, key_back, value_grad]).astype(jnp.bfloat16)
        grad_qkv_w = jnp.einsum(
            "td,ite->ide", norm_one, grad_proj, preferred_element_type=jnp.float32
        )
        grad_qkv_b = jnp.sum(grad_proj.astype(jnp.float32), axis=1).reshape(qkv_b.shape)
        first = jnp.einsum("ite,ide->td", grad_proj, qkv_w, preferred_element_type=jnp.float32)
        second = jnp.einsum("tf,df->td", grad_pre, up_w, preferred_element_type=jnp.float32)
        both_full = lax.psum(jnp.concatenate([first, second], axis=1), "mp")
        input_one, gain_one_grad, shift_one_grad = norm_one_back(both_full[:, :width])
        input_two, gain_two_grad, shift_two_grad = norm_two_back(both_full[:, width:])
        input_grads.append((grad_rows_full + input_one + input_two).astype(jnp.bfloat16))
        step_terms = (
            grad_qkv_w,
            grad_qkv_b,
            grad_dense_w,
            column_sums,
            grad_up_w,
            grad_up_b,
            grad_down_w,
            column_sums,
            gain_one_grad,
            shift_one_grad,
            gain_two_grad,
            shift_two_grad,
        )
        grad_sums = jax.tree.map(jnp.add, grad_sums, step_terms)
    owned = (
        lax.psum_scatter(grad_sums[0], ("dp", "seq"), scatter_dimension=1, tiled=True),
        lax.psum_scatter(grad_sums[1], ("dp", "seq"), scatter_dimension=2, tiled=True),
        lax.psum_scatter(grad_sums[2], ("dp", "seq"), scatter_dimension=1, tiled=True),
        lax.psum_scatter(grad_sums[3], ("dp", "seq"), scatter_dimension=0, tiled=True),
        lax.psum_scatter(grad_sums[4], ("dp", "seq"), scatter_dimension=0, tiled=True),
        lax.psum_scatter(grad_sums[5], ("dp", "seq"), scatter_dimension=1, tiled=True),
        lax.psum_scatter(grad_sums[6], ("dp", "seq"), scatter_dimension=1, tiled=True),
        lax.psum_scatter(grad_sums[7], ("dp", "seq"), scatter_dimension=0, tiled=True),
        lax.psum_scatter(grad_sums[8], ("dp", "seq"), scatter_dimension=0, tiled=True),
        lax.psum_scatter(grad_sums[9], ("dp", "seq"), scatter_dimension=0, tiled=True),
        lax.psum_scatter(grad_sums[10], ("dp", "seq"), scatter_dimension=0, tiled=True),
        lax.psum_scatter(grad_sums[11], ("dp", "seq"), scatter_dimension=0, tiled=True),
    )
    norm_owned = (owned[8], owned[9], owned[10], owned[11])
    return (
        jnp.stack(mixed_rows),
        jnp.stack(input_grads),
        owned[0],
        owned[1],
        owned[2],
        owned[3],
        owned[4],
        owned[5],
        owned[6],
        owned[7],
        norm_owned[0],
        norm_owned[1],
        norm_owned[2],
        norm_owned[3],
    )


def solution(mesh):
    placed = (
        P("dp", "seq", None),
        P("dp", "seq"),
        P(None, ("dp", "seq"), "mp"),
        P(None, "mp", ("dp", "seq")),
        P("mp", ("dp", "seq")),
        P(("dp", "seq")),
        P(("dp", "seq"), "mp"),
        P("mp", ("dp", "seq")),
        P("mp", ("dp", "seq")),
        P(("dp", "seq")),
        P(("dp", "seq")),
        P(("dp", "seq")),
        P(("dp", "seq")),
        P(("dp", "seq")),
        P("dp", "seq", None),
    )
    return jax.shard_map(
        body,
        mesh=mesh,
        in_specs=placed,
        out_specs=(
            P("dp", "seq", None),
            P("dp", "seq", None),
            P(None, ("dp", "seq"), "mp"),
            P(None, "mp", ("dp", "seq")),
            P("mp", ("dp", "seq")),
            P(("dp", "seq")),
            P(("dp", "seq"), "mp"),
            P("mp", ("dp", "seq")),
            P("mp", ("dp", "seq")),
            P(("dp", "seq")),
            P(("dp", "seq")),
            P(("dp", "seq")),
            P(("dp", "seq")),
            P(("dp", "seq")),
        ),
        check_vma=False,
    )
```

profile of v0, /device:TPU:0, one launch (start us, length us, event | category | flops | bytes accessed | tf_op | source)
XLA Modules:
  0.0 2427.8 jit_solution(7969845716218213946)
XLA Ops:
  14.3 25.7 %all-reduce.30 = (bf16[768]{0:T(1024)(128)(2,1)S(1)}, bf16[768]{0:T(1024)(128)(2,1)S(1)}, bf16[768]{0:T(1024)(128)(2,1)S(1)}, bf16[768]{0:T(1024)(128)(2,1)S(1)}...) all-reduce(bf16[768]{0:T(1024)(128)(2,1)S(1)} %dynamic-update-slice, ...), channel_id=1, replica_groups=mesh['dp'=4,'seq'=2,'mp'=4] {'dp','seq'}, use_global_device_ids=true, to_apply=%add.19 | all-reduce | flops 4608 | bytes 18432
  46.5 22.8 all_gather.36
  115.3 17.2 all_gather.78
  154.1 38.1 %fusion = (f32[3,2048]{1,0:T(4,128)S(1)}, f32[3,2048,4096]{2,1,0:T(8,128)}) fusion(pred[2048,4096]{1,0:T(8,128)(4,1)} %broadcast_compare_fusion.1, bf16[4096,3,64]{0,2,1:T(8,128)(2,1)} %all-gather.10.cloned.1.call-done, bf16[2048,3,48]{0,2,1:T(8,128)(2,1)S(1)} %slice.339, bf16[2048,3,16]{0,2,1:T(8,128)(2,1)S(1)} %get-tuple-element.156), kind=kOutput, calls=%fused_computation.10 | convolution fusion | flops 3298289664 | bytes 111435776 | tf_op jit(solution)/shard_map/qhd,khd->hqk/dot_general | solution.py:37
  192.2 34.6 %exponential_reduce_fusion.1 = f32[3,2048]{1,0:T(4,128)S(1)} fusion(f32[3,2048,4096]{2,1,0:T(8,128)} %get-tuple-element.184, f32[3,2048]{1,0:T(4,128)S(1)} %get-tuple-element.183, pred[2048,4096]{1,0:T(8,128)(4,1)} %broadcast_compare_fusion.1), kind=kLoop, calls=%fused_computation.8 | loop fusion | flops 100657152 | bytes 109101056 | tf_op jit(solution)/shard_map/reduce_sum | solution.py:47
  226.9 72.2 %multiply_reduce_fusion.1 = (f32[3,2048]{1,0:T(4,128)S(1)}, f32[3,2048,4096]{2,1,0:T(8,128)}) fusion(f32[3,2048,4096]{2,1,0:T(8,128)} %get-tuple-element.184, f32[3,2048]{1,0:T(4,128)S(1)} %log_add_fusion.1, pred[2048,4096]{1,0:T(8,128)(4,1)} %broadcast_compare_fusion.1, bf16[2048,3,64]{0,2,1:T(8,128)(2,1)S(1)} %bitcast.377, ...), kind=kOutput, calls=%fused_computation.3 | convolution fusion | flops 3347048448 | bytes 212123648 | tf_op jit(solution)/shard_map/qhd,khd->hqk/dot_general | solution.py:55
  299.1 81.4 %multiply_convert_fusion.1 = bf16[3,2048,4096]{2,1,0:T(8,128)(2,1)} fusion(f32[3,2048,4096]{2,1,0:T(8,128)} %get-tuple-element.186, f32[3,2048,4096]{2,1,0:T(8,128)} %get-tuple-element.184, f32[3,2048]{1,0:T(4,128)S(1)} %get-tuple-element.185, f32[3,2048]{1,0:T(4,128)S(1)} %log_add_fusion.1, pred[2048,4096]{1,0:T(8,128)(4,1)} %broadcast_compare_fusion.1), kind=kLoop, calls=%fused_computation.2 | loop fusion | flops 150994944 | bytes 260096000 | tf_op jit(solution)/shard_map/convert_element_type | solution.py:57
  380.6 22.1 convolution_multiply_fusion.1
  404.1 21.8 fusion.103
  426.0 40.1 %fusion.156 = f32[3,64,4096]{2,1,0:T(8,128)} fusion(bf16[2048,3,64]{0,2,1:T(8,128)(2,1)} %bitcast.378, f32[3,2048,4096]{2,1,0:T(8,128)} %get-tuple-element.184, f32[3,2048]{1,0:T(4,128)S(1)} %log_add_fusion.1, pred[2048,4096]{1,0:T(8,128)(4,1)} %broadcast_compare_fusion.1), kind=kOutput, calls=%fused_computation.274 | convolution fusion | flops 3321888768 | bytes 113008640 | tf_op jit(solution)/shard_map/hqk,qhd->khd/dot_general | solution.py:210
  466.3 20.2 multiply_convert_fusion.3
  543.8 412.2 %all-reduce.34.cloned.1.call-done = f32[2048,1536]{1,0:T(8,128)} async-done(((f32[2048,1536]{1,0:T(8,128)}), f32[2048,1536]{1,0:T(8,128)}) %all-reduce.34.cloned.1.call-update) | async-done | bytes 12582928 | tf_op jit(solution)/shard_map/psum | solution.py:233
  973.8 39.3 %convolution_convert_fusion.1 = bf16[3,64,2048]{2,1,0:T(8,128)(2,1)} fusion(bf16[4096,3,64]{0,2,1:T(8,128)(2,1)S(1)} %copy-done.30, f32[3,2048,4096]{2,1,0:T(8,128)} %get-tuple-element.184, f32[3,2048]{1,0:T(4,128)S(1)} %log_add_fusion.1, pred[2048,4096]{1,0:T(8,128)(4,1)} %broadcast_compare_fusion.1), kind=kOutput, calls=%fused_computation.161 | convolution fusion | flops 3322281984 | bytes 111435776 | tf_op jit(solution)/shard_map/hqk,khd->qhd/dot_general | solution.py:49
  1015.9 37.9 %fusion.1 = (f32[3,2048]{1,0:T(4,128)S(1)}, f32[3,2048,4096]{2,1,0:T(8,128)}) fusion(pred[2048,4096]{1,0:T(8,128)(4,1)} %broadcast_compare_fusion, bf16[4096,3,64]{0,2,1:T(8,128)(2,1)} %all-gather.18.cloned.1.call-done, bf16[2048,3,48]{0,2,1:T(8,128)(2,1)S(1)} %slice.337, bf16[2048,3,16]{0,2,1:T(8,128)(2,1)S(1)} %copy-done.50), kind=kOutput, calls=%fused_computation.11 | convolution fusion | flops 3298289664 | bytes 111435776 | tf_op jit(solution)/shard_map/qhd,khd->hqk/dot_general | solution.py:37
  1053.8 34.4 %exponential_reduce_fusion = f32[3,2048]{1,0:T(4,128)S(1)} fusion(f32[3,2048,4096]{2,1,0:T(8,128)} %get-tuple-element.189, f32[3,2048]{1,0:T(4,128)S(1)} %get-tuple-element.188, pred[2048,4096]{1,0:T(8,128)(4,1)} %broadcast_compare_fusion), kind=kLoop, calls=%fused_computation.5 | loop fusion | flops 100657152 | bytes 109101056 | tf_op jit(solution)/shard_map/reduce_sum | solution.py:47
  1088.3 72.1 %multiply_reduce_fusion = (f32[3,2048]{1,0:T(4,128)S(1)}, f32[3,2048,4096]{2,1,0:T(8,128)}) fusion(f32[3,2048,4096]{2,1,0:T(8,128)} %get-tuple-element.189, f32[3,2048]{1,0:T(4,128)S(1)} %log_add_fusion, pred[2048,4096]{1,0:T(8,128)(4,1)} %broadcast_compare_fusion, bf16[2048,3,64]{0,2,1:T(8,128)(2,1)S(1)} %bitcast.375, ...), kind=kOutput, calls=%fused_computation.1 | convolution fusion | flops 3347048448 | bytes 212123648 | tf_op jit(solution)/shard_map/qhd,khd->hqk/dot_general | solution.py:55
  1160.5 81.4 %multiply_convert_fusion = bf16[3,2048,4096]{2,1,0:T(8,128)(2,1)} fusion(f32[3,2048,4096]{2,1,0:T(8,128)} %get-tuple-element.191, f32[3,2048,4096]{2,1,0:T(8,128)} %get-tuple-element.189, f32[3,2048]{1,0:T(4,128)S(1)} %get-tuple-element.190, f32[3,2048]{1,0:T(4,128)S(1)} %log_add_fusion, pred[2048,4096]{1,0:T(8,128)(4,1)} %broadcast_compare_fusion), kind=kLoop, calls=%fused_computation | loop fusion | flops 150994944 | bytes 260096000 | tf_op jit(solution)/shard_map/convert_element_type | solution.py:57
  1241.9 22.3 convolution_multiply_fusion
  1271.8 38.6 %fusion.153 = f32[3,64,4096]{2,1,0:T(8,128)} fusion(bf16[2048,3,64]{0,2,1:T(8,128)(2,1)S(1)} %bitcast.376, f32[3,2048,4096]{2,1,0:T(8,128)} %get-tuple-element.189, f32[3,2048]{1,0:T(4,128)S(1)} %log_add_fusion, pred[2048,4096]{1,0:T(8,128)(4,1)S(1)} %copy-done), kind=kOutput, calls=%fused_computation.273 | convolution fusion | flops 3321888768 | bytes 113008640 | tf_op jit(solution)/shard_map/hqk,qhd->khd/dot_general | solution.py:210
  1317.8 18.7 multiply_convert_fusion.2
  1342.9 38.2 %convolution_convert_fusion = bf16[3,64,2048]{2,1,0:T(8,128)(2,1)S(1)} fusion(bf16[4096,3,64]{0,2,1:T(8,128)(2,1)S(1)} %copy-done.31, f32[3,2048,4096]{2,1,0:T(8,128)} %get-tuple-element.189, f32[3,2048]{1,0:T(4,128)S(1)} %log_add_fusion, pred[2048,4096]{1,0:T(8,128)(4,1)} %broadcast_compare_fusion), kind=kOutput, calls=%fused_computation.160 | convolution fusion | flops 3322281984 | bytes 111435776 | tf_op jit(solution)/shard_map/hqk,khd->qhd/dot_general | solution.py:49
  1385.6 21.5 fusion.102
  1498.1 830.6 %all-reduce.36.cloned.1.call-done = (f32[2048,768]{1,0:T(8,128)}, f32[2048,768]{1,0:T(8,128)}, f32[2048,1536]{1,0:T(8,128)}) async-done(((f32[2048,768]{1,0:T(8,128)}, f32[2048,768]{1,0:T(8,128)}, f32[2048,1536]{1,0:T(8,128)}), (f32[2048,768]{1,0:T(8,128)}, f32[2048,768]{1,0:T(8,128)}, f32[2048,1536]{1,0:T(8,128)})) %all-reduce.36.cloned.1.call-update) | async-done | bytes 25165840 | tf_op jit(solution)/shard_map/psum | solution.py:145
  2374.7 24.3 %all-reduce.28 = (f32[3,3,64]{2,1,0:T(4,128)S(1)}, f32[768]{0:T(1024)S(1)}, f32[768]{0:T(1024)S(1)}, f32[768]{0:T(1024)S(1)}, f32[768]{0:T(1024)S(1)}, /*index=5*/f32[768]{0:T(1024)S(1)}) all-reduce(f32[3,3,64]{2,1,0:T(4,128)S(1)} %add.335, f32[768]{0:T(1024)S(1)} %add.337, ...), channel_id=7, replica_groups=mesh['dp'=4,'seq'=2,'mp'=4] {'dp','seq'}, use_global_device_ids=true, to_apply=%region_29.30.clone | all-reduce | flops 4416 | bytes 35328
  (439 shorter events, 341.9 us)
Async XLA Ops:
  7.2 146.9 %all-gather.10.cloned.1.call-start = ((), (), s32[]{:S(2)}) async-start(), calls=%async_computation.10 | async-start | bytes 2359296 | tf_op jit(solution)/shard_map/all_gather | solution.py:136
  96.9 129.9 %all-gather.8.cloned.1.call-start = ((), (), s32[]{:S(2)}) async-start(), calls=%async_computation.9 | async-start | bytes 2359296 | tf_op jit(solution)/shard_map/all_gather | solution.py:137
  99.4 366.9 %all-gather.12.cloned.1.call-start = ((), (), s32[]{:S(2)}) async-start(), calls=%async_computation.11 | async-start | bytes 1327104 | tf_op jit(solution)/shard_map/all_gather | solution.py:89
  100.2 386.3 %all-gather.14.cloned.1.call-start = ((), (), s32[]{:S(2)}) async-start(), calls=%async_computation.12 | async-start | bytes 1327104 | tf_op jit(solution)/shard_map/all_gather | solution.py:91
  100.7 403.1 %reduce-scatter.17.cloned.1.call-start = ((), (), s32[]{:S(2)}) async-start(), calls=%async_computation.15 | async-start | bytes 4718592 | tf_op jit(solution)/shard_map/reduce_scatter | solution.py:214
  402.7 107.8 %reduce-scatter.19.cloned.1.call-start = ((), (), s32[]{:S(2)}) async-start(), calls=%async_computation.16 | async-start | bytes 4718592 | tf_op jit(solution)/shard_map/reduce_scatter | solution.py:217
  466.2 489.8 %all-reduce.34.cloned.1.call-start = ((), (), s32[]{:S(2)}) async-start(), calls=%async_computation.17 | async-start | bytes 25165824 | tf_op jit(solution)/shard_map/psum | solution.py:233
  529.7 486.2 %all-gather.18.cloned.1.call-start = ((), (), s32[]{:S(2)}) async-start(), calls=%async_computation.14 | async-start | bytes 2359296 | tf_op jit(solution)/shard_map/all_gather | solution.py:136
  530.4 434.5 %copy-start.54 = (f32[2048]{0:T(1024)}, f32[2048]{0:T(1024)S(1)}, u32[]{:S(2)}) copy-start(f32[2048]{0:T(1024)S(1)} %broadcast_multiply_fusion) | copy-start | bytes 24580
  530.8 441.2 %copy-start.34 = (f32[2048,16]{0,1:T(8,128)}, f32[2048,16]{0,1:T(8,128)S(1)}, u32[]{:S(2)}) copy-start(f32[2048,16]{0,1:T(8,128)S(1)} %get-tuple-element.198) | copy-start | bytes 393220
  530.8 441.2 %copy-start.38 = (f32[2048,16]{0,1:T(8,128)}, f32[2048,16]{0,1:T(8,128)S(1)}, u32[]{:S(2)}) copy-start(f32[2048,16]{0,1:T(8,128)S(1)} %get-tuple-element.199) | copy-start | bytes 393220
  530.8 425.2 %copy-start.61 = (f32[768]{0:T(1024)S(1)}, f32[768]{0:T(1024)}, u32[]{:S(2)}) copy-start(f32[768]{0:T(1024)} %copy-done.60) | copy-start | bytes 9220
  543.8 421.1 %copy-start.43 = (bf16[3,768,192]{1,2,0:T(8,128)(2,1)S(1)}, bf16[3,768,192]{1,2,0:T(8,128)(2,1)}, u32[]{:S(2)}) copy-start(bf16[3,768,192]{1,2,0:T(8,128)(2,1)} %copy-done.42) | copy-start | bytes 2654212
  543.8 421.1 %copy-start.90 = (f32[768]{0:T(1024)S(1)}, f32[768]{0:T(1024)}, u32[]{:S(2)}) copy-start(f32[768]{0:T(1024)} %copy-done.89) | copy-start | bytes 9220
  973.7 114.6 %all-gather.16.cloned.1.call-start = ((), (), s32[]{:S(2)}) async-start(), calls=%async_computation.13 | async-start | bytes 2359296 | tf_op jit(solution)/shard_map/all_gather | solution.py:137
  1015.9 396.0 %reduce-scatter.21.cloned.1.call-start = ((), (), s32[]{:S(2)}) async-start(), calls=%async_computation.18 | async-start | bytes 4718592 | tf_op jit(solution)/shard_map/reduce_scatter | solution.py:214
  1264.2 152.5 %reduce-scatter.23.cloned.1.call-start = ((), (), s32[]{:S(2)}) async-start(), calls=%async_computation.19 | async-start | bytes 4718592 | tf_op jit(solution)/shard_map/reduce_scatter | solution.py:217
  1310.5 180.7 %reduce-scatter.33.cloned.1.call-start = ((), (), s32[]{:S(2)}) async-start(), calls=%async_computation.24 | async-start | bytes 73728
  1342.8 149.7 %reduce-scatter.31.cloned.1.call-start = ((), (), s32[]{:S(2)}) async-start(), calls=%async_computation.23 | async-start | bytes 884736
  1411.6 84.6 %reduce-scatter.29.cloned.1.call-start = ((), (), s32[]{:S(2)}) async-start(), calls=%async_computation.22 | async-start | bytes 2211840
  1433.6 895.1 %all-reduce.36.cloned.1.call-start = ((), (), s32[]{:S(2)}) async-start(), calls=%async_computation.25 | async-start | bytes 50331648 | tf_op jit(solution)/shard_map/psum | solution.py:145
  1464.2 947.5 %reduce-scatter.25.cloned.1.call-start = ((), (), s32[]{:S(2)}) async-start(), calls=%async_computation.20 | async-start | bytes 2654208 | tf_op jit(solution)/shard_map/reduce_scatter | solution.py:257
  1477.8 942.7 %reduce-scatter.27.cloned.1.call-start = ((), (), s32[]{:S(2)}) async-start(), calls=%async_computation.21 | async-start | bytes 2654208 | tf_op jit(solution)/shard_map/reduce_scatter | solution.py:259
  1492.6 852.3 %slice-start.2 = ((s8[6291456]{0:T(1024)(128)(4,1)}), s8[2097152]{0:T(1024)(128)(4,1)S(1)}, s32[]{:S(2)}) async-start(s8[6291456]{0:T(1024)(128)(4,1)} %bitcast.326), calls=%async_computation.28 | async-start | bytes 4194304
  (113 other events, 1860.5 us)
Sparse Core Ops, SparseCore 0:
  97.0 28.3 all-gather.9
  127.0 27.3 all-gather.7
  156.2 24.0 all-gather.11
  182.1 24.0 all-gather.13
  402.8 44.0 reduce-scatter.16
  466.3 44.1 reduce-scatter.18
  529.9 426.0 all-reduce.33
  973.8 26.1 all-gather.17
  1016.0 26.0 all-gather.15
  1264.3 42.4 reduce-scatter.20
  1310.6 42.7 reduce-scatter.22
  1356.8 33.2 reduce-scatter.32
  1411.7 34.3 reduce-scatter.30
  1449.7 40.2 reduce-scatter.28
  1493.3 835.3 all-reduce.35
  2332.8 41.3 reduce-scatter.24
  2378.0 42.4 reduce-scatter.26
where the time goes:
time: 2440 us; the launch traced here: 2430 us
  waiting for transfers between devices  1260 us (52%)
  matrix products  615 us (25%)
  other arithmetic  355 us (15%)
  blocking collectives  128 us (5%)
  local copies, waits for them, and re-layouts  54 us (2%)
    psum x1, waiting for transfers between devices, body(): lax.psum(jnp.dot(attended_low, dense_w, preferred_element_type=jnp.float3...  831 us
    psum x1, waiting for transfers between devices, body(): both_full = lax.psum(jnp.concatenate([first, second], axis=1), 'mp')  412 us
    convert_element_type x2, other arithmetic, score_grads(): grad_scores = (soft_full * (grad_soft - row_terms)).astype(jnp.bfloat16)  163 us
    dot_general x2, matrix products, score_grads(): jnp.einsum('qhd,khd->hqk', grad_out, values_all, preferred_element_type=j...  144 us
    dot_general x2, matrix products, body(): jnp.einsum('hqk,qhd->khd', soft_low, grad_out, preferred_element_type=jnp...  78.8 us
    dot_general x2, matrix products, attend(): jnp.einsum('hqk,khd->qhd', soft_low, values_all, preferred_element_type=j...  77.5 us
    dot_general x2, matrix products, masked_scores(): jnp.einsum('qhd,khd->hqk', queries, keys_all, preferred_element_type=jnp....  76 us
    reduce_sum x2, other arithmetic, attend(): jnp.sum(jnp.exp(scores - row_max), axis=-1, keepdims=True)  69 us
  transfers between devices with their start and end apart: 17, of which 4 were waited for; matrix products, arithmetic and copies ran while one was open for 32% of the time, Pallas kernels for 0%

commit v1 on v0

v1 whole, which is shorter than its diff:
```python
import functools

import jax
import jax.numpy as jnp
from jax import lax
from jax.experimental import pallas as pl
from jax.experimental.pallas import tpu as pltpu
from jax.sharding import Mesh
from jax.sharding import PartitionSpec as P

HD = 64
ROT = 16
LANES = 128
F32 = jnp.float32
BF16 = jnp.bfloat16
LOG2E = 1.4426950408889634
norm_eps = 1e-05
masked_value = -1e30
vmem_bytes = 60 * 2**20

NN = (((1,), (0,)), ((), ()))
NT = (((1,), (1,)), ((), ()))
TN = (((0,), (0,)), ((), ()))


def dot(left, right, dims):
    return lax.dot_general(left, right, dims, preferred_element_type=F32)


def normalise(rows):
    centre = jnp.mean(rows, axis=-1, keepdims=True)
    deviate = rows - centre
    spread = jnp.mean(deviate * deviate, axis=-1, keepdims=True)
    scale = lax.rsqrt(spread + norm_eps)
    return deviate * scale, scale


def turn(chunk, cosines, sine_low, sine_high):
    half = ROT // 2
    return (
        chunk * cosines
        + pltpu.roll(chunk, LANES - half, 1) * sine_low
        + pltpu.roll(chunk, half, 1) * sine_high
    )


def whole(shape):
    return pl.BlockSpec(shape, lambda *_: (0,) * len(shape))


def params(**kwargs):
    return pltpu.CompilerParams(vmem_limit_bytes=vmem_bytes, **kwargs)


def front_kernel(
    which, x_ref, dy_ref, w_ref, wb_ref, dense_ref, gain_ref, shift_ref, cos_ref, low_ref, high_ref,
    q_ref, kv_ref, do_ref,
):
    half = q_ref.shape[1]
    xhat, _ = normalise(x_ref[0].astype(F32))
    normed = (xhat * gain_ref[...] + shift_ref[...]).astype(BF16)
    proj = dot(normed, w_ref[...], NN) + wb_ref[...]
    cosines, low, high = cos_ref[...], low_ref[...], high_ref[...]
    for j in range(half // LANES):
        at = slice(j * LANES, (j + 1) * LANES)
        query = turn(proj[:, at], cosines, low, high).astype(BF16)
        q_ref[:, at] = query * BF16(HD**-0.5)
        key = proj[:, half + j * LANES : half + (j + 1) * LANES]
        kv_ref[:, at] = turn(key, cosines, low, high).astype(BF16)
    kv_ref[:, half:] = proj[:, 2 * half :].astype(BF16)
    do_ref[...] = dot(dy_ref[0], dense_ref[...], NN).astype(BF16)


def front(which, x, dy, w, wb, dense, gain, shift, tables):
    _, rows, width = x.shape
    half = dense.shape[1]
    step = min(512, rows)
    chosen = pl.BlockSpec((1, step, width), lambda i, which: (which[0], i, 0))
    by_row = lambda cols: pl.BlockSpec((step, cols), lambda i, *_: (i, 0))
    return pl.pallas_call(
        front_kernel,
        grid_spec=pltpu.PrefetchScalarGridSpec(
            num_scalar_prefetch=1,
            grid=(rows // step,),
            in_specs=[chosen, chosen, whole(w.shape), whole(wb.shape), whole(dense.shape),
                      whole(gain.shape), whole(shift.shape)] + [by_row(LANES)] * 3,
            out_specs=[by_row(half), by_row(2 * half), by_row(half)],
        ),
        out_shape=[
            jax.ShapeDtypeStruct((rows, half), BF16),
            jax.ShapeDtypeStruct((rows, 2 * half), BF16),
            jax.ShapeDtypeStruct((rows, half), BF16),
        ],
        compiler_params=params(),
        cost_estimate=pl.CostEstimate(
            flops=2 * rows * width * 4 * half, bytes_accessed=12 * rows * width, transcendentals=0
        ),
        name="front",
    )(which, x, dy, w, wb, dense, gain, shift, *tables)


def feed_kernel(
    which, x_ref, dy_ref, up_ref, upb_ref, down_ref, gain_ref, shift_ref, gain_col, shift_col,
    part_ref, dx_ref, gup_ref, gdown_ref, vec_ref, gupb_ref,
    up_acc, down_acc, sum_acc, dy_acc,
):
    step = pl.program_id(0)

    @pl.when(step == 0)
    def _():
        up_acc[...] = jnp.zeros_like(up_acc)
        down_acc[...] = jnp.zeros_like(down_acc)
        sum_acc[...] = jnp.zeros_like(sum_acc)
        dy_acc[...] = jnp.zeros_like(dy_acc)

    xhat, _ = normalise(x_ref[0].astype(F32))
    dy = dy_ref[0]
    normed = (xhat * gain_ref[...] + shift_ref[...]).astype(BF16)
    hidden = dot(normed, up_ref[...], NN) + upb_ref[...]
    share = 0.5 * (1.0 + lax.erf(hidden * F32(0.5**0.5)))
    act = (hidden * share).astype(BF16)
    slope = share + hidden * (jnp.exp(hidden * hidden * -0.5) * F32(0.3989422804014327))
    part_ref[...] = dot(act, down_ref[...], NT).astype(part_ref.dtype)
    grad = dot(dy, down_ref[...], NN) * slope
    grad_low = grad.astype(BF16)
    dx_ref[...] = (dot(grad_low, up_ref[...], NT) * gain_ref[...]).astype(dx_ref.dtype)
    up_acc[...] += dot(xhat.astype(BF16), grad_low, TN)
    down_acc[...] += dot(dy, act, TN)
    sum_acc[...] += jnp.sum(grad_low.astype(F32), axis=0, keepdims=True)
    dy_acc[...] += jnp.sum(dy.astype(F32), axis=0, keepdims=True)

    @pl.when(step == pl.num_programs(0) - 1)
    def _():
        sums = sum_acc[...]
        raw = up_acc[...]
        up = up_ref[...].astype(F32)
        gup_ref[...] = (raw * gain_col[...] + shift_col[...] * sums).astype(gup_ref.dtype)
        gdown_ref[...] = down_acc[...].astype(gdown_ref.dtype)
        gupb_ref[...] = sums
        lane = lax.broadcasted_iota(jnp.int32, vec_ref.shape, 1)
        gain_grad = jnp.sum(raw * up, axis=1, keepdims=True)
        shift_grad = jnp.sum(up * sums, axis=1, keepdims=True)
        dy_col = jnp.transpose(jnp.broadcast_to(dy_acc[...], (LANES, dy_acc.shape[1])))
        vec_ref[...] = jnp.where(
            lane == 0, dy_col * 0.5,
            jnp.where(lane == 3, gain_grad, jnp.where(lane == 4, shift_grad, 0.0)),
        )


def feed(which, x, dy, up, upb, down, gain, shift, gain_col, shift_col):
    _, rows, width = x.shape
    units = up.shape[1]
    step = min(256, rows)
    chosen = pl.BlockSpec((1, step, width), lambda i, which: (which[0], i, 0))
    by_row = pl.BlockSpec((step, width), lambda i, *_: (i, 0))
    return pl.pallas_call(
        feed_kernel,
        grid_spec=pltpu.PrefetchScalarGridSpec(
            num_scalar_prefetch=1,
            grid=(rows // step,),
            in_specs=[chosen, chosen, whole(up.shape), whole(upb.shape), whole(down.shape),
                      whole(gain.shape), whole(shift.shape), whole(gain_col.shape), whole(shift_col.shape)],
            out_specs=[by_row, by_row, whole((width, units)), whole((width, units)),
                       whole((width, LANES)), whole((1, units))],
            scratch_shapes=[pltpu.VMEM((width, units), F32), pltpu.VMEM((width, units), F32),
                            pltpu.VMEM((1, units), F32), pltpu.VMEM((1, width), F32)],
        ),
        out_shape=[
            jax.ShapeDtypeStruct((rows, width), BF16),
            jax.ShapeDtypeStruct((rows, width), BF16),
            jax.ShapeDtypeStruct((width, units), BF16),
            jax.ShapeDtypeStruct((width, units), BF16),
            jax.ShapeDtypeStruct((width, LANES), F32),
            jax.ShapeDtypeStruct((1, units), F32),
        ],
        compiler_params=params(),
        cost_estimate=pl.CostEstimate(
            flops=12 * rows * width * units, bytes_accessed=24 * width * units, transcendentals=2 * rows * units
        ),
        name="feed",
    )(which, x, dy, up, upb, down, gain, shift, gain_col, shift_col)


def lane_fold(values, combine):
    total = values[:, :LANES]
    for j in range(1, values.shape[1] // LANES):
        total = combine(total, values[:, j * LANES : (j + 1) * LANES])
    return total


def attention_kernel(
    runs, slots, q_ref, g_ref, k_ref, v_ref, o_ref, dq_ref, dk_ref, dv_ref,
    score_ref, soft_ref, acc_ref, *, block, per_run,
):
    step = pl.program_id(1)

    @pl.when(step == 0)
    def _():
        dk_ref[...] = jnp.zeros_like(dk_ref)
        dv_ref[...] = jnp.zeros_like(dv_ref)

    full = runs[step // per_run] * per_run + step % per_run
    lane = lax.broadcasted_iota(jnp.int32, (block, LANES), 1)
    heads = (lane < HD, lane >= HD)
    both_q, both_g = q_ref[...], g_ref[...]
    queries = [jnp.where(mine, both_q, jnp.zeros_like(both_q)) for mine in heads]
    grads = [jnp.where(mine, both_g, jnp.zeros_like(both_g)) for mine in heads]

    def rows_of(at):
        start = (slots[at // per_run] * per_run + at % per_run) * block
        return pl.ds(pl.multiple_of(start, block), block)

    def score(at, tops, masked):
        keys = k_ref[rows_of(at), :]
        out = []
        for h in range(2):
            scores = dot(queries[h], keys, NT)
            if masked:
                row = lax.broadcasted_iota(jnp.int32, (block, block), 0)
                col = lax.broadcasted_iota(jnp.int32, (block, block), 1)
                scores = jnp.where(col <= row, scores, masked_value)
            score_ref[h, at] = scores
            out.append(jnp.maximum(tops[h], lane_fold(scores, jnp.maximum)))
        return tuple(out)

    least = jnp.full((block, LANES), masked_value, F32)
    tops = lax.fori_loop(0, full, lambda at, carry: score(at, carry, False), (least, least))
    tops = score(full, tops, True)
    tops = [jnp.max(top, axis=1, keepdims=True) * F32(LOG2E) for top in tops]

    acc_ref[...] = jnp.zeros_like(acc_ref)

    def weigh(at, totals):
        values = v_ref[rows_of(at), :]
        out = []
        for h in range(2):
            soft = jnp.exp2(score_ref[h, at] * F32(LOG2E) - tops[h])
            out.append(totals[h] + lane_fold(soft, jnp.add))
            soft_low = soft.astype(BF16)
            soft_ref[h, at] = soft_low
            acc_ref[h] += dot(soft_low, values, NN)
        return tuple(out)

    nought = jnp.zeros((block, LANES), F32)
    totals = lax.fori_loop(0, full + 1, weigh, (nought, nought))
    shares = [1.0 / jnp.sum(total, axis=1, keepdims=True) for total in totals]
    attended = jnp.where(heads[0], acc_ref[0] * shares[0], acc_ref[1] * shares[1])
    o_ref[...] = attended.astype(o_ref.dtype)
    product = attended * both_g.astype(F32)
    row_terms = [
        jnp.sum(jnp.where(heads[h], product, 0.0), axis=1, keepdims=True) * shares[h] for h in range(2)
    ]
    scaled = [(grads[h].astype(F32) * shares[h]).astype(BF16) for h in range(2)]

    acc_ref[...] = jnp.zeros_like(acc_ref)

    def back(at, carry):
        there = rows_of(at)
        keys, values = k_ref[there, :], v_ref[there, :]
        key_terms, value_terms = [], []
        for h in range(2):
            soft_low = soft_ref[h, at]
            grad_soft = dot(scaled[h], values, NT)
            grad_score = (soft_low.astype(F32) * (grad_soft - row_terms[h])).astype(BF16)
            acc_ref[h] += dot(grad_score, keys, NN)
            key_terms.append(dot(grad_score, queries[h], TN))
            value_terms.append(dot(soft_low, scaled[h], TN))
        dk_ref[there, :] += key_terms[0] + key_terms[1]
        dv_ref[there, :] += value_terms[0] + value_terms[1]
        return carry

    lax.fori_loop(0, full + 1, back, 0)
    dq_ref[...] = (jnp.where(heads[0], acc_ref[0], acc_ref[1]) * F32(HD**-0.5)).astype(dq_ref.dtype)


def attention(runs, slots, q, g, kv):
    rows, width = q.shape
    keys = kv.shape[0]
    run_rows = rows // 2
    block = min(512, run_rows)
    per_run = run_rows // block
    pairs = width // LANES
    by_query = pl.BlockSpec((block, LANES), lambda p, i, *_: (i, p))
    return pl.pallas_call(
        functools.partial(attention_kernel, block=block, per_run=per_run),
        grid_spec=pltpu.PrefetchScalarGridSpec(
            num_scalar_prefetch=2,
            grid=(pairs, rows // block),
            in_specs=[
                by_query,
                by_query,
                pl.BlockSpec((keys, LANES), lambda p, i, *_: (0, p)),
                pl.BlockSpec((keys, LANES), lambda p, i, *_: (0, pairs + p)),
            ],
            out_specs=[
                by_query,
                by_query,
                pl.BlockSpec((keys, LANES), lambda p, i, *_: (0, p)),
                pl.BlockSpec((keys, LANES), lambda p, i, *_: (0, p)),
            ],
            scratch_shapes=[
                pltpu.VMEM((2, keys // block, block, block), F32),
                pltpu.VMEM((2, keys // block, block, block), BF16),
                pltpu.VMEM((2, block, LANES), F32),
            ],
        ),
        out_shape=[
            jax.ShapeDtypeStruct((rows, width), BF16),
            jax.ShapeDtypeStruct((rows, width), BF16),
            jax.ShapeDtypeStruct((keys, width), F32),
            jax.ShapeDtypeStruct((keys, width), F32),
        ],
        compiler_params=params(),
        cost_estimate=pl.CostEstimate(
            flops=24 * rows * keys * width, bytes_accessed=24 * keys * width,
            transcendentals=rows * keys * pairs,
        ),
        name="attention",
    )(runs, slots, q, g, kv, kv)


def back_kernel(
    dq_ref, own_k, own_v, got_ref, w_ref, gain_ref, dx_in, cos_ref, low_ref, high_ref, dproj_ref, dx_ref
):
    half = dq_ref.shape[1]
    cosines, low, high = cos_ref[...], low_ref[...], high_ref[...]
    for j in range(half // LANES):
        at = slice(j * LANES, (j + 1) * LANES)
        query = dq_ref[:, at].astype(F32)
        dproj_ref[:, at] = turn(query, cosines, -low, -high).astype(BF16)
        key = own_k[:, at] + got_ref[:, at].astype(F32)
        dproj_ref[:, half + j * LANES : half + (j + 1) * LANES] = turn(key, cosines, -low, -high).astype(BF16)
    dproj_ref[:, 2 * half :] = (own_v[...] + got_ref[:, half:].astype(F32)).astype(BF16)
    summed = dot(dproj_ref[...], w_ref[...], NT) * gain_ref[...] + dx_in[...].astype(F32)
    dx_ref[...] = summed.astype(dx_ref.dtype)


def back(dq, dk, dv, got, w, gain, dx_part, tables):
    rows, half = dq.shape
    width = w.shape[0]
    step = min(512, rows)
    by_row = lambda cols: pl.BlockSpec((step, cols), lambda i: (i, 0))
    return pl.pallas_call(
        back_kernel,
        grid=(rows // step,),
        in_specs=[by_row(half), by_row(half), by_row(half), by_row(2 * half), whole(w.shape),
                  whole(gain.shape), by_row(width)] + [by_row(LANES)] * 3,
        out_specs=[by_row(3 * half), by_row(width)],
        out_shape=[
            jax.ShapeDtypeStruct((rows, 3 * half), BF16),
            jax.ShapeDtypeStruct((rows, width), BF16),
        ],
        compiler_params=params(),
        cost_estimate=pl.CostEstimate(
            flops=6 * rows * width * half, bytes_accessed=12 * rows * width, transcendentals=0
        ),
        name="back",
    )(dq, dk, dv, got, w, gain, dx_part, *tables)


def weight_kernel(
    which, x_ref, dy_ref, dproj_ref, o_ref, w_ref, gain_col, shift_col,
    gqkv_ref, gdense_ref, vec_ref, gb_ref, acc, dense_acc, sum_acc,
):
    step = pl.program_id(0)

    @pl.when(step == 0)
    def _():
        acc[...] = jnp.zeros_like(acc)
        dense_acc[...] = jnp.zeros_like(dense_acc)
        sum_acc[...] = jnp.zeros_like(sum_acc)

    xhat, _ = normalise(x_ref[0].astype(F32))
    dproj = dproj_ref[...]
    acc[...] += dot(xhat.astype(BF16), dproj, TN)
    dense_acc[...] += dot(dy_ref[0], o_ref[...], TN)
    sum_acc[...] += jnp.sum(dproj.astype(F32), axis=0, keepdims=True)

    @pl.when(step == pl.num_programs(0) - 1)
    def _():
        sums, raw, w = sum_acc[...], acc[...], w_ref[...].astype(F32)
        gqkv_ref[...] = (raw * gain_col[...] + shift_col[...] * sums).astype(gqkv_ref.dtype)
        gdense_ref[...] = dense_acc[...].astype(gdense_ref.dtype)
        gb_ref[...] = sums
        lane = lax.broadcasted_iota(jnp.int32, vec_ref.shape, 1)
        gain_grad = jnp.sum(raw * w, axis=1, keepdims=True)
        shift_grad = jnp.sum(w * sums, axis=1, keepdims=True)
        vec_ref[...] = jnp.where(lane == 1, gain_grad, jnp.where(lane == 2, shift_grad, 0.0))


def weight_grads(which, x, dy, dproj, o, w, gain_col, shift_col):
    _, rows, width = x.shape
    half = o.shape[1]
    step = min(512, rows)
    chosen = pl.BlockSpec((1, step, width), lambda i, which: (which[0], i, 0))
    by_row = lambda cols: pl.BlockSpec((step, cols), lambda i, *_: (i, 0))
    return pl.pallas_call(
        weight_kernel,
        grid_spec=pltpu.PrefetchScalarGridSpec(
            num_scalar_prefetch=1,
            grid=(rows // step,),
            in_specs=[chosen, chosen, by_row(3 * half), by_row(half), whole(w.shape),
                      whole(gain_col.shape), whole(shift_col.shape)],
            out_specs=[whole((width, 3 * half)), whole((width, half)), whole((width, LANES)), whole((1, 3 * half))],
            scratch_shapes=[pltpu.VMEM((width, 3 * half), F32), pltpu.VMEM((width, half), F32),
                            pltpu.VMEM((1, 3 * half), F32)],
        ),
        out_shape=[
            jax.ShapeDtypeStruct((width, 3 * half), BF16),
            jax.ShapeDtypeStruct((width, half), BF16),
            jax.ShapeDtypeStruct((width, LANES), F32),
            jax.ShapeDtypeStruct((1, 3 * half), F32),
        ],
        compiler_params=params(),
        cost_estimate=pl.CostEstimate(
            flops=8 * rows * width * half, bytes_accessed=12 * rows * width, transcendentals=0
        ),
        name="weight_grads",
    )(which, x, dy, dproj, o, w, gain_col, shift_col)


def norm_back_kernel(which, x_ref, dy_ref, kept_ref, got_ref, out_ref):
    xhat, scale = normalise(x_ref[0].astype(F32))
    grad = kept_ref[...].astype(F32) + got_ref[...].astype(F32)
    centre = jnp.mean(grad, axis=-1, keepdims=True)
    along = jnp.mean(grad * xhat, axis=-1, keepdims=True)
    out_ref[...] = (dy_ref[0].astype(F32) + scale * (grad - centre - xhat * along)).astype(out_ref.dtype)


def norm_back(which, x, dy, kept, got):
    rows, width = got.shape
    step = min(512, rows)
    blocks = rows // step
    chosen = pl.BlockSpec((1, step, width), lambda i, which: (which[0], which[1] * blocks + i, 0))
    return pl.pallas_call(
        norm_back_kernel,
        grid_spec=pltpu.PrefetchScalarGridSpec(
            num_scalar_prefetch=1,
            grid=(blocks,),
            in_specs=[chosen, chosen,
                      pl.BlockSpec((step, width), lambda i, which: (which[1] * blocks + i, 0)),
                      pl.BlockSpec((step, width), lambda i, *_: (i, 0))],
            out_specs=pl.BlockSpec((step, width), lambda i, *_: (i, 0)),
        ),
        out_shape=jax.ShapeDtypeStruct((rows, width), BF16),
        compiler_params=params(),
        cost_estimate=pl.CostEstimate(
            flops=20 * rows * width, bytes_accessed=10 * rows * width, transcendentals=0
        ),
        name="norm_back",
    )(which, x, dy, kept, got)


def swap(values, axis):
    return lax.ppermute(values, axis, [(0, 1), (1, 0)])


def rotation_tables(positions):
    half = ROT // 2
    frequency = jnp.power(F32(10000.0), -2.0 * jnp.arange(half, dtype=F32) / ROT)
    angles = frequency[:, None] * positions.astype(F32)[None, :]
    cosines, sines = lax.optimization_barrier((jnp.cos(angles), jnp.sin(angles)))
    cosines, sines = cosines.T, sines.T
    rows = positions.shape[0]
    rest = jnp.zeros((rows, HD - ROT), F32)
    blank = jnp.zeros((rows, half), F32)
    per_head = (
        jnp.concatenate([cosines, cosines, rest + 1.0], axis=1),
        jnp.concatenate([-sines, blank, rest], axis=1),
        jnp.concatenate([blank, sines, rest], axis=1),
    )
    return tuple(jnp.tile(table, (1, LANES // HD)) for table in per_head)


def body(
    tokens, places, w_qkv, b_qkv, w_dense, b_dense, w_up, b_up, w_down, b_down,
    norm1_gain, norm1_bias, norm2_gain, norm2_bias, out_grad, *, seq_size, owners,
):
    _, rows, width = tokens.shape
    share = width // owners
    heads = b_qkv.shape[1]
    cols = heads * HD
    units = w_up.shape[1]
    splits = ("dp", "seq", "mh")
    side, part = lax.axis_index("mh"), lax.axis_index("ml")
    which = jnp.stack([side, part]).astype(jnp.int32)

    def column(vector):
        vector = vector.reshape(-1)
        return jnp.pad(vector, (0, share - vector.shape[0]))[:, None]

    small = jnp.concatenate(
        [column(v) for v in (b_dense, b_down, norm1_gain, norm1_bias, norm2_gain, norm2_bias, b_qkv, b_up)],
        axis=1,
    )
    small = jnp.pad(small, ((0, 0), (0, LANES - small.shape[1])))
    first = jnp.concatenate([w_qkv.transpose(1, 0, 2).reshape(share, 3 * cols), w_dense.T, small], axis=1)
    second = jnp.concatenate([w_up, w_down.T], axis=1)
    first = lax.all_gather(first, splits, axis=0, tiled=True).reshape(owners, 2, share, -1)
    second = lax.all_gather(second, splits, axis=0, tiled=True).reshape(owners, 2, share, -1)

    def laid(pack, start, count):
        piece = pack[:, :, :, start : start + count].transpose(0, 2, 1, 3)
        return piece.reshape(width, 2, count)

    qkv_w = laid(first, 0, 3 * cols).reshape(width, 2, 3, cols).transpose(0, 2, 1, 3).reshape(width, 6 * cols)
    dense_w = laid(first, 3 * cols, cols).reshape(width, 2 * cols)
    up_w = laid(second, 0, units).reshape(width, 2 * units)
    down_w = laid(second, units, units).reshape(width, 2 * units)
    small = first[:, :, :, 4 * cols :].astype(F32)
    vectors = small[:, 0].reshape(width, LANES)
    piece = HD // owners
    qkv_b = small[:, :, : 3 * heads * piece, 6].reshape(owners, 2, 3, heads, piece)
    qkv_b = qkv_b.transpose(2, 1, 3, 0, 4).reshape(1, 6 * cols)
    up_rows, up_cols = b_up.shape
    up_b = small[:, :, :, 7].reshape(owners, 2, up_rows, up_cols).transpose(1, 2, 0, 3).reshape(1, 2 * units)
    row_of = lambda index: vectors[:, index].reshape(1, width)
    column_of = lambda index: vectors[:, index].reshape(width, 1)

    my_places = lax.dynamic_index_in_dim(places, side, 0, keepdims=False)
    run_rows = rows // 2
    runs = jnp.stack([my_places[0], my_places[run_rows]]) // run_rows
    if seq_size == 2:
        all_runs = jnp.concatenate([runs, swap(runs, "seq")])
    else:
        all_runs = lax.all_gather(runs, "seq", axis=0, tiled=True)
    order = jnp.arange(2 * seq_size, dtype=jnp.int32)
    slots = jnp.sum(jnp.where(all_runs[None, :] == order[:, None], order[None, :], 0), axis=1)
    tables = rotation_tables(my_places)

    q, kv, grad_o = front(which, tokens, out_grad, qkv_w, qkv_b, dense_w, row_of(2), row_of(3), tables)
    if seq_size == 2:
        kv_all = jnp.concatenate([kv, swap(kv, "seq")], axis=0)
    else:
        kv_all = lax.all_gather(kv, "seq", axis=0, tiled=True)

    mlp_part, mlp_dx, grad_up, grad_down, mlp_vectors, grad_up_b = feed(
        which, tokens, out_grad, up_w, up_b, down_w, row_of(4), row_of(5), column_of(4), column_of(5)
    )

    def spread(grad):
        return grad.reshape(owners, share, 2, -1).transpose(0, 2, 1, 3)

    def scatter(pack):
        return lax.psum_scatter(
            pack.reshape(owners * 2 * share, -1), splits, scatter_dimension=0, tiled=True
        )

    owned_second = scatter(jnp.concatenate([spread(grad_up), spread(grad_down)], axis=3))

    attended, dq, dk, dv = attention(runs, slots, q, grad_o, kv_all)

    half_rows = rows // 2

    def half_of(array, index):
        return lax.dynamic_slice_in_dim(array, index * half_rows, half_rows, axis=0)

    def branch_sum(index):
        product = lax.dot_general(half_of(attended, index), dense_w, NT, preferred_element_type=F32)
        return product + half_of(mlp_part, index).astype(F32)

    got_mixed = swap(branch_sum(1 - part).astype(BF16), "ml")
    my_tokens = lax.dynamic_slice(tokens, (side, part * half_rows, 0), (1, half_rows, width))[0]
    mixed = branch_sum(part) + got_mixed.astype(F32) + my_tokens.astype(F32) + row_of(0) + row_of(1)
    mixed = lax.all_gather(mixed.astype(BF16), ("mh", "ml"), axis=0, tiled=True).reshape(tokens.shape)

    if seq_size == 2:
        got = swap(jnp.concatenate([dk[rows:], dv[rows:]], axis=1).astype(BF16), "seq")
        dk, dv = dk[:rows], dv[:rows]
    else:
        got = lax.psum_scatter(
            jnp.concatenate([dk, dv], axis=1).astype(BF16), "seq", scatter_dimension=0, tiled=True
        )
        dk = dv = jnp.zeros(dq.shape, F32)
    dproj, dx = back(dq, dk, dv, got, qkv_w, row_of(2), mlp_dx, tables)
    got_dx = swap(half_of(dx, 1 - part), "ml")
    input_grad = norm_back(which, tokens, out_grad, dx, got_dx)
    input_grad = lax.all_gather(input_grad, ("mh", "ml"), axis=0, tiled=True).reshape(tokens.shape)

    grad_qkv, grad_dense, qkv_vectors, grad_qkv_b = weight_grads(
        which, tokens, out_grad, dproj, attended, qkv_w, column_of(2), column_of(3)
    )

    vector_grads = (mlp_vectors + qkv_vectors)[:, :5].reshape(owners, 1, share, 5)
    vector_grads = jnp.broadcast_to(vector_grads, (owners, 2, share, 5))
    bias_qkv = grad_qkv_b.reshape(3, 2, heads, owners, piece).transpose(3, 1, 0, 2, 4)
    bias_qkv = bias_qkv.reshape(owners, 2, 3 * heads * piece)
    bias_qkv = jnp.pad(bias_qkv, ((0, 0), (0, 0), (0, share - 3 * heads * piece)))[..., None]
    bias_up = grad_up_b.reshape(2, up_rows, owners, up_cols).transpose(2, 0, 1, 3).reshape(owners, 2, share, 1)
    tail = jnp.concatenate([vector_grads, bias_qkv, bias_up], axis=3)
    tail = jnp.pad(tail, ((0, 0), (0, 0), (0, 0), (0, LANES - 7))).astype(BF16)
    grad_qkv = grad_qkv.reshape(owners, share, 3, 2, cols).transpose(0, 3, 1, 2, 4)
    grad_qkv = grad_qkv.reshape(owners, 2, share, 3 * cols)
    owned_first = scatter(jnp.concatenate([grad_qkv, spread(grad_dense), tail], axis=3)).astype(F32)
    owned_second = owned_second.astype(F32)

    vectors = owned_first[:, 4 * cols :]
    norms = vectors[:, :5]
    norms = norms + swap(norms, "ml")
    bias_grad = norms[:, 0]
    return (
        mixed,
        input_grad,
        owned_first[:, : 3 * cols].reshape(share, 3, cols).transpose(1, 0, 2),
        vectors[: 3 * heads * piece, 5].reshape(b_qkv.shape),
        owned_first[:, 3 * cols : 4 * cols].T,
        bias_grad,
        owned_second[:, :units],
        vectors[:, 6].reshape(b_up.shape),
        owned_second[:, units:].T,
        bias_grad,
        norms[:, 1],
        norms[:, 2],
        norms[:, 3],
        norms[:, 4],
    )


def solution(mesh):
    dp, seq, mp = (mesh.shape[axis] for axis in ("dp", "seq", "mp"))
    split = Mesh(mesh.devices.reshape(dp, seq, 2, mp // 2), ("dp", "seq", "mh", "ml"))
    mp, owner = ("mh", "ml"), ("dp", "seq")
    row = P("dp", "seq", None)
    vector = P(owner)
    weights = (
        P(None, owner, mp), P(None, mp, owner), P(mp, owner), vector, P(owner, mp), P(mp, owner),
        P(mp, owner), vector, vector, vector, vector, vector,
    )
    return jax.shard_map(
        functools.partial(body, seq_size=seq, owners=dp * seq),
        mesh=split,
        in_specs=(row, P("dp", "seq")) + weights + (row,),
        out_specs=(row, row) + weights,
        check_vma=False,
    )
```

time: 2440 us -> 890 us (0.36)
  waiting for transfers between devices: 1260 us -> 468 us
  matrix products: 615 us -> 8.93 us
  other arithmetic: 355 us -> 27.5 us
  Pallas kernels: 0 us -> 232 us
  blocking collectives: 128 us -> 0 us
  local copies, waits for them, and re-layouts: 54 us -> 124 us
    psum x2 -> x0, waiting for transfers between devices: 1240 us -> none  [the longest x1 831 us: body(): lax.psum(jnp.dot(attended_low, dense_w, preferred_element_type=jnp.float3...]
    dot_general x34 -> x2, matrix products: 607 us -> 8.93 us  [branch_sum(): lax.dot_general(half_of(attended, index), dense_w, NT, preferred_element_...]
    all_gather x6 -> x4, waiting for transfers between devices: 0.1 us -> 270 us  [the longest x1 115 us: body(): lax.all_gather(input_grad, ('mh', 'ml'), axis=0, tiled=True)]
    pallas_call x0 -> x6, Pallas kernels: none -> 232 us  [the longest x1 144 us: attention(): pl.pallas_call(functools.partial(attention_kernel, block=block, per_run=p...]
    ppermute x0 -> x6, waiting for transfers between devices: none -> 177 us  [swap(): return lax.ppermute(values, axis, [(0, 1), (1, 0)])]
    convert_element_type x10 -> x4, other arithmetic: 164 us -> 2.84 us  [the longest x1 1.06 us: body(): small = first[:, :, :, 4 * cols:].astype(F32)]
    reduce_sum x11 -> x1, other arithmetic: 128 us -> 0.63 us  [body(): jnp.sum(jnp.where(all_runs[None, :] == order[:, None], order[None, :], 0)...]
    all_gather x5 -> x0, blocking collectives: 77.6 us -> none  [the longest x1 22.8 us: body(): lax.all_gather(w_qkv, ('dp', 'seq'), axis=1, tiled=True)]
  transfers between devices with their start and end apart: 17 -> 12, of which waited for: 4 -> 8; matrix products, arithmetic and copies ran while one was open for 32% -> 10% of each run, Pallas kernels for 0% -> 22%
where the time goes in v1:
time: 890 us; the launch traced here: 882 us
  waiting for transfers between devices  468 us (53%)
  Pallas kernels  232 us (26%)
  local copies, waits for them, and re-layouts  124 us (14%)
  other arithmetic  27.5 us (3%)
  between operations  15 us (2%)
  matrix products  8.93 us (1%)
    ppermute x6, waiting for transfers between devices, swap(): return lax.ppermute(values, axis, [(0, 1), (1, 0)])  177 us
    pallas_call x1, Pallas kernels, attention(): pl.pallas_call(functools.partial(attention_kernel, block=block, per_run=p...  144 us
    all_gather x1, waiting for transfers between devices, body(): lax.all_gather(input_grad, ('mh', 'ml'), axis=0, tiled=True)  115 us
    all_gather x1, waiting for transfers between devices, body(): lax.all_gather(mixed.astype(BF16), ('mh', 'ml'), axis=0, tiled=True)  113 us
    all_gather x1, waiting for transfers between devices, body(): lax.all_gather(first, splits, axis=0, tiled=True)  42.2 us
    pallas_call x1, Pallas kernels, feed(): pl.pallas_call(feed_kernel, grid_spec=pltpu.PrefetchScalarGridSpec(num_sc...  42.2 us
    unnamed x47, local copies, waits for them, and re-layouts  28.1 us
    reduce_scatter x1, waiting for transfers between devices, scatter(): lax.psum_scatter(pack.reshape(owners * 2 * share, -1), splits, scatter_di...  20.5 us
  transfers between devices with their start and end apart: 12, of which 8 were waited for; matrix products, arithmetic and copies ran while one was open for 10% of the time, Pallas kernels for 22%

profile of v1, /device:TPU:0, one launch (start us, length us, event | category | flops | bytes accessed | tf_op | source)
XLA Modules:
  0.0 882.3 jit_solution(2299061686854511537)
XLA Ops:
  18.7 42.2 %all-gather.5.cloned.1.call-done = bf16[1536,896]{1,0:T(8,128)(2,1)} async-done(((bf16[96,896]{1,0:T(8,128)(2,1)}), bf16[1536,896]{1,0:T(8,128)(2,1)}) %all-gather.5.cloned.1.call-update) | async-done | bytes 2752528 | tf_op jit(solution)/shard_map/all_gather | solution.py:499
  87.3 12.3 %front.1 = (bf16[2048,384]{1,0:T(8,128)(2,1)}, bf16[2048,768]{1,0:T(8,128)(2,1)}, bf16[2048,384]{1,0:T(8,128)(2,1)}) custom-call(s32[2]{0:T(128)} %pad_add_fusion.2.which, bf16[2,2048,768]{2,1,0:T(8,128)(2,1)} %x_ref.7, bf16[2,2048,768]{2,1,0:T(8,128)(2,1)} %dy_ref.7, bf16[768,1152]{1,0:T(8,128)(2,1)} %copy.109.w_ref, f32[1,1152]{1,0:T(1,128)} %reshape.127.wb_ref, ...), custom_call_target="tpu_custom_call" | custom-call | flops 4831838208 | bytes 18874368 | tf_op jit(solution)/shard_map/front/pallas_call | solution.py:80
  105.2 79.8 %collective-permute-done = s32[2]{0:T(128)S(1)} collective-permute-done((s32[2]{0:T(128)S(1)}, s32[2]{0:T(128)S(1)}, u32[]{:S(2)}, u32[]{:S(2)}) %collective-permute-start) | collective-permute-done | bytes 40 | tf_op jit(solution)/shard_map/ppermute | solution.py:455
  188.2 6.0 pad_maximum_fusion.k_ref.v_ref
  194.2 144.3 %attention.1 = (bf16[2048,384]{1,0:T(8,128)(2,1)}, bf16[2048,384]{1,0:T(8,128)(2,1)}, f32[4096,384]{1,0:T(8,128)}, f32[4096,384]{1,0:T(8,128)}) custom-call(s32[2]{0:T(128)} %copy-done.18, s32[4]{0:T(128)} %select_reduce_fusion.slots, bf16[2048,384]{1,0:T(8,128)(2,1)} %get-tuple-element.37.q_ref, bf16[2048,384]{1,0:T(8,128)(2,1)} %get-tuple-element.38.g_ref, ...), custom_call_target="tpu_custom_call" | custom-call | flops 77309411328 | bytes 37748736 | tf_op jit(solution)/shard_map/attention/pallas_call | solution.py:284
  362.4 42.2 %feed.1 = (bf16[2048,768]{1,0:T(8,128)(2,1)}, bf16[2048,768]{1,0:T(8,128)(2,1)}, bf16[768,1536]{1,0:T(8,128)(2,1)}, bf16[768,1536]{1,0:T(8,128)(2,1)}, f32[768,128]{1,0:T(8,128)}, /*index=5*/f32[1,1536]{1,0:T(1,128)}) custom-call(s32[2]{0:T(128)} %pad_add_fusion.2.which, bf16[2,2048,768]{2,1,0:T(8,128)(2,1)} %x_ref.7, bf16[2,2048,768]{2,1,0:T(8,128)(2,1)} %dy_ref.7, ...), custom_call_target="tpu_custom_call" | custom-call | flops 28991029248 | bytes 28311552 | tf_op jit(solution)/shard_map/feed/pallas_call | solution.py:156
  406.4 12.6 %collective-permute-done.3.got_ref = bf16[2048,768]{1,0:T(8,128)(2,1)S(1)} collective-permute-done((bf16[2048,768]{1,0:T(8,128)(2,1)}, bf16[2048,768]{1,0:T(8,128)(2,1)S(1)}, u32[]{:S(2)}, u32[]{:S(2)}) %collective-permute-start.3) | collective-permute-done | bytes 3145760 | tf_op jit(solution)/shard_map/ppermute | solution.py:455
  420.6 12.6 %back.1 = (bf16[2048,1152]{1,0:T(8,128)(2,1)}, bf16[2048,768]{1,0:T(8,128)(2,1)}) custom-call(bf16[2048,384]{1,0:T(8,128)(2,1)} %get-tuple-element.42.dq_ref, f32[2048,384]{1,0:T(8,128)} %slice.134.own_k, f32[2048,384]{1,0:T(8,128)} %slice.135.own_v, bf16[2048,768]{1,0:T(8,128)(2,1)} %copy-done.5, bf16[768,1152]{1,0:T(8,128)(2,1)} %copy.109.w_ref, ...), custom_call_target="tpu_custom_call" | custom-call | flops 3623878656 | bytes 18874368 | tf_op jit(solution)/shard_map/back/pallas_call | solution.py:343
  433.2 15.3 %weight_grads.1 = (bf16[768,1152]{1,0:T(8,128)(2,1)}, bf16[768,384]{1,0:T(8,128)(2,1)}, f32[768,128]{1,0:T(8,128)}, f32[1,1152]{1,0:T(1,128)}) custom-call(s32[2]{0:T(128)} %pad_add_fusion.2.which, bf16[2,2048,768]{2,1,0:T(8,128)(2,1)} %x_ref.7, bf16[2,2048,768]{2,1,0:T(8,128)(2,1)} %dy_ref.7, bf16[2048,1152]{1,0:T(8,128)(2,1)} %get-tuple-element.47.dproj_ref, ...), custom_call_target="tpu_custom_call" | custom-call | flops 4831838208 | bytes 18874368 | tf_op jit(solution)/shard_map/weight_grads/pallas_call | solution.py:397
  448.5 6.0 reshape.132
  454.5 5.7 copy.122
  460.2 7.8 concatenate.54
  478.1 5.2 reshape.139
  483.3 6.0 reshape.140
  489.4 8.0 pad_maximum_fusion.1
  497.3 5.6 copy.130
  508.1 43.7 %collective-permute-done.2 = bf16[1024,768]{1,0:T(8,128)(2,1)S(1)} collective-permute-done((bf16[1024,768]{1,0:T(8,128)(2,1)}, bf16[1024,768]{1,0:T(8,128)(2,1)S(1)}, u32[]{:S(2)}, u32[]{:S(2)}) %collective-permute-start.2) | collective-permute-done | bytes 1572896 | tf_op jit(solution)/shard_map/ppermute | solution.py:455
  552.9 5.4 fusion.2
  558.8 41.1 %collective-permute-done.4.got_ref = bf16[1024,768]{1,0:T(8,128)(2,1)S(1)} collective-permute-done((bf16[1024,768]{1,0:T(8,128)(2,1)S(1)}, bf16[1024,768]{1,0:T(8,128)(2,1)S(1)}, u32[]{:S(2)}, u32[]{:S(2)}) %collective-permute-start.4) | collective-permute-done | bytes 1572896 | tf_op jit(solution)/shard_map/ppermute | solution.py:455
  601.0 5.8 norm_back.1
  613.9 20.5 %reduce-scatter.5.cloned.1.call-done = bf16[96,1536]{1,0:T(8,128)(2,1)} async-done(((bf16[1536,1536]{1,0:T(8,128)(2,1)}), bf16[96,1536]{1,0:T(8,128)(2,1)}) %reduce-scatter.5.cloned.1.call-update) | async-done | bytes 294928 | tf_op jit(solution)/shard_map/reduce_scatter | solution.py:545
  637.8 112.9 %all-gather.9.cloned.1.call-done = bf16[4096,768]{1,0:T(8,128)(2,1)} async-done(((bf16[1024,768]{1,0:T(8,128)(2,1)}), bf16[4096,768]{1,0:T(8,128)(2,1)}) %all-gather.9.cloned.1.call-update) | async-done | bytes 6291472 | tf_op jit(solution)/shard_map/all_gather | solution.py:565
  750.7 115.0 %all-gather.11.cloned.1.call-done = bf16[4096,768]{1,0:T(8,128)(2,1)} async-done(((bf16[1024,768]{1,0:T(8,128)(2,1)}), bf16[4096,768]{1,0:T(8,128)(2,1)}) %all-gather.11.cloned.1.call-update) | async-done | bytes 6291472 | tf_op jit(solution)/shard_map/all_gather | solution.py:578
  866.3 6.0 copy.145
  (164 shorter events, 105.5 us)
Async XLA Ops:
  7.2 53.8 %all-gather.5.cloned.1.call-start = ((), (), s32[]{:S(2)}) async-start(), calls=%async_computation.2 | async-start | bytes 2924544 | tf_op jit(solution)/shard_map/all_gather | solution.py:499
  12.3 338.7 %all-gather.7.cloned.1.call-start = ((), (), s32[]{:S(2)}) async-start(), calls=%async_computation.3 | async-start | bytes 5013504 | tf_op jit(solution)/shard_map/all_gather | solution.py:500
  80.8 5.4 copy-start.6
  87.3 13.8 %copy-start.11 = (bf16[768,96]{0,1:T(8,128)(2,1)S(1)}, bf16[768,96]{0,1:T(8,128)(2,1)}, u32[]{:S(2)}) copy-start(bf16[768,96]{0,1:T(8,128)(2,1)} %param.23) | copy-start | bytes 442372
  87.3 13.8 %copy-start.12 = (bf16[96,768]{1,0:T(8,128)(2,1)S(1)}, bf16[96,768]{1,0:T(8,128)(2,1)}, u32[]{:S(2)}) copy-start(bf16[96,768]{1,0:T(8,128)(2,1)} %param.21) | copy-start | bytes 442372
  99.6 88.6 %collective-permute-start.1 = (bf16[2048,768]{1,0:T(8,128)(2,1)}, bf16[2048,768]{1,0:T(8,128)(2,1)}, u32[]{:S(2)}, u32[]{:S(2)}) collective-permute-start(bf16[2048,768]{1,0:T(8,128)(2,1)} %get-tuple-element.39), channel_id=1, source_target_pairs={{0,4},{4,0},{1,5},{5,1},{2,6},{6,2},{3,7},{7,3},{8,12},{12,8},{9,1... | collective-permute-start | bytes 9437192 | tf_op jit(solution)/shard_map/ppermute | solution.py:455
  101.9 505.0 %reduce-scatter.7.cloned.1.call-start = ((), (), s32[]{:S(2)}) async-start(), calls=%async_computation.7 | async-start | bytes 2924544
  104.6 89.6 %copy-start.18 = (s32[2]{0:T(128)}, s32[2]{0:T(128)S(1)}, u32[]{:S(2)}) copy-start(s32[2]{0:T(128)S(1)} %and_select_fusion.runs) | copy-start | bytes 28
  104.6 80.4 %collective-permute-start = (s32[2]{0:T(128)S(1)}, s32[2]{0:T(128)S(1)}, u32[]{:S(2)}, u32[]{:S(2)}) collective-permute-start(s32[2]{0:T(128)S(1)} %and_select_fusion.runs), channel_id=1, source_target_pairs={{0,4},{4,0},{1,5},{5,1},{2,6},{6,2},{3,7},{7,3},{8,12},{12,8},{9,1... | collective-permute-start | bytes 32 | tf_op jit(solution)/shard_map/ppermute | solution.py:455
  340.5 4.9 copy-start.4
  349.3 69.7 %collective-permute-start.3 = (bf16[2048,768]{1,0:T(8,128)(2,1)}, bf16[2048,768]{1,0:T(8,128)(2,1)S(1)}, u32[]{:S(2)}, u32[]{:S(2)}) collective-permute-start(bf16[2048,768]{1,0:T(8,128)(2,1)} %pad_maximum_fusion.2), channel_id=1, source_target_pairs={{0,4},{4,0},{1,5},{5,1},{2,6},{6,2},{3,7},{7,3},{8,12},{12,8},{9,1... | collective-permute-start | bytes 9437192 | tf_op jit(solution)/shard_map/ppermute | solution.py:455
  460.2 7.8 copy-start.9
  468.1 4.0 copy-start.7
  478.1 156.4 %reduce-scatter.5.cloned.1.call-start = ((), (), s32[]{:S(2)}) async-start(), calls=%async_computation.6 | async-start | bytes 5013504 | tf_op jit(solution)/shard_map/reduce_scatter | solution.py:545
  503.0 49.9 %copy-start.14 = (f32[768]{0:T(1024)S(1)}, f32[768]{0:T(1024)}, u32[]{:S(2)}) copy-start(f32[768]{0:T(1024)} %get-tuple-element.56) | copy-start | bytes 9220
  503.0 49.9 %copy-start.15 = (f32[768]{0:T(1024)S(1)}, f32[768]{0:T(1024)}, u32[]{:S(2)}) copy-start(f32[768]{0:T(1024)} %get-tuple-element.61) | copy-start | bytes 9220
  503.0 247.7 %all-gather.9.cloned.1.call-start = ((), (), s32[]{:S(2)}) async-start(), calls=%async_computation.4 | async-start | bytes 7864320 | tf_op jit(solution)/shard_map/all_gather | solution.py:565
  508.1 43.7 %collective-permute-start.2 = (bf16[1024,768]{1,0:T(8,128)(2,1)}, bf16[1024,768]{1,0:T(8,128)(2,1)S(1)}, u32[]{:S(2)}, u32[]{:S(2)}) collective-permute-start(bf16[1024,768]{1,0:T(8,128)(2,1)} %add_convert_fusion), channel_id=1, source_target_pairs={{0,1},{1,0},{2,3},{3,2},{4,5},{5,4},{6,7},{7,6},{8,9},{9,8},{10,11... | collective-permute-start | bytes 4718600 | tf_op jit(solution)/shard_map/ppermute | solution.py:455
  552.9 5.5 copy-start
  558.3 307.5 %all-gather.11.cloned.1.call-start = ((), (), s32[]{:S(2)}) async-start(), calls=%async_computation.5 | async-start | bytes 7864320 | tf_op jit(solution)/shard_map/all_gather | solution.py:578
  558.5 41.4 %collective-permute-start.4 = (bf16[1024,768]{1,0:T(8,128)(2,1)S(1)}, bf16[1024,768]{1,0:T(8,128)(2,1)S(1)}, u32[]{:S(2)}, u32[]{:S(2)}) collective-permute-start(bf16[1024,768]{1,0:T(8,128)(2,1)S(1)} %constant_dynamic-slice_fusion), channel_id=1, source_target_pairs={{0,1},{1,0},{2,3},{3,2},{4,5},{5,4},{6,7},{7,6},{8,9},{9,8},{10,11... | collective-permute-start | bytes 4718600 | tf_op jit(solution)/shard_map/ppermute | solution.py:455
  608.0 5.4 collective-permute-start.5
  613.9 258.4 %copy-start.16 = (f32[96]{0:T(128)}, f32[96]{0:T(128)S(1)}, u32[]{:S(2)}) copy-start(f32[96]{0:T(128)S(1)} %get-tuple-element.126) | copy-start | bytes 1156
  866.3 6.0 copy-start.1
  (7 other events, 11.7 us)
Sparse Core Ops, SparseCore 0:
  12.4 48.4 all-gather.4
  102.0 56.6 all-gather.6
  478.2 67.8 reduce-scatter.6
  550.9 83.4 reduce-scatter.4
  636.4 114.2 all-gather.8
  752.1 113.5 all-gather.10

commit v2 on v1

--- a/solution.py
+++ b/solution.py
@@ -50,6 +50,55 @@
 
 def params(**kwargs):
     return pltpu.CompilerParams(vmem_limit_bytes=vmem_bytes, **kwargs)
+
+
+def place_first_kernel(where, one_ref, two_ref, qkv_ref, dense_ref, small_ref):
+    cols = one_ref.shape[-1] // 2
+    near = where[0] == 0
+    one = [one_ref[0, j] for j in range(2)]
+    two = [two_ref[0, j] for j in range(2)]
+    one = (jnp.where(near, one[0], one[1]), jnp.where(near, one[1], one[0]))
+    two = (jnp.where(near, two[0], two[1]), jnp.where(near, two[1], two[0]))
+    pieces = [one[j][:, i * cols : (i + 1) * cols] for i in range(2) for j in range(2)]
+    pieces += [two[j][:, :cols] for j in range(2)]
+    qkv_ref[...] = jnp.concatenate(pieces, axis=1)
+    dense_ref[...] = jnp.concatenate([two[j][:, cols : 2 * cols] for j in range(2)], axis=1)
+    small_ref[...] = jnp.concatenate([two[j][:, 2 * cols :] for j in range(2)], axis=1).astype(F32)
+
+
+def place_second_kernel(where, one_ref, two_ref, up_ref, down_ref):
+    near = where[0] == 0
+    for ref, out in ((one_ref, up_ref), (two_ref, down_ref)):
+        units = ref.shape[-1]
+        out[:, :units] = jnp.where(near, ref[0, 0], ref[0, 1])
+        out[:, units:] = jnp.where(near, ref[0, 1], ref[0, 0])
+
+
+def place(kernel, where, one, two, widths, types):
+    owners, _, share, _ = one.shape
+
+    def spec(array, low, high):
+        def index(i, where):
+            bits = i ^ where[1]
+            upper, lower, across = bits // 4, (bits // 2) % 2, bits % 2
+            near, far = (across, upper) if low == "seq" else (upper, across)
+            return (lower * 4 + far * 2 + near, 0, 0, 0)
+
+        return pl.BlockSpec((1,) + array.shape[1:], index)
+
+    return pl.pallas_call(
+        kernel,
+        grid_spec=pltpu.PrefetchScalarGridSpec(
+            num_scalar_prefetch=1,
+            grid=(owners,),
+            in_specs=[spec(one, "seq", "dp"), spec(two, "dp", "seq")],
+            out_specs=[pl.BlockSpec((share, width), lambda i, *_: (i, 0)) for width in widths],
+        ),
+        out_shape=[jax.ShapeDtypeStruct((owners * share, width), kind) for width, kind in zip(widths, types)],
+        compiler_params=params(),
+        cost_estimate=pl.CostEstimate(flops=0, bytes_accessed=8 * one.size, transcendentals=0),
+        name="place",
+    )(where, one, two)
 
 
 def front_kernel(
@@ -188,17 +237,23 @@
     return total
 
 
-def attention_kernel(
-    runs, slots, q_ref, g_ref, k_ref, v_ref, o_ref, dq_ref, dk_ref, dv_ref,
-    score_ref, soft_ref, acc_ref, *, block, per_run,
-):
+def attention_kernel(runs, slots, q_ref, g_ref, *refs, block, per_run, parts, first, carried):
+    k_parts, v_parts, refs = refs[:parts], refs[parts : 2 * parts], refs[2 * parts :]
+    if carried:
+        dk_in, dv_in, refs = refs[0], refs[1], refs[2:]
+    o_ref, dq_ref, dk_ref, dv_ref, k_ref, v_ref, score_ref, soft_ref, acc_ref = refs
     step = pl.program_id(1)
 
     @pl.when(step == 0)
     def _():
-        dk_ref[...] = jnp.zeros_like(dk_ref)
-        dv_ref[...] = jnp.zeros_like(dv_ref)
-
+        for j in range(parts):
+            there = pl.ds(j * k_parts[j].shape[0], k_parts[j].shape[0])
+            k_ref[there, :] = k_parts[j][...]
+            v_ref[there, :] = v_parts[j][...]
+        dk_ref[...] = dk_in[...] if carried else jnp.zeros_like(dk_ref)
+        dv_ref[...] = dv_in[...] if carried else jnp.zeros_like(dv_ref)
+
+    step = step + first
     full = runs[step // per_run] * per_run + step % per_run
     lane = lax.broadcasted_iota(jnp.int32, (block, LANES), 1)
     heads = (lane < HD, lane >= HD)
@@ -273,50 +328,54 @@
     dq_ref[...] = (jnp.where(heads[0], acc_ref[0], acc_ref[1]) * F32(HD**-0.5)).astype(dq_ref.dtype)
 
 
-def attention(runs, slots, q, g, kv):
+def attention(runs, slots, q, g, kv_parts, first=0, last=None, carry=None, pair=None):
     rows, width = q.shape
-    keys = kv.shape[0]
+    keys = sum(kv.shape[0] for kv in kv_parts)
     run_rows = rows // 2
     block = min(512, run_rows)
     per_run = run_rows // block
+    first, last = (0, rows // block) if last is None else (first * per_run, last * per_run)
     pairs = width // LANES
-    by_query = pl.BlockSpec((block, LANES), lambda p, i, *_: (i, p))
+    count, base = (pairs, 0) if pair is None else (1, pair)
+    done = (last - first) * block
+    by_query = pl.BlockSpec((block, LANES), lambda p, i, *_: (first + i, base + p))
+    by_key = [pl.BlockSpec((kv.shape[0], LANES), lambda p, i, *_: (0, base + p)) for kv in kv_parts]
+    by_value = [pl.BlockSpec((kv.shape[0], LANES), lambda p, i, *_: (0, pairs + base + p)) for kv in kv_parts]
+    of_query = pl.BlockSpec((block, LANES), lambda p, i, *_: (i, p))
+    of_key = pl.BlockSpec((keys, LANES), lambda p, i, *_: (0, p))
+    from_key = pl.BlockSpec((keys, LANES), lambda p, i, *_: (0, base + p))
+    carry = () if carry is None else tuple(carry)
+    kernel = functools.partial(
+        attention_kernel, block=block, per_run=per_run, parts=len(kv_parts), first=first, carried=bool(carry)
+    )
     return pl.pallas_call(
-        functools.partial(attention_kernel, block=block, per_run=per_run),
+        kernel,
         grid_spec=pltpu.PrefetchScalarGridSpec(
             num_scalar_prefetch=2,
-            grid=(pairs, rows // block),
-            in_specs=[
-                by_query,
-                by_query,
-                pl.BlockSpec((keys, LANES), lambda p, i, *_: (0, p)),
-                pl.BlockSpec((keys, LANES), lambda p, i, *_: (0, pairs + p)),
-            ],
-            out_specs=[
-                by_query,
-                by_query,
-                pl.BlockSpec((keys, LANES), lambda p, i, *_: (0, p)),
-                pl.BlockSpec((keys, LANES), lambda p, i, *_: (0, p)),
-            ],
+            grid=(count, last - first),
+            in_specs=[by_query, by_query, *by_key, *by_value] + [from_key] * len(carry),
+            out_specs=[of_query, of_query, of_key, of_key],
             scratch_shapes=[
+                pltpu.VMEM((keys, LANES), BF16),
+                pltpu.VMEM((keys, LANES), BF16),
                 pltpu.VMEM((2, keys // block, block, block), F32),
                 pltpu.VMEM((2, keys // block, block, block), BF16),
                 pltpu.VMEM((2, block, LANES), F32),
             ],
         ),
         out_shape=[
-            jax.ShapeDtypeStruct((rows, width), BF16),
-            jax.ShapeDtypeStruct((rows, width), BF16),
-            jax.ShapeDtypeStruct((keys, width), F32),
-            jax.ShapeDtypeStruct((keys, width), F32),
+            jax.ShapeDtypeStruct((done, count * LANES), BF16),
+            jax.ShapeDtypeStruct((done, count * LANES), BF16),
+            jax.ShapeDtypeStruct((keys, count * LANES), F32),
+            jax.ShapeDtypeStruct((keys, count * LANES), F32),
         ],
         compiler_params=params(),
         cost_estimate=pl.CostEstimate(
-            flops=24 * rows * keys * width, bytes_accessed=24 * keys * width,
-            transcendentals=rows * keys * pairs,
+            flops=40 * done * keys * count * LANES, bytes_accessed=24 * keys * width,
+            transcendentals=done * keys * count,
         ),
         name="attention",
-    )(runs, slots, q, g, kv, kv)
+    )(runs, slots, q, g, *kv_parts, *kv_parts, *carry)
 
 
 def back_kernel(
@@ -455,6 +514,35 @@
     return lax.ppermute(values, axis, [(0, 1), (1, 0)])
 
 
+def across(values, bit):
+    return lax.ppermute(values, "dp", [(i, i ^ bit) for i in range(4)])
+
+
+def gather_half(values, seq_first):
+    values = jnp.concatenate([values[None], swap(values, "mh")[None]], axis=0)
+    steps = [lambda v: swap(v, "seq"), lambda v: across(v, 2)]
+    for step in steps if seq_first else steps[::-1]:
+        values = jnp.concatenate([values, step(values)], axis=0)
+    values = jnp.concatenate([values, across(values, 1)], axis=0)
+    return values.reshape(8, 2, *values.shape[1:])
+
+
+def line_gather(mine, index):
+    axes, count = ("mh", "ml"), 4
+    up = [(i, i + 1) for i in range(count - 1)]
+    down = [(i + 1, i) for i in range(count - 1)]
+    from_below, from_above = [mine], [mine]
+    for _ in range(count - 1):
+        from_below.append(lax.ppermute(from_below[-1], axes, up))
+        from_above.append(lax.ppermute(from_above[-1], axes, down))
+    out = jnp.zeros((count,) + mine.shape, mine.dtype)
+    out = lax.dynamic_update_index_in_dim(out, mine, index, 0)
+    for back in (2, 1, 3):
+        piece = jnp.where(index >= back, from_below[back], from_above[count - back])
+        out = lax.dynamic_update_index_in_dim(out, piece, (index - back) % count, 0)
+    return out
+
+
 def rotation_tables(positions):
     half = ROT // 2
     frequency = jnp.power(F32(10000.0), -2.0 * jnp.arange(half, dtype=F32) / ROT)
@@ -481,9 +569,11 @@
     heads = b_qkv.shape[1]
     cols = heads * HD
     units = w_up.shape[1]
-    splits = ("dp", "seq", "mh")
     side, part = lax.axis_index("mh"), lax.axis_index("ml")
+    index = 2 * side + part
+    owner = lax.axis_index("dp") * seq_size + lax.axis_index("seq")
     which = jnp.stack([side, part]).astype(jnp.int32)
+    where = jnp.stack([side, owner]).astype(jnp.int32)
 
     def column(vector):
         vector = vector.reshape(-1)
@@ -494,28 +584,37 @@
         axis=1,
     )
     small = jnp.pad(small, ((0, 0), (0, LANES - small.shape[1])))
-    first = jnp.concatenate([w_qkv.transpose(1, 0, 2).reshape(share, 3 * cols), w_dense.T, small], axis=1)
-    second = jnp.concatenate([w_up, w_down.T], axis=1)
-    first = lax.all_gather(first, splits, axis=0, tiled=True).reshape(owners, 2, share, -1)
-    second = lax.all_gather(second, splits, axis=0, tiled=True).reshape(owners, 2, share, -1)
-
-    def laid(pack, start, count):
-        piece = pack[:, :, :, start : start + count].transpose(0, 2, 1, 3)
-        return piece.reshape(width, 2, count)
-
-    qkv_w = laid(first, 0, 3 * cols).reshape(width, 2, 3, cols).transpose(0, 2, 1, 3).reshape(width, 6 * cols)
-    dense_w = laid(first, 3 * cols, cols).reshape(width, 2 * cols)
-    up_w = laid(second, 0, units).reshape(width, 2 * units)
-    down_w = laid(second, units, units).reshape(width, 2 * units)
-    small = first[:, :, :, 4 * cols :].astype(F32)
-    vectors = small[:, 0].reshape(width, LANES)
+    one = w_qkv[:2].transpose(1, 0, 2).reshape(share, 2 * cols)
+    two = jnp.concatenate([w_qkv[2], w_dense.T, small], axis=1)
+    three, four = w_up, w_down.T
+    first_widths, second_widths = (6 * cols, 2 * cols, 2 * LANES), (2 * units, 2 * units)
+    if owners == 8 and seq_size == 2:
+        one, two = gather_half(one, True), gather_half(two, False)
+        qkv_w, dense_w, small = place(place_first_kernel, where, one, two, first_widths, (BF16, BF16, F32))
+        three, four = lax.optimization_barrier((three, four, one, two))[:2]
+        three, four = gather_half(three, True), gather_half(four, False)
+        up_w, down_w = place(place_second_kernel, where, three, four, second_widths, (BF16, BF16))
+    else:
+
+        def gather(values):
+            values = lax.all_gather(values, ("dp", "seq", "mh"), axis=0, tiled=True)
+            return values.reshape(owners, 2, share, -1).transpose(0, 2, 1, 3).reshape(width, 2, -1)
+
+        one, two, three, four = gather(one), gather(two), gather(three), gather(four)
+        qkv_w = jnp.concatenate([one[:, :, :cols], one[:, :, cols:], two[:, :, :cols]], axis=1)
+        qkv_w, dense_w = qkv_w.reshape(width, 6 * cols), two[:, :, cols : 2 * cols].reshape(width, 2 * cols)
+        small = two[:, :, 2 * cols :].reshape(width, 2 * LANES).astype(F32)
+        up_w, down_w = three.reshape(width, 2 * units), four.reshape(width, 2 * units)
+    vectors = small[:, :8]
     piece = HD // owners
-    qkv_b = small[:, :, : 3 * heads * piece, 6].reshape(owners, 2, 3, heads, piece)
-    qkv_b = qkv_b.transpose(2, 1, 3, 0, 4).reshape(1, 6 * cols)
+    biases = small.reshape(owners, share, 2, LANES)
+    qkv_b = biases[:, : 3 * heads * piece, :, 6].reshape(owners, 3, heads, piece, 2)
+    qkv_b = qkv_b.transpose(1, 4, 2, 0, 3).reshape(1, 6 * cols)
     up_rows, up_cols = b_up.shape
-    up_b = small[:, :, :, 7].reshape(owners, 2, up_rows, up_cols).transpose(1, 2, 0, 3).reshape(1, 2 * units)
-    row_of = lambda index: vectors[:, index].reshape(1, width)
-    column_of = lambda index: vectors[:, index].reshape(width, 1)
+    up_b = biases[..., 7].reshape(owners, up_rows, up_cols, 2).transpose(3, 1, 0, 2).reshape(1, 2 * units)
+    by_row = vectors.T
+    row_of = lambda at: by_row[at].reshape(1, width)
+    column_of = lambda at: vectors[:, at].reshape(width, 1)
 
     my_places = lax.dynamic_index_in_dim(places, side, 0, keepdims=False)
     run_rows = rows // 2
@@ -530,84 +629,91 @@
 
     q, kv, grad_o = front(which, tokens, out_grad, qkv_w, qkv_b, dense_w, row_of(2), row_of(3), tables)
     if seq_size == 2:
-        kv_all = jnp.concatenate([kv, swap(kv, "seq")], axis=0)
+        kv_parts = (kv, swap(kv, "seq"))
     else:
-        kv_all = lax.all_gather(kv, "seq", axis=0, tiled=True)
+        kv_parts = (lax.all_gather(kv, "seq", axis=0, tiled=True),)
 
     mlp_part, mlp_dx, grad_up, grad_down, mlp_vectors, grad_up_b = feed(
         which, tokens, out_grad, up_w, up_b, down_w, row_of(4), row_of(5), column_of(4), column_of(5)
     )
-
-    def spread(grad):
-        return grad.reshape(owners, share, 2, -1).transpose(0, 2, 1, 3)
-
-    def scatter(pack):
-        return lax.psum_scatter(
-            pack.reshape(owners * 2 * share, -1), splits, scatter_dimension=0, tiled=True
-        )
-
-    owned_second = scatter(jnp.concatenate([spread(grad_up), spread(grad_down)], axis=3))
-
-    attended, dq, dk, dv = attention(runs, slots, q, grad_o, kv_all)
-
-    half_rows = rows // 2
-
-    def half_of(array, index):
-        return lax.dynamic_slice_in_dim(array, index * half_rows, half_rows, axis=0)
-
-    def branch_sum(index):
-        product = lax.dot_general(half_of(attended, index), dense_w, NT, preferred_element_type=F32)
-        return product + half_of(mlp_part, index).astype(F32)
-
-    got_mixed = swap(branch_sum(1 - part).astype(BF16), "ml")
-    my_tokens = lax.dynamic_slice(tokens, (side, part * half_rows, 0), (1, half_rows, width))[0]
-    mixed = branch_sum(part) + got_mixed.astype(F32) + my_tokens.astype(F32) + row_of(0) + row_of(1)
-    mixed = lax.all_gather(mixed.astype(BF16), ("mh", "ml"), axis=0, tiled=True).reshape(tokens.shape)
+    q, mlp_part = lax.optimization_barrier((q, mlp_part))
+
+    quarter = rows // 4
+
+    def mixed_of(run, attended):
+        def branch_sum(at):
+            there = lax.dynamic_slice_in_dim(attended, at * quarter, quarter, axis=0)
+            other = lax.dynamic_slice_in_dim(mlp_part, run * run_rows + at * quarter, quarter, axis=0)
+            return lax.dot_general(there, dense_w, NT, preferred_element_type=F32) + other.astype(F32)
+
+        got = swap(branch_sum(1 - part).astype(BF16), "ml")
+        mine = lax.dynamic_slice(tokens, (side, run * run_rows + part * quarter, 0), (1, quarter, width))[0]
+        return (branch_sum(part) + got.astype(F32) + mine.astype(F32) + row_of(0) + row_of(1)).astype(BF16)
+
+    o_early, dq_early, dk, dv = attention(runs, slots, q, grad_o, kv_parts, 0, 1)
+    mixed_early = lax.all_gather(mixed_of(0, o_early), ("mh", "ml"), axis=0, tiled=True)
+    o_late, dq_late, dk, dv = attention(runs, slots, q, grad_o, kv_parts, 1, 2, (dk, dv))
+    mixed_late = line_gather(mixed_of(1, o_late), index)
+    mixed = jnp.concatenate(
+        [mixed_early.reshape(2, run_rows, width), mixed_late.reshape(2, run_rows, width)], axis=1
+    )
 
     if seq_size == 2:
         got = swap(jnp.concatenate([dk[rows:], dv[rows:]], axis=1).astype(BF16), "seq")
-        dk, dv = dk[:rows], dv[:rows]
     else:
         got = lax.psum_scatter(
             jnp.concatenate([dk, dv], axis=1).astype(BF16), "seq", scatter_dimension=0, tiled=True
         )
-        dk = dv = jnp.zeros(dq.shape, F32)
+        dk = dv = jnp.zeros(q.shape, F32)
+    dq = jnp.concatenate([dq_early, dq_late], axis=0)
     dproj, dx = back(dq, dk, dv, got, qkv_w, row_of(2), mlp_dx, tables)
-    got_dx = swap(half_of(dx, 1 - part), "ml")
-    input_grad = norm_back(which, tokens, out_grad, dx, got_dx)
-    input_grad = lax.all_gather(input_grad, ("mh", "ml"), axis=0, tiled=True).reshape(tokens.shape)
-
+    half_rows = rows // 2
+    got_dx = swap(lax.dynamic_slice_in_dim(dx, (1 - part) * half_rows, half_rows, axis=0), "ml")
+    input_grad = line_gather(norm_back(which, tokens, out_grad, dx, got_dx), index).reshape(tokens.shape)
+
+    attended = jnp.concatenate([o_early, o_late], axis=0)
     grad_qkv, grad_dense, qkv_vectors, grad_qkv_b = weight_grads(
         which, tokens, out_grad, dproj, attended, qkv_w, column_of(2), column_of(3)
     )
 
-    vector_grads = (mlp_vectors + qkv_vectors)[:, :5].reshape(owners, 1, share, 5)
-    vector_grads = jnp.broadcast_to(vector_grads, (owners, 2, share, 5))
-    bias_qkv = grad_qkv_b.reshape(3, 2, heads, owners, piece).transpose(3, 1, 0, 2, 4)
-    bias_qkv = bias_qkv.reshape(owners, 2, 3 * heads * piece)
-    bias_qkv = jnp.pad(bias_qkv, ((0, 0), (0, 0), (0, share - 3 * heads * piece)))[..., None]
-    bias_up = grad_up_b.reshape(2, up_rows, owners, up_cols).transpose(2, 0, 1, 3).reshape(owners, 2, share, 1)
-    tail = jnp.concatenate([vector_grads, bias_qkv, bias_up], axis=3)
-    tail = jnp.pad(tail, ((0, 0), (0, 0), (0, 0), (0, LANES - 7))).astype(BF16)
-    grad_qkv = grad_qkv.reshape(owners, share, 3, 2, cols).transpose(0, 3, 1, 2, 4)
-    grad_qkv = grad_qkv.reshape(owners, 2, share, 3 * cols)
-    owned_first = scatter(jnp.concatenate([grad_qkv, spread(grad_dense), tail], axis=3)).astype(F32)
-    owned_second = owned_second.astype(F32)
-
-    vectors = owned_first[:, 4 * cols :]
+    def scatter(grads):
+        return lax.psum_scatter(grads, ("dp", "seq"), scatter_dimension=0, tiled=True)
+
+    def settle(sums):
+        sums = sums.astype(F32)
+        mine = lax.dynamic_index_in_dim(sums, side, 1, keepdims=False)
+        other = lax.dynamic_index_in_dim(sums, 1 - side, 1, keepdims=False)
+        return mine + swap(other.astype(BF16), "mh").astype(F32)
+
+    owned_up = settle(scatter(grad_up).reshape(share, 2, units))
+    owned_down = settle(scatter(grad_down).reshape(share, 2, units))
+    vector_grads = (mlp_vectors + qkv_vectors)[:, None, :5]
+    vector_grads = jnp.broadcast_to(vector_grads, (width, 2, 5))
+    bias_qkv = grad_qkv_b.reshape(3, 2, heads, owners, piece).transpose(3, 0, 2, 4, 1)
+    bias_qkv = bias_qkv.reshape(owners, 3 * heads * piece, 2)
+    bias_qkv = jnp.pad(bias_qkv, ((0, 0), (0, share - 3 * heads * piece), (0, 0))).reshape(width, 2, 1)
+    bias_up = grad_up_b.reshape(2, up_rows, owners, up_cols).transpose(2, 1, 3, 0).reshape(width, 2, 1)
+    tail = jnp.concatenate([vector_grads, bias_qkv, bias_up], axis=2)
+    tail = jnp.pad(tail, ((0, 0), (0, 0), (0, LANES // 2 - 7))).astype(BF16).reshape(width, LANES)
+    first = scatter(jnp.concatenate([grad_qkv, grad_dense, tail], axis=1))
+    owned_qkv = first[:, : 6 * cols].reshape(share, 3, 2, cols).transpose(0, 2, 1, 3).reshape(share, 2, 3 * cols)
+    owned_dense = first[:, 6 * cols : 8 * cols].reshape(share, 2, cols)
+    owned_tail = first[:, 8 * cols :].reshape(share, 2, LANES // 2)
+    owned = settle(jnp.concatenate([owned_qkv, owned_dense, owned_tail], axis=2))
+    vectors = owned[:, 4 * cols :]
     norms = vectors[:, :5]
     norms = norms + swap(norms, "ml")
     bias_grad = norms[:, 0]
     return (
         mixed,
         input_grad,
-        owned_first[:, : 3 * cols].reshape(share, 3, cols).transpose(1, 0, 2),
+        owned[:, : 3 * cols].reshape(share, 3, cols).transpose(1, 0, 2),
         vectors[: 3 * heads * piece, 5].reshape(b_qkv.shape),
-        owned_first[:, 3 * cols : 4 * cols].T,
+        owned[:, 3 * cols : 4 * cols].T,
         bias_grad,
-        owned_second[:, :units],
+        owned_up,
         vectors[:, 6].reshape(b_up.shape),
-        owned_second[:, units:].T,
+        owned_down.T,
         bias_grad,
         norms[:, 1],
         norms[:, 2],

time: 890 us -> 770 us (0.87)
  the two profiles are of different devices: /device:TPU:0 before, /device:TPU:4 now
where the time goes in v2:
time: 770 us; the launch traced here: 760 us
  waiting for transfers between devices  290 us (38%)
  Pallas kernels  256 us (33%)
  local copies, waits for them, and re-layouts  73.9 us (10%)
  starting transfers between devices  70.4 us (9%)
  other arithmetic  47.6 us (6%)
  between operations  16.1 us (2%)
    ppermute x18, waiting for transfers between devices, swap(): return lax.ppermute(values, axis, [(0, 1), (1, 0)])  231 us
    pallas_call x2, Pallas kernels, attention(): pl.pallas_call(kernel, grid_spec=pltpu.PrefetchScalarGridSpec(num_scalar_...  153 us
    ppermute x6, waiting for transfers between devices, line_gather(): from_above.append(lax.ppermute(from_above[-1], axes, down))  53.8 us
    pallas_call x1, Pallas kernels, feed(): pl.pallas_call(feed_kernel, grid_spec=pltpu.PrefetchScalarGridSpec(num_sc...  42.2 us
    ppermute x6, starting transfers between devices, line_gather(): from_below.append(lax.ppermute(from_below[-1], axes, up))  31.5 us
    ppermute x18, starting transfers between devices, swap(): return lax.ppermute(values, axis, [(0, 1), (1, 0)])  28.3 us
    unnamed x69, local copies, waits for them, and re-layouts  17.4 us
    pallas_call x1, Pallas kernels, weight_grads(): pl.pallas_call(weight_kernel, grid_spec=pltpu.PrefetchScalarGridSpec(num_...  15.4 us
  transfers between devices with their start and end apart: 42, of which 19 were waited for; matrix products, arithmetic and copies ran while one was open for 15% of the time, Pallas kernels for 34%

profile of v2, /device:TPU:4, one launch (start us, length us, event | category | flops | bytes accessed | tf_op | source)
XLA Modules:
  0.0 759.6 jit_solution(14280535308215178925)
XLA Ops:
  52.8 7.2 place.2
  79.8 12.2 %front.1 = (bf16[2048,384]{1,0:T(8,128)(2,1)}, bf16[2048,768]{1,0:T(8,128)(2,1)}, bf16[2048,384]{1,0:T(8,128)(2,1)}) custom-call(s32[2]{0:T(128)} %pad_add_fusion.2.which, bf16[2,2048,768]{2,1,0:T(8,128)(2,1)} %x_ref.7, bf16[2,2048,768]{2,1,0:T(8,128)(2,1)} %dy_ref.7, bf16[768,1152]{1,0:T(8,128)(2,1)} %get-tuple-element.48.w_ref, ...), custom_call_target="tpu_custom_call" | custom-call | flops 4831838208 | bytes 18874368 | tf_op jit(solution)/shard_map/front/pallas_call | solution.py:129
  108.4 7.5 place.3
  115.9 42.2 %feed.1 = (bf16[2048,768]{1,0:T(8,128)(2,1)}, bf16[2048,768]{1,0:T(8,128)(2,1)}, bf16[768,1536]{1,0:T(8,128)(2,1)}, bf16[768,1536]{1,0:T(8,128)(2,1)}, f32[768,128]{1,0:T(8,128)}, /*index=5*/f32[1,1536]{1,0:T(1,128)}) custom-call(s32[2]{0:T(128)} %pad_add_fusion.2.which, bf16[2,2048,768]{2,1,0:T(8,128)(2,1)} %x_ref.7, bf16[2,2048,768]{2,1,0:T(8,128)(2,1)} %dy_ref.7, ...), custom_call_target="tpu_custom_call" | custom-call | flops 28991029248 | bytes 28311552 | tf_op jit(solution)/shard_map/feed/pallas_call | solution.py:205
  158.1 9.7 %collective-permute-done.17.refs_1_.refs_3_ = bf16[2048,768]{1,0:T(8,128)(2,1)} collective-permute-done((bf16[2048,768]{1,0:T(8,128)(2,1)}, bf16[2048,768]{1,0:T(8,128)(2,1)}, u32[]{:S(2)}, u32[]{:S(2)}) %collective-permute-start.17) | collective-permute-done | bytes 3145760 | tf_op jit(solution)/shard_map/ppermute | solution.py:514
  167.8 32.5 %attention.2 = (bf16[1024,384]{1,0:T(8,128)(2,1)}, bf16[1024,384]{1,0:T(8,128)(2,1)}, f32[4096,384]{1,0:T(8,128)}, f32[4096,384]{1,0:T(8,128)}) custom-call(s32[2]{0:T(128)} %copy-done.23, s32[4]{0:T(128)} %select_reduce_fusion.slots, bf16[2048,384]{1,0:T(8,128)(2,1)} %get-tuple-element.59.q_ref, bf16[2048,384]{1,0:T(8,128)(2,1)} %get-tuple-element.60.g_ref, ...), custom_call_target="tpu_custom_call" | custom-call | flops 64424509440 | bytes 37748736 | tf_op jit(solution)/shard_map/attention/pallas_call | solution.py:351
  200.4 120.2 %attention.3 = (bf16[1024,384]{1,0:T(8,128)(2,1)}, bf16[1024,384]{1,0:T(8,128)(2,1)}, f32[4096,384]{1,0:T(8,128)}, f32[4096,384]{1,0:T(8,128)}) custom-call(s32[2]{0:T(128)} %copy-done.23, s32[4]{0:T(128)} %select_reduce_fusion.slots, bf16[2048,384]{1,0:T(8,128)(2,1)} %get-tuple-element.59.q_ref, bf16[2048,384]{1,0:T(8,128)(2,1)} %get-tuple-element.60.g_ref, ...), custom_call_target="tpu_custom_call" | custom-call | flops 64424509440 | bytes 37748736 | tf_op jit(solution)/shard_map/attention/pallas_call | solution.py:351
  332.4 73.2 %collective-permute-done.26.got_ref = bf16[2048,768]{1,0:T(8,128)(2,1)S(1)} collective-permute-done((bf16[2048,768]{1,0:T(8,128)(2,1)}, bf16[2048,768]{1,0:T(8,128)(2,1)S(1)}, u32[]{:S(2)}, u32[]{:S(2)}) %collective-permute-start.26) | collective-permute-done | bytes 3145760 | tf_op jit(solution)/shard_map/ppermute | solution.py:514
  407.2 12.7 %back.1 = (bf16[2048,1152]{1,0:T(8,128)(2,1)}, bf16[2048,768]{1,0:T(8,128)(2,1)}) custom-call(bf16[2048,384]{1,0:T(8,128)(2,1)} %pad_maximum_fusion.3.dq_ref, f32[4096,384]{1,0:T(8,128)} %get-tuple-element.69.own_k, f32[4096,384]{1,0:T(8,128)} %get-tuple-element.70.own_v, bf16[2048,768]{1,0:T(8,128)(2,1)} %copy-done.4, ...), custom_call_target="tpu_custom_call" | custom-call | flops 3623878656 | bytes 18874368 | tf_op jit(solution)/shard_map/back/pallas_call | solution.py:402
  419.9 15.4 %weight_grads.1 = (bf16[768,1152]{1,0:T(8,128)(2,1)}, bf16[768,384]{1,0:T(8,128)(2,1)}, f32[768,128]{1,0:T(8,128)}, f32[1,1152]{1,0:T(1,128)}) custom-call(s32[2]{0:T(128)} %pad_add_fusion.2.which, bf16[2,2048,768]{2,1,0:T(8,128)(2,1)} %x_ref.7, bf16[2,2048,768]{2,1,0:T(8,128)(2,1)} %dy_ref.7, bf16[2048,1152]{1,0:T(8,128)(2,1)} %get-tuple-element.73.dproj_ref, ...), custom_call_target="tpu_custom_call" | custom-call | flops 4831838208 | bytes 18874368 | tf_op jit(solution)/shard_map/weight_grads/pallas_call | solution.py:456
  452.8 12.9 %collective-permute-done.18 = bf16[512,768]{1,0:T(8,128)(2,1)} collective-permute-done((bf16[512,768]{1,0:T(8,128)(2,1)}, bf16[512,768]{1,0:T(8,128)(2,1)}, u32[]{:S(2)}, u32[]{:S(2)}) %collective-permute-start.18) | collective-permute-done | bytes 786464 | tf_op jit(solution)/shard_map/ppermute | solution.py:514
  469.4 17.1 %collective-permute-done.19 = bf16[512,768]{1,0:T(8,128)(2,1)} collective-permute-done((bf16[512,768]{1,0:T(8,128)(2,1)S(1)}, bf16[512,768]{1,0:T(8,128)(2,1)}, u32[]{:S(2)}, u32[]{:S(2)}) %collective-permute-start.19) | collective-permute-done | bytes 786464 | tf_op jit(solution)/shard_map/ppermute | solution.py:514
  491.1 5.5 collective-permute-start.20
  496.6 70.3 %collective-permute-done.27.got_ref = bf16[1024,768]{1,0:T(8,128)(2,1)} collective-permute-done((bf16[1024,768]{1,0:T(8,128)(2,1)}, bf16[1024,768]{1,0:T(8,128)(2,1)}, u32[]{:S(2)}, u32[]{:S(2)}) %collective-permute-start.27) | collective-permute-done | bytes 1572896 | tf_op jit(solution)/shard_map/ppermute | solution.py:514
  566.9 5.7 norm_back.1
  573.8 9.9 %collective-permute-done.22 = bf16[512,768]{1,0:T(8,128)(2,1)} collective-permute-done((bf16[512,768]{1,0:T(8,128)(2,1)}, bf16[512,768]{1,0:T(8,128)(2,1)}, u32[]{:S(2)}, u32[]{:S(2)}) %collective-permute-start.22) | collective-permute-done | bytes 786464 | tf_op jit(solution)/shard_map/ppermute | solution.py:537
  585.0 5.5 collective-permute-start.21
  594.5 37.8 %collective-permute-done.23 = bf16[512,768]{1,0:T(8,128)(2,1)} collective-permute-done((bf16[512,768]{1,0:T(8,128)(2,1)}, bf16[512,768]{1,0:T(8,128)(2,1)}, u32[]{:S(2)}, u32[]{:S(2)}) %collective-permute-start.23) | collective-permute-done | bytes 786464 | tf_op jit(solution)/shard_map/ppermute | solution.py:537
  633.5 5.7 collective-permute-start.25
  653.9 7.0 collective-permute-done.36
  668.5 8.8 %collective-permute-start.29 = (bf16[1024,768]{1,0:T(8,128)(2,1)}, bf16[1024,768]{1,0:T(8,128)(2,1)}, u32[]{:S(2)}, u32[]{:S(2)}) collective-permute-start(bf16[1024,768]{1,0:T(8,128)(2,1)} %collective-permute-done.28), channel_id=1, source_target_pairs={{0,1},{1,2},{2,3},{4,5},{5,6},{6,7},{8,9},{9,10},{10,11},{12,13},{... | collective-permute-start | bytes 4718600 | tf_op jit(solution)/shard_map/ppermute | solution.py:536
  695.4 6.1 collective-permute-done.31
  707.9 8.8 %collective-permute-done.34 = bf16[96,832]{0,1:T(8,128)(2,1)S(1)} collective-permute-done((bf16[96,832]{0,1:T(8,128)(2,1)}, bf16[96,832]{0,1:T(8,128)(2,1)S(1)}, u32[]{:S(2)}, u32[]{:S(2)}) %collective-permute-start.34) | collective-permute-done | bytes 159776 | tf_op jit(solution)/shard_map/ppermute | solution.py:514
  724.9 17.5 %collective-permute-done.35 = f32[96,5]{0,1:T(8,128)S(1)} collective-permute-done((f32[96,5]{0,1:T(8,128)S(1)}, f32[96,5]{0,1:T(8,128)S(1)}, u32[]{:S(2)}, u32[]{:S(2)}) %collective-permute-start.35) | collective-permute-done | bytes 1952 | tf_op jit(solution)/shard_map/ppermute | solution.py:514
  (270 shorter events, 192.2 us)
Async XLA Ops:
  8.0 632.6 %reduce-scatter.6.cloned.1.call-start = ((), (), s32[]{:S(2)}) async-start(), calls=%async_computation.5 | async-start | bytes 2654208 | tf_op jit(solution)/shard_map/reduce_scatter | solution.py:680
  73.0 19.0 %collective-permute-start.15 = (bf16[4,96,768]{2,1,0:T(8,128)(2,1)}, bf16[4,96,768]{2,1,0:T(8,128)(2,1)S(1)}, u32[]{:S(2)}, u32[]{:S(2)}) collective-permute-start(bf16[4,96,768]{2,1,0:T(8,128)(2,1)} %pad_maximum_fusion.10), channel_id=1, source_target_pairs={{0,4},{4,0},{1,5},{5,1},{2,6},{6,2},{3,7},{7,3},{8,12},{12,8},{9,1... | collective-permute-start | bytes 1769480 | tf_op jit(solution)/shard_map/ppermute | solution.py:514
  97.5 70.3 %collective-permute-start.17 = (bf16[2048,768]{1,0:T(8,128)(2,1)}, bf16[2048,768]{1,0:T(8,128)(2,1)}, u32[]{:S(2)}, u32[]{:S(2)}) collective-permute-start(bf16[2048,768]{1,0:T(8,128)(2,1)} %get-tuple-element.61.refs_0_.refs_2_), channel_id=1, source_target_pairs={{0,4},{4,0},{1,5},{5,1},{2,6},{6,2},{3,7},{7,3},{8,12},{12,8},{9,1... | collective-permute-start | bytes 9437192 | tf_op jit(solution)/shard_map/ppermute | solution.py:514
  158.1 489.6 %reduce-scatter.8.cloned.1.call-start = ((), (), s32[]{:S(2)}) async-start(), calls=%async_computation.6 | async-start | bytes 2654208 | tf_op jit(solution)/shard_map/reduce_scatter | solution.py:680
  326.6 78.9 %collective-permute-start.26 = (bf16[2048,768]{1,0:T(8,128)(2,1)}, bf16[2048,768]{1,0:T(8,128)(2,1)S(1)}, u32[]{:S(2)}, u32[]{:S(2)}) collective-permute-start(bf16[2048,768]{1,0:T(8,128)(2,1)} %pad_maximum_fusion.1), channel_id=1, source_target_pairs={{0,4},{4,0},{1,5},{5,1},{2,6},{6,2},{3,7},{7,3},{8,12},{12,8},{9,1... | collective-permute-start | bytes 9437192 | tf_op jit(solution)/shard_map/ppermute | solution.py:514
  327.9 356.6 %reduce-scatter.4.cloned.1.call-start = ((), (), s32[]{:S(2)}) async-start(), calls=%async_computation.4 | async-start | bytes 2875392 | tf_op jit(solution)/shard_map/reduce_scatter | solution.py:680
  440.7 262.1 %all-gather.2.cloned.1.call-start = ((), (), s32[]{:S(2)}) async-start(), calls=%async_computation.3 | async-start | bytes 3932160 | tf_op jit(solution)/shard_map/all_gather | solution.py:654
  444.6 21.1 %collective-permute-start.18 = (bf16[512,768]{1,0:T(8,128)(2,1)}, bf16[512,768]{1,0:T(8,128)(2,1)}, u32[]{:S(2)}, u32[]{:S(2)}) collective-permute-start(bf16[512,768]{1,0:T(8,128)(2,1)} %add_convert_fusion.1), channel_id=1, source_target_pairs={{0,1},{1,0},{2,3},{3,2},{4,5},{5,4},{6,7},{7,6},{8,9},{9,8},{10,11... | collective-permute-start | bytes 2359304 | tf_op jit(solution)/shard_map/ppermute | solution.py:514
  448.9 37.6 %collective-permute-start.19 = (bf16[512,768]{1,0:T(8,128)(2,1)S(1)}, bf16[512,768]{1,0:T(8,128)(2,1)}, u32[]{:S(2)}, u32[]{:S(2)}) collective-permute-start(bf16[512,768]{1,0:T(8,128)(2,1)S(1)} %add_convert_fusion), channel_id=1, source_target_pairs={{0,1},{1,0},{2,3},{3,2},{4,5},{5,4},{6,7},{7,6},{8,9},{9,8},{10,11... | collective-permute-start | bytes 2359304 | tf_op jit(solution)/shard_map/ppermute | solution.py:514
  450.8 116.0 %collective-permute-start.27 = (bf16[1024,768]{1,0:T(8,128)(2,1)}, bf16[1024,768]{1,0:T(8,128)(2,1)}, u32[]{:S(2)}, u32[]{:S(2)}) collective-permute-start(bf16[1024,768]{1,0:T(8,128)(2,1)} %constant_dynamic-slice_fusion.4), channel_id=1, source_target_pairs={{0,1},{1,0},{2,3},{3,2},{4,5},{5,4},{6,7},{7,6},{8,9},{9,8},{10,11... | collective-permute-start | bytes 4718600 | tf_op jit(solution)/shard_map/ppermute | solution.py:514
  489.8 93.9 %collective-permute-start.22 = (bf16[512,768]{1,0:T(8,128)(2,1)}, bf16[512,768]{1,0:T(8,128)(2,1)}, u32[]{:S(2)}, u32[]{:S(2)}) collective-permute-start(bf16[512,768]{1,0:T(8,128)(2,1)} %get-tuple-element.85), channel_id=1, source_target_pairs={{1,0},{2,1},{3,2},{5,4},{6,5},{7,6},{9,8},{10,9},{11,10},{13,12},{... | collective-permute-start | bytes 2359304 | tf_op jit(solution)/shard_map/ppermute | solution.py:537
  491.1 93.9 %collective-permute-start.20 = (bf16[512,768]{1,0:T(8,128)(2,1)}, bf16[512,768]{1,0:T(8,128)(2,1)}, u32[]{:S(2)}, u32[]{:S(2)}) collective-permute-start(bf16[512,768]{1,0:T(8,128)(2,1)} %get-tuple-element.85), channel_id=1, source_target_pairs={{0,1},{1,2},{2,3},{4,5},{5,6},{6,7},{8,9},{9,10},{10,11},{12,13},{... | collective-permute-start | bytes 2359304 | tf_op jit(solution)/shard_map/ppermute | solution.py:536
  572.5 88.4 %collective-permute-start.30 = (bf16[1024,768]{1,0:T(8,128)(2,1)}, bf16[1024,768]{1,0:T(8,128)(2,1)}, u32[]{:S(2)}, u32[]{:S(2)}) collective-permute-start(bf16[1024,768]{1,0:T(8,128)(2,1)} %norm_back.1), channel_id=1, source_target_pairs={{1,0},{2,1},{3,2},{5,4},{6,5},{7,6},{9,8},{10,9},{11,10},{13,12},{... | collective-permute-start | bytes 4718600 | tf_op jit(solution)/shard_map/ppermute | solution.py:537
  583.7 48.5 %collective-permute-start.23 = (bf16[512,768]{1,0:T(8,128)(2,1)}, bf16[512,768]{1,0:T(8,128)(2,1)}, u32[]{:S(2)}, u32[]{:S(2)}) collective-permute-start(bf16[512,768]{1,0:T(8,128)(2,1)} %collective-permute-done.22), channel_id=1, source_target_pairs={{1,0},{2,1},{3,2},{5,4},{6,5},{7,6},{9,8},{10,9},{11,10},{13,12},{... | collective-permute-start | bytes 2359304 | tf_op jit(solution)/shard_map/ppermute | solution.py:537
  585.0 48.5 %collective-permute-start.21 = (bf16[512,768]{1,0:T(8,128)(2,1)}, bf16[512,768]{1,0:T(8,128)(2,1)}, u32[]{:S(2)}, u32[]{:S(2)}) collective-permute-start(bf16[512,768]{1,0:T(8,128)(2,1)} %collective-permute-done.20), channel_id=1, source_target_pairs={{0,1},{1,2},{2,3},{4,5},{5,6},{6,7},{8,9},{9,10},{10,11},{12,13},{... | collective-permute-start | bytes 2359304 | tf_op jit(solution)/shard_map/ppermute | solution.py:536
  590.5 78.0 %collective-permute-start.28 = (bf16[1024,768]{1,0:T(8,128)(2,1)}, bf16[1024,768]{1,0:T(8,128)(2,1)}, u32[]{:S(2)}, u32[]{:S(2)}) collective-permute-start(bf16[1024,768]{1,0:T(8,128)(2,1)} %norm_back.1), channel_id=1, source_target_pairs={{0,1},{1,2},{2,3},{4,5},{5,6},{6,7},{8,9},{9,10},{10,11},{12,13},{... | collective-permute-start | bytes 4718600 | tf_op jit(solution)/shard_map/ppermute | solution.py:536
  632.2 45.1 %collective-permute-start.24 = (bf16[512,768]{1,0:T(8,128)(2,1)}, bf16[512,768]{1,0:T(8,128)(2,1)}, u32[]{:S(2)}, u32[]{:S(2)}) collective-permute-start(bf16[512,768]{1,0:T(8,128)(2,1)} %collective-permute-done.23), channel_id=1, source_target_pairs={{1,0},{2,1},{3,2},{5,4},{6,5},{7,6},{9,8},{10,9},{11,10},{13,12},{... | collective-permute-start | bytes 2359304 | tf_op jit(solution)/shard_map/ppermute | solution.py:537
  633.5 45.2 %collective-permute-start.25 = (bf16[512,768]{1,0:T(8,128)(2,1)}, bf16[512,768]{1,0:T(8,128)(2,1)}, u32[]{:S(2)}, u32[]{:S(2)}) collective-permute-start(bf16[512,768]{1,0:T(8,128)(2,1)} %collective-permute-done.21), channel_id=1, source_target_pairs={{0,1},{1,2},{2,3},{4,5},{5,6},{6,7},{8,9},{9,10},{10,11},{12,13},{... | collective-permute-start | bytes 2359304 | tf_op jit(solution)/shard_map/ppermute | solution.py:536
  660.9 40.6 %collective-permute-start.31 = (bf16[1024,768]{1,0:T(8,128)(2,1)}, bf16[1024,768]{1,0:T(8,128)(2,1)}, u32[]{:S(2)}, u32[]{:S(2)}) collective-permute-start(bf16[1024,768]{1,0:T(8,128)(2,1)} %collective-permute-done.30), channel_id=1, source_target_pairs={{1,0},{2,1},{3,2},{5,4},{6,5},{7,6},{9,8},{10,9},{11,10},{13,12},{... | collective-permute-start | bytes 4718600 | tf_op jit(solution)/shard_map/ppermute | solution.py:537
  668.5 51.5 %collective-permute-start.29 = (bf16[1024,768]{1,0:T(8,128)(2,1)}, bf16[1024,768]{1,0:T(8,128)(2,1)}, u32[]{:S(2)}, u32[]{:S(2)}) collective-permute-start(bf16[1024,768]{1,0:T(8,128)(2,1)} %collective-permute-done.28), channel_id=1, source_target_pairs={{0,1},{1,2},{2,3},{4,5},{5,6},{6,7},{8,9},{9,10},{10,11},{12,13},{... | collective-permute-start | bytes 4718600 | tf_op jit(solution)/shard_map/ppermute | solution.py:536
  695.3 21.4 %collective-permute-start.34 = (bf16[96,832]{0,1:T(8,128)(2,1)}, bf16[96,832]{0,1:T(8,128)(2,1)S(1)}, u32[]{:S(2)}, u32[]{:S(2)}) collective-permute-start(bf16[96,832]{0,1:T(8,128)(2,1)} %fusion.17), channel_id=1, source_target_pairs={{0,2},{2,0},{1,3},{3,1},{4,6},{6,4},{5,7},{7,5},{8,10},{10,8},{9,1... | collective-permute-start | bytes 479240 | tf_op jit(solution)/shard_map/ppermute | solution.py:514
  701.5 44.4 %collective-permute-start.32 = (bf16[1024,768]{1,0:T(8,128)(2,1)}, bf16[1024,768]{1,0:T(8,128)(2,1)}, u32[]{:S(2)}, u32[]{:S(2)}) collective-permute-start(bf16[1024,768]{1,0:T(8,128)(2,1)} %collective-permute-done.31), channel_id=1, source_target_pairs={{1,0},{2,1},{3,2},{5,4},{6,5},{7,6},{9,8},{10,9},{11,10},{13,12},{... | collective-permute-start | bytes 4718600 | tf_op jit(solution)/shard_map/ppermute | solution.py:537
  716.8 25.7 %collective-permute-start.35 = (f32[96,5]{0,1:T(8,128)S(1)}, f32[96,5]{0,1:T(8,128)S(1)}, u32[]{:S(2)}, u32[]{:S(2)}) collective-permute-start(f32[96,5]{0,1:T(8,128)S(1)} %slice.172), channel_id=1, source_target_pairs={{0,1},{1,0},{2,3},{3,2},{4,5},{5,4},{6,7},{7,6},{8,9},{9,8},{10,11... | collective-permute-start | bytes 5768 | tf_op jit(solution)/shard_map/ppermute | solution.py:514
  720.0 28.8 %collective-permute-start.33 = (bf16[1024,768]{1,0:T(8,128)(2,1)}, bf16[1024,768]{1,0:T(8,128)(2,1)S(1)}, u32[]{:S(2)}, u32[]{:S(2)}) collective-permute-start(bf16[1024,768]{1,0:T(8,128)(2,1)} %collective-permute-done.29), channel_id=1, source_target_pairs={{0,1},{1,2},{2,3},{4,5},{5,6},{6,7},{8,9},{9,10},{10,11},{12,13},{... | collective-permute-start | bytes 4718600 | tf_op jit(solution)/shard_map/ppermute | solution.py:536
  (42 other events, 311.1 us)
Sparse Core Ops, SparseCore 0:
  158.2 43.4 reduce-scatter.5
  328.0 53.3 reduce-scatter.7
  440.8 45.0 reduce-scatter.3
Sparse Core Ops, SparseCore 1:
  468.9 110.5 all-gather.1

commit v3 on v2

--- a/solution.py
+++ b/solution.py
@@ -237,184 +237,322 @@
     return total
 
 
-def attention_kernel(runs, slots, q_ref, g_ref, *refs, block, per_run, parts, first, carried):
+def pick_heads(both, heads):
+    return [jnp.where(mine, both, jnp.zeros_like(both)) for mine in heads]
+
+
+def attend_kernel(info, slots, q_ref, g_ref, dense_ref, prior_ref, *refs, block, run_rows, parts, run):
     k_parts, v_parts, refs = refs[:parts], refs[parts : 2 * parts], refs[2 * parts :]
-    if carried:
-        dk_in, dv_in, refs = refs[0], refs[1], refs[2:]
-    o_ref, dq_ref, dk_ref, dv_ref, k_ref, v_ref, score_ref, soft_ref, acc_ref = refs
-    step = pl.program_id(1)
-
-    @pl.when(step == 0)
-    def _():
+    o_ref, stat_ref, send_ref, keep_ref, k_ref, v_ref, score_ref, acc_ref, branch_ref = refs
+    per_run = run_rows // block
+    pair, place_in_run = pl.program_id(0), pl.program_id(1)
+    full = info[run]
+
+    @pl.when((pair == 0) & (place_in_run == 0))
+    def _():
+        branch_ref[...] = prior_ref[...].astype(F32)
+
+    @pl.when(place_in_run == 0)
+    def _():
+        at = 0
         for j in range(parts):
-            there = pl.ds(j * k_parts[j].shape[0], k_parts[j].shape[0])
+            there = pl.ds(at, k_parts[j].shape[0])
             k_ref[there, :] = k_parts[j][...]
             v_ref[there, :] = v_parts[j][...]
-        dk_ref[...] = dk_in[...] if carried else jnp.zeros_like(dk_ref)
-        dv_ref[...] = dv_in[...] if carried else jnp.zeros_like(dv_ref)
-
-    step = step + first
-    full = runs[step // per_run] * per_run + step % per_run
+            at += k_parts[j].shape[0]
+
     lane = lax.broadcasted_iota(jnp.int32, (block, LANES), 1)
     heads = (lane < HD, lane >= HD)
-    both_q, both_g = q_ref[...], g_ref[...]
-    queries = [jnp.where(mine, both_q, jnp.zeros_like(both_q)) for mine in heads]
-    grads = [jnp.where(mine, both_g, jnp.zeros_like(both_g)) for mine in heads]
-
-    def rows_of(at):
-        start = (slots[at // per_run] * per_run + at % per_run) * block
-        return pl.ds(pl.multiple_of(start, block), block)
-
-    def score(at, tops, masked):
-        keys = k_ref[rows_of(at), :]
-        out = []
-        for h in range(2):
-            scores = dot(queries[h], keys, NT)
-            if masked:
-                row = lax.broadcasted_iota(jnp.int32, (block, block), 0)
-                col = lax.broadcasted_iota(jnp.int32, (block, block), 1)
-                scores = jnp.where(col <= row, scores, masked_value)
-            score_ref[h, at] = scores
-            out.append(jnp.maximum(tops[h], lane_fold(scores, jnp.maximum)))
-        return tuple(out)
-
-    least = jnp.full((block, LANES), masked_value, F32)
-    tops = lax.fori_loop(0, full, lambda at, carry: score(at, carry, False), (least, least))
-    tops = score(full, tops, True)
-    tops = [jnp.max(top, axis=1, keepdims=True) * F32(LOG2E) for top in tops]
-
-    acc_ref[...] = jnp.zeros_like(acc_ref)
-
-    def weigh(at, totals):
-        values = v_ref[rows_of(at), :]
-        out = []
-        for h in range(2):
-            soft = jnp.exp2(score_ref[h, at] * F32(LOG2E) - tops[h])
-            out.append(totals[h] + lane_fold(soft, jnp.add))
-            soft_low = soft.astype(BF16)
-            soft_ref[h, at] = soft_low
-            acc_ref[h] += dot(soft_low, values, NN)
-        return tuple(out)
-
-    nought = jnp.zeros((block, LANES), F32)
-    totals = lax.fori_loop(0, full + 1, weigh, (nought, nought))
-    shares = [1.0 / jnp.sum(total, axis=1, keepdims=True) for total in totals]
-    attended = jnp.where(heads[0], acc_ref[0] * shares[0], acc_ref[1] * shares[1])
-    o_ref[...] = attended.astype(o_ref.dtype)
-    product = attended * both_g.astype(F32)
-    row_terms = [
-        jnp.sum(jnp.where(heads[h], product, 0.0), axis=1, keepdims=True) * shares[h] for h in range(2)
-    ]
-    scaled = [(grads[h].astype(F32) * shares[h]).astype(BF16) for h in range(2)]
-
-    acc_ref[...] = jnp.zeros_like(acc_ref)
-
-    def back(at, carry):
-        there = rows_of(at)
-        keys, values = k_ref[there, :], v_ref[there, :]
-        key_terms, value_terms = [], []
-        for h in range(2):
-            soft_low = soft_ref[h, at]
-            grad_soft = dot(scaled[h], values, NT)
-            grad_score = (soft_low.astype(F32) * (grad_soft - row_terms[h])).astype(BF16)
-            acc_ref[h] += dot(grad_score, keys, NN)
-            key_terms.append(dot(grad_score, queries[h], TN))
-            value_terms.append(dot(soft_low, scaled[h], TN))
-        dk_ref[there, :] += key_terms[0] + key_terms[1]
-        dv_ref[there, :] += value_terms[0] + value_terms[1]
-        return carry
-
-    lax.fori_loop(0, full + 1, back, 0)
-    dq_ref[...] = (jnp.where(heads[0], acc_ref[0], acc_ref[1]) * F32(HD**-0.5)).astype(dq_ref.dtype)
-
-
-def attention(runs, slots, q, g, kv_parts, first=0, last=None, carry=None, pair=None):
+
+    def rows_of(at, count):
+        return pl.ds(pl.multiple_of(slots[at] * run_rows, run_rows), count)
+
+    def one_block(within):
+        queries = pick_heads(q_ref[...], heads)
+        seen = (within + 1) * block
+
+        def score(at, tops, last):
+            count = seen if last else run_rows
+            keys = k_ref[rows_of(at, count), :]
+            out = []
+            for h in range(2):
+                scores = dot(queries[h], keys, NT)
+                if last:
+                    row = lax.broadcasted_iota(jnp.int32, (block, count), 0)
+                    col = lax.broadcasted_iota(jnp.int32, (block, count), 1)
+                    scores = jnp.where(col <= row + within * block, scores, masked_value)
+                score_ref[h, at, :, :count] = scores
+                out.append(jnp.maximum(tops[h], lane_fold(scores, jnp.maximum)))
+            return tuple(out)
+
+        least = jnp.full((block, LANES), masked_value, F32)
+        tops = lax.fori_loop(0, full, lambda at, carry: score(at, carry, False), (least, least))
+        tops = score(full, tops, True)
+        tops = [jnp.max(top, axis=1, keepdims=True) * F32(LOG2E) for top in tops]
+
+        acc_ref[...] = jnp.zeros_like(acc_ref)
+
+        def weigh(at, totals, last):
+            count = seen if last else run_rows
+            values = v_ref[rows_of(at, count), :]
+            out = []
+            for h in range(2):
+                soft = jnp.exp2(score_ref[h, at, :, :count] * F32(LOG2E) - tops[h])
+                out.append(totals[h] + lane_fold(soft, jnp.add))
+                acc_ref[h] += dot(soft.astype(BF16), values, NN)
+            return tuple(out)
+
+        nought = jnp.zeros((block, LANES), F32)
+        totals = lax.fori_loop(0, full, lambda at, carry: weigh(at, carry, False), (nought, nought))
+        totals = weigh(full, totals, True)
+        totals = [jnp.sum(total, axis=1, keepdims=True) for total in totals]
+        attended = jnp.where(heads[0], acc_ref[0] / totals[0], acc_ref[1] / totals[1])
+        o_ref[...] = attended.astype(o_ref.dtype)
+        mine = pl.ds(within * block, block)
+        branch_ref[mine, :] += dot(attended.astype(BF16), dense_ref[...], NT)
+        product = attended * g_ref[...].astype(F32)
+        row_terms = [jnp.sum(jnp.where(mine, product, 0.0), axis=1, keepdims=True) for mine in heads]
+        logs = [tops[h] + jnp.log2(totals[h]) for h in range(2)]
+        stats = jnp.where(lane == 0, logs[0], jnp.where(lane == 1, logs[1], 0.0))
+        stats = jnp.where(lane == 2, row_terms[0], jnp.where(lane == 3, row_terms[1], stats))
+        stat_ref[...] = jnp.transpose(stats)[:8]
+
+    for within in range(per_run):
+        pl.when(place_in_run == within)(functools.partial(one_block, within))
+
+    @pl.when((pair == pl.num_programs(0) - 1) & (place_in_run == per_run - 1))
+    def _():
+        half = run_rows // 2
+        send_ref[...] = branch_ref[pl.ds(pl.multiple_of((1 - info[2]) * half, half), half), :].astype(BF16)
+        keep_ref[...] = branch_ref[pl.ds(pl.multiple_of(info[2] * half, half), half), :]
+
+
+def attend(info, slots, q, g, kv_parts, dense, prior, run):
+    rows, width = q.shape
+    model = dense.shape[0]
+    keys = sum(kv.shape[0] for kv in kv_parts)
+    run_rows = rows // 2
+    block = min(512, run_rows)
+    per_run = run_rows // block
+    pairs = width // LANES
+    by_query = pl.BlockSpec((block, LANES), lambda p, i, *_: (run * per_run + i, p))
+    by_key = [pl.BlockSpec((kv.shape[0], LANES), lambda p, i, *_: (0, p)) for kv in kv_parts]
+    by_value = [pl.BlockSpec((kv.shape[0], LANES), lambda p, i, *_: (0, pairs + p)) for kv in kv_parts]
+    kernel = functools.partial(attend_kernel, block=block, run_rows=run_rows, parts=len(kv_parts), run=run)
+    return pl.pallas_call(
+        kernel,
+        grid_spec=pltpu.PrefetchScalarGridSpec(
+            num_scalar_prefetch=2,
+            grid=(pairs, per_run),
+            in_specs=[
+                by_query, by_query,
+                pl.BlockSpec((model, LANES), lambda p, i, *_: (0, p)),
+                pl.BlockSpec((run_rows, model), lambda p, i, *_: (run, 0)),
+                *by_key, *by_value,
+            ],
+            out_specs=[
+                pl.BlockSpec((block, LANES), lambda p, i, *_: (i, p)),
+                pl.BlockSpec((8, block), lambda p, i, *_: (p, i)),
+                whole((run_rows // 2, model)),
+                whole((run_rows // 2, model)),
+            ],
+            scratch_shapes=[
+                pltpu.VMEM((keys, LANES), BF16),
+                pltpu.VMEM((keys, LANES), BF16),
+                pltpu.VMEM((2, keys // run_rows, block, run_rows), F32),
+                pltpu.VMEM((2, block, LANES), F32),
+                pltpu.VMEM((run_rows, model), F32),
+            ],
+        ),
+        out_shape=[
+            jax.ShapeDtypeStruct((run_rows, width), BF16),
+            jax.ShapeDtypeStruct((8 * pairs, run_rows), F32),
+            jax.ShapeDtypeStruct((run_rows // 2, model), BF16),
+            jax.ShapeDtypeStruct((run_rows // 2, model), F32),
+        ],
+        compiler_params=params(),
+        cost_estimate=pl.CostEstimate(
+            flops=24 * run_rows * keys * width, bytes_accessed=12 * keys * width,
+            transcendentals=run_rows * keys * pairs,
+        ),
+        name="attend",
+    )(info, slots, q, g, dense, prior, *kv_parts, *kv_parts)
+
+
+def attend_back_kernel(info, slots, q_ref, g_ref, stat_ref, *refs, block, run_rows, parts, home):
+    k_parts, v_parts, refs = refs[:parts], refs[parts : 2 * parts], refs[2 * parts :]
+    dq_ref, dk_out, dv_out, refs = refs[0], refs[1], refs[2], refs[3:]
+    if home:
+        back_ref, refs = refs[0], refs[1:]
+    k_ref, v_ref, dk_ref, dv_ref, acc_ref = refs
+    per_run = run_rows // block
+    step = pl.program_id(0)
+    full = info[step // per_run]
+
+    @pl.when(step == 0)
+    def _():
+        at = 0
+        for j in range(parts):
+            there = pl.ds(at, k_parts[j].shape[0])
+            k_ref[there, :] = k_parts[j][...]
+            v_ref[there, :] = v_parts[j][...]
+            at += k_parts[j].shape[0]
+        dk_ref[...] = jnp.zeros_like(dk_ref)
+        dv_ref[...] = jnp.zeros_like(dv_ref)
+
+    lane = lax.broadcasted_iota(jnp.int32, (block, LANES), 1)
+    heads = (lane < HD, lane >= HD)
+
+    def rows_of(at, count):
+        return pl.ds(pl.multiple_of(slots[at] * run_rows, run_rows), count)
+
+    def one_block(within):
+        queries, grads = pick_heads(q_ref[...], heads), pick_heads(g_ref[...], heads)
+        stats = jnp.transpose(stat_ref[...])
+        logs, row_terms = [stats[:, h : h + 1] for h in range(2)], [stats[:, 2 + h : 3 + h] for h in range(2)]
+        seen = (within + 1) * block
+        acc_ref[...] = jnp.zeros_like(acc_ref)
+
+        def back(at, last):
+            count = seen if last else run_rows
+            there = rows_of(at, count)
+            keys, values = k_ref[there, :], v_ref[there, :]
+            key_terms, value_terms = [], []
+            for h in range(2):
+                soft = jnp.exp2(dot(queries[h], keys, NT) * F32(LOG2E) - logs[h])
+                if last:
+                    row = lax.broadcasted_iota(jnp.int32, (block, count), 0)
+                    col = lax.broadcasted_iota(jnp.int32, (block, count), 1)
+                    soft = jnp.where(col <= row + within * block, soft, 0.0)
+                grad_soft = dot(grads[h], values, NT)
+                grad_score = (soft * (grad_soft - row_terms[h])).astype(BF16)
+                acc_ref[h] += dot(grad_score, keys, NN)
+                key_terms.append(dot(grad_score, queries[h], TN))
+                value_terms.append(dot(soft.astype(BF16), grads[h], TN))
+            dk_ref[there, :] += key_terms[0] + key_terms[1]
+            dv_ref[there, :] += value_terms[0] + value_terms[1]
+
+        def back_whole(at, carry):
+            back(at, False)
+            return carry
+
+        lax.fori_loop(0, full, back_whole, 0)
+        back(full, True)
+        dq_ref[...] = (jnp.where(heads[0], acc_ref[0], acc_ref[1]) * F32(HD**-0.5)).astype(dq_ref.dtype)
+
+    for within in range(per_run):
+        pl.when(step % per_run == within)(functools.partial(one_block, within))
+
+    @pl.when(step == pl.num_programs(0) - 1)
+    def _():
+        own = dk_out.shape[0]
+        dk_out[...] = dk_ref[:own, :]
+        dv_out[...] = dv_ref[:own, :]
+        if home:
+            back_ref[:, :LANES] = dk_ref[home:, :].astype(BF16)
+            back_ref[:, LANES:] = dv_ref[home:, :].astype(BF16)
+
+
+def attend_back(info, slots, q, g, stats, kv_parts, pair, home):
     rows, width = q.shape
     keys = sum(kv.shape[0] for kv in kv_parts)
     run_rows = rows // 2
     block = min(512, run_rows)
-    per_run = run_rows // block
-    first, last = (0, rows // block) if last is None else (first * per_run, last * per_run)
     pairs = width // LANES
-    count, base = (pairs, 0) if pair is None else (1, pair)
-    done = (last - first) * block
-    by_query = pl.BlockSpec((block, LANES), lambda p, i, *_: (first + i, base + p))
-    by_key = [pl.BlockSpec((kv.shape[0], LANES), lambda p, i, *_: (0, base + p)) for kv in kv_parts]
-    by_value = [pl.BlockSpec((kv.shape[0], LANES), lambda p, i, *_: (0, pairs + base + p)) for kv in kv_parts]
-    of_query = pl.BlockSpec((block, LANES), lambda p, i, *_: (i, p))
-    of_key = pl.BlockSpec((keys, LANES), lambda p, i, *_: (0, p))
-    from_key = pl.BlockSpec((keys, LANES), lambda p, i, *_: (0, base + p))
-    carry = () if carry is None else tuple(carry)
+    own = home or keys
+    by_query = pl.BlockSpec((block, LANES), lambda i, *_: (i, pair))
+    by_key = [pl.BlockSpec((kv.shape[0], LANES), lambda i, *_: (0, pair)) for kv in kv_parts]
+    by_value = [pl.BlockSpec((kv.shape[0], LANES), lambda i, *_: (0, pairs + pair)) for kv in kv_parts]
     kernel = functools.partial(
-        attention_kernel, block=block, per_run=per_run, parts=len(kv_parts), first=first, carried=bool(carry)
+        attend_back_kernel, block=block, run_rows=run_rows, parts=len(kv_parts), home=home
     )
+    out_specs = [pl.BlockSpec((block, LANES), lambda i, *_: (i, 0)), whole((own, LANES)), whole((own, LANES))]
+    out_shape = [
+        jax.ShapeDtypeStruct((rows, LANES), BF16),
+        jax.ShapeDtypeStruct((own, LANES), F32),
+        jax.ShapeDtypeStruct((own, LANES), F32),
+    ]
+    if home:
+        out_specs.append(whole((keys - home, 2 * LANES)))
+        out_shape.append(jax.ShapeDtypeStruct((keys - home, 2 * LANES), BF16))
     return pl.pallas_call(
         kernel,
         grid_spec=pltpu.PrefetchScalarGridSpec(
             num_scalar_prefetch=2,
-            grid=(count, last - first),
-            in_specs=[by_query, by_query, *by_key, *by_value] + [from_key] * len(carry),
-            out_specs=[of_query, of_query, of_key, of_key],
+            grid=(rows // block,),
+            in_specs=[by_query, by_query, pl.BlockSpec((8, block), lambda i, *_: (pair, i)), *by_key, *by_value],
+            out_specs=out_specs,
             scratch_shapes=[
                 pltpu.VMEM((keys, LANES), BF16),
                 pltpu.VMEM((keys, LANES), BF16),
-                pltpu.VMEM((2, keys // block, block, block), F32),
-                pltpu.VMEM((2, keys // block, block, block), BF16),
+                pltpu.VMEM((keys, LANES), F32),
+                pltpu.VMEM((keys, LANES), F32),
                 pltpu.VMEM((2, block, LANES), F32),
             ],
         ),
-        out_shape=[
-            jax.ShapeDtypeStruct((done, count * LANES), BF16),
-            jax.ShapeDtypeStruct((done, count * LANES), BF16),
-            jax.ShapeDtypeStruct((keys, count * LANES), F32),
-            jax.ShapeDtypeStruct((keys, count * LANES), F32),
-        ],
+        out_shape=out_shape,
         compiler_params=params(),
         cost_estimate=pl.CostEstimate(
-            flops=40 * done * keys * count * LANES, bytes_accessed=24 * keys * width,
-            transcendentals=done * keys * count,
-        ),
-        name="attention",
-    )(runs, slots, q, g, *kv_parts, *kv_parts, *carry)
-
-
-def back_kernel(
-    dq_ref, own_k, own_v, got_ref, w_ref, gain_ref, dx_in, cos_ref, low_ref, high_ref, dproj_ref, dx_ref
-):
+            flops=30 * rows * keys * LANES, bytes_accessed=12 * keys * width, transcendentals=rows * keys
+        ),
+        name="attend_back",
+    )(info, slots, q, g, stats, *kv_parts, *kv_parts)
+
+
+def back_kernel(which, dq_ref, *refs, pairs):
+    own_k, refs = refs[:pairs], refs[pairs:]
+    own_v, refs = refs[:pairs], refs[pairs:]
+    got, refs = refs[:pairs], refs[pairs:]
+    w_ref, gain_ref, dx_in, cos_ref, low_ref, high_ref, dproj_ref, send_ref, keep_ref = refs
     half = dq_ref.shape[1]
     cosines, low, high = cos_ref[...], low_ref[...], high_ref[...]
-    for j in range(half // LANES):
+    for j in range(pairs):
         at = slice(j * LANES, (j + 1) * LANES)
         query = dq_ref[:, at].astype(F32)
         dproj_ref[:, at] = turn(query, cosines, -low, -high).astype(BF16)
-        key = own_k[:, at] + got_ref[:, at].astype(F32)
+        key = own_k[j][...] + got[j][:, :LANES].astype(F32)
         dproj_ref[:, half + j * LANES : half + (j + 1) * LANES] = turn(key, cosines, -low, -high).astype(BF16)
-    dproj_ref[:, 2 * half :] = (own_v[...] + got_ref[:, half:].astype(F32)).astype(BF16)
+        value = own_v[j][...] + got[j][:, LANES:].astype(F32)
+        dproj_ref[:, 2 * half + j * LANES : 2 * half + (j + 1) * LANES] = value.astype(BF16)
     summed = dot(dproj_ref[...], w_ref[...], NT) * gain_ref[...] + dx_in[...].astype(F32)
-    dx_ref[...] = summed.astype(dx_ref.dtype)
-
-
-def back(dq, dk, dv, got, w, gain, dx_part, tables):
+    mine = pl.program_id(0) % 2 == which[1]
+
+    @pl.when(mine)
+    def _():
+        keep_ref[...] = summed
+
+    @pl.when(jnp.logical_not(mine))
+    def _():
+        send_ref[...] = summed.astype(send_ref.dtype)
+
+
+def back(which, dq, dk, dv, got, w, gain, dx_part, tables):
     rows, half = dq.shape
     width = w.shape[0]
-    step = min(512, rows)
-    by_row = lambda cols: pl.BlockSpec((step, cols), lambda i: (i, 0))
+    step = rows // 4
+    pairs = len(dk)
+    by_row = lambda cols: pl.BlockSpec((step, cols), lambda i, *_: (i, 0))
+    by_run = pl.BlockSpec((step, width), lambda i, *_: (i // 2, 0))
     return pl.pallas_call(
-        back_kernel,
-        grid=(rows // step,),
-        in_specs=[by_row(half), by_row(half), by_row(half), by_row(2 * half), whole(w.shape),
-                  whole(gain.shape), by_row(width)] + [by_row(LANES)] * 3,
-        out_specs=[by_row(3 * half), by_row(width)],
+        functools.partial(back_kernel, pairs=pairs),
+        grid_spec=pltpu.PrefetchScalarGridSpec(
+            num_scalar_prefetch=1,
+            grid=(4,),
+            in_specs=[by_row(half)] + [by_row(LANES)] * (2 * pairs) + [by_row(2 * LANES)] * pairs
+            + [whole(w.shape), whole(gain.shape), by_row(width)] + [by_row(LANES)] * 3,
+            out_specs=[by_row(3 * half), by_run, by_run],
+        ),
         out_shape=[
             jax.ShapeDtypeStruct((rows, 3 * half), BF16),
-            jax.ShapeDtypeStruct((rows, width), BF16),
+            jax.ShapeDtypeStruct((rows // 2, width), BF16),
+            jax.ShapeDtypeStruct((rows // 2, width), F32),
         ],
         compiler_params=params(),
         cost_estimate=pl.CostEstimate(
             flops=6 * rows * width * half, bytes_accessed=12 * rows * width, transcendentals=0
         ),
         name="back",
-    )(dq, dk, dv, got, w, gain, dx_part, *tables)
+    )(which, dq, *dk, *dv, *got, w, gain, dx_part, *tables)
 
 
 def weight_kernel(
@@ -486,18 +624,20 @@
     out_ref[...] = (dy_ref[0].astype(F32) + scale * (grad - centre - xhat * along)).astype(out_ref.dtype)
 
 
-def norm_back(which, x, dy, kept, got):
+def norm_back(which, x, dy, kept, got, run):
     rows, width = got.shape
-    step = min(512, rows)
+    step = min(256, rows)
     blocks = rows // step
-    chosen = pl.BlockSpec((1, step, width), lambda i, which: (which[0], which[1] * blocks + i, 0))
+    chosen = pl.BlockSpec(
+        (1, step, width), lambda i, which: (which[0], (2 * run + which[1]) * blocks + i, 0)
+    )
     return pl.pallas_call(
         norm_back_kernel,
         grid_spec=pltpu.PrefetchScalarGridSpec(
             num_scalar_prefetch=1,
             grid=(blocks,),
             in_specs=[chosen, chosen,
-                      pl.BlockSpec((step, width), lambda i, which: (which[1] * blocks + i, 0)),
+                      pl.BlockSpec((step, width), lambda i, *_: (run * blocks + i, 0)),
                       pl.BlockSpec((step, width), lambda i, *_: (i, 0))],
             out_specs=pl.BlockSpec((step, width), lambda i, *_: (i, 0)),
         ),
@@ -508,6 +648,39 @@
         ),
         name="norm_back",
     )(which, x, dy, kept, got)
+
+
+def lay_kernel(index, *refs):
+    pieces, out, sems = refs[:-2], refs[-2], refs[-1]
+    half = pieces[0].shape[0]
+    copies = []
+    for j, piece in enumerate(pieces):
+        run, back = j // 4, j % 4
+        slot = lax.rem(index[0] + (4 - back), 4)
+        start = pl.multiple_of(lax.rem(slot, 2) * half, half) + run * 2 * half
+        there = out.at[slot // 2, pl.ds(pl.multiple_of(start, half), half), :]
+        copies.append(pltpu.make_async_copy(piece, there, sems.at[j]))
+        copies[-1].start()
+    for copy in copies:
+        copy.wait()
+
+
+def lay(index, early, late):
+    half, width = early[0].shape
+    anywhere = pl.BlockSpec(memory_space=pl.ANY)
+    return pl.pallas_call(
+        lay_kernel,
+        grid_spec=pltpu.PrefetchScalarGridSpec(
+            num_scalar_prefetch=1,
+            grid=(),
+            in_specs=[anywhere] * 8,
+            out_specs=anywhere,
+            scratch_shapes=[pltpu.SemaphoreType.DMA((8,))],
+        ),
+        out_shape=jax.ShapeDtypeStruct((2, 4 * half, width), BF16),
+        cost_estimate=pl.CostEstimate(flops=0, bytes_accessed=32 * half * width, transcendentals=0),
+        name="lay",
+    )(index[None], *early, *late)
 
 
 def swap(values, axis):
@@ -527,20 +700,9 @@
     return values.reshape(8, 2, *values.shape[1:])
 
 
-def line_gather(mine, index):
-    axes, count = ("mh", "ml"), 4
-    up = [(i, i + 1) for i in range(count - 1)]
-    down = [(i + 1, i) for i in range(count - 1)]
-    from_below, from_above = [mine], [mine]
-    for _ in range(count - 1):
-        from_below.append(lax.ppermute(from_below[-1], axes, up))
-        from_above.append(lax.ppermute(from_above[-1], axes, down))
-    out = jnp.zeros((count,) + mine.shape, mine.dtype)
-    out = lax.dynamic_update_index_in_dim(out, mine, index, 0)
-    for back in (2, 1, 3):
-        piece = jnp.where(index >= back, from_below[back], from_above[count - back])
-        out = lax.dynamic_update_index_in_dim(out, piece, (index - back) % count, 0)
-    return out
+def round_mp(mine):
+    axes = ("mh", "ml")
+    return [mine] + [lax.ppermute(mine, axes, [(i, (i + k) % 4) for i in range(4)]) for k in (1, 2, 3)]
 
 
 def rotation_tables(positions):
@@ -570,7 +732,7 @@
     cols = heads * HD
     units = w_up.shape[1]
     side, part = lax.axis_index("mh"), lax.axis_index("ml")
-    index = 2 * side + part
+    index = (2 * side + part).astype(jnp.int32)
     owner = lax.axis_index("dp") * seq_size + lax.axis_index("seq")
     which = jnp.stack([side, part]).astype(jnp.int32)
     where = jnp.stack([side, owner]).astype(jnp.int32)
@@ -587,13 +749,16 @@
     one = w_qkv[:2].transpose(1, 0, 2).reshape(share, 2 * cols)
     two = jnp.concatenate([w_qkv[2], w_dense.T, small], axis=1)
     three, four = w_up, w_down.T
-    first_widths, second_widths = (6 * cols, 2 * cols, 2 * LANES), (2 * units, 2 * units)
+    first_widths = (6 * cols, 2 * cols, 2 * LANES)
     if owners == 8 and seq_size == 2:
         one, two = gather_half(one, True), gather_half(two, False)
         qkv_w, dense_w, small = place(place_first_kernel, where, one, two, first_widths, (BF16, BF16, F32))
-        three, four = lax.optimization_barrier((three, four, one, two))[:2]
-        three, four = gather_half(three, True), gather_half(four, False)
-        up_w, down_w = place(place_second_kernel, where, three, four, second_widths, (BF16, BF16))
+        three = jnp.concatenate([three, four], axis=1)
+        other = swap(three, "mh")
+        three = jnp.concatenate([jnp.where(side == 0, three, other), jnp.where(side == 0, other, three)], axis=1)
+        three = lax.all_gather(three, ("dp", "seq"), axis=0, tiled=True)
+        up_w = jnp.concatenate([three[:, :units], three[:, 2 * units : 3 * units]], axis=1)
+        down_w = jnp.concatenate([three[:, units : 2 * units], three[:, 3 * units :]], axis=1)
     else:
 
         def gather(values):
@@ -636,40 +801,51 @@
     mlp_part, mlp_dx, grad_up, grad_down, mlp_vectors, grad_up_b = feed(
         which, tokens, out_grad, up_w, up_b, down_w, row_of(4), row_of(5), column_of(4), column_of(5)
     )
-    q, mlp_part = lax.optimization_barrier((q, mlp_part))
-
+    info = jnp.concatenate([runs, which[1:]])
     quarter = rows // 4
 
-    def mixed_of(run, attended):
-        def branch_sum(at):
-            there = lax.dynamic_slice_in_dim(attended, at * quarter, quarter, axis=0)
-            other = lax.dynamic_slice_in_dim(mlp_part, run * run_rows + at * quarter, quarter, axis=0)
-            return lax.dot_general(there, dense_w, NT, preferred_element_type=F32) + other.astype(F32)
-
-        got = swap(branch_sum(1 - part).astype(BF16), "ml")
+    def finish(run, kept, got):
         mine = lax.dynamic_slice(tokens, (side, run * run_rows + part * quarter, 0), (1, quarter, width))[0]
-        return (branch_sum(part) + got.astype(F32) + mine.astype(F32) + row_of(0) + row_of(1)).astype(BF16)
-
-    o_early, dq_early, dk, dv = attention(runs, slots, q, grad_o, kv_parts, 0, 1)
-    mixed_early = lax.all_gather(mixed_of(0, o_early), ("mh", "ml"), axis=0, tiled=True)
-    o_late, dq_late, dk, dv = attention(runs, slots, q, grad_o, kv_parts, 1, 2, (dk, dv))
-    mixed_late = line_gather(mixed_of(1, o_late), index)
-    mixed = jnp.concatenate(
-        [mixed_early.reshape(2, run_rows, width), mixed_late.reshape(2, run_rows, width)], axis=1
-    )
-
-    if seq_size == 2:
-        got = swap(jnp.concatenate([dk[rows:], dv[rows:]], axis=1).astype(BF16), "seq")
-    else:
-        got = lax.psum_scatter(
-            jnp.concatenate([dk, dv], axis=1).astype(BF16), "seq", scatter_dimension=0, tiled=True
-        )
-        dk = dv = jnp.zeros(q.shape, F32)
-    dq = jnp.concatenate([dq_early, dq_late], axis=0)
-    dproj, dx = back(dq, dk, dv, got, qkv_w, row_of(2), mlp_dx, tables)
-    half_rows = rows // 2
-    got_dx = swap(lax.dynamic_slice_in_dim(dx, (1 - part) * half_rows, half_rows, axis=0), "ml")
-    input_grad = line_gather(norm_back(which, tokens, out_grad, dx, got_dx), index).reshape(tokens.shape)
+        return (kept + got.astype(F32) + mine.astype(F32) + row_of(0) + row_of(1)).astype(BF16)
+
+    o_early, stat_early, send, keep_early = attend(info, slots, q, grad_o, kv_parts, dense_w, mlp_part, 0)
+    got_early = swap(send, "ml")
+    q_late, send = lax.optimization_barrier((q, send))
+    o_late, stat_late, send, keep_late = attend(info, slots, q_late, grad_o, kv_parts, dense_w, mlp_part, 1)
+    got_late = swap(send, "ml")
+    mixed_early = finish(0, keep_early, got_early)
+    stats, mixed_early = lax.optimization_barrier((jnp.concatenate([stat_early, stat_late], axis=1), mixed_early))
+    mixed_early = round_mp(mixed_early)
+
+    home = rows if seq_size == 2 else 0
+    dq, dk, dv, got = [], [], [], []
+    q_next = q
+    for pair in range(q.shape[1] // LANES):
+        outs = attend_back(info, slots, q_next, grad_o, stats, kv_parts, pair, home)
+        dq.append(outs[0])
+        if home:
+            dk.append(outs[1])
+            dv.append(outs[2])
+            got.append(swap(outs[3], "seq"))
+            tied = outs[3]
+        else:
+            both = jnp.concatenate([outs[1], outs[2]], axis=1).astype(BF16)
+            got.append(lax.psum_scatter(both, "seq", scatter_dimension=0, tiled=True))
+            dk.append(jnp.zeros((rows, LANES), F32))
+            dv.append(jnp.zeros((rows, LANES), F32))
+            tied = outs[0]
+        if pair == 0:
+            mixed_late = finish(1, keep_late, got_late)
+            q_next, _, mixed_late = lax.optimization_barrier((q, tied, mixed_late))
+            mixed_late = round_mp(mixed_late)
+        else:
+            q_next, _ = lax.optimization_barrier((q, tied))
+    mixed = lay(index, mixed_early, mixed_late)
+    dq = jnp.concatenate(dq, axis=1)
+    dproj, send, keep = back(which, dq, dk, dv, got, qkv_w, row_of(2), mlp_dx, tables)
+    got = [swap(send[run * quarter : (run + 1) * quarter], "ml") for run in range(2)]
+    input_grad = [round_mp(norm_back(which, tokens, out_grad, keep, got[run], run)) for run in range(2)]
+    input_grad = lay(index, *input_grad)
 
     attended = jnp.concatenate([o_early, o_late], axis=0)
     grad_qkv, grad_dense, qkv_vectors, grad_qkv_b = weight_grads(

time: 770 us -> 1100 us (1.43)
  the two profiles are of different devices: /device:TPU:4 before, /device:TPU:0 now
where the time goes in v3:
time: 1100 us
  Pallas kernels  653 us (59%)
  waiting for transfers between devices  269 us (24%)
  starting transfers between devices  92.7 us (8%)
  local copies, waits for them, and re-layouts  38.3 us (3%)
  other arithmetic  27.4 us (2%)
  between operations  15 us (1%)
    pallas_call x2, Pallas kernels, lay(): pl.pallas_call(lay_kernel, grid_spec=pltpu.PrefetchScalarGridSpec(num_sca...  384 us
    ppermute x18, waiting for transfers between devices, swap(): return lax.ppermute(values, axis, [(0, 1), (1, 0)])  204 us
    pallas_call x3, Pallas kernels, attend_back(): pl.pallas_call(kernel, grid_spec=pltpu.PrefetchScalarGridSpec(num_scalar_...  101 us
    pallas_call x2, Pallas kernels, attend(): pl.pallas_call(kernel, grid_spec=pltpu.PrefetchScalarGridSpec(num_scalar_...  68.8 us
    ppermute x12, waiting for transfers between devices, round_mp(): lax.ppermute(mine, axes, [(i, (i + k) % 4) for i in range(4)])  55.8 us
    ppermute x12, starting transfers between devices, round_mp(): lax.ppermute(mine, axes, [(i, (i + k) % 4) for i in range(4)])  50.1 us
    pallas_call x1, Pallas kernels, feed(): pl.pallas_call(feed_kernel, grid_spec=pltpu.PrefetchScalarGridSpec(num_sc...  42.3 us
    ppermute x18, starting transfers between devices, swap(): return lax.ppermute(values, axis, [(0, 1), (1, 0)])  39.2 us
  transfers between devices with their start and end apart: 38, of which 18 were waited for; matrix products, arithmetic and copies ran while one was open for 5% of the time, Pallas kernels for 58%

profile of v3, /device:TPU:0, one launch (start us, length us, event | category | flops | bytes accessed | tf_op | source)
XLA Modules:
  0.0 1095.7 jit_solution(5769217600570051259)
XLA Ops:
  12.5 13.3 %collective-permute-done.9 = bf16[96,1536]{1,0:T(8,128)(2,1)S(1)} collective-permute-done((bf16[96,1536]{1,0:T(8,128)(2,1)S(1)}, bf16[96,1536]{1,0:T(8,128)(2,1)S(1)}, u32[]{:S(2)}, u32[]{:S(2)}) %collective-permute-start.9) | collective-permute-done | bytes 294944 | tf_op jit(solution)/shard_map/ppermute | solution.py:687
  86.5 12.2 %front.1 = (bf16[2048,384]{1,0:T(8,128)(2,1)}, bf16[2048,768]{1,0:T(8,128)(2,1)}, bf16[2048,384]{1,0:T(8,128)(2,1)}) custom-call(s32[2]{0:T(128)} %pad_add_fusion.3.which, bf16[2,2048,768]{2,1,0:T(8,128)(2,1)} %x_ref.9, bf16[2,2048,768]{2,1,0:T(8,128)(2,1)} %dy_ref.9, bf16[768,1152]{1,0:T(8,128)(2,1)} %get-tuple-element.61.w_ref.refs_9_, ...), custom_call_target="tpu_custom_call" | custom-call | flops 4831838208 | bytes 18874368 | tf_op jit(solution)/shard_map/front/pallas_call | solution.py:129
  108.0 42.3 %feed.1 = (bf16[2048,768]{1,0:T(8,128)(2,1)}, bf16[2048,768]{1,0:T(8,128)(2,1)}, bf16[768,1536]{1,0:T(8,128)(2,1)}, bf16[768,1536]{1,0:T(8,128)(2,1)}, f32[768,128]{1,0:T(8,128)}, /*index=5*/f32[1,1536]{1,0:T(1,128)}) custom-call(s32[2]{0:T(128)} %pad_add_fusion.3.which, bf16[2,2048,768]{2,1,0:T(8,128)(2,1)} %x_ref.9, bf16[2,2048,768]{2,1,0:T(8,128)(2,1)} %dy_ref.9, ...), custom_call_target="tpu_custom_call" | custom-call | flops 28991029248 | bytes 28311552 | tf_op jit(solution)/shard_map/feed/pallas_call | solution.py:205
  150.3 19.7 %collective-permute-done.10.refs_1_.refs_3_ = bf16[2048,768]{1,0:T(8,128)(2,1)} collective-permute-done((bf16[2048,768]{1,0:T(8,128)(2,1)}, bf16[2048,768]{1,0:T(8,128)(2,1)}, u32[]{:S(2)}, u32[]{:S(2)}) %collective-permute-start.10) | collective-permute-done | bytes 3145760 | tf_op jit(solution)/shard_map/ppermute | solution.py:687
  169.9 18.5 %attend.2 = (bf16[1024,384]{1,0:T(8,128)(2,1)}, f32[24,1024]{1,0:T(8,128)}, bf16[512,768]{1,0:T(8,128)(2,1)}, f32[512,768]{1,0:T(8,128)}) custom-call(s32[3]{0:T(128)} %pad_add_fusion.1.info, s32[4]{0:T(128)} %select_reduce_fusion.slots, bf16[2048,384]{1,0:T(8,128)(2,1)} %get-tuple-element.85.q_ref, bf16[2048,384]{1,0:T(8,128)(2,1)} %get-tuple-element.67.g_ref, ...), custom_call_target="tpu_custom_call" | custom-call | flops 38654705664 | bytes 18874368 | tf_op jit(solution)/shard_map/attend/pallas_call | solution.py:342
  188.5 50.2 %attend.3 = (bf16[1024,384]{1,0:T(8,128)(2,1)}, f32[24,1024]{1,0:T(8,128)}, bf16[512,768]{1,0:T(8,128)(2,1)}, f32[512,768]{1,0:T(8,128)}) custom-call(s32[3]{0:T(128)} %pad_add_fusion.1.info, s32[4]{0:T(128)} %select_reduce_fusion.slots, bf16[2048,384]{1,0:T(8,128)(2,1)} %get-tuple-element.85.q_ref, bf16[2048,384]{1,0:T(8,128)(2,1)} %get-tuple-element.67.g_ref, ...), custom_call_target="tpu_custom_call" | custom-call | flops 38654705664 | bytes 18874368 | tf_op jit(solution)/shard_map/attend/pallas_call | solution.py:342
  241.7 17.8 %collective-permute-done.15 = bf16[512,768]{1,0:T(8,128)(2,1)S(1)} collective-permute-done((bf16[512,768]{1,0:T(8,128)(2,1)}, bf16[512,768]{1,0:T(8,128)(2,1)S(1)}, u32[]{:S(2)}, u32[]{:S(2)}) %collective-permute-start.15) | collective-permute-done | bytes 786464 | tf_op jit(solution)/shard_map/ppermute | solution.py:687
  259.5 16.2 %collective-permute-done.11 = bf16[512,768]{1,0:T(8,128)(2,1)S(1)} collective-permute-done((bf16[512,768]{1,0:T(8,128)(2,1)}, bf16[512,768]{1,0:T(8,128)(2,1)S(1)}, u32[]{:S(2)}, u32[]{:S(2)}) %collective-permute-start.11) | collective-permute-done | bytes 786464 | tf_op jit(solution)/shard_map/ppermute | solution.py:687
  279.7 33.6 %attend_back.3 = (bf16[2048,128]{1,0:T(8,128)(2,1)}, f32[2048,128]{1,0:T(8,128)}, f32[2048,128]{1,0:T(8,128)}, bf16[2048,256]{1,0:T(8,128)(2,1)}) custom-call(s32[3]{0:T(128)} %pad_add_fusion.1.info, s32[4]{0:T(128)} %select_reduce_fusion.slots, bf16[2048,384]{1,0:T(8,128)(2,1)} %get-tuple-element.85.q_ref, bf16[2048,384]{1,0:T(8,128)(2,1)} %get-tuple-element.67.g_ref, ...), custom_call_target="tpu_custom_call" | custom-call | flops 32212254720 | bytes 18874368 | tf_op jit(solution)/shard_map/attend_back/pallas_call | solution.py:478
  313.3 33.7 %attend_back.4 = (bf16[2048,128]{1,0:T(8,128)(2,1)}, f32[2048,128]{1,0:T(8,128)}, f32[2048,128]{1,0:T(8,128)}, bf16[2048,256]{1,0:T(8,128)(2,1)}) custom-call(s32[3]{0:T(128)} %pad_add_fusion.1.info, s32[4]{0:T(128)} %select_reduce_fusion.slots, bf16[2048,384]{1,0:T(8,128)(2,1)} %get-tuple-element.85.q_ref, bf16[2048,384]{1,0:T(8,128)(2,1)} %get-tuple-element.67.g_ref, ...), custom_call_target="tpu_custom_call" | custom-call | flops 32212254720 | bytes 18874368 | tf_op jit(solution)/shard_map/attend_back/pallas_call | solution.py:478
  347.0 33.8 %attend_back.5 = (bf16[2048,128]{1,0:T(8,128)(2,1)}, f32[2048,128]{1,0:T(8,128)}, f32[2048,128]{1,0:T(8,128)}, bf16[2048,256]{1,0:T(8,128)(2,1)}) custom-call(s32[3]{0:T(128)} %pad_add_fusion.1.info, s32[4]{0:T(128)} %select_reduce_fusion.slots, bf16[2048,384]{1,0:T(8,128)(2,1)} %get-tuple-element.85.q_ref, bf16[2048,384]{1,0:T(8,128)(2,1)} %get-tuple-element.67.g_ref, ...), custom_call_target="tpu_custom_call" | custom-call | flops 32212254720 | bytes 18874368 | tf_op jit(solution)/shard_map/attend_back/pallas_call | solution.py:478
  388.5 18.6 %collective-permute-done.21.refs_8_ = bf16[2048,256]{1,0:T(8,128)(2,1)S(1)} collective-permute-done((bf16[2048,256]{1,0:T(8,128)(2,1)}, bf16[2048,256]{1,0:T(8,128)(2,1)S(1)}, u32[]{:S(2)}, u32[]{:S(2)}) %collective-permute-start.21) | collective-permute-done | bytes 1048608 | tf_op jit(solution)/shard_map/ppermute | solution.py:687
  407.2 22.6 %collective-permute-done.20.refs_7_ = bf16[2048,256]{1,0:T(8,128)(2,1)} collective-permute-done((bf16[2048,256]{1,0:T(8,128)(2,1)}, bf16[2048,256]{1,0:T(8,128)(2,1)}, u32[]{:S(2)}, u32[]{:S(2)}) %collective-permute-start.20) | collective-permute-done | bytes 1048608 | tf_op jit(solution)/shard_map/ppermute | solution.py:687
  429.7 21.0 %collective-permute-done.19.refs_6_ = bf16[2048,256]{1,0:T(8,128)(2,1)} collective-permute-done((bf16[2048,256]{1,0:T(8,128)(2,1)}, bf16[2048,256]{1,0:T(8,128)(2,1)}, u32[]{:S(2)}, u32[]{:S(2)}) %collective-permute-start.19) | collective-permute-done | bytes 1048608 | tf_op jit(solution)/shard_map/ppermute | solution.py:687
  450.8 14.4 %back.1 = (bf16[2048,1152]{1,0:T(8,128)(2,1)}, bf16[1024,768]{1,0:T(8,128)(2,1)}, f32[1024,768]{1,0:T(8,128)}) custom-call(s32[2]{0:T(128)} %pad_add_fusion.3.which, bf16[2048,384]{1,0:T(8,128)(2,1)} %pad_maximum_fusion.3.dq_ref, f32[2048,128]{1,0:T(8,128)} %get-tuple-element.87.refs_0_, f32[2048,128]{1,0:T(8,128)} %get-tuple-element.88.refs_1_, ...), custom_call_target="tpu_custom_call" | custom-call | flops 3623878656 | bytes 18874368 | tf_op jit(solution)/shard_map/back/pallas_call | solution.py:536
  465.2 15.4 %weight_grads.1 = (bf16[768,1152]{1,0:T(8,128)(2,1)}, bf16[768,384]{1,0:T(8,128)(2,1)}, f32[768,128]{1,0:T(8,128)}, f32[1,1152]{1,0:T(1,128)}) custom-call(s32[2]{0:T(128)} %pad_add_fusion.3.which, bf16[2,2048,768]{2,1,0:T(8,128)(2,1)} %x_ref.9, bf16[2,2048,768]{2,1,0:T(8,128)(2,1)} %dy_ref.9, bf16[2048,1152]{1,0:T(8,128)(2,1)} %get-tuple-element.97.dproj_ref, ...), custom_call_target="tpu_custom_call" | custom-call | flops 4831838208 | bytes 18874368 | tf_op jit(solution)/shard_map/weight_grads/pallas_call | solution.py:594
  497.2 46.1 %collective-permute-done.26.got_ref = bf16[512,768]{1,0:T(8,128)(2,1)S(1)} collective-permute-done((bf16[512,768]{1,0:T(8,128)(2,1)S(1)}, bf16[512,768]{1,0:T(8,128)(2,1)S(1)}, u32[]{:S(2)}, u32[]{:S(2)}) %collective-permute-start.26) | collective-permute-done | bytes 786464 | tf_op jit(solution)/shard_map/ppermute | solution.py:687
  551.3 13.2 %collective-permute-done.22.got_ref = bf16[512,768]{1,0:T(8,128)(2,1)S(1)} collective-permute-done((bf16[512,768]{1,0:T(8,128)(2,1)}, bf16[512,768]{1,0:T(8,128)(2,1)S(1)}, u32[]{:S(2)}, u32[]{:S(2)}) %collective-permute-start.22) | collective-permute-done | bytes 786464 | tf_op jit(solution)/shard_map/ppermute | solution.py:687
  569.4 41.4 %collective-permute-done.18.refs_7_ = bf16[512,768]{1,0:T(8,128)(2,1)} collective-permute-done((bf16[512,768]{1,0:T(8,128)(2,1)S(1)}, bf16[512,768]{1,0:T(8,128)(2,1)}, u32[]{:S(2)}, u32[]{:S(2)}) %collective-permute-start.18) | collective-permute-done | bytes 786464 | tf_op jit(solution)/shard_map/ppermute | solution.py:705
  610.8 21.1 %collective-permute-start.29 = (bf16[512,768]{1,0:T(8,128)(2,1)S(1)}, bf16[512,768]{1,0:T(8,128)(2,1)S(1)}, u32[]{:S(2)}, u32[]{:S(2)}) collective-permute-start(bf16[512,768]{1,0:T(8,128)(2,1)S(1)} %copy-done.1), channel_id=1, source_target_pairs={{0,3},{1,0},{2,1},{3,2},{4,7},{5,4},{6,5},{7,6},{8,11},{9,8},{10,9... | collective-permute-start | bytes 2359304 | tf_op jit(solution)/shard_map/ppermute | solution.py:705
  631.9 14.4 %collective-permute-done.14.refs_3_ = bf16[512,768]{1,0:T(8,128)(2,1)} collective-permute-done((bf16[512,768]{1,0:T(8,128)(2,1)S(1)}, bf16[512,768]{1,0:T(8,128)(2,1)}, u32[]{:S(2)}, u32[]{:S(2)}) %collective-permute-start.14) | collective-permute-done | bytes 786464 | tf_op jit(solution)/shard_map/ppermute | solution.py:705
  646.4 18.9 %collective-permute-start.24 = (bf16[512,768]{1,0:T(8,128)(2,1)}, bf16[512,768]{1,0:T(8,128)(2,1)S(1)}, u32[]{:S(2)}, u32[]{:S(2)}) collective-permute-start(bf16[512,768]{1,0:T(8,128)(2,1)} %norm_back.2.refs_0_), channel_id=1, source_target_pairs={{0,2},{1,3},{2,0},{3,1},{4,6},{5,7},{6,4},{7,5},{8,10},{9,11},{10,... | collective-permute-start | bytes 2359304 | tf_op jit(solution)/shard_map/ppermute | solution.py:705
  669.0 191.8 %lay.2 = bf16[2,2048,768]{2,1,0:T(8,128)(2,1)} custom-call(s32[1]{0:T(128)} %bitcast.index, bf16[512,768]{1,0:T(8,128)(2,1)} %copy-done.3, bf16[512,768]{1,0:T(8,128)(2,1)} %collective-permute-done.12.refs_1_, bf16[512,768]{1,0:T(8,128)(2,1)} %collective-permute-done.13.refs_2_, bf16[512,768]{1,0:T(8,128)(2,1)} %collective-permute-done.14.refs_3_, ...), custom_call_target="tpu_custom_call" | custom-call | bytes 12582912 | tf_op jit(solution)/shard_map/lay/pallas_call | solution.py:671
  862.2 191.8 %lay.3 = bf16[2,2048,768]{2,1,0:T(8,128)(2,1)} custom-call(s32[1]{0:T(128)} %bitcast.index, bf16[512,768]{1,0:T(8,128)(2,1)} %norm_back.2.refs_0_, bf16[512,768]{1,0:T(8,128)(2,1)} %collective-permute-done.23.refs_1_, bf16[512,768]{1,0:T(8,128)(2,1)} %copy-done.14, bf16[512,768]{1,0:T(8,128)(2,1)} %collective-permute-done.25.refs_3_, ...), custom_call_target="tpu_custom_call" | custom-call | bytes 12582912 | tf_op jit(solution)/shard_map/lay/pallas_call | solution.py:671
  (269 shorter events, 158.8 us)
Async XLA Ops:
  7.2 95.7 %all-gather.2.cloned.1.call-start = ((), (), s32[]{:S(2)}) async-start(), calls=%async_computation.3 | async-start | bytes 5308416 | tf_op jit(solution)/shard_map/all_gather | solution.py:759
  27.8 1026.2 %reduce-scatter.6.cloned.1.call-start = ((), (), s32[]{:S(2)}) async-start(), calls=%async_computation.5 | async-start | bytes 2654208 | tf_op jit(solution)/shard_map/reduce_scatter | solution.py:856
  98.7 71.3 %collective-permute-start.10 = (bf16[2048,768]{1,0:T(8,128)(2,1)}, bf16[2048,768]{1,0:T(8,128)(2,1)}, u32[]{:S(2)}, u32[]{:S(2)}) collective-permute-start(bf16[2048,768]{1,0:T(8,128)(2,1)} %get-tuple-element.69.refs_0_.refs_2_), channel_id=1, source_target_pairs={{0,4},{4,0},{1,5},{5,1},{2,6},{6,2},{3,7},{7,3},{8,12},{12,8},{9,1... | collective-permute-start | bytes 9437192 | tf_op jit(solution)/shard_map/ppermute | solution.py:687
  188.5 879.2 %reduce-scatter.8.cloned.1.call-start = ((), (), s32[]{:S(2)}) async-start(), calls=%async_computation.6 | async-start | bytes 2654208 | tf_op jit(solution)/shard_map/reduce_scatter | solution.py:856
  238.8 20.6 %collective-permute-start.15 = (bf16[512,768]{1,0:T(8,128)(2,1)}, bf16[512,768]{1,0:T(8,128)(2,1)S(1)}, u32[]{:S(2)}, u32[]{:S(2)}) collective-permute-start(bf16[512,768]{1,0:T(8,128)(2,1)} %get-tuple-element.79), channel_id=1, source_target_pairs={{0,1},{1,0},{2,3},{3,2},{4,5},{5,4},{6,7},{7,6},{8,9},{9,8},{10,11... | collective-permute-start | bytes 2359304 | tf_op jit(solution)/shard_map/ppermute | solution.py:687
  240.1 35.5 %collective-permute-start.11 = (bf16[512,768]{1,0:T(8,128)(2,1)}, bf16[512,768]{1,0:T(8,128)(2,1)S(1)}, u32[]{:S(2)}, u32[]{:S(2)}) collective-permute-start(bf16[512,768]{1,0:T(8,128)(2,1)} %get-tuple-element.71), channel_id=1, source_target_pairs={{0,1},{1,0},{2,3},{3,2},{4,5},{5,4},{6,7},{7,6},{8,9},{9,8},{10,11... | collective-permute-start | bytes 2359304 | tf_op jit(solution)/shard_map/ppermute | solution.py:687
  240.9 832.2 %reduce-scatter.4.cloned.1.call-start = ((), (), s32[]{:S(2)}) async-start(), calls=%async_computation.4 | async-start | bytes 2875392 | tf_op jit(solution)/shard_map/reduce_scatter | solution.py:856
  380.8 26.4 %collective-permute-start.21 = (bf16[2048,256]{1,0:T(8,128)(2,1)}, bf16[2048,256]{1,0:T(8,128)(2,1)S(1)}, u32[]{:S(2)}, u32[]{:S(2)}) collective-permute-start(bf16[2048,256]{1,0:T(8,128)(2,1)} %get-tuple-element.93), channel_id=1, source_target_pairs={{0,4},{4,0},{1,5},{5,1},{2,6},{6,2},{3,7},{7,3},{8,12},{12,8},{9,1... | collective-permute-start | bytes 3145736 | tf_op jit(solution)/shard_map/ppermute | solution.py:687
  381.7 48.1 %collective-permute-start.20 = (bf16[2048,256]{1,0:T(8,128)(2,1)}, bf16[2048,256]{1,0:T(8,128)(2,1)}, u32[]{:S(2)}, u32[]{:S(2)}) collective-permute-start(bf16[2048,256]{1,0:T(8,128)(2,1)} %get-tuple-element.84), channel_id=1, source_target_pairs={{0,4},{4,0},{1,5},{5,1},{2,6},{6,2},{3,7},{7,3},{8,12},{12,8},{9,1... | collective-permute-start | bytes 3145736 | tf_op jit(solution)/shard_map/ppermute | solution.py:687
  382.9 67.9 %collective-permute-start.19 = (bf16[2048,256]{1,0:T(8,128)(2,1)}, bf16[2048,256]{1,0:T(8,128)(2,1)}, u32[]{:S(2)}, u32[]{:S(2)}) collective-permute-start(bf16[2048,256]{1,0:T(8,128)(2,1)} %get-tuple-element.77), channel_id=1, source_target_pairs={{0,4},{4,0},{1,5},{5,1},{2,6},{6,2},{3,7},{7,3},{8,12},{12,8},{9,1... | collective-permute-start | bytes 3145736 | tf_op jit(solution)/shard_map/ppermute | solution.py:687
  490.6 52.7 %collective-permute-start.26 = (bf16[512,768]{1,0:T(8,128)(2,1)S(1)}, bf16[512,768]{1,0:T(8,128)(2,1)S(1)}, u32[]{:S(2)}, u32[]{:S(2)}) collective-permute-start(bf16[512,768]{1,0:T(8,128)(2,1)S(1)} %get-tuple-element.118), channel_id=1, source_target_pairs={{0,1},{1,0},{2,3},{3,2},{4,5},{5,4},{6,7},{7,6},{8,9},{9,8},{10,11... | collective-permute-start | bytes 2359304 | tf_op jit(solution)/shard_map/ppermute | solution.py:687
  492.0 56.3 %collective-permute-start.16 = (bf16[512,768]{1,0:T(8,128)(2,1)S(1)}, bf16[512,768]{1,0:T(8,128)(2,1)}, u32[]{:S(2)}, u32[]{:S(2)}) collective-permute-start(bf16[512,768]{1,0:T(8,128)(2,1)S(1)} %get-tuple-element.80.refs_4_), channel_id=1, source_target_pairs={{0,1},{1,2},{2,3},{3,0},{4,5},{5,6},{6,7},{7,4},{8,9},{9,10},{10,1... | collective-permute-start | bytes 2359304 | tf_op jit(solution)/shard_map/ppermute | solution.py:705
  492.7 55.7 %collective-permute-start.17 = (bf16[512,768]{1,0:T(8,128)(2,1)S(1)}, bf16[512,768]{1,0:T(8,128)(2,1)}, u32[]{:S(2)}, u32[]{:S(2)}) collective-permute-start(bf16[512,768]{1,0:T(8,128)(2,1)S(1)} %get-tuple-element.80.refs_4_), channel_id=1, source_target_pairs={{0,2},{1,3},{2,0},{3,1},{4,6},{5,7},{6,4},{7,5},{8,10},{9,11},{10,... | collective-permute-start | bytes 2359304 | tf_op jit(solution)/shard_map/ppermute | solution.py:705
  494.5 70.0 %collective-permute-start.22 = (bf16[512,768]{1,0:T(8,128)(2,1)}, bf16[512,768]{1,0:T(8,128)(2,1)S(1)}, u32[]{:S(2)}, u32[]{:S(2)}) collective-permute-start(bf16[512,768]{1,0:T(8,128)(2,1)} %get-tuple-element.119), channel_id=1, source_target_pairs={{0,1},{1,0},{2,3},{3,2},{4,5},{5,4},{6,7},{7,6},{8,9},{9,8},{10,11... | collective-permute-start | bytes 2359304 | tf_op jit(solution)/shard_map/ppermute | solution.py:687
  496.4 114.4 %collective-permute-start.18 = (bf16[512,768]{1,0:T(8,128)(2,1)S(1)}, bf16[512,768]{1,0:T(8,128)(2,1)}, u32[]{:S(2)}, u32[]{:S(2)}) collective-permute-start(bf16[512,768]{1,0:T(8,128)(2,1)S(1)} %get-tuple-element.80.refs_4_), channel_id=1, source_target_pairs={{0,3},{1,0},{2,1},{3,2},{4,7},{5,4},{6,5},{7,6},{8,11},{9,8},{10,9... | collective-permute-start | bytes 2359304 | tf_op jit(solution)/shard_map/ppermute | solution.py:705
  543.3 67.5 %collective-permute-start.12 = (bf16[512,768]{1,0:T(8,128)(2,1)S(1)}, bf16[512,768]{1,0:T(8,128)(2,1)}, u32[]{:S(2)}, u32[]{:S(2)}) collective-permute-start(bf16[512,768]{1,0:T(8,128)(2,1)S(1)} %get-tuple-element.75.refs_0_), channel_id=1, source_target_pairs={{0,1},{1,2},{2,3},{3,0},{4,5},{5,6},{6,7},{7,4},{8,9},{9,10},{10,1... | collective-permute-start | bytes 2359304 | tf_op jit(solution)/shard_map/ppermute | solution.py:705
  548.3 83.7 %collective-permute-start.13 = (bf16[512,768]{1,0:T(8,128)(2,1)S(1)}, bf16[512,768]{1,0:T(8,128)(2,1)}, u32[]{:S(2)}, u32[]{:S(2)}) collective-permute-start(bf16[512,768]{1,0:T(8,128)(2,1)S(1)} %get-tuple-element.75.refs_0_), channel_id=1, source_target_pairs={{0,2},{1,3},{2,0},{3,1},{4,6},{5,7},{6,4},{7,5},{8,10},{9,11},{10,... | collective-permute-start | bytes 2359304 | tf_op jit(solution)/shard_map/ppermute | solution.py:705
  548.4 98.0 %collective-permute-start.14 = (bf16[512,768]{1,0:T(8,128)(2,1)S(1)}, bf16[512,768]{1,0:T(8,128)(2,1)}, u32[]{:S(2)}, u32[]{:S(2)}) collective-permute-start(bf16[512,768]{1,0:T(8,128)(2,1)S(1)} %get-tuple-element.75.refs_0_), channel_id=1, source_target_pairs={{0,3},{1,0},{2,1},{3,2},{4,7},{5,4},{6,5},{7,6},{8,11},{9,8},{10,9... | collective-permute-start | bytes 2359304 | tf_op jit(solution)/shard_map/ppermute | solution.py:705
  564.5 100.8 %collective-permute-start.27 = (bf16[512,768]{1,0:T(8,128)(2,1)}, bf16[512,768]{1,0:T(8,128)(2,1)}, u32[]{:S(2)}, u32[]{:S(2)}) collective-permute-start(bf16[512,768]{1,0:T(8,128)(2,1)} %norm_back.3.refs_4_), channel_id=1, source_target_pairs={{0,1},{1,2},{2,3},{3,0},{4,5},{5,6},{6,7},{7,4},{8,9},{9,10},{10,1... | collective-permute-start | bytes 2359304 | tf_op jit(solution)/shard_map/ppermute | solution.py:705
  610.8 250.0 %collective-permute-start.28 = (bf16[512,768]{1,0:T(8,128)(2,1)S(1)}, bf16[512,768]{1,0:T(8,128)(2,1)S(1)}, u32[]{:S(2)}, u32[]{:S(2)}) collective-permute-start(bf16[512,768]{1,0:T(8,128)(2,1)S(1)} %copy-done.1), channel_id=1, source_target_pairs={{0,2},{1,3},{2,0},{3,1},{4,6},{5,7},{6,4},{7,5},{8,10},{9,11},{10,... | collective-permute-start | bytes 2359304 | tf_op jit(solution)/shard_map/ppermute | solution.py:705
  610.8 250.0 %collective-permute-start.29 = (bf16[512,768]{1,0:T(8,128)(2,1)S(1)}, bf16[512,768]{1,0:T(8,128)(2,1)S(1)}, u32[]{:S(2)}, u32[]{:S(2)}) collective-permute-start(bf16[512,768]{1,0:T(8,128)(2,1)S(1)} %copy-done.1), channel_id=1, source_target_pairs={{0,3},{1,0},{2,1},{3,2},{4,7},{5,4},{6,5},{7,6},{8,11},{9,8},{10,9... | collective-permute-start | bytes 2359304 | tf_op jit(solution)/shard_map/ppermute | solution.py:705
  631.9 228.9 %collective-permute-start.23 = (bf16[512,768]{1,0:T(8,128)(2,1)}, bf16[512,768]{1,0:T(8,128)(2,1)}, u32[]{:S(2)}, u32[]{:S(2)}) collective-permute-start(bf16[512,768]{1,0:T(8,128)(2,1)} %norm_back.2.refs_0_), channel_id=1, source_target_pairs={{0,1},{1,2},{2,3},{3,0},{4,5},{5,6},{6,7},{7,4},{8,9},{9,10},{10,1... | collective-permute-start | bytes 2359304 | tf_op jit(solution)/shard_map/ppermute | solution.py:705
  646.4 214.4 %collective-permute-start.24 = (bf16[512,768]{1,0:T(8,128)(2,1)}, bf16[512,768]{1,0:T(8,128)(2,1)S(1)}, u32[]{:S(2)}, u32[]{:S(2)}) collective-permute-start(bf16[512,768]{1,0:T(8,128)(2,1)} %norm_back.2.refs_0_), channel_id=1, source_target_pairs={{0,2},{1,3},{2,0},{3,1},{4,6},{5,7},{6,4},{7,5},{8,10},{9,11},{10,... | collective-permute-start | bytes 2359304 | tf_op jit(solution)/shard_map/ppermute | solution.py:705
  665.3 195.6 %collective-permute-start.25 = (bf16[512,768]{1,0:T(8,128)(2,1)}, bf16[512,768]{1,0:T(8,128)(2,1)}, u32[]{:S(2)}, u32[]{:S(2)}) collective-permute-start(bf16[512,768]{1,0:T(8,128)(2,1)} %norm_back.2.refs_0_), channel_id=1, source_target_pairs={{0,3},{1,0},{2,1},{3,2},{4,7},{5,4},{6,5},{7,6},{8,11},{9,8},{10,9... | collective-permute-start | bytes 2359304 | tf_op jit(solution)/shard_map/ppermute | solution.py:705
  (53 other events, 1118.4 us)
Sparse Core Ops, SparseCore 0:
  27.9 45.7 all-gather.1
  188.6 55.2 reduce-scatter.5
  247.6 42.4 reduce-scatter.7
  488.4 43.6 reduce-scatter.3

commit v4 on v3

--- a/solution.py
+++ b/solution.py
@@ -17,6 +17,8 @@
 norm_eps = 1e-05
 masked_value = -1e30
 vmem_bytes = 60 * 2**20
+brief = pl.CostEstimate(flops=1, bytes_accessed=1, transcendentals=0)
+long = pl.CostEstimate(flops=2**33, bytes_accessed=2**24, transcendentals=0)
 
 NN = (((1,), (0,)), ((), ()))
 NT = (((1,), (1,)), ((), ()))
@@ -42,6 +44,11 @@
         + pltpu.roll(chunk, LANES - half, 1) * sine_low
         + pltpu.roll(chunk, half, 1) * sine_high
     )
+
+longest = pl.CostEstimate(flops=2**36, bytes_accessed=2**27, transcendentals=0)
+
+
+anywhere = pl.BlockSpec(memory_space=pl.ANY)
 
 
 def whole(shape):
@@ -66,12 +73,25 @@
     small_ref[...] = jnp.concatenate([two[j][:, 2 * cols :] for j in range(2)], axis=1).astype(F32)
 
 
-def place_second_kernel(where, one_ref, two_ref, up_ref, down_ref):
-    near = where[0] == 0
-    for ref, out in ((one_ref, up_ref), (two_ref, down_ref)):
-        units = ref.shape[-1]
-        out[:, :units] = jnp.where(near, ref[0, 0], ref[0, 1])
-        out[:, units:] = jnp.where(near, ref[0, 1], ref[0, 0])
+def place_second_kernel(pack_ref, up_ref, down_ref):
+    units = pack_ref.shape[-1] // 2
+    for j in range(2):
+        up_ref[:, j * units : (j + 1) * units] = pack_ref[0, j, :, :units]
+        down_ref[:, j * units : (j + 1) * units] = pack_ref[0, j, :, units:]
+
+
+def place_second(pack):
+    owners, _, share, width = pack.shape
+    return pl.pallas_call(
+        place_second_kernel,
+        grid=(owners,),
+        in_specs=[pl.BlockSpec((1,) + pack.shape[1:], lambda i: (i, 0, 0, 0))],
+        out_specs=[pl.BlockSpec((share, width), lambda i: (i, 0))] * 2,
+        out_shape=[jax.ShapeDtypeStruct((owners * share, width), BF16)] * 2,
+        compiler_params=params(),
+        cost_estimate=brief,
+        name="place_second",
+    )(pack)
 
 
 def place(kernel, where, one, two, widths, types):
@@ -96,7 +116,7 @@
         ),
         out_shape=[jax.ShapeDtypeStruct((owners * share, width), kind) for width, kind in zip(widths, types)],
         compiler_params=params(),
-        cost_estimate=pl.CostEstimate(flops=0, bytes_accessed=8 * one.size, transcendentals=0),
+        cost_estimate=brief,
         name="place",
     )(where, one, two)
 
@@ -141,18 +161,58 @@
             jax.ShapeDtypeStruct((rows, half), BF16),
         ],
         compiler_params=params(),
-        cost_estimate=pl.CostEstimate(
-            flops=2 * rows * width * 4 * half, bytes_accessed=12 * rows * width, transcendentals=0
-        ),
+        cost_estimate=brief,
         name="front",
     )(which, x, dy, w, wb, dense, gain, shift, *tables)
 
 
 def feed_kernel(
-    which, x_ref, dy_ref, up_ref, upb_ref, down_ref, gain_ref, shift_ref, gain_col, shift_col,
-    part_ref, dx_ref, gup_ref, gdown_ref, vec_ref, gupb_ref,
-    up_acc, down_acc, sum_acc, dy_acc,
+    which, x_ref, dy_ref, up_ref, upb_ref, down_ref, gain_ref, shift_ref, part_ref, dx_ref, act_ref, grad_ref
 ):
+    xhat, _ = normalise(x_ref[0].astype(F32))
+    normed = (xhat * gain_ref[...] + shift_ref[...]).astype(BF16)
+    hidden = dot(normed, up_ref[...], NN) + upb_ref[...]
+    share = 0.5 * (1.0 + lax.erf(hidden * F32(0.5**0.5)))
+    act = (hidden * share).astype(BF16)
+    act_ref[...] = act
+    slope = share + hidden * (jnp.exp(hidden * hidden * -0.5) * F32(0.3989422804014327))
+    part_ref[...] = dot(act, down_ref[...], NT).astype(part_ref.dtype)
+    grad_low = (dot(dy_ref[0], down_ref[...], NN) * slope).astype(BF16)
+    grad_ref[...] = grad_low
+    dx_ref[...] = (dot(grad_low, up_ref[...], NT) * gain_ref[...]).astype(dx_ref.dtype)
+
+
+def feed(which, x, dy, up, upb, down, gain, shift):
+    _, rows, width = x.shape
+    units = up.shape[1]
+    step = min(256, rows)
+    chosen = pl.BlockSpec((1, step, width), lambda i, which: (which[0], i, 0))
+    by_row = lambda cols: pl.BlockSpec((step, cols), lambda i, *_: (i, 0))
+    return pl.pallas_call(
+        feed_kernel,
+        grid_spec=pltpu.PrefetchScalarGridSpec(
+            num_scalar_prefetch=1,
+            grid=(rows // step,),
+            in_specs=[chosen, chosen, whole(up.shape), whole(upb.shape), whole(down.shape),
+                      whole(gain.shape), whole(shift.shape)],
+            out_specs=[by_row(width), by_row(width), by_row(units), by_row(units)],
+        ),
+        out_shape=[
+            jax.ShapeDtypeStruct((rows, width), BF16),
+            jax.ShapeDtypeStruct((rows, width), BF16),
+            jax.ShapeDtypeStruct((rows, units), BF16),
+            jax.ShapeDtypeStruct((rows, units), BF16),
+        ],
+        compiler_params=params(),
+        cost_estimate=brief,
+        name="feed",
+    )(which, x, dy, up, upb, down, gain, shift)
+
+
+def feed_grads_kernel(
+    which, x_ref, dy_ref, act_ref, grad_ref, up_ref, gain_col, shift_col, *refs
+):
+    both_ref, vec_ref, gupb_ref, up_acc, down_acc, sum_acc, dy_acc = refs[-7:]
     step = pl.program_id(0)
 
     @pl.when(step == 0)
@@ -163,28 +223,19 @@
         dy_acc[...] = jnp.zeros_like(dy_acc)
 
     xhat, _ = normalise(x_ref[0].astype(F32))
-    dy = dy_ref[0]
-    normed = (xhat * gain_ref[...] + shift_ref[...]).astype(BF16)
-    hidden = dot(normed, up_ref[...], NN) + upb_ref[...]
-    share = 0.5 * (1.0 + lax.erf(hidden * F32(0.5**0.5)))
-    act = (hidden * share).astype(BF16)
-    slope = share + hidden * (jnp.exp(hidden * hidden * -0.5) * F32(0.3989422804014327))
-    part_ref[...] = dot(act, down_ref[...], NT).astype(part_ref.dtype)
-    grad = dot(dy, down_ref[...], NN) * slope
-    grad_low = grad.astype(BF16)
-    dx_ref[...] = (dot(grad_low, up_ref[...], NT) * gain_ref[...]).astype(dx_ref.dtype)
-    up_acc[...] += dot(xhat.astype(BF16), grad_low, TN)
-    down_acc[...] += dot(dy, act, TN)
-    sum_acc[...] += jnp.sum(grad_low.astype(F32), axis=0, keepdims=True)
+    dy, grad = dy_ref[0], grad_ref[...]
+    up_acc[...] += dot(xhat.astype(BF16), grad, TN)
+    down_acc[...] += dot(dy, act_ref[...], TN)
+    sum_acc[...] += jnp.sum(grad.astype(F32), axis=0, keepdims=True)
     dy_acc[...] += jnp.sum(dy.astype(F32), axis=0, keepdims=True)
 
     @pl.when(step == pl.num_programs(0) - 1)
     def _():
-        sums = sum_acc[...]
-        raw = up_acc[...]
+        sums, raw = sum_acc[...], up_acc[...]
         up = up_ref[...].astype(F32)
-        gup_ref[...] = (raw * gain_col[...] + shift_col[...] * sums).astype(gup_ref.dtype)
-        gdown_ref[...] = down_acc[...].astype(gdown_ref.dtype)
+        units = up.shape[1]
+        both_ref[:, :units] = (raw * gain_col[...] + shift_col[...] * sums).astype(both_ref.dtype)
+        both_ref[:, units:] = down_acc[...].astype(both_ref.dtype)
         gupb_ref[...] = sums
         lane = lax.broadcasted_iota(jnp.int32, vec_ref.shape, 1)
         gain_grad = jnp.sum(raw * up, axis=1, keepdims=True)
@@ -196,38 +247,32 @@
         )
 
 
-def feed(which, x, dy, up, upb, down, gain, shift, gain_col, shift_col):
+def feed_grads(which, x, dy, act, grad, up, gain_col, shift_col, after=()):
     _, rows, width = x.shape
     units = up.shape[1]
-    step = min(256, rows)
+    step = min(512, rows)
     chosen = pl.BlockSpec((1, step, width), lambda i, which: (which[0], i, 0))
-    by_row = pl.BlockSpec((step, width), lambda i, *_: (i, 0))
-    return pl.pallas_call(
-        feed_kernel,
+    by_row = pl.BlockSpec((step, units), lambda i, *_: (i, 0))
+    return pl.pallas_call(
+        feed_grads_kernel,
         grid_spec=pltpu.PrefetchScalarGridSpec(
             num_scalar_prefetch=1,
             grid=(rows // step,),
-            in_specs=[chosen, chosen, whole(up.shape), whole(upb.shape), whole(down.shape),
-                      whole(gain.shape), whole(shift.shape), whole(gain_col.shape), whole(shift_col.shape)],
-            out_specs=[by_row, by_row, whole((width, units)), whole((width, units)),
-                       whole((width, LANES)), whole((1, units))],
+            in_specs=[chosen, chosen, by_row, by_row, whole(up.shape),
+                      whole(gain_col.shape), whole(shift_col.shape)] + [anywhere] * len(after),
+            out_specs=[whole((width, 2 * units)), whole((width, LANES)), whole((1, units))],
             scratch_shapes=[pltpu.VMEM((width, units), F32), pltpu.VMEM((width, units), F32),
                             pltpu.VMEM((1, units), F32), pltpu.VMEM((1, width), F32)],
         ),
         out_shape=[
-            jax.ShapeDtypeStruct((rows, width), BF16),
-            jax.ShapeDtypeStruct((rows, width), BF16),
-            jax.ShapeDtypeStruct((width, units), BF16),
-            jax.ShapeDtypeStruct((width, units), BF16),
+            jax.ShapeDtypeStruct((width, 2 * units), BF16),
             jax.ShapeDtypeStruct((width, LANES), F32),
             jax.ShapeDtypeStruct((1, units), F32),
         ],
         compiler_params=params(),
-        cost_estimate=pl.CostEstimate(
-            flops=12 * rows * width * units, bytes_accessed=24 * width * units, transcendentals=2 * rows * units
-        ),
-        name="feed",
-    )(which, x, dy, up, upb, down, gain, shift, gain_col, shift_col)
+        cost_estimate=long,
+        name="feed_grads",
+    )(which, x, dy, act, grad, up, gain_col, shift_col, *after)
 
 
 def lane_fold(values, combine):
@@ -241,8 +286,8 @@
     return [jnp.where(mine, both, jnp.zeros_like(both)) for mine in heads]
 
 
-def attend_kernel(info, slots, q_ref, g_ref, dense_ref, prior_ref, *refs, block, run_rows, parts, run):
-    k_parts, v_parts, refs = refs[:parts], refs[parts : 2 * parts], refs[2 * parts :]
+def attend_kernel(info, slots, q_ref, g_ref, dense_ref, prior_ref, *refs, block, run_rows, parts, run, ties):
+    k_parts, v_parts, refs = refs[:parts], refs[parts : 2 * parts], refs[2 * parts + ties :]
     o_ref, stat_ref, send_ref, keep_ref, k_ref, v_ref, score_ref, acc_ref, branch_ref = refs
     per_run = run_rows // block
     pair, place_in_run = pl.program_id(0), pl.program_id(1)
@@ -327,7 +372,7 @@
         keep_ref[...] = branch_ref[pl.ds(pl.multiple_of(info[2] * half, half), half), :]
 
 
-def attend(info, slots, q, g, kv_parts, dense, prior, run):
+def attend(info, slots, q, g, kv_parts, dense, prior, run, after=()):
     rows, width = q.shape
     model = dense.shape[0]
     keys = sum(kv.shape[0] for kv in kv_parts)
@@ -338,7 +383,9 @@
     by_query = pl.BlockSpec((block, LANES), lambda p, i, *_: (run * per_run + i, p))
     by_key = [pl.BlockSpec((kv.shape[0], LANES), lambda p, i, *_: (0, p)) for kv in kv_parts]
     by_value = [pl.BlockSpec((kv.shape[0], LANES), lambda p, i, *_: (0, pairs + p)) for kv in kv_parts]
-    kernel = functools.partial(attend_kernel, block=block, run_rows=run_rows, parts=len(kv_parts), run=run)
+    kernel = functools.partial(
+        attend_kernel, block=block, run_rows=run_rows, parts=len(kv_parts), run=run, ties=len(after)
+    )
     return pl.pallas_call(
         kernel,
         grid_spec=pltpu.PrefetchScalarGridSpec(
@@ -349,7 +396,7 @@
                 pl.BlockSpec((model, LANES), lambda p, i, *_: (0, p)),
                 pl.BlockSpec((run_rows, model), lambda p, i, *_: (run, 0)),
                 *by_key, *by_value,
-            ],
+            ] + [anywhere] * len(after),
             out_specs=[
                 pl.BlockSpec((block, LANES), lambda p, i, *_: (i, p)),
                 pl.BlockSpec((8, block), lambda p, i, *_: (p, i)),
@@ -371,16 +418,13 @@
             jax.ShapeDtypeStruct((run_rows // 2, model), F32),
         ],
         compiler_params=params(),
-        cost_estimate=pl.CostEstimate(
-            flops=24 * run_rows * keys * width, bytes_accessed=12 * keys * width,
-            transcendentals=run_rows * keys * pairs,
-        ),
+        cost_estimate=brief,
         name="attend",
-    )(info, slots, q, g, dense, prior, *kv_parts, *kv_parts)
-
-
-def attend_back_kernel(info, slots, q_ref, g_ref, stat_ref, *refs, block, run_rows, parts, home):
-    k_parts, v_parts, refs = refs[:parts], refs[parts : 2 * parts], refs[2 * parts :]
+    )(info, slots, q, g, dense, prior, *kv_parts, *kv_parts, *after)
+
+
+def attend_back_kernel(info, slots, q_ref, g_ref, stat_ref, *refs, block, run_rows, parts, home, ties):
+    k_parts, v_parts, refs = refs[:parts], refs[parts : 2 * parts], refs[2 * parts + ties :]
     dq_ref, dk_out, dv_out, refs = refs[0], refs[1], refs[2], refs[3:]
     if home:
         back_ref, refs = refs[0], refs[1:]
@@ -453,7 +497,7 @@
             back_ref[:, LANES:] = dv_ref[home:, :].astype(BF16)
 
 
-def attend_back(info, slots, q, g, stats, kv_parts, pair, home):
+def attend_back(info, slots, q, g, stats, kv_parts, pair, home, after=()):
     rows, width = q.shape
     keys = sum(kv.shape[0] for kv in kv_parts)
     run_rows = rows // 2
@@ -464,7 +508,7 @@
     by_key = [pl.BlockSpec((kv.shape[0], LANES), lambda i, *_: (0, pair)) for kv in kv_parts]
     by_value = [pl.BlockSpec((kv.shape[0], LANES), lambda i, *_: (0, pairs + pair)) for kv in kv_parts]
     kernel = functools.partial(
-        attend_back_kernel, block=block, run_rows=run_rows, parts=len(kv_parts), home=home
+        attend_back_kernel, block=block, run_rows=run_rows, parts=len(kv_parts), home=home, ties=len(after)
     )
     out_specs = [pl.BlockSpec((block, LANES), lambda i, *_: (i, 0)), whole((own, LANES)), whole((own, LANES))]
     out_shape = [
@@ -480,7 +524,8 @@
         grid_spec=pltpu.PrefetchScalarGridSpec(
             num_scalar_prefetch=2,
             grid=(rows // block,),
-            in_specs=[by_query, by_query, pl.BlockSpec((8, block), lambda i, *_: (pair, i)), *by_key, *by_value],
+            in_specs=[by_query, by_query, pl.BlockSpec((8, block), lambda i, *_: (pair, i)), *by_key, *by_value]
+            + [anywhere] * len(after),
             out_specs=out_specs,
             scratch_shapes=[
                 pltpu.VMEM((keys, LANES), BF16),
@@ -492,18 +537,17 @@
         ),
         out_shape=out_shape,
         compiler_params=params(),
-        cost_estimate=pl.CostEstimate(
-            flops=30 * rows * keys * LANES, bytes_accessed=12 * keys * width, transcendentals=rows * keys
-        ),
+        cost_estimate=long,
         name="attend_back",
-    )(info, slots, q, g, stats, *kv_parts, *kv_parts)
+    )(info, slots, q, g, stats, *kv_parts, *kv_parts, *after)
 
 
 def back_kernel(which, dq_ref, *refs, pairs):
     own_k, refs = refs[:pairs], refs[pairs:]
     own_v, refs = refs[:pairs], refs[pairs:]
     got, refs = refs[:pairs], refs[pairs:]
-    w_ref, gain_ref, dx_in, cos_ref, low_ref, high_ref, dproj_ref, send_ref, keep_ref = refs
+    w_ref, gain_ref, dx_in, cos_ref, low_ref, high_ref = refs[:6]
+    dproj_ref, send_ref, keep_ref = refs[-3:]
     half = dq_ref.shape[1]
     cosines, low, high = cos_ref[...], low_ref[...], high_ref[...]
     for j in range(pairs):
@@ -526,7 +570,7 @@
         send_ref[...] = summed.astype(send_ref.dtype)
 
 
-def back(which, dq, dk, dv, got, w, gain, dx_part, tables):
+def back(which, dq, dk, dv, got, w, gain, dx_part, tables, after=()):
     rows, half = dq.shape
     width = w.shape[0]
     step = rows // 4
@@ -539,7 +583,8 @@
             num_scalar_prefetch=1,
             grid=(4,),
             in_specs=[by_row(half)] + [by_row(LANES)] * (2 * pairs) + [by_row(2 * LANES)] * pairs
-            + [whole(w.shape), whole(gain.shape), by_row(width)] + [by_row(LANES)] * 3,
+            + [whole(w.shape), whole(gain.shape), by_row(width)] + [by_row(LANES)] * 3
+            + [anywhere] * len(after),
             out_specs=[by_row(3 * half), by_run, by_run],
         ),
         out_shape=[
@@ -548,17 +593,15 @@
             jax.ShapeDtypeStruct((rows // 2, width), F32),
         ],
         compiler_params=params(),
-        cost_estimate=pl.CostEstimate(
-            flops=6 * rows * width * half, bytes_accessed=12 * rows * width, transcendentals=0
-        ),
+        cost_estimate=brief,
         name="back",
-    )(which, dq, *dk, *dv, *got, w, gain, dx_part, *tables)
+    )(which, dq, *dk, *dv, *got, w, gain, dx_part, *tables, *after)
 
 
 def weight_kernel(
-    which, x_ref, dy_ref, dproj_ref, o_ref, w_ref, gain_col, shift_col,
-    gqkv_ref, gdense_ref, vec_ref, gb_ref, acc, dense_acc, sum_acc,
+    which, x_ref, dy_ref, dproj_ref, o_ref, w_ref, gain_col, shift_col, *refs
 ):
+    gqkv_ref, gdense_ref, vec_ref, gb_ref, acc, dense_acc, sum_acc = refs[-7:]
     step = pl.program_id(0)
 
     @pl.when(step == 0)
@@ -585,7 +628,7 @@
         vec_ref[...] = jnp.where(lane == 1, gain_grad, jnp.where(lane == 2, shift_grad, 0.0))
 
 
-def weight_grads(which, x, dy, dproj, o, w, gain_col, shift_col):
+def weight_grads(which, x, dy, dproj, o, w, gain_col, shift_col, after=()):
     _, rows, width = x.shape
     half = o.shape[1]
     step = min(512, rows)
@@ -597,7 +640,7 @@
             num_scalar_prefetch=1,
             grid=(rows // step,),
             in_specs=[chosen, chosen, by_row(3 * half), by_row(half), whole(w.shape),
-                      whole(gain_col.shape), whole(shift_col.shape)],
+                      whole(gain_col.shape), whole(shift_col.shape)] + [anywhere] * len(after),
             out_specs=[whole((width, 3 * half)), whole((width, half)), whole((width, LANES)), whole((1, 3 * half))],
             scratch_shapes=[pltpu.VMEM((width, 3 * half), F32), pltpu.VMEM((width, half), F32),
                             pltpu.VMEM((1, 3 * half), F32)],
@@ -609,14 +652,13 @@
             jax.ShapeDtypeStruct((1, 3 * half), F32),
         ],
         compiler_params=params(),
-        cost_estimate=pl.CostEstimate(
-            flops=8 * rows * width * half, bytes_accessed=12 * rows * width, transcendentals=0
-        ),
+        cost_estimate=long,
         name="weight_grads",
-    )(which, x, dy, dproj, o, w, gain_col, shift_col)
-
-
-def norm_back_kernel(which, x_ref, dy_ref, kept_ref, got_ref, out_ref):
+    )(which, x, dy, dproj, o, w, gain_col, shift_col, *after)
+
+
+def norm_back_kernel(which, x_ref, dy_ref, kept_ref, got_ref, *refs):
+    out_ref = refs[-1]
     xhat, scale = normalise(x_ref[0].astype(F32))
     grad = kept_ref[...].astype(F32) + got_ref[...].astype(F32)
     centre = jnp.mean(grad, axis=-1, keepdims=True)
@@ -624,7 +666,7 @@
     out_ref[...] = (dy_ref[0].astype(F32) + scale * (grad - centre - xhat * along)).astype(out_ref.dtype)
 
 
-def norm_back(which, x, dy, kept, got, run):
+def norm_back(which, x, dy, kept, got, run, after=()):
     rows, width = got.shape
     step = min(256, rows)
     blocks = rows // step
@@ -638,48 +680,97 @@
             grid=(blocks,),
             in_specs=[chosen, chosen,
                       pl.BlockSpec((step, width), lambda i, *_: (run * blocks + i, 0)),
-                      pl.BlockSpec((step, width), lambda i, *_: (i, 0))],
+                      pl.BlockSpec((step, width), lambda i, *_: (i, 0))] + [anywhere] * len(after),
             out_specs=pl.BlockSpec((step, width), lambda i, *_: (i, 0)),
         ),
         out_shape=jax.ShapeDtypeStruct((rows, width), BF16),
         compiler_params=params(),
-        cost_estimate=pl.CostEstimate(
-            flops=20 * rows * width, bytes_accessed=10 * rows * width, transcendentals=0
-        ),
+        cost_estimate=longest,
         name="norm_back",
-    )(which, x, dy, kept, got)
-
-
-def lay_kernel(index, *refs):
-    pieces, out, sems = refs[:-2], refs[-2], refs[-1]
-    half = pieces[0].shape[0]
-    copies = []
-    for j, piece in enumerate(pieces):
-        run, back = j // 4, j % 4
-        slot = lax.rem(index[0] + (4 - back), 4)
-        start = pl.multiple_of(lax.rem(slot, 2) * half, half) + run * 2 * half
-        there = out.at[slot // 2, pl.ds(pl.multiple_of(start, half), half), :]
-        copies.append(pltpu.make_async_copy(piece, there, sems.at[j]))
-        copies[-1].start()
-    for copy in copies:
-        copy.wait()
-
-
-def lay(index, early, late):
-    half, width = early[0].shape
-    anywhere = pl.BlockSpec(memory_space=pl.ANY)
-    return pl.pallas_call(
-        lay_kernel,
+    )(which, x, dy, kept, got, *after)
+
+
+def finish_kernel(which, x_ref, kept_ref, got_ref, one_ref, two_ref, *refs):
+    summed = kept_ref[...] + got_ref[...].astype(F32) + x_ref[0].astype(F32) + one_ref[...] + two_ref[...]
+    refs[-1][...] = summed.astype(BF16)
+
+
+def finish(which, x, kept, got, one, two, run, after=()):
+    rows, width = got.shape
+    step = min(256, rows)
+    blocks = rows // step
+    by_row = pl.BlockSpec((step, width), lambda i, *_: (i, 0))
+    return pl.pallas_call(
+        finish_kernel,
         grid_spec=pltpu.PrefetchScalarGridSpec(
             num_scalar_prefetch=1,
-            grid=(),
-            in_specs=[anywhere] * 8,
-            out_specs=anywhere,
-            scratch_shapes=[pltpu.SemaphoreType.DMA((8,))],
+            grid=(blocks,),
+            in_specs=[
+                pl.BlockSpec((1, step, width), lambda i, which: (which[0], (2 * run + which[1]) * blocks + i, 0)),
+                by_row, by_row, whole(one.shape), whole(two.shape),
+            ] + [anywhere] * len(after),
+            out_specs=by_row,
+        ),
+        out_shape=jax.ShapeDtypeStruct((rows, width), BF16),
+        compiler_params=params(),
+        cost_estimate=brief,
+        name="finish",
+    )(which, x, kept, got, one, two, *after)
+
+
+def lay_kernel(early_ref, late_ref, *refs):
+    out = refs[-1]
+    run = pl.program_id(0) % 2
+
+    @pl.when(run == 0)
+    def _():
+        out[0] = early_ref[...]
+
+    @pl.when(run == 1)
+    def _():
+        out[0] = late_ref[...]
+
+
+def lay_gathered(early, late, after=()):
+    rows, width = early.shape[0] // 2, early.shape[1]
+    half = pl.BlockSpec((rows, width), lambda i: (i // 2, 0))
+    return pl.pallas_call(
+        lay_kernel,
+        grid=(4,),
+        in_specs=[half, half] + [anywhere] * len(after),
+        out_specs=pl.BlockSpec((1, rows, width), lambda i: (i // 2, i % 2, 0)),
+        out_shape=jax.ShapeDtypeStruct((2, 2 * rows, width), BF16),
+        compiler_params=params(),
+        cost_estimate=brief,
+        name="lay_gathered",
+    )(early, late, *after)
+
+
+def lay_round_kernel(index, *refs):
+    out = refs[-1]
+    run, slot = pl.program_id(0) // 4, pl.program_id(0) % 4
+    back = (index[0] + 4 - slot) % 4
+    for j in range(8):
+
+        @pl.when((run == j // 4) & (back == j % 4))
+        def _(j=j):
+            out[0] = refs[j][...]
+
+
+def lay_round(index, early, late):
+    half, width = early[0].shape
+    return pl.pallas_call(
+        lay_round_kernel,
+        grid_spec=pltpu.PrefetchScalarGridSpec(
+            num_scalar_prefetch=1,
+            grid=(8,),
+            in_specs=[whole((half, width))] * 8,
+            out_specs=pl.BlockSpec((1, half, width), lambda i, *_: ((i % 4) // 2, 2 * (i // 4) + i % 2, 0)),
         ),
         out_shape=jax.ShapeDtypeStruct((2, 4 * half, width), BF16),
-        cost_estimate=pl.CostEstimate(flops=0, bytes_accessed=32 * half * width, transcendentals=0),
-        name="lay",
+        compiler_params=params(),
+        cost_estimate=brief,
+        name="lay_round",
     )(index[None], *early, *late)
 
 
@@ -753,12 +844,8 @@
     if owners == 8 and seq_size == 2:
         one, two = gather_half(one, True), gather_half(two, False)
         qkv_w, dense_w, small = place(place_first_kernel, where, one, two, first_widths, (BF16, BF16, F32))
-        three = jnp.concatenate([three, four], axis=1)
-        other = swap(three, "mh")
-        three = jnp.concatenate([jnp.where(side == 0, three, other), jnp.where(side == 0, other, three)], axis=1)
-        three = lax.all_gather(three, ("dp", "seq"), axis=0, tiled=True)
-        up_w = jnp.concatenate([three[:, :units], three[:, 2 * units : 3 * units]], axis=1)
-        down_w = jnp.concatenate([three[:, units : 2 * units], three[:, 3 * units :]], axis=1)
+        pack = lax.all_gather(jnp.concatenate([three, four], axis=1), ("dp", "seq", "mh"), axis=0, tiled=True)
+        up_w, down_w = place_second(pack.reshape(owners, 2, share, 2 * units))
     else:
 
         def gather(values):
@@ -798,59 +885,60 @@
     else:
         kv_parts = (lax.all_gather(kv, "seq", axis=0, tiled=True),)
 
-    mlp_part, mlp_dx, grad_up, grad_down, mlp_vectors, grad_up_b = feed(
-        which, tokens, out_grad, up_w, up_b, down_w, row_of(4), row_of(5), column_of(4), column_of(5)
-    )
+    mlp_part, mlp_dx, act, mlp_grad = feed(which, tokens, out_grad, up_w, up_b, down_w, row_of(4), row_of(5))
     info = jnp.concatenate([runs, which[1:]])
     quarter = rows // 4
 
-    def finish(run, kept, got):
-        mine = lax.dynamic_slice(tokens, (side, run * run_rows + part * quarter, 0), (1, quarter, width))[0]
-        return (kept + got.astype(F32) + mine.astype(F32) + row_of(0) + row_of(1)).astype(BF16)
-
     o_early, stat_early, send, keep_early = attend(info, slots, q, grad_o, kv_parts, dense_w, mlp_part, 0)
     got_early = swap(send, "ml")
-    q_late, send = lax.optimization_barrier((q, send))
-    o_late, stat_late, send, keep_late = attend(info, slots, q_late, grad_o, kv_parts, dense_w, mlp_part, 1)
+    o_late, stat_late, send, keep_late = attend(
+        info, slots, q, grad_o, kv_parts, dense_w, mlp_part, 1, (o_early,)
+    )
     got_late = swap(send, "ml")
-    mixed_early = finish(0, keep_early, got_early)
-    stats, mixed_early = lax.optimization_barrier((jnp.concatenate([stat_early, stat_late], axis=1), mixed_early))
-    mixed_early = round_mp(mixed_early)
+    stats = jnp.concatenate([stat_early, stat_late], axis=1)
+    mixed_early = finish(which, tokens, keep_early, got_early, row_of(0), row_of(1), 0, (o_late,))
+    after = (mixed_early,)
+    mixed_early = lax.all_gather(mixed_early, ("mh", "ml"), axis=0, tiled=True)
 
     home = rows if seq_size == 2 else 0
     dq, dk, dv, got = [], [], [], []
-    q_next = q
     for pair in range(q.shape[1] // LANES):
-        outs = attend_back(info, slots, q_next, grad_o, stats, kv_parts, pair, home)
+        outs = attend_back(info, slots, q, grad_o, stats, kv_parts, pair, home, after)
+        after = (outs[0],)
         dq.append(outs[0])
         if home:
             dk.append(outs[1])
             dv.append(outs[2])
             got.append(swap(outs[3], "seq"))
-            tied = outs[3]
         else:
             both = jnp.concatenate([outs[1], outs[2]], axis=1).astype(BF16)
             got.append(lax.psum_scatter(both, "seq", scatter_dimension=0, tiled=True))
             dk.append(jnp.zeros((rows, LANES), F32))
             dv.append(jnp.zeros((rows, LANES), F32))
-            tied = outs[0]
         if pair == 0:
-            mixed_late = finish(1, keep_late, got_late)
-            q_next, _, mixed_late = lax.optimization_barrier((q, tied, mixed_late))
-            mixed_late = round_mp(mixed_late)
-        else:
-            q_next, _ = lax.optimization_barrier((q, tied))
-    mixed = lay(index, mixed_early, mixed_late)
+            mixed_late = finish(which, tokens, keep_late, got_late, row_of(0), row_of(1), 1, after)
+            after = (outs[0], mixed_late)
+            mixed_late = lax.all_gather(mixed_late, ("mh", "ml"), axis=0, tiled=True)
+        elif pair > 0:
+            after = (outs[0], got[pair - 1])
+    feed_weights, mlp_vectors, grad_up_b = feed_grads(
+        which, tokens, out_grad, act, mlp_grad, up_w, column_of(4), column_of(5), after + (mixed_early,)
+    )
     dq = jnp.concatenate(dq, axis=1)
-    dproj, send, keep = back(which, dq, dk, dv, got, qkv_w, row_of(2), mlp_dx, tables)
+    dproj, send, keep = back(
+        which, dq, dk, dv, got, qkv_w, row_of(2), mlp_dx, tables, (grad_up_b,)
+    )
+    mixed = lay_gathered(mixed_early, mixed_late, (dproj,))
     got = [swap(send[run * quarter : (run + 1) * quarter], "ml") for run in range(2)]
-    input_grad = [round_mp(norm_back(which, tokens, out_grad, keep, got[run], run)) for run in range(2)]
-    input_grad = lay(index, *input_grad)
-
     attended = jnp.concatenate([o_early, o_late], axis=0)
     grad_qkv, grad_dense, qkv_vectors, grad_qkv_b = weight_grads(
-        which, tokens, out_grad, dproj, attended, qkv_w, column_of(2), column_of(3)
-    )
+        which, tokens, out_grad, dproj, attended, qkv_w, column_of(2), column_of(3), (mixed_late,)
+    )
+    ties = ((grad_qkv_b,), ())
+    input_grad = [
+        round_mp(norm_back(which, tokens, out_grad, keep, got[run], run, ties[run])) for run in range(2)
+    ]
+    input_grad = lay_round(index, *input_grad)
 
     def scatter(grads):
         return lax.psum_scatter(grads, ("dp", "seq"), scatter_dimension=0, tiled=True)
@@ -861,8 +949,6 @@
         other = lax.dynamic_index_in_dim(sums, 1 - side, 1, keepdims=False)
         return mine + swap(other.astype(BF16), "mh").astype(F32)
 
-    owned_up = settle(scatter(grad_up).reshape(share, 2, units))
-    owned_down = settle(scatter(grad_down).reshape(share, 2, units))
     vector_grads = (mlp_vectors + qkv_vectors)[:, None, :5]
     vector_grads = jnp.broadcast_to(vector_grads, (width, 2, 5))
     bias_qkv = grad_qkv_b.reshape(3, 2, heads, owners, piece).transpose(3, 0, 2, 4, 1)
@@ -871,11 +957,14 @@
     bias_up = grad_up_b.reshape(2, up_rows, owners, up_cols).transpose(2, 1, 3, 0).reshape(width, 2, 1)
     tail = jnp.concatenate([vector_grads, bias_qkv, bias_up], axis=2)
     tail = jnp.pad(tail, ((0, 0), (0, 0), (0, LANES // 2 - 7))).astype(BF16).reshape(width, LANES)
-    first = scatter(jnp.concatenate([grad_qkv, grad_dense, tail], axis=1))
+    packed = scatter(jnp.concatenate([grad_qkv, grad_dense, tail, feed_weights], axis=1))
+    first, owned_feed = packed[:, : 8 * cols + LANES], packed[:, 8 * cols + LANES :]
+    owned_feed = owned_feed.reshape(share, 2, 2, units).transpose(0, 2, 1, 3).reshape(share, 2, 2 * units)
     owned_qkv = first[:, : 6 * cols].reshape(share, 3, 2, cols).transpose(0, 2, 1, 3).reshape(share, 2, 3 * cols)
     owned_dense = first[:, 6 * cols : 8 * cols].reshape(share, 2, cols)
     owned_tail = first[:, 8 * cols :].reshape(share, 2, LANES // 2)
-    owned = settle(jnp.concatenate([owned_qkv, owned_dense, owned_tail], axis=2))
+    owned = settle(jnp.concatenate([owned_feed, owned_qkv, owned_dense, owned_tail], axis=2))
+    owned_feed, owned = owned[:, : 2 * units], owned[:, 2 * units :]
     vectors = owned[:, 4 * cols :]
     norms = vectors[:, :5]
     norms = norms + swap(norms, "ml")
@@ -887,9 +976,9 @@
         vectors[: 3 * heads * piece, 5].reshape(b_qkv.shape),
         owned[:, 3 * cols : 4 * cols].T,
         bias_grad,
-        owned_up,
+        owned_feed[:, :units],
         vectors[:, 6].reshape(b_up.shape),
-        owned_down.T,
+        owned_feed[:, units:].T,
         bias_grad,
         norms[:, 1],
         norms[:, 2],

time: 1100 us -> 648 us (0.59)
  Pallas kernels: 653 us -> 306 us
  waiting for transfers between devices: 269 us -> 210 us
  starting transfers between devices: 92.7 us -> 37.2 us
  local copies, waits for them, and re-layouts: 38.3 us -> 49.8 us
    pallas_call x2 -> x6, Pallas kernels: 384 us -> 49.4 us  [the longest x1 21.8 us: feed_grads(): pl.pallas_call(feed_grads_kernel, grid_spec=pltpu.PrefetchScalarGridSpec(...]
    ppermute x12 -> x6, starting transfers between devices: 50.1 us -> 7.63 us  [round_mp(): lax.ppermute(mine, axes, [(i, (i + k) % 4) for i in range(4)])]
    ppermute x18 -> x15, waiting for transfers between devices: 204 us -> 165 us  [swap(): return lax.ppermute(values, axis, [(0, 1), (1, 0)])]
    ppermute x12 -> x6, waiting for transfers between devices: 55.8 us -> 40.6 us  [round_mp(): lax.ppermute(mine, axes, [(i, (i + k) % 4) for i in range(4)])]
    pallas_call x1, Pallas kernels: 42.3 us -> 28.9 us  [feed(): pl.pallas_call(feed_kernel, grid_spec=pltpu.PrefetchScalarGridSpec(num_sc...]
    ppermute x18 -> x15, starting transfers between devices: 39.2 us -> 25.9 us  [swap(): return lax.ppermute(values, axis, [(0, 1), (1, 0)])]
    unnamed x88 -> x74, local copies, waits for them, and re-layouts: 8.16 us -> 20 us
  transfers between devices with their start and end apart: 38 -> 29, of which waited for: 18 -> 15; matrix products, arithmetic and copies ran while one was open for 5% -> 7% of each run, Pallas kernels for 58% -> 40%
where the time goes in v4:
time: 648 us; the launch traced here: 639 us
  Pallas kernels  306 us (47%)
  waiting for transfers between devices  210 us (32%)
  local copies, waits for them, and re-layouts  49.8 us (8%)
  starting transfers between devices  37.2 us (6%)
  other arithmetic  20.4 us (3%)
  between operations  15 us (2%)
    ppermute x15, waiting for transfers between devices, swap(): return lax.ppermute(values, axis, [(0, 1), (1, 0)])  165 us
    pallas_call x3, Pallas kernels, attend_back(): pl.pallas_call(kernel, grid_spec=pltpu.PrefetchScalarGridSpec(num_scalar_...  101 us
    pallas_call x2, Pallas kernels, attend(): pl.pallas_call(kernel, grid_spec=pltpu.PrefetchScalarGridSpec(num_scalar_...  69.2 us
    ppermute x6, waiting for transfers between devices, round_mp(): lax.ppermute(mine, axes, [(i, (i + k) % 4) for i in range(4)])  40.6 us
    pallas_call x1, Pallas kernels, feed(): pl.pallas_call(feed_kernel, grid_spec=pltpu.PrefetchScalarGridSpec(num_sc...  28.9 us
    ppermute x15, starting transfers between devices, swap(): return lax.ppermute(values, axis, [(0, 1), (1, 0)])  25.9 us
    pallas_call x1, Pallas kernels, feed_grads(): pl.pallas_call(feed_grads_kernel, grid_spec=pltpu.PrefetchScalarGridSpec(...  21.8 us
    unnamed x74, local copies, waits for them, and re-layouts  20 us
  transfers between devices with their start and end apart: 29, of which 15 were waited for; matrix products, arithmetic and copies ran while one was open for 7% of the time, Pallas kernels for 40%

profile of v4, /device:TPU:0, one launch (start us, length us, event | category | flops | bytes accessed | tf_op | source)
XLA Modules:
  0.0 638.9 jit_solution(2529398289692383653)
XLA Ops:
  20.7 8.3 %collective-permute-done.1 = bf16[96,384]{1,0:T(8,128)(2,1)S(1)} collective-permute-done((bf16[96,384]{1,0:T(8,128)(2,1)S(1)}, bf16[96,384]{1,0:T(8,128)(2,1)S(1)}, u32[]{:S(2)}, u32[]{:S(2)}) %collective-permute-start.1) | collective-permute-done | bytes 73760 | tf_op jit(solution)/shard_map/ppermute | solution.py:778
  51.0 7.2 %place.1 = (bf16[768,1152]{1,0:T(8,128)(2,1)}, bf16[768,384]{1,0:T(8,128)(2,1)}, f32[768,256]{1,0:T(8,128)}) custom-call(s32[2]{0:T(128)} %pad_add_fusion.4.where, bf16[8,2,96,384]{3,2,1,0:T(8,128)(2,1)} %bitcast.105, bf16[8,2,96,512]{3,2,1,0:T(8,128)(2,1)} %bitcast.98), custom_call_target="tpu_custom_call" | custom-call | flops 1 | bytes 1 | tf_op jit(solution)/shard_map/place/pallas_call | solution.py:109
  62.4 12.2 %front.1 = (bf16[2048,384]{1,0:T(8,128)(2,1)}, bf16[2048,768]{1,0:T(8,128)(2,1)}, bf16[2048,384]{1,0:T(8,128)(2,1)}) custom-call(s32[2]{0:T(128)} %pad_add_fusion.which, bf16[2,2048,768]{2,1,0:T(8,128)(2,1)} %x_ref.15, bf16[2,2048,768]{2,1,0:T(8,128)(2,1)} %dy_ref.11, bf16[768,1152]{1,0:T(8,128)(2,1)} %get-tuple-element.58.w_ref.refs_9_, ...), custom_call_target="tpu_custom_call" | custom-call | flops 1 | bytes 1 | tf_op jit(solution)/shard_map/front/pallas_call | solution.py:149
  79.3 65.9 %collective-permute-done = s32[2]{0:T(128)S(1)} collective-permute-done((s32[2]{0:T(128)S(1)}, s32[2]{0:T(128)S(1)}, u32[]{:S(2)}, u32[]{:S(2)}) %collective-permute-start) | collective-permute-done | bytes 40 | tf_op jit(solution)/shard_map/ppermute | solution.py:778
  150.9 6.9 %place_second.1 = (bf16[768,1536]{1,0:T(8,128)(2,1)}, bf16[768,1536]{1,0:T(8,128)(2,1)}) custom-call(bf16[8,2,96,1536]{3,2,1,0:T(8,128)(2,1)} %bitcast.93), custom_call_target="tpu_custom_call" | custom-call | flops 1 | bytes 1 | tf_op jit(solution)/shard_map/place_second/pallas_call | solution.py:85
  157.8 28.9 %feed.1 = (bf16[2048,768]{1,0:T(8,128)(2,1)}, bf16[2048,768]{1,0:T(8,128)(2,1)}, bf16[2048,1536]{1,0:T(8,128)(2,1)}, bf16[2048,1536]{1,0:T(8,128)(2,1)}) custom-call(s32[2]{0:T(128)} %pad_add_fusion.which, bf16[2,2048,768]{2,1,0:T(8,128)(2,1)} %x_ref.15, bf16[2,2048,768]{2,1,0:T(8,128)(2,1)} %dy_ref.11, bf16[768,1536]{1,0:T(8,128)(2,1)} %get-tuple-element.65.up_ref, ...), custom_call_target="tpu_custom_call" | custom-call | flops 1 | bytes 1 | tf_op jit(solution)/shard_map/feed/pallas_call | solution.py:191
  188.3 29.3 %attend.2 = (bf16[1024,384]{1,0:T(8,128)(2,1)}, f32[24,1024]{1,0:T(8,128)}, bf16[512,768]{1,0:T(8,128)(2,1)}, f32[512,768]{1,0:T(8,128)}) custom-call(s32[3]{0:T(128)} %pad_add_fusion.2.info, s32[4]{0:T(128)} %select_reduce_fusion.slots, bf16[2048,384]{1,0:T(8,128)(2,1)} %get-tuple-element.63.q_ref, bf16[2048,384]{1,0:T(8,128)(2,1)} %get-tuple-element.64.g_ref, ...), custom_call_target="tpu_custom_call" | custom-call | flops 1 | bytes 1 | tf_op jit(solution)/shard_map/attend/pallas_call | solution.py:389
  217.6 5.5 collective-permute-start.10
  223.1 40.0 %attend.3 = (bf16[1024,384]{1,0:T(8,128)(2,1)}, f32[24,1024]{1,0:T(8,128)}, bf16[512,768]{1,0:T(8,128)(2,1)}, f32[512,768]{1,0:T(8,128)}) custom-call(s32[3]{0:T(128)} %pad_add_fusion.2.info, s32[4]{0:T(128)} %select_reduce_fusion.slots, bf16[2048,384]{1,0:T(8,128)(2,1)} %get-tuple-element.63.q_ref, bf16[2048,384]{1,0:T(8,128)(2,1)} %get-tuple-element.64.g_ref, ...), custom_call_target="tpu_custom_call" | custom-call | flops 1 | bytes 1 | tf_op jit(solution)/shard_map/attend/pallas_call | solution.py:389
  268.5 33.5 %attend_back.3 = (bf16[2048,128]{1,0:T(8,128)(2,1)}, f32[2048,128]{1,0:T(8,128)}, f32[2048,128]{1,0:T(8,128)}, bf16[2048,256]{1,0:T(8,128)(2,1)}) custom-call(s32[3]{0:T(128)} %pad_add_fusion.2.info, s32[4]{0:T(128)} %select_reduce_fusion.slots, bf16[2048,384]{1,0:T(8,128)(2,1)} %get-tuple-element.63.q_ref, bf16[2048,384]{1,0:T(8,128)(2,1)} %get-tuple-element.64.g_ref, ...), custom_call_target="tpu_custom_call" | custom-call | flops 8589934592 | bytes 16777216 | tf_op jit(solution)/shard_map/attend_back/pallas_call | solution.py:522
  302.1 15.9 %collective-permute-done.11.got_ref = bf16[512,768]{1,0:T(8,128)(2,1)S(1)} collective-permute-done((bf16[512,768]{1,0:T(8,128)(2,1)S(1)}, bf16[512,768]{1,0:T(8,128)(2,1)S(1)}, u32[]{:S(2)}, u32[]{:S(2)}) %collective-permute-start.11) | collective-permute-done | bytes 786464 | tf_op jit(solution)/shard_map/ppermute | solution.py:778
  326.4 33.8 %attend_back.4 = (bf16[2048,128]{1,0:T(8,128)(2,1)}, f32[2048,128]{1,0:T(8,128)}, f32[2048,128]{1,0:T(8,128)}, bf16[2048,256]{1,0:T(8,128)(2,1)}) custom-call(s32[3]{0:T(128)} %pad_add_fusion.2.info, s32[4]{0:T(128)} %select_reduce_fusion.slots, bf16[2048,384]{1,0:T(8,128)(2,1)} %get-tuple-element.63.q_ref, bf16[2048,384]{1,0:T(8,128)(2,1)} %get-tuple-element.64.g_ref, ...), custom_call_target="tpu_custom_call" | custom-call | flops 8589934592 | bytes 16777216 | tf_op jit(solution)/shard_map/attend_back/pallas_call | solution.py:522
  363.1 33.8 %attend_back.5 = (bf16[2048,128]{1,0:T(8,128)(2,1)}, f32[2048,128]{1,0:T(8,128)}, f32[2048,128]{1,0:T(8,128)}, bf16[2048,256]{1,0:T(8,128)(2,1)}) custom-call(s32[3]{0:T(128)} %pad_add_fusion.2.info, s32[4]{0:T(128)} %select_reduce_fusion.slots, bf16[2048,384]{1,0:T(8,128)(2,1)} %get-tuple-element.63.q_ref, bf16[2048,384]{1,0:T(8,128)(2,1)} %get-tuple-element.64.g_ref, ...), custom_call_target="tpu_custom_call" | custom-call | flops 8589934592 | bytes 16777216 | tf_op jit(solution)/shard_map/attend_back/pallas_call | solution.py:522
  400.7 21.8 %feed_grads.1 = (bf16[768,3072]{1,0:T(8,128)(2,1)}, f32[768,128]{1,0:T(8,128)}, f32[1,1536]{1,0:T(1,128)}) custom-call(s32[2]{0:T(128)} %pad_add_fusion.which, bf16[2,2048,768]{2,1,0:T(8,128)(2,1)} %x_ref.15, bf16[2,2048,768]{2,1,0:T(8,128)(2,1)} %dy_ref.11, bf16[2048,1536]{1,0:T(8,128)(2,1)} %get-tuple-element.90.act_ref, ...), custom_call_target="tpu_custom_call" | custom-call | flops 8589934592 | bytes 16777216 | tf_op jit(solution)/shard_map/feed_grads/pallas_call | solution.py:256
  423.5 14.6 %back.1 = (bf16[2048,1152]{1,0:T(8,128)(2,1)}, bf16[1024,768]{1,0:T(8,128)(2,1)}, f32[1024,768]{1,0:T(8,128)}) custom-call(s32[2]{0:T(128)} %pad_add_fusion.which, bf16[2048,384]{1,0:T(8,128)(2,1)} %pad_maximum_fusion.1.dq_ref, f32[2048,128]{1,0:T(8,128)} %get-tuple-element.81.refs_0_, f32[2048,128]{1,0:T(8,128)} %get-tuple-element.82.refs_1_, ...), custom_call_target="tpu_custom_call" | custom-call | flops 1 | bytes 1 | tf_op jit(solution)/shard_map/back/pallas_call | solution.py:580
  438.2 15.4 %weight_grads.1 = (bf16[768,1152]{1,0:T(8,128)(2,1)}, bf16[768,384]{1,0:T(8,128)(2,1)}, f32[768,128]{1,0:T(8,128)}, f32[1,1152]{1,0:T(1,128)}) custom-call(s32[2]{0:T(128)} %pad_add_fusion.which, bf16[2,2048,768]{2,1,0:T(8,128)(2,1)} %x_ref.15, bf16[2,2048,768]{2,1,0:T(8,128)(2,1)} %dy_ref.11, bf16[2048,1152]{1,0:T(8,128)(2,1)} %get-tuple-element.93.refs_0_.dproj_ref, ...), custom_call_target="tpu_custom_call" | custom-call | flops 8589934592 | bytes 16777216 | tf_op jit(solution)/shard_map/weight_grads/pallas_call | solution.py:637
  458.1 5.8 pad_maximum_fusion
  466.5 28.7 %collective-permute-done.19.got_ref = bf16[512,768]{1,0:T(8,128)(2,1)S(1)} collective-permute-done((bf16[512,768]{1,0:T(8,128)(2,1)}, bf16[512,768]{1,0:T(8,128)(2,1)S(1)}, u32[]{:S(2)}, u32[]{:S(2)}) %collective-permute-start.19) | collective-permute-done | bytes 786464 | tf_op jit(solution)/shard_map/ppermute | solution.py:778
  504.2 33.1 %collective-permute-done.15.got_ref = bf16[512,768]{1,0:T(8,128)(2,1)S(1)} collective-permute-done((bf16[512,768]{1,0:T(8,128)(2,1)S(1)}, bf16[512,768]{1,0:T(8,128)(2,1)S(1)}, u32[]{:S(2)}, u32[]{:S(2)}) %collective-permute-start.15) | collective-permute-done | bytes 786464 | tf_op jit(solution)/shard_map/ppermute | solution.py:778
  560.8 6.8 %lay_gathered.1 = bf16[2,2048,768]{2,1,0:T(8,128)(2,1)} custom-call(bf16[2048,768]{1,0:T(8,128)(2,1)} %all-gather.6.cloned.1.call-done.refs_2_.early_ref, bf16[2048,768]{1,0:T(8,128)(2,1)} %all-gather.8.cloned.1.call-done.late_ref.refs_0_, bf16[2048,1152]{1,0:T(8,128)(2,1)} %get-tuple-element.93.refs_0_.dproj_ref), custom_call_target="tpu_custom_call" | custom-call | flops 1 | bytes 1 | tf_op jit(solution)/shard_map/lay_gathered/pallas_call | solution.py:737
  567.6 5.9 collective-permute-done.16.refs_1_
  573.5 29.8 %collective-permute-done.17.refs_2_ = bf16[512,768]{1,0:T(8,128)(2,1)} collective-permute-done((bf16[512,768]{1,0:T(8,128)(2,1)}, bf16[512,768]{1,0:T(8,128)(2,1)}, u32[]{:S(2)}, u32[]{:S(2)}) %collective-permute-start.17) | collective-permute-done | bytes 786464 | tf_op jit(solution)/shard_map/ppermute | solution.py:796
  603.3 6.9 %lay_round.1 = bf16[2,2048,768]{2,1,0:T(8,128)(2,1)} custom-call(s32[1]{0:T(128)} %bitcast.31.index, bf16[512,768]{1,0:T(8,128)(2,1)} %norm_back.2.refs_0_, bf16[512,768]{1,0:T(8,128)(2,1)} %collective-permute-done.16.refs_1_, bf16[512,768]{1,0:T(8,128)(2,1)} %collective-permute-done.17.refs_2_, bf16[512,768]{1,0:T(8,128)(2,1)} %collective-permute-done.18.refs_3_, ...), custom_call_target="tpu_custom_call" | custom-call | flops 1 | bytes 1 | tf_op jit(solution)/shard_map/lay_round/pallas_call | solution.py:762
  610.7 11.1 %collective-permute-done.23 = bf16[96,2368]{1,0:T(8,128)(2,1)} collective-permute-done((bf16[96,2368]{1,0:T(8,128)(2,1)}, bf16[96,2368]{1,0:T(8,128)(2,1)}, u32[]{:S(2)}, u32[]{:S(2)}) %collective-permute-start.23) | collective-permute-done | bytes 454688 | tf_op jit(solution)/shard_map/ppermute | solution.py:778
  (241 shorter events, 123.2 us)
Async XLA Ops:
  7.2 143.7 %all-gather.4.cloned.1.call-start = ((), (), s32[]{:S(2)}) async-start(), calls=%async_computation.1 | async-start | bytes 5013504 | tf_op jit(solution)/shard_map/all_gather | solution.py:847
  9.0 390.7 %all-gather.6.cloned.1.call-start = ((), (), s32[]{:S(2)}) async-start(), calls=%async_computation.2 | async-start | bytes 3932160 | tf_op jit(solution)/shard_map/all_gather | solution.py:901
  13.9 16.8 %collective-permute-start.5 = (bf16[96,512]{1,0:T(8,128)(2,1)S(1)}, bf16[96,512]{1,0:T(8,128)(2,1)S(1)}, u32[]{:S(2)}, u32[]{:S(2)}) collective-permute-start(bf16[96,512]{1,0:T(8,128)(2,1)S(1)} %get-tuple-element.173), channel_id=1, source_target_pairs={{0,2},{2,0},{1,3},{3,1},{4,6},{6,4},{5,7},{7,5},{8,10},{10,8},{9,1... | collective-permute-start | bytes 294920 | tf_op jit(solution)/shard_map/ppermute | solution.py:778
  19.0 9.9 %collective-permute-start.1 = (bf16[96,384]{1,0:T(8,128)(2,1)S(1)}, bf16[96,384]{1,0:T(8,128)(2,1)S(1)}, u32[]{:S(2)}, u32[]{:S(2)}) collective-permute-start(bf16[96,384]{1,0:T(8,128)(2,1)S(1)} %reshape.120), channel_id=1, source_target_pairs={{0,2},{2,0},{1,3},{3,1},{4,6},{6,4},{5,7},{7,5},{8,10},{10,8},{9,1... | collective-permute-start | bytes 221192 | tf_op jit(solution)/shard_map/ppermute | solution.py:778
  35.0 11.0 %collective-permute-start.3 = (bf16[4,96,384]{2,1,0:T(8,128)(2,1)}, bf16[4,96,384]{2,1,0:T(8,128)(2,1)S(1)}, u32[]{:S(2)}, u32[]{:S(2)}) collective-permute-start(bf16[4,96,384]{2,1,0:T(8,128)(2,1)} %pad_maximum_fusion.6), channel_id=1, source_target_pairs={{0,16},{8,24},{16,0},{24,8},{1,17},{9,25},{17,1},{25,9},{2,18},{10... | collective-permute-start | bytes 884744 | tf_op jit(solution)/shard_map/ppermute | solution.py:782
  38.8 8.6 %collective-permute-start.7 = (bf16[4,96,512]{2,1,0:T(8,128)(2,1)}, bf16[4,96,512]{2,1,0:T(8,128)(2,1)S(1)}, u32[]{:S(2)}, u32[]{:S(2)}) collective-permute-start(bf16[4,96,512]{2,1,0:T(8,128)(2,1)} %pad_maximum_fusion.5), channel_id=1, source_target_pairs={{0,4},{4,0},{1,5},{5,1},{2,6},{6,2},{3,7},{7,3},{8,12},{12,8},{9,1... | collective-permute-start | bytes 1179656 | tf_op jit(solution)/shard_map/ppermute | solution.py:778
  74.6 112.1 %collective-permute-start.9 = (bf16[2048,768]{1,0:T(8,128)(2,1)}, bf16[2048,768]{1,0:T(8,128)(2,1)S(1)}, u32[]{:S(2)}, u32[]{:S(2)}) collective-permute-start(bf16[2048,768]{1,0:T(8,128)(2,1)} %get-tuple-element.68.refs_0_.refs_2_), channel_id=1, source_target_pairs={{0,4},{4,0},{1,5},{5,1},{2,6},{6,2},{3,7},{7,3},{8,12},{12,8},{9,1... | collective-permute-start | bytes 9437192 | tf_op jit(solution)/shard_map/ppermute | solution.py:778
  78.2 67.0 %collective-permute-start = (s32[2]{0:T(128)S(1)}, s32[2]{0:T(128)S(1)}, u32[]{:S(2)}, u32[]{:S(2)}) collective-permute-start(s32[2]{0:T(128)S(1)} %and_select_fusion), channel_id=1, source_target_pairs={{0,4},{4,0},{1,5},{5,1},{2,6},{6,2},{3,7},{7,3},{8,12},{12,8},{9,1... | collective-permute-start | bytes 32 | tf_op jit(solution)/shard_map/ppermute | solution.py:778
  217.6 45.5 %collective-permute-start.10 = (bf16[512,768]{1,0:T(8,128)(2,1)}, bf16[512,768]{1,0:T(8,128)(2,1)S(1)}, u32[]{:S(2)}, u32[]{:S(2)}) collective-permute-start(bf16[512,768]{1,0:T(8,128)(2,1)} %get-tuple-element.70), channel_id=1, source_target_pairs={{0,1},{1,0},{2,3},{3,2},{4,5},{5,4},{6,7},{7,6},{8,9},{9,8},{10,11... | collective-permute-start | bytes 2359304 | tf_op jit(solution)/shard_map/ppermute | solution.py:778
  267.7 170.5 %all-gather.8.cloned.1.call-start = ((), (), s32[]{:S(2)}) async-start(), calls=%async_computation.3 | async-start | bytes 3932160 | tf_op jit(solution)/shard_map/all_gather | solution.py:921
  267.7 50.2 %collective-permute-start.11 = (bf16[512,768]{1,0:T(8,128)(2,1)S(1)}, bf16[512,768]{1,0:T(8,128)(2,1)S(1)}, u32[]{:S(2)}, u32[]{:S(2)}) collective-permute-start(bf16[512,768]{1,0:T(8,128)(2,1)S(1)} %copy-done.26), channel_id=1, source_target_pairs={{0,1},{1,0},{2,3},{3,2},{4,5},{5,4},{6,7},{7,6},{8,9},{9,8},{10,11... | collective-permute-start | bytes 2359304 | tf_op jit(solution)/shard_map/ppermute | solution.py:778
  322.3 223.7 %reduce-scatter.2.cloned.1.call-start = ((), (), s32[]{:S(2)}) async-start(), calls=%async_computation.4 | async-start | bytes 8183808 | tf_op jit(solution)/shard_map/reduce_scatter | solution.py:944
  325.0 37.1 %collective-permute-start.12 = (bf16[2048,256]{1,0:T(8,128)(2,1)}, bf16[2048,256]{1,0:T(8,128)(2,1)S(1)}, u32[]{:S(2)}, u32[]{:S(2)}) collective-permute-start(bf16[2048,256]{1,0:T(8,128)(2,1)} %get-tuple-element.79), channel_id=1, source_target_pairs={{0,4},{4,0},{1,5},{5,1},{2,6},{6,2},{3,7},{7,3},{8,12},{12,8},{9,1... | collective-permute-start | bytes 3145736 | tf_op jit(solution)/shard_map/ppermute | solution.py:778
  360.1 39.5 %collective-permute-start.13 = (bf16[2048,256]{1,0:T(8,128)(2,1)}, bf16[2048,256]{1,0:T(8,128)(2,1)S(1)}, u32[]{:S(2)}, u32[]{:S(2)}) collective-permute-start(bf16[2048,256]{1,0:T(8,128)(2,1)} %get-tuple-element.87), channel_id=1, source_target_pairs={{0,4},{4,0},{1,5},{5,1},{2,6},{6,2},{3,7},{7,3},{8,12},{12,8},{9,1... | collective-permute-start | bytes 3145736 | tf_op jit(solution)/shard_map/ppermute | solution.py:778
  397.0 25.5 %collective-permute-start.14 = (bf16[2048,256]{1,0:T(8,128)(2,1)}, bf16[2048,256]{1,0:T(8,128)(2,1)S(1)}, u32[]{:S(2)}, u32[]{:S(2)}) collective-permute-start(bf16[2048,256]{1,0:T(8,128)(2,1)} %get-tuple-element.88), channel_id=1, source_target_pairs={{0,4},{4,0},{1,5},{5,1},{2,6},{6,2},{3,7},{7,3},{8,12},{12,8},{9,1... | collective-permute-start | bytes 3145736 | tf_op jit(solution)/shard_map/ppermute | solution.py:778
  457.3 37.9 %collective-permute-start.19 = (bf16[512,768]{1,0:T(8,128)(2,1)}, bf16[512,768]{1,0:T(8,128)(2,1)S(1)}, u32[]{:S(2)}, u32[]{:S(2)}) collective-permute-start(bf16[512,768]{1,0:T(8,128)(2,1)} %get-tuple-element.174), channel_id=1, source_target_pairs={{0,1},{1,0},{2,3},{3,2},{4,5},{5,4},{6,7},{7,6},{8,9},{9,8},{10,11... | collective-permute-start | bytes 2359304 | tf_op jit(solution)/shard_map/ppermute | solution.py:778
  465.0 72.3 %collective-permute-start.15 = (bf16[512,768]{1,0:T(8,128)(2,1)S(1)}, bf16[512,768]{1,0:T(8,128)(2,1)S(1)}, u32[]{:S(2)}, u32[]{:S(2)}) collective-permute-start(bf16[512,768]{1,0:T(8,128)(2,1)S(1)} %copy-done.16), channel_id=1, source_target_pairs={{0,1},{1,0},{2,3},{3,2},{4,5},{5,4},{6,7},{7,6},{8,9},{9,8},{10,11... | collective-permute-start | bytes 2359304 | tf_op jit(solution)/shard_map/ppermute | solution.py:778
  500.4 41.8 %collective-permute-start.20 = (bf16[512,768]{1,0:T(8,128)(2,1)}, bf16[512,768]{1,0:T(8,128)(2,1)}, u32[]{:S(2)}, u32[]{:S(2)}) collective-permute-start(bf16[512,768]{1,0:T(8,128)(2,1)} %norm_back.3.refs_4_), channel_id=1, source_target_pairs={{0,1},{1,2},{2,3},{3,0},{4,5},{5,6},{6,7},{7,4},{8,9},{9,10},{10,1... | collective-permute-start | bytes 2359304 | tf_op jit(solution)/shard_map/ppermute | solution.py:796
  500.4 55.4 %collective-permute-start.21 = (bf16[512,768]{1,0:T(8,128)(2,1)}, bf16[512,768]{1,0:T(8,128)(2,1)}, u32[]{:S(2)}, u32[]{:S(2)}) collective-permute-start(bf16[512,768]{1,0:T(8,128)(2,1)} %norm_back.3.refs_4_), channel_id=1, source_target_pairs={{0,2},{1,3},{2,0},{3,1},{4,6},{5,7},{6,4},{7,5},{8,10},{9,11},{10,... | collective-permute-start | bytes 2359304 | tf_op jit(solution)/shard_map/ppermute | solution.py:796
  500.4 67.2 %collective-permute-start.22 = (bf16[512,768]{1,0:T(8,128)(2,1)}, bf16[512,768]{1,0:T(8,128)(2,1)}, u32[]{:S(2)}, u32[]{:S(2)}) collective-permute-start(bf16[512,768]{1,0:T(8,128)(2,1)} %norm_back.3.refs_4_), channel_id=1, source_target_pairs={{0,3},{1,0},{2,1},{3,2},{4,7},{5,4},{6,5},{7,6},{8,11},{9,8},{10,9... | collective-permute-start | bytes 2359304 | tf_op jit(solution)/shard_map/ppermute | solution.py:796
  542.2 31.3 %collective-permute-start.16 = (bf16[512,768]{1,0:T(8,128)(2,1)}, bf16[512,768]{1,0:T(8,128)(2,1)}, u32[]{:S(2)}, u32[]{:S(2)}) collective-permute-start(bf16[512,768]{1,0:T(8,128)(2,1)} %norm_back.2.refs_0_), channel_id=1, source_target_pairs={{0,1},{1,2},{2,3},{3,0},{4,5},{5,6},{6,7},{7,4},{8,9},{9,10},{10,1... | collective-permute-start | bytes 2359304 | tf_op jit(solution)/shard_map/ppermute | solution.py:796
  542.2 61.1 %collective-permute-start.17 = (bf16[512,768]{1,0:T(8,128)(2,1)}, bf16[512,768]{1,0:T(8,128)(2,1)}, u32[]{:S(2)}, u32[]{:S(2)}) collective-permute-start(bf16[512,768]{1,0:T(8,128)(2,1)} %norm_back.2.refs_0_), channel_id=1, source_target_pairs={{0,2},{1,3},{2,0},{3,1},{4,6},{5,7},{6,4},{7,5},{8,10},{9,11},{10,... | collective-permute-start | bytes 2359304 | tf_op jit(solution)/shard_map/ppermute | solution.py:796
  542.2 61.1 %collective-permute-start.18 = (bf16[512,768]{1,0:T(8,128)(2,1)}, bf16[512,768]{1,0:T(8,128)(2,1)}, u32[]{:S(2)}, u32[]{:S(2)}) collective-permute-start(bf16[512,768]{1,0:T(8,128)(2,1)} %norm_back.2.refs_0_), channel_id=1, source_target_pairs={{0,3},{1,0},{2,1},{3,2},{4,7},{5,4},{6,5},{7,6},{8,11},{9,8},{10,9... | collective-permute-start | bytes 2359304 | tf_op jit(solution)/shard_map/ppermute | solution.py:796
  555.8 65.9 %collective-permute-start.23 = (bf16[96,2368]{1,0:T(8,128)(2,1)}, bf16[96,2368]{1,0:T(8,128)(2,1)}, u32[]{:S(2)}, u32[]{:S(2)}) collective-permute-start(bf16[96,2368]{1,0:T(8,128)(2,1)} %fusion), channel_id=1, source_target_pairs={{0,2},{2,0},{1,3},{3,1},{4,6},{6,4},{5,7},{7,5},{8,10},{10,8},{9,1... | collective-permute-start | bytes 1363976 | tf_op jit(solution)/shard_map/ppermute | solution.py:778
  (38 other events, 176.6 us)
Sparse Core Ops, SparseCore 0:
  10.9 63.3 all-gather.3
  267.8 69.3 all-gather.5
  338.8 62.7 all-gather.7
  464.0 66.4 reduce-scatter.1

commit v5 on v4

--- a/solution.py
+++ b/solution.py
@@ -657,6 +657,31 @@
     )(which, x, dy, dproj, o, w, gain_col, shift_col, *after)
 
 
+def join_kernel(*refs):
+    out = refs[-1]
+    at = 0
+    for ref in refs[:-1]:
+        out[:, at : at + ref.shape[1]] = ref[...]
+        at += ref.shape[1]
+
+
+def join(arrays):
+    rows = arrays[0].shape[0]
+    step = rows // 4
+    widths = [array.shape[1] for array in arrays]
+    by_row = lambda cols: pl.BlockSpec((step, cols), lambda i: (i, 0))
+    return pl.pallas_call(
+        join_kernel,
+        grid=(4,),
+        in_specs=[by_row(width) for width in widths],
+        out_specs=by_row(sum(widths)),
+        out_shape=jax.ShapeDtypeStruct((rows, sum(widths)), BF16),
+        compiler_params=params(),
+        cost_estimate=brief,
+        name="join",
+    )(*arrays)
+
+
 def norm_back_kernel(which, x_ref, dy_ref, kept_ref, got_ref, *refs):
     out_ref = refs[-1]
     xhat, scale = normalise(x_ref[0].astype(F32))
@@ -828,12 +853,16 @@
     which = jnp.stack([side, part]).astype(jnp.int32)
     where = jnp.stack([side, owner]).astype(jnp.int32)
 
+    run_rows = rows // 2
+    held = places[:, ::run_rows] // run_rows
+
     def column(vector):
         vector = vector.reshape(-1)
         return jnp.pad(vector, (0, share - vector.shape[0]))[:, None]
 
     small = jnp.concatenate(
-        [column(v) for v in (b_dense, b_down, norm1_gain, norm1_bias, norm2_gain, norm2_bias, b_qkv, b_up)],
+        [column(v) for v in (b_dense, b_down, norm1_gain, norm1_bias, norm2_gain, norm2_bias, b_qkv, b_up,
+                            held.astype(BF16))],
         axis=1,
     )
     small = jnp.pad(small, ((0, 0), (0, LANES - small.shape[1])))
@@ -869,9 +898,11 @@
     column_of = lambda at: vectors[:, at].reshape(width, 1)
 
     my_places = lax.dynamic_index_in_dim(places, side, 0, keepdims=False)
-    run_rows = rows // 2
-    runs = jnp.stack([my_places[0], my_places[run_rows]]) // run_rows
-    if seq_size == 2:
+    runs = lax.dynamic_index_in_dim(held, side, 0, keepdims=False)
+    if owners == 8 and seq_size == 2:
+        other = lax.dynamic_slice(small, ((owner ^ 1) * share + 2 * side, 8), (2, 1))[:, 0]
+        all_runs = jnp.concatenate([runs, (other + 0.5).astype(jnp.int32)])
+    elif seq_size == 2:
         all_runs = jnp.concatenate([runs, swap(runs, "seq")])
     else:
         all_runs = lax.all_gather(runs, "seq", axis=0, tiled=True)
@@ -915,11 +946,11 @@
             got.append(lax.psum_scatter(both, "seq", scatter_dimension=0, tiled=True))
             dk.append(jnp.zeros((rows, LANES), F32))
             dv.append(jnp.zeros((rows, LANES), F32))
-        if pair == 0:
+        if pair == 1:
             mixed_late = finish(which, tokens, keep_late, got_late, row_of(0), row_of(1), 1, after)
-            after = (outs[0], mixed_late)
+            after = (outs[0], mixed_late, got[0])
             mixed_late = lax.all_gather(mixed_late, ("mh", "ml"), axis=0, tiled=True)
-        elif pair > 0:
+        elif pair > 1:
             after = (outs[0], got[pair - 1])
     feed_weights, mlp_vectors, grad_up_b = feed_grads(
         which, tokens, out_grad, act, mlp_grad, up_w, column_of(4), column_of(5), after + (mixed_early,)
@@ -934,11 +965,9 @@
     grad_qkv, grad_dense, qkv_vectors, grad_qkv_b = weight_grads(
         which, tokens, out_grad, dproj, attended, qkv_w, column_of(2), column_of(3), (mixed_late,)
     )
-    ties = ((grad_qkv_b,), ())
-    input_grad = [
-        round_mp(norm_back(which, tokens, out_grad, keep, got[run], run, ties[run])) for run in range(2)
-    ]
-    input_grad = lay_round(index, *input_grad)
+    ties = ((grad_qkv_b,), (grad_qkv_b,))
+    input_grad = [norm_back(which, tokens, out_grad, keep, got[run], run, ties[run]) for run in range(2)]
+    input_grad = lay_round(index, *[round_mp(rows_done) for rows_done in input_grad])
 
     def scatter(grads):
         return lax.psum_scatter(grads, ("dp", "seq"), scatter_dimension=0, tiled=True)
@@ -957,7 +986,7 @@
     bias_up = grad_up_b.reshape(2, up_rows, owners, up_cols).transpose(2, 1, 3, 0).reshape(width, 2, 1)
     tail = jnp.concatenate([vector_grads, bias_qkv, bias_up], axis=2)
     tail = jnp.pad(tail, ((0, 0), (0, 0), (0, LANES // 2 - 7))).astype(BF16).reshape(width, LANES)
-    packed = scatter(jnp.concatenate([grad_qkv, grad_dense, tail, feed_weights], axis=1))
+    packed = scatter(join((grad_qkv, grad_dense, tail, feed_weights)))
     first, owned_feed = packed[:, : 8 * cols + LANES], packed[:, 8 * cols + LANES :]
     owned_feed = owned_feed.reshape(share, 2, 2, units).transpose(0, 2, 1, 3).reshape(share, 2, 2 * units)
     owned_qkv = first[:, : 6 * cols].reshape(share, 3, 2, cols).transpose(0, 2, 1, 3).reshape(share, 2, 3 * cols)

time: 648 us -> 619 us (0.955)
  waiting for transfers between devices: 210 us -> 184 us
  Pallas kernels: 306 us -> 313 us
  other arithmetic: 20.4 us -> 13.9 us
    ppermute x15 -> x14, waiting for transfers between devices: 165 us -> 111 us  [swap(): return lax.ppermute(values, axis, [(0, 1), (1, 0)])]
    ppermute x6, waiting for transfers between devices: 40.6 us -> 57.3 us  [round_mp(): lax.ppermute(mine, axes, [(i, (i + k) % 4) for i in range(4)])]
    reduce_scatter x1, waiting for transfers between devices: 0.01 us -> 11.9 us  [scatter(): lax.psum_scatter(grads, ('dp', 'seq'), scatter_dimension=0, tiled=True)]
    ppermute x15 -> x14, starting transfers between devices: 25.9 us -> 19.2 us  [swap(): return lax.ppermute(values, axis, [(0, 1), (1, 0)])]
    unnamed x74 -> x70, local copies, waits for them, and re-layouts: 20 us -> 18.2 us
  transfers between devices with their start and end apart: 29 -> 28, of which waited for: 15 -> 13; matrix products, arithmetic and copies ran while one was open for 7% -> 8% of each run, Pallas kernels for 40% -> 46%
where the time goes in v5:
time: 619 us; the launch traced here: 609 us
  Pallas kernels  313 us (51%)
  waiting for transfers between devices  184 us (30%)
  local copies, waits for them, and re-layouts  49.2 us (8%)
  starting transfers between devices  34.2 us (6%)
  between operations  15 us (2%)
  other arithmetic  13.9 us (2%)
    ppermute x14, waiting for transfers between devices, swap(): return lax.ppermute(values, axis, [(0, 1), (1, 0)])  111 us
    pallas_call x3, Pallas kernels, attend_back(): pl.pallas_call(kernel, grid_spec=pltpu.PrefetchScalarGridSpec(num_scalar_...  101 us
    pallas_call x2, Pallas kernels, attend(): pl.pallas_call(kernel, grid_spec=pltpu.PrefetchScalarGridSpec(num_scalar_...  69.3 us
    ppermute x6, waiting for transfers between devices, round_mp(): lax.ppermute(mine, axes, [(i, (i + k) % 4) for i in range(4)])  57.3 us
    pallas_call x1, Pallas kernels, feed(): pl.pallas_call(feed_kernel, grid_spec=pltpu.PrefetchScalarGridSpec(num_sc...  28.9 us
    pallas_call x1, Pallas kernels, feed_grads(): pl.pallas_call(feed_grads_kernel, grid_spec=pltpu.PrefetchScalarGridSpec(...  21.8 us
    ppermute x14, starting transfers between devices, swap(): return lax.ppermute(values, axis, [(0, 1), (1, 0)])  19.2 us
    unnamed x70, local copies, waits for them, and re-layouts  18.2 us
  transfers between devices with their start and end apart: 28, of which 13 were waited for; matrix products, arithmetic and copies ran while one was open for 8% of the time, Pallas kernels for 46%

profile of v5, /device:TPU:0, one launch (start us, length us, event | category | flops | bytes accessed | tf_op | source)
XLA Modules:
  0.0 608.7 jit_solution(154982288170690932)
XLA Ops:
  21.6 8.6 %collective-permute-done = bf16[96,384]{1,0:T(8,128)(2,1)S(1)} collective-permute-done((bf16[96,384]{1,0:T(8,128)(2,1)S(1)}, bf16[96,384]{1,0:T(8,128)(2,1)S(1)}, u32[]{:S(2)}, u32[]{:S(2)}) %collective-permute-start) | collective-permute-done | bytes 73760 | tf_op jit(solution)/shard_map/ppermute | solution.py:803
  52.9 7.2 %place.1 = (bf16[768,1152]{1,0:T(8,128)(2,1)}, bf16[768,384]{1,0:T(8,128)(2,1)}, f32[768,256]{1,0:T(8,128)}) custom-call(s32[2]{0:T(128)} %pad_add_fusion.2.where, bf16[8,2,96,384]{3,2,1,0:T(8,128)(2,1)} %bitcast.107, bf16[8,2,96,512]{3,2,1,0:T(8,128)(2,1)} %bitcast.100), custom_call_target="tpu_custom_call" | custom-call | flops 1 | bytes 1 | tf_op jit(solution)/shard_map/place/pallas_call | solution.py:109
  64.4 12.3 %front.1 = (bf16[2048,384]{1,0:T(8,128)(2,1)}, bf16[2048,768]{1,0:T(8,128)(2,1)}, bf16[2048,384]{1,0:T(8,128)(2,1)}) custom-call(s32[2]{0:T(128)} %pad_add_fusion.which, bf16[2,2048,768]{2,1,0:T(8,128)(2,1)} %x_ref.15, bf16[2,2048,768]{2,1,0:T(8,128)(2,1)} %dy_ref.11, bf16[768,1152]{1,0:T(8,128)(2,1)} %get-tuple-element.59.w_ref.refs_9_, ...), custom_call_target="tpu_custom_call" | custom-call | flops 1 | bytes 1 | tf_op jit(solution)/shard_map/front/pallas_call | solution.py:149
  84.7 6.9 %place_second.1 = (bf16[768,1536]{1,0:T(8,128)(2,1)}, bf16[768,1536]{1,0:T(8,128)(2,1)}) custom-call(bf16[8,2,96,1536]{3,2,1,0:T(8,128)(2,1)} %bitcast.95), custom_call_target="tpu_custom_call" | custom-call | flops 1 | bytes 1 | tf_op jit(solution)/shard_map/place_second/pallas_call | solution.py:85
  91.6 28.9 %feed.1 = (bf16[2048,768]{1,0:T(8,128)(2,1)}, bf16[2048,768]{1,0:T(8,128)(2,1)}, bf16[2048,1536]{1,0:T(8,128)(2,1)}, bf16[2048,1536]{1,0:T(8,128)(2,1)}) custom-call(s32[2]{0:T(128)} %pad_add_fusion.which, bf16[2,2048,768]{2,1,0:T(8,128)(2,1)} %x_ref.15, bf16[2,2048,768]{2,1,0:T(8,128)(2,1)} %dy_ref.11, bf16[768,1536]{1,0:T(8,128)(2,1)} %get-tuple-element.65.up_ref, ...), custom_call_target="tpu_custom_call" | custom-call | flops 1 | bytes 1 | tf_op jit(solution)/shard_map/feed/pallas_call | solution.py:191
  120.4 26.7 %collective-permute-done.8.refs_1_.refs_3_ = bf16[2048,768]{1,0:T(8,128)(2,1)S(1)} collective-permute-done((bf16[2048,768]{1,0:T(8,128)(2,1)}, bf16[2048,768]{1,0:T(8,128)(2,1)S(1)}, u32[]{:S(2)}, u32[]{:S(2)}) %collective-permute-start.8) | collective-permute-done | bytes 3145760 | tf_op jit(solution)/shard_map/ppermute | solution.py:803
  148.7 29.3 %attend.2 = (bf16[1024,384]{1,0:T(8,128)(2,1)}, f32[24,1024]{1,0:T(8,128)}, bf16[512,768]{1,0:T(8,128)(2,1)}, f32[512,768]{1,0:T(8,128)}) custom-call(s32[3]{0:T(128)} %pad_add_fusion.1.info, s32[4]{0:T(128)} %select_reduce_fusion.slots, bf16[2048,384]{1,0:T(8,128)(2,1)} %get-tuple-element.63.q_ref, bf16[2048,384]{1,0:T(8,128)(2,1)} %get-tuple-element.64.g_ref, ...), custom_call_target="tpu_custom_call" | custom-call | flops 1 | bytes 1 | tf_op jit(solution)/shard_map/attend/pallas_call | solution.py:389
  181.4 40.0 %attend.3 = (bf16[1024,384]{1,0:T(8,128)(2,1)}, f32[24,1024]{1,0:T(8,128)}, bf16[512,768]{1,0:T(8,128)(2,1)}, f32[512,768]{1,0:T(8,128)}) custom-call(s32[3]{0:T(128)} %pad_add_fusion.1.info, s32[4]{0:T(128)} %select_reduce_fusion.slots, bf16[2048,384]{1,0:T(8,128)(2,1)} %get-tuple-element.63.q_ref, bf16[2048,384]{1,0:T(8,128)(2,1)} %get-tuple-element.64.g_ref, ...), custom_call_target="tpu_custom_call" | custom-call | flops 1 | bytes 1 | tf_op jit(solution)/shard_map/attend/pallas_call | solution.py:389
  226.9 33.5 %attend_back.3 = (bf16[2048,128]{1,0:T(8,128)(2,1)}, f32[2048,128]{1,0:T(8,128)}, f32[2048,128]{1,0:T(8,128)}, bf16[2048,256]{1,0:T(8,128)(2,1)}) custom-call(s32[3]{0:T(128)} %pad_add_fusion.1.info, s32[4]{0:T(128)} %select_reduce_fusion.slots, bf16[2048,384]{1,0:T(8,128)(2,1)} %get-tuple-element.63.q_ref, bf16[2048,384]{1,0:T(8,128)(2,1)} %get-tuple-element.64.g_ref, ...), custom_call_target="tpu_custom_call" | custom-call | flops 8589934592 | bytes 16777216 | tf_op jit(solution)/shard_map/attend_back/pallas_call | solution.py:522
  260.3 33.7 %attend_back.4 = (bf16[2048,128]{1,0:T(8,128)(2,1)}, f32[2048,128]{1,0:T(8,128)}, f32[2048,128]{1,0:T(8,128)}, bf16[2048,256]{1,0:T(8,128)(2,1)}) custom-call(s32[3]{0:T(128)} %pad_add_fusion.1.info, s32[4]{0:T(128)} %select_reduce_fusion.slots, bf16[2048,384]{1,0:T(8,128)(2,1)} %get-tuple-element.63.q_ref, bf16[2048,384]{1,0:T(8,128)(2,1)} %get-tuple-element.64.g_ref, ...), custom_call_target="tpu_custom_call" | custom-call | flops 8589934592 | bytes 16777216 | tf_op jit(solution)/shard_map/attend_back/pallas_call | solution.py:522
  303.7 21.3 %collective-permute-done.11.refs_6_ = bf16[2048,256]{1,0:T(8,128)(2,1)S(1)} collective-permute-done((bf16[2048,256]{1,0:T(8,128)(2,1)}, bf16[2048,256]{1,0:T(8,128)(2,1)S(1)}, u32[]{:S(2)}, u32[]{:S(2)}) %collective-permute-start.11) | collective-permute-done | bytes 1048608 | tf_op jit(solution)/shard_map/ppermute | solution.py:803
  326.0 33.5 %attend_back.5 = (bf16[2048,128]{1,0:T(8,128)(2,1)}, f32[2048,128]{1,0:T(8,128)}, f32[2048,128]{1,0:T(8,128)}, bf16[2048,256]{1,0:T(8,128)(2,1)}) custom-call(s32[3]{0:T(128)} %pad_add_fusion.1.info, s32[4]{0:T(128)} %select_reduce_fusion.slots, bf16[2048,384]{1,0:T(8,128)(2,1)} %get-tuple-element.63.q_ref, bf16[2048,384]{1,0:T(8,128)(2,1)} %get-tuple-element.64.g_ref, ...), custom_call_target="tpu_custom_call" | custom-call | flops 8589934592 | bytes 16777216 | tf_op jit(solution)/shard_map/attend_back/pallas_call | solution.py:522
  363.1 21.8 %feed_grads.1 = (bf16[768,3072]{1,0:T(8,128)(2,1)}, f32[768,128]{1,0:T(8,128)}, f32[1,1536]{1,0:T(1,128)}) custom-call(s32[2]{0:T(128)} %pad_add_fusion.which, bf16[2,2048,768]{2,1,0:T(8,128)(2,1)} %x_ref.15, bf16[2,2048,768]{2,1,0:T(8,128)(2,1)} %dy_ref.11, bf16[2048,1536]{1,0:T(8,128)(2,1)} %get-tuple-element.90.act_ref, ...), custom_call_target="tpu_custom_call" | custom-call | flops 8589934592 | bytes 16777216 | tf_op jit(solution)/shard_map/feed_grads/pallas_call | solution.py:256
  385.9 14.4 %back.1 = (bf16[2048,1152]{1,0:T(8,128)(2,1)}, bf16[1024,768]{1,0:T(8,128)(2,1)}, f32[1024,768]{1,0:T(8,128)}) custom-call(s32[2]{0:T(128)} %pad_add_fusion.which, bf16[2048,384]{1,0:T(8,128)(2,1)} %pad_maximum_fusion.dq_ref, f32[2048,128]{1,0:T(8,128)} %get-tuple-element.81.refs_0_, f32[2048,128]{1,0:T(8,128)} %get-tuple-element.82.refs_1_, ...), custom_call_target="tpu_custom_call" | custom-call | flops 1 | bytes 1 | tf_op jit(solution)/shard_map/back/pallas_call | solution.py:580
  404.0 15.4 %weight_grads.1 = (bf16[768,1152]{1,0:T(8,128)(2,1)}, bf16[768,384]{1,0:T(8,128)(2,1)}, f32[768,128]{1,0:T(8,128)}, f32[1,1152]{1,0:T(1,128)}) custom-call(s32[2]{0:T(128)} %pad_add_fusion.which, bf16[2,2048,768]{2,1,0:T(8,128)(2,1)} %x_ref.15, bf16[2,2048,768]{2,1,0:T(8,128)(2,1)} %dy_ref.11, bf16[2048,1152]{1,0:T(8,128)(2,1)} %get-tuple-element.93.refs_0_.dproj_ref, ...), custom_call_target="tpu_custom_call" | custom-call | flops 8589934592 | bytes 16777216 | tf_op jit(solution)/shard_map/weight_grads/pallas_call | solution.py:637
  422.7 6.4 %join.1 = bf16[768,4736]{1,0:T(8,128)(2,1)} custom-call(bf16[768,1152]{1,0:T(8,128)(2,1)} %get-tuple-element.97.refs_0_, bf16[768,384]{1,0:T(8,128)(2,1)} %get-tuple-element.98.refs_1_, bf16[768,128]{1,0:T(8,128)(2,1)} %copy.151.refs_2_, bf16[768,3072]{1,0:T(8,128)(2,1)} %get-tuple-element.101.refs_3_), custom_call_target="tpu_custom_call" | custom-call | flops 1 | bytes 1 | tf_op jit(solution)/shard_map/join/pallas_call | solution.py:673
  430.2 4.3 norm_back.3.refs_4_
  441.5 36.8 %collective-permute-done.14.got_ref = bf16[512,768]{1,0:T(8,128)(2,1)S(1)} collective-permute-done((bf16[512,768]{1,0:T(8,128)(2,1)S(1)}, bf16[512,768]{1,0:T(8,128)(2,1)S(1)}, u32[]{:S(2)}, u32[]{:S(2)}) %collective-permute-start.14) | collective-permute-done | bytes 786464 | tf_op jit(solution)/shard_map/ppermute | solution.py:803
  487.2 11.9 %reduce-scatter.2.cloned.1.call-done = bf16[96,4736]{1,0:T(8,128)(2,1)} async-done(((bf16[768,4736]{1,0:T(8,128)(2,1)}), bf16[96,4736]{1,0:T(8,128)(2,1)}) %reduce-scatter.2.cloned.1.call-update) | async-done | bytes 909328 | tf_op jit(solution)/shard_map/reduce_scatter | solution.py:973
  506.2 6.8 %lay_gathered.1 = bf16[2,2048,768]{2,1,0:T(8,128)(2,1)} custom-call(bf16[2048,768]{1,0:T(8,128)(2,1)} %all-gather.6.cloned.1.call-done.refs_2_.early_ref, bf16[2048,768]{1,0:T(8,128)(2,1)} %all-gather.8.cloned.1.call-done.late_ref.refs_0_, bf16[2048,1152]{1,0:T(8,128)(2,1)} %get-tuple-element.93.refs_0_.dproj_ref), custom_call_target="tpu_custom_call" | custom-call | flops 1 | bytes 1 | tf_op jit(solution)/shard_map/lay_gathered/pallas_call | solution.py:762
  513.7 7.2 %collective-permute-done.15.refs_1_ = bf16[512,768]{1,0:T(8,128)(2,1)} collective-permute-done((bf16[512,768]{1,0:T(8,128)(2,1)}, bf16[512,768]{1,0:T(8,128)(2,1)}, u32[]{:S(2)}, u32[]{:S(2)}) %collective-permute-start.15) | collective-permute-done | bytes 786464 | tf_op jit(solution)/shard_map/ppermute | solution.py:821
  520.9 49.5 %collective-permute-done.16.refs_2_ = bf16[512,768]{1,0:T(8,128)(2,1)} collective-permute-done((bf16[512,768]{1,0:T(8,128)(2,1)}, bf16[512,768]{1,0:T(8,128)(2,1)}, u32[]{:S(2)}, u32[]{:S(2)}) %collective-permute-start.16) | collective-permute-done | bytes 786464 | tf_op jit(solution)/shard_map/ppermute | solution.py:821
  570.4 6.9 %lay_round.1 = bf16[2,2048,768]{2,1,0:T(8,128)(2,1)} custom-call(s32[1]{0:T(128)} %bitcast.31.index, bf16[512,768]{1,0:T(8,128)(2,1)} %norm_back.2.refs_0_, bf16[512,768]{1,0:T(8,128)(2,1)} %collective-permute-done.15.refs_1_, bf16[512,768]{1,0:T(8,128)(2,1)} %collective-permute-done.16.refs_2_, bf16[512,768]{1,0:T(8,128)(2,1)} %collective-permute-done.17.refs_3_, ...), custom_call_target="tpu_custom_call" | custom-call | flops 1 | bytes 1 | tf_op jit(solution)/shard_map/lay_round/pallas_call | solution.py:787
  577.7 13.9 %collective-permute-done.22 = bf16[96,2368]{1,0:T(8,128)(2,1)} collective-permute-done((bf16[96,2368]{1,0:T(8,128)(2,1)}, bf16[96,2368]{1,0:T(8,128)(2,1)}, u32[]{:S(2)}, u32[]{:S(2)}) %collective-permute-start.22) | collective-permute-done | bytes 454688 | tf_op jit(solution)/shard_map/ppermute | solution.py:803
  (238 shorter events, 116.6 us)
Async XLA Ops:
  7.2 77.5 %all-gather.4.cloned.1.call-start = ((), (), s32[]{:S(2)}) async-start(), calls=%async_computation.1 | async-start | bytes 5013504 | tf_op jit(solution)/shard_map/all_gather | solution.py:876
  9.0 353.1 %all-gather.6.cloned.1.call-start = ((), (), s32[]{:S(2)}) async-start(), calls=%async_computation.2 | async-start | bytes 3932160 | tf_op jit(solution)/shard_map/all_gather | solution.py:932
  14.8 17.2 %collective-permute-start.4 = (bf16[96,512]{1,0:T(8,128)(2,1)S(1)}, bf16[96,512]{1,0:T(8,128)(2,1)S(1)}, u32[]{:S(2)}, u32[]{:S(2)}) collective-permute-start(bf16[96,512]{1,0:T(8,128)(2,1)S(1)} %get-tuple-element.173), channel_id=1, source_target_pairs={{0,2},{2,0},{1,3},{3,1},{4,6},{6,4},{5,7},{7,5},{8,10},{10,8},{9,1... | collective-permute-start | bytes 294920 | tf_op jit(solution)/shard_map/ppermute | solution.py:803
  20.0 10.2 %collective-permute-start = (bf16[96,384]{1,0:T(8,128)(2,1)S(1)}, bf16[96,384]{1,0:T(8,128)(2,1)S(1)}, u32[]{:S(2)}, u32[]{:S(2)}) collective-permute-start(bf16[96,384]{1,0:T(8,128)(2,1)S(1)} %reshape.124), channel_id=1, source_target_pairs={{0,2},{2,0},{1,3},{3,1},{4,6},{6,4},{5,7},{7,5},{8,10},{10,8},{9,1... | collective-permute-start | bytes 221192 | tf_op jit(solution)/shard_map/ppermute | solution.py:803
  32.1 8.4 %collective-permute-start.5 = (bf16[2,96,512]{2,1,0:T(8,128)(2,1)S(1)}, bf16[2,96,512]{2,1,0:T(8,128)(2,1)S(1)}, u32[]{:S(2)}, u32[]{:S(2)}) collective-permute-start(bf16[2,96,512]{2,1,0:T(8,128)(2,1)S(1)} %pad_maximum_fusion.7), channel_id=1, source_target_pairs={{0,16},{8,24},{16,0},{24,8},{1,17},{9,25},{17,1},{25,9},{2,18},{10... | collective-permute-start | bytes 589832 | tf_op jit(solution)/shard_map/ppermute | solution.py:807
  36.2 10.8 %collective-permute-start.2 = (bf16[4,96,384]{2,1,0:T(8,128)(2,1)}, bf16[4,96,384]{2,1,0:T(8,128)(2,1)S(1)}, u32[]{:S(2)}, u32[]{:S(2)}) collective-permute-start(bf16[4,96,384]{2,1,0:T(8,128)(2,1)} %pad_maximum_fusion.5), channel_id=1, source_target_pairs={{0,16},{8,24},{16,0},{24,8},{1,17},{9,25},{17,1},{25,9},{2,18},{10... | collective-permute-start | bytes 884744 | tf_op jit(solution)/shard_map/ppermute | solution.py:807
  41.3 8.0 %collective-permute-start.6 = (bf16[4,96,512]{2,1,0:T(8,128)(2,1)}, bf16[4,96,512]{2,1,0:T(8,128)(2,1)S(1)}, u32[]{:S(2)}, u32[]{:S(2)}) collective-permute-start(bf16[4,96,512]{2,1,0:T(8,128)(2,1)} %pad_maximum_fusion.4), channel_id=1, source_target_pairs={{0,4},{4,0},{1,5},{5,1},{2,6},{6,2},{3,7},{7,3},{8,12},{12,8},{9,1... | collective-permute-start | bytes 1179656 | tf_op jit(solution)/shard_map/ppermute | solution.py:803
  76.7 70.4 %collective-permute-start.8 = (bf16[2048,768]{1,0:T(8,128)(2,1)}, bf16[2048,768]{1,0:T(8,128)(2,1)S(1)}, u32[]{:S(2)}, u32[]{:S(2)}) collective-permute-start(bf16[2048,768]{1,0:T(8,128)(2,1)} %get-tuple-element.68.refs_0_.refs_2_), channel_id=1, source_target_pairs={{0,4},{4,0},{1,5},{5,1},{2,6},{6,2},{3,7},{7,3},{8,12},{12,8},{9,1... | collective-permute-start | bytes 9437192 | tf_op jit(solution)/shard_map/ppermute | solution.py:803
  178.0 43.4 %collective-permute-start.9 = (bf16[512,768]{1,0:T(8,128)(2,1)}, bf16[512,768]{1,0:T(8,128)(2,1)S(1)}, u32[]{:S(2)}, u32[]{:S(2)}) collective-permute-start(bf16[512,768]{1,0:T(8,128)(2,1)} %get-tuple-element.70), channel_id=1, source_target_pairs={{0,1},{1,0},{2,3},{3,2},{4,5},{5,4},{6,7},{7,6},{8,9},{9,8},{10,11... | collective-permute-start | bytes 2359304 | tf_op jit(solution)/shard_map/ppermute | solution.py:803
  226.0 178.0 %all-gather.8.cloned.1.call-start = ((), (), s32[]{:S(2)}) async-start(), calls=%async_computation.3 | async-start | bytes 3932160 | tf_op jit(solution)/shard_map/all_gather | solution.py:952
  226.1 68.0 %collective-permute-start.10 = (bf16[512,768]{1,0:T(8,128)(2,1)S(1)}, bf16[512,768]{1,0:T(8,128)(2,1)S(1)}, u32[]{:S(2)}, u32[]{:S(2)}) collective-permute-start(bf16[512,768]{1,0:T(8,128)(2,1)S(1)} %copy-done.25), channel_id=1, source_target_pairs={{0,1},{1,0},{2,3},{3,2},{4,5},{5,4},{6,7},{7,6},{8,9},{9,8},{10,11... | collective-permute-start | bytes 2359304 | tf_op jit(solution)/shard_map/ppermute | solution.py:803
  298.6 200.4 %reduce-scatter.2.cloned.1.call-start = ((), (), s32[]{:S(2)}) async-start(), calls=%async_computation.4 | async-start | bytes 8183808 | tf_op jit(solution)/shard_map/reduce_scatter | solution.py:973
  298.7 26.4 %collective-permute-start.11 = (bf16[2048,256]{1,0:T(8,128)(2,1)}, bf16[2048,256]{1,0:T(8,128)(2,1)S(1)}, u32[]{:S(2)}, u32[]{:S(2)}) collective-permute-start(bf16[2048,256]{1,0:T(8,128)(2,1)} %get-tuple-element.79), channel_id=1, source_target_pairs={{0,4},{4,0},{1,5},{5,1},{2,6},{6,2},{3,7},{7,3},{8,12},{12,8},{9,1... | collective-permute-start | bytes 3145736 | tf_op jit(solution)/shard_map/ppermute | solution.py:803
  302.7 59.4 %collective-permute-start.12 = (bf16[2048,256]{1,0:T(8,128)(2,1)}, bf16[2048,256]{1,0:T(8,128)(2,1)S(1)}, u32[]{:S(2)}, u32[]{:S(2)}) collective-permute-start(bf16[2048,256]{1,0:T(8,128)(2,1)} %get-tuple-element.87), channel_id=1, source_target_pairs={{0,4},{4,0},{1,5},{5,1},{2,6},{6,2},{3,7},{7,3},{8,12},{12,8},{9,1... | collective-permute-start | bytes 3145736 | tf_op jit(solution)/shard_map/ppermute | solution.py:803
  359.6 25.3 %collective-permute-start.13 = (bf16[2048,256]{1,0:T(8,128)(2,1)}, bf16[2048,256]{1,0:T(8,128)(2,1)S(1)}, u32[]{:S(2)}, u32[]{:S(2)}) collective-permute-start(bf16[2048,256]{1,0:T(8,128)(2,1)} %get-tuple-element.88), channel_id=1, source_target_pairs={{0,4},{4,0},{1,5},{5,1},{2,6},{6,2},{3,7},{7,3},{8,12},{12,8},{9,1... | collective-permute-start | bytes 3145736 | tf_op jit(solution)/shard_map/ppermute | solution.py:803
  401.8 27.5 %collective-permute-start.18 = (bf16[512,768]{1,0:T(8,128)(2,1)S(1)}, bf16[512,768]{1,0:T(8,128)(2,1)S(1)}, u32[]{:S(2)}, u32[]{:S(2)}) collective-permute-start(bf16[512,768]{1,0:T(8,128)(2,1)S(1)} %get-tuple-element.176), channel_id=1, source_target_pairs={{0,1},{1,0},{2,3},{3,2},{4,5},{5,4},{6,7},{7,6},{8,9},{9,8},{10,11... | collective-permute-start | bytes 2359304 | tf_op jit(solution)/shard_map/ppermute | solution.py:803
  429.2 49.2 %collective-permute-start.14 = (bf16[512,768]{1,0:T(8,128)(2,1)S(1)}, bf16[512,768]{1,0:T(8,128)(2,1)S(1)}, u32[]{:S(2)}, u32[]{:S(2)}) collective-permute-start(bf16[512,768]{1,0:T(8,128)(2,1)S(1)} %get-tuple-element.177), channel_id=1, source_target_pairs={{0,1},{1,0},{2,3},{3,2},{4,5},{5,4},{6,7},{7,6},{8,9},{9,8},{10,11... | collective-permute-start | bytes 2359304 | tf_op jit(solution)/shard_map/ppermute | solution.py:803
  434.5 48.8 %collective-permute-start.19 = (bf16[512,768]{1,0:T(8,128)(2,1)}, bf16[512,768]{1,0:T(8,128)(2,1)}, u32[]{:S(2)}, u32[]{:S(2)}) collective-permute-start(bf16[512,768]{1,0:T(8,128)(2,1)} %norm_back.3.refs_4_), channel_id=1, source_target_pairs={{0,1},{1,2},{2,3},{3,0},{4,5},{5,6},{6,7},{7,4},{8,9},{9,10},{10,1... | collective-permute-start | bytes 2359304 | tf_op jit(solution)/shard_map/ppermute | solution.py:821
  436.5 67.3 %collective-permute-start.20 = (bf16[512,768]{1,0:T(8,128)(2,1)}, bf16[512,768]{1,0:T(8,128)(2,1)}, u32[]{:S(2)}, u32[]{:S(2)}) collective-permute-start(bf16[512,768]{1,0:T(8,128)(2,1)} %norm_back.3.refs_4_), channel_id=1, source_target_pairs={{0,2},{1,3},{2,0},{3,1},{4,6},{5,7},{6,4},{7,5},{8,10},{9,11},{10,... | collective-permute-start | bytes 2359304 | tf_op jit(solution)/shard_map/ppermute | solution.py:821
  440.6 73.1 %collective-permute-start.21 = (bf16[512,768]{1,0:T(8,128)(2,1)}, bf16[512,768]{1,0:T(8,128)(2,1)}, u32[]{:S(2)}, u32[]{:S(2)}) collective-permute-start(bf16[512,768]{1,0:T(8,128)(2,1)} %norm_back.3.refs_4_), channel_id=1, source_target_pairs={{0,3},{1,0},{2,1},{3,2},{4,7},{5,4},{6,5},{7,6},{8,11},{9,8},{10,9... | collective-permute-start | bytes 2359304 | tf_op jit(solution)/shard_map/ppermute | solution.py:821
  483.3 37.6 %collective-permute-start.15 = (bf16[512,768]{1,0:T(8,128)(2,1)}, bf16[512,768]{1,0:T(8,128)(2,1)}, u32[]{:S(2)}, u32[]{:S(2)}) collective-permute-start(bf16[512,768]{1,0:T(8,128)(2,1)} %norm_back.2.refs_0_), channel_id=1, source_target_pairs={{0,1},{1,2},{2,3},{3,0},{4,5},{5,6},{6,7},{7,4},{8,9},{9,10},{10,1... | collective-permute-start | bytes 2359304 | tf_op jit(solution)/shard_map/ppermute | solution.py:821
  483.3 87.0 %collective-permute-start.16 = (bf16[512,768]{1,0:T(8,128)(2,1)}, bf16[512,768]{1,0:T(8,128)(2,1)}, u32[]{:S(2)}, u32[]{:S(2)}) collective-permute-start(bf16[512,768]{1,0:T(8,128)(2,1)} %norm_back.2.refs_0_), channel_id=1, source_target_pairs={{0,2},{1,3},{2,0},{3,1},{4,6},{5,7},{6,4},{7,5},{8,10},{9,11},{10,... | collective-permute-start | bytes 2359304 | tf_op jit(solution)/shard_map/ppermute | solution.py:821
  483.4 87.0 %collective-permute-start.17 = (bf16[512,768]{1,0:T(8,128)(2,1)}, bf16[512,768]{1,0:T(8,128)(2,1)}, u32[]{:S(2)}, u32[]{:S(2)}) collective-permute-start(bf16[512,768]{1,0:T(8,128)(2,1)} %norm_back.2.refs_0_), channel_id=1, source_target_pairs={{0,3},{1,0},{2,1},{3,2},{4,7},{5,4},{6,5},{7,6},{8,11},{9,8},{10,9... | collective-permute-start | bytes 2359304 | tf_op jit(solution)/shard_map/ppermute | solution.py:821
  503.8 87.8 %collective-permute-start.22 = (bf16[96,2368]{1,0:T(8,128)(2,1)}, bf16[96,2368]{1,0:T(8,128)(2,1)}, u32[]{:S(2)}, u32[]{:S(2)}) collective-permute-start(bf16[96,2368]{1,0:T(8,128)(2,1)} %fusion), channel_id=1, source_target_pairs={{0,2},{2,0},{1,3},{3,1},{4,6},{6,4},{5,7},{7,5},{8,10},{10,8},{9,1... | collective-permute-start | bytes 1363976 | tf_op jit(solution)/shard_map/ppermute | solution.py:803
  (35 other events, 233.2 us)
Sparse Core Ops, SparseCore 0:
  10.9 63.2 all-gather.3
  226.1 69.3 all-gather.5
  298.8 66.4 all-gather.7
  429.3 69.6 reduce-scatter.1

commit v6 on v5

--- a/solution.py
+++ b/solution.py
@@ -75,18 +75,21 @@
 
 def place_second_kernel(pack_ref, up_ref, down_ref):
     units = pack_ref.shape[-1] // 2
-    for j in range(2):
-        up_ref[:, j * units : (j + 1) * units] = pack_ref[0, j, :, :units]
-        down_ref[:, j * units : (j + 1) * units] = pack_ref[0, j, :, units:]
+    share = pack_ref.shape[2]
+    for i in range(2):
+        rows = slice(i * share, (i + 1) * share)
+        for j in range(2):
+            up_ref[rows, j * units : (j + 1) * units] = pack_ref[i, j, :, :units]
+            down_ref[rows, j * units : (j + 1) * units] = pack_ref[i, j, :, units:]
 
 
 def place_second(pack):
     owners, _, share, width = pack.shape
     return pl.pallas_call(
         place_second_kernel,
-        grid=(owners,),
-        in_specs=[pl.BlockSpec((1,) + pack.shape[1:], lambda i: (i, 0, 0, 0))],
-        out_specs=[pl.BlockSpec((share, width), lambda i: (i, 0))] * 2,
+        grid=(owners // 2,),
+        in_specs=[pl.BlockSpec((2,) + pack.shape[1:], lambda i: (i, 0, 0, 0))],
+        out_specs=[pl.BlockSpec((2 * share, width), lambda i: (i, 0))] * 2,
         out_shape=[jax.ShapeDtypeStruct((owners * share, width), BF16)] * 2,
         compiler_params=params(),
         cost_estimate=brief,
@@ -123,9 +126,10 @@
 
 def front_kernel(
     which, x_ref, dy_ref, w_ref, wb_ref, dense_ref, gain_ref, shift_ref, cos_ref, low_ref, high_ref,
-    q_ref, kv_ref, do_ref,
+    q_ref, kv_most, kv_last, do_ref,
 ):
     half = q_ref.shape[1]
+    most = kv_most.shape[1] // 2
     xhat, _ = normalise(x_ref[0].astype(F32))
     normed = (xhat * gain_ref[...] + shift_ref[...]).astype(BF16)
     proj = dot(normed, w_ref[...], NN) + wb_ref[...]
@@ -134,9 +138,13 @@
         at = slice(j * LANES, (j + 1) * LANES)
         query = turn(proj[:, at], cosines, low, high).astype(BF16)
         q_ref[:, at] = query * BF16(HD**-0.5)
-        key = proj[:, half + j * LANES : half + (j + 1) * LANES]
-        kv_ref[:, at] = turn(key, cosines, low, high).astype(BF16)
-    kv_ref[:, half:] = proj[:, 2 * half :].astype(BF16)
+        key = turn(proj[:, half + j * LANES : half + (j + 1) * LANES], cosines, low, high).astype(BF16)
+        if j * LANES < most:
+            kv_most[:, at] = key
+        else:
+            kv_last[:, :LANES] = key
+    kv_most[:, most:] = proj[:, 2 * half : 2 * half + most].astype(BF16)
+    kv_last[:, LANES:] = proj[:, 2 * half + most :].astype(BF16)
     do_ref[...] = dot(dy_ref[0], dense_ref[...], NN).astype(BF16)
 
 
@@ -153,11 +161,12 @@
             grid=(rows // step,),
             in_specs=[chosen, chosen, whole(w.shape), whole(wb.shape), whole(dense.shape),
                       whole(gain.shape), whole(shift.shape)] + [by_row(LANES)] * 3,
-            out_specs=[by_row(half), by_row(2 * half), by_row(half)],
+            out_specs=[by_row(half), by_row(2 * half - 2 * LANES), by_row(2 * LANES), by_row(half)],
         ),
         out_shape=[
             jax.ShapeDtypeStruct((rows, half), BF16),
-            jax.ShapeDtypeStruct((rows, 2 * half), BF16),
+            jax.ShapeDtypeStruct((rows, 2 * half - 2 * LANES), BF16),
+            jax.ShapeDtypeStruct((rows, 2 * LANES), BF16),
             jax.ShapeDtypeStruct((rows, half), BF16),
         ],
         compiler_params=params(),
@@ -286,9 +295,14 @@
     return [jnp.where(mine, both, jnp.zeros_like(both)) for mine in heads]
 
 
-def attend_kernel(info, slots, q_ref, g_ref, dense_ref, prior_ref, *refs, block, run_rows, parts, run, ties):
+def attend_kernel(info, slots, q_ref, g_ref, dense_ref, prior_ref, *refs, block, run_rows, parts, run, ties, split):
     k_parts, v_parts, refs = refs[:parts], refs[parts : 2 * parts], refs[2 * parts + ties :]
-    o_ref, stat_ref, send_ref, keep_ref, k_ref, v_ref, score_ref, acc_ref, branch_ref = refs
+    o_ref, stat_ref, refs = refs[0], refs[1], refs[2:]
+    if split:
+        send_ref, keep_ref, refs = refs[0], refs[1], refs[2:]
+    else:
+        sum_ref, refs = refs[0], refs[1:]
+    k_ref, v_ref, score_ref, acc_ref, branch_ref = refs
     per_run = run_rows // block
     pair, place_in_run = pl.program_id(0), pl.program_id(1)
     full = info[run]
@@ -367,24 +381,30 @@
 
     @pl.when((pair == pl.num_programs(0) - 1) & (place_in_run == per_run - 1))
     def _():
-        half = run_rows // 2
-        send_ref[...] = branch_ref[pl.ds(pl.multiple_of((1 - info[2]) * half, half), half), :].astype(BF16)
-        keep_ref[...] = branch_ref[pl.ds(pl.multiple_of(info[2] * half, half), half), :]
-
-
-def attend(info, slots, q, g, kv_parts, dense, prior, run, after=()):
+        if split:
+            half = run_rows // 2
+            send_ref[...] = branch_ref[pl.ds(pl.multiple_of((1 - info[2]) * half, half), half), :].astype(BF16)
+            keep_ref[...] = branch_ref[pl.ds(pl.multiple_of(info[2] * half, half), half), :]
+        else:
+            sum_ref[...] = branch_ref[...]
+
+
+def attend(info, slots, q, g, kv_parts, dense, prior, run, base, after=()):
     rows, width = q.shape
     model = dense.shape[0]
     keys = sum(kv.shape[0] for kv in kv_parts)
     run_rows = rows // 2
     block = min(512, run_rows)
     per_run = run_rows // block
-    pairs = width // LANES
-    by_query = pl.BlockSpec((block, LANES), lambda p, i, *_: (run * per_run + i, p))
+    pairs = kv_parts[0].shape[1] // (2 * LANES)
+    split = (base + pairs) * LANES == width
+    prior_row = run if prior.shape[0] == rows else 0
+    by_query = pl.BlockSpec((block, LANES), lambda p, i, *_: (run * per_run + i, base + p))
     by_key = [pl.BlockSpec((kv.shape[0], LANES), lambda p, i, *_: (0, p)) for kv in kv_parts]
     by_value = [pl.BlockSpec((kv.shape[0], LANES), lambda p, i, *_: (0, pairs + p)) for kv in kv_parts]
     kernel = functools.partial(
-        attend_kernel, block=block, run_rows=run_rows, parts=len(kv_parts), run=run, ties=len(after)
+        attend_kernel, block=block, run_rows=run_rows, parts=len(kv_parts), run=run,
+        ties=len(after), split=split,
     )
     return pl.pallas_call(
         kernel,
@@ -393,16 +413,14 @@
             grid=(pairs, per_run),
             in_specs=[
                 by_query, by_query,
-                pl.BlockSpec((model, LANES), lambda p, i, *_: (0, p)),
-                pl.BlockSpec((run_rows, model), lambda p, i, *_: (run, 0)),
+                pl.BlockSpec((model, LANES), lambda p, i, *_: (0, base + p)),
+                pl.BlockSpec((run_rows, model), lambda p, i, *_: (prior_row, 0)),
                 *by_key, *by_value,
             ] + [anywhere] * len(after),
             out_specs=[
                 pl.BlockSpec((block, LANES), lambda p, i, *_: (i, p)),
                 pl.BlockSpec((8, block), lambda p, i, *_: (p, i)),
-                whole((run_rows // 2, model)),
-                whole((run_rows // 2, model)),
-            ],
+            ] + ([whole((run_rows // 2, model))] * 2 if split else [whole((run_rows, model))]),
             scratch_shapes=[
                 pltpu.VMEM((keys, LANES), BF16),
                 pltpu.VMEM((keys, LANES), BF16),
@@ -412,11 +430,12 @@
             ],
         ),
         out_shape=[
-            jax.ShapeDtypeStruct((run_rows, width), BF16),
+            jax.ShapeDtypeStruct((run_rows, pairs * LANES), BF16),
             jax.ShapeDtypeStruct((8 * pairs, run_rows), F32),
+        ] + ([
             jax.ShapeDtypeStruct((run_rows // 2, model), BF16),
             jax.ShapeDtypeStruct((run_rows // 2, model), F32),
-        ],
+        ] if split else [jax.ShapeDtypeStruct((run_rows, model), F32)]),
         compiler_params=params(),
         cost_estimate=brief,
         name="attend",
@@ -497,16 +516,16 @@
             back_ref[:, LANES:] = dv_ref[home:, :].astype(BF16)
 
 
-def attend_back(info, slots, q, g, stats, kv_parts, pair, home, after=()):
+def attend_back(info, slots, q, g, stats, kv_parts, pair, at, home, after=()):
     rows, width = q.shape
     keys = sum(kv.shape[0] for kv in kv_parts)
     run_rows = rows // 2
     block = min(512, run_rows)
-    pairs = width // LANES
+    pairs = kv_parts[0].shape[1] // (2 * LANES)
     own = home or keys
     by_query = pl.BlockSpec((block, LANES), lambda i, *_: (i, pair))
-    by_key = [pl.BlockSpec((kv.shape[0], LANES), lambda i, *_: (0, pair)) for kv in kv_parts]
-    by_value = [pl.BlockSpec((kv.shape[0], LANES), lambda i, *_: (0, pairs + pair)) for kv in kv_parts]
+    by_key = [pl.BlockSpec((kv.shape[0], LANES), lambda i, *_: (0, at)) for kv in kv_parts]
+    by_value = [pl.BlockSpec((kv.shape[0], LANES), lambda i, *_: (0, pairs + at)) for kv in kv_parts]
     kernel = functools.partial(
         attend_back_kernel, block=block, run_rows=run_rows, parts=len(kv_parts), home=home, ties=len(after)
     )
@@ -910,31 +929,51 @@
     slots = jnp.sum(jnp.where(all_runs[None, :] == order[:, None], order[None, :], 0), axis=1)
     tables = rotation_tables(my_places)
 
-    q, kv, grad_o = front(which, tokens, out_grad, qkv_w, qkv_b, dense_w, row_of(2), row_of(3), tables)
+    q, kv_most, kv_last, grad_o = front(
+        which, tokens, out_grad, qkv_w, qkv_b, dense_w, row_of(2), row_of(3), tables
+    )
     if seq_size == 2:
-        kv_parts = (kv, swap(kv, "seq"))
+        kv_most, kv_last = (kv_most, swap(kv_most, "seq")), (kv_last, swap(kv_last, "seq"))
     else:
-        kv_parts = (lax.all_gather(kv, "seq", axis=0, tiled=True),)
-
+        kv_most = (lax.all_gather(kv_most, "seq", axis=0, tiled=True),)
+        kv_last = (lax.all_gather(kv_last, "seq", axis=0, tiled=True),)
+    pairs = q.shape[1] // LANES
     mlp_part, mlp_dx, act, mlp_grad = feed(which, tokens, out_grad, up_w, up_b, down_w, row_of(4), row_of(5))
     info = jnp.concatenate([runs, which[1:]])
     quarter = rows // 4
 
-    o_early, stat_early, send, keep_early = attend(info, slots, q, grad_o, kv_parts, dense_w, mlp_part, 0)
+    def forward(kv_parts, prior, run, base, after):
+        return attend(info, slots, q, grad_o, kv_parts, dense_w, prior, run, base, after)
+
+    o_most_early, stat_most_early, summed_early = forward(kv_most, mlp_part, 0, 0, ())
+    o_most_late, stat_most_late, summed_late = forward(kv_most, mlp_part, 1, 0, (o_most_early,))
+    o_last_early, stat_last_early, send, keep_early = forward(kv_last, summed_early, 0, pairs - 1, (o_most_late,))
     got_early = swap(send, "ml")
-    o_late, stat_late, send, keep_late = attend(
-        info, slots, q, grad_o, kv_parts, dense_w, mlp_part, 1, (o_early,)
-    )
+    o_last_late, stat_last_late, send, keep_late = forward(kv_last, summed_late, 1, pairs - 1, (o_last_early,))
     got_late = swap(send, "ml")
-    stats = jnp.concatenate([stat_early, stat_late], axis=1)
-    mixed_early = finish(which, tokens, keep_early, got_early, row_of(0), row_of(1), 0, (o_late,))
+    stats = jnp.concatenate(
+        [
+            jnp.concatenate([stat_most_early, stat_last_early], axis=0),
+            jnp.concatenate([stat_most_late, stat_last_late], axis=0),
+        ],
+        axis=1,
+    )
+    attended = jnp.concatenate(
+        [
+            jnp.concatenate([o_most_early, o_last_early], axis=1),
+            jnp.concatenate([o_most_late, o_last_late], axis=1),
+        ],
+        axis=0,
+    )
+    mixed_early = finish(which, tokens, keep_early, got_early, row_of(0), row_of(1), 0, (o_last_late,))
     after = (mixed_early,)
     mixed_early = lax.all_gather(mixed_early, ("mh", "ml"), axis=0, tiled=True)
 
     home = rows if seq_size == 2 else 0
     dq, dk, dv, got = [], [], [], []
-    for pair in range(q.shape[1] // LANES):
-        outs = attend_back(info, slots, q, grad_o, stats, kv_parts, pair, home, after)
+    for pair in range(pairs):
+        kv_parts, at = (kv_last, 0) if pair == pairs - 1 else (kv_most, pair)
+        outs = attend_back(info, slots, q, grad_o, stats, kv_parts, pair, at, home, after)
         after = (outs[0],)
         dq.append(outs[0])
         if home:
@@ -947,8 +986,8 @@
             dk.append(jnp.zeros((rows, LANES), F32))
             dv.append(jnp.zeros((rows, LANES), F32))
         if pair == 1:
-            mixed_late = finish(which, tokens, keep_late, got_late, row_of(0), row_of(1), 1, after)
-            after = (outs[0], mixed_late, got[0])
+            mixed_late = finish(which, tokens, keep_late, got_late, row_of(0), row_of(1), 1, (outs[0], got[0]))
+            after = (outs[0], mixed_late)
             mixed_late = lax.all_gather(mixed_late, ("mh", "ml"), axis=0, tiled=True)
         elif pair > 1:
             after = (outs[0], got[pair - 1])
@@ -961,7 +1000,6 @@
     )
     mixed = lay_gathered(mixed_early, mixed_late, (dproj,))
     got = [swap(send[run * quarter : (run + 1) * quarter], "ml") for run in range(2)]
-    attended = jnp.concatenate([o_early, o_late], axis=0)
     grad_qkv, grad_dense, qkv_vectors, grad_qkv_b = weight_grads(
         which, tokens, out_grad, dproj, attended, qkv_w, column_of(2), column_of(3), (mixed_late,)
     )

time: 619 us -> 598 us (0.966)
  waiting for transfers between devices: 184 us -> 156 us
  Pallas kernels: 313 us -> 322 us
    ppermute x14 -> x15, waiting for transfers between devices: 111 us -> 63.4 us  [swap(): return lax.ppermute(values, axis, [(0, 1), (1, 0)])]
    reduce_scatter x1, waiting for transfers between devices: 11.9 us -> 31.9 us  [scatter(): lax.psum_scatter(grads, ('dp', 'seq'), scatter_dimension=0, tiled=True)]
    pallas_call x2 -> x4, Pallas kernels: 69.3 us -> 80.5 us  [attend(): pl.pallas_call(kernel, grid_spec=pltpu.PrefetchScalarGridSpec(num_scalar_...]
    unnamed x70 -> x77, local copies, waits for them, and re-layouts: 18.2 us -> 17.8 us
    ppermute x14 -> x15, starting transfers between devices: 19.2 us -> 19.6 us  [swap(): return lax.ppermute(values, axis, [(0, 1), (1, 0)])]
  transfers between devices with their start and end apart: 28 -> 29, of which waited for: 13 -> 11; matrix products, arithmetic and copies ran while one was open for 8% -> 8% of each run, Pallas kernels for 46% -> 52%
where the time goes in v6:
time: 598 us; the launch traced here: 588 us
  Pallas kernels  322 us (54%)
  waiting for transfers between devices  156 us (26%)
  local copies, waits for them, and re-layouts  48.9 us (8%)
  starting transfers between devices  31.6 us (5%)
  between operations  15 us (3%)
  other arithmetic  14.7 us (2%)
    pallas_call x3, Pallas kernels, attend_back(): pl.pallas_call(kernel, grid_spec=pltpu.PrefetchScalarGridSpec(num_scalar_...  101 us
    pallas_call x4, Pallas kernels, attend(): pl.pallas_call(kernel, grid_spec=pltpu.PrefetchScalarGridSpec(num_scalar_...  80.5 us
    ppermute x15, waiting for transfers between devices, swap(): return lax.ppermute(values, axis, [(0, 1), (1, 0)])  63.4 us
    ppermute x6, waiting for transfers between devices, round_mp(): lax.ppermute(mine, axes, [(i, (i + k) % 4) for i in range(4)])  56.4 us
    reduce_scatter x1, waiting for transfers between devices, scatter(): lax.psum_scatter(grads, ('dp', 'seq'), scatter_dimension=0, tiled=True)  31.9 us
    pallas_call x1, Pallas kernels, feed(): pl.pallas_call(feed_kernel, grid_spec=pltpu.PrefetchScalarGridSpec(num_sc...  28.9 us
    pallas_call x1, Pallas kernels, feed_grads(): pl.pallas_call(feed_grads_kernel, grid_spec=pltpu.PrefetchScalarGridSpec(...  21.8 us
    ppermute x15, starting transfers between devices, swap(): return lax.ppermute(values, axis, [(0, 1), (1, 0)])  19.6 us
  transfers between devices with their start and end apart: 29, of which 11 were waited for; matrix products, arithmetic and copies ran while one was open for 8% of the time, Pallas kernels for 52%

profile of v6, /device:TPU:0, one launch (start us, length us, event | category | flops | bytes accessed | tf_op | source)
XLA Modules:
  0.0 588.3 jit_solution(13707782252829780444)
XLA Ops:
  21.6 8.6 %collective-permute-done = bf16[96,384]{1,0:T(8,128)(2,1)S(1)} collective-permute-done((bf16[96,384]{1,0:T(8,128)(2,1)S(1)}, bf16[96,384]{1,0:T(8,128)(2,1)S(1)}, u32[]{:S(2)}, u32[]{:S(2)}) %collective-permute-start) | collective-permute-done | bytes 73760 | tf_op jit(solution)/shard_map/ppermute | solution.py:822
  52.9 7.2 %place.1 = (bf16[768,1152]{1,0:T(8,128)(2,1)}, bf16[768,384]{1,0:T(8,128)(2,1)}, f32[768,256]{1,0:T(8,128)}) custom-call(s32[2]{0:T(128)} %pad_add_fusion.2.where, bf16[8,2,96,384]{3,2,1,0:T(8,128)(2,1)} %bitcast.107, bf16[8,2,96,512]{3,2,1,0:T(8,128)(2,1)} %bitcast.100), custom_call_target="tpu_custom_call" | custom-call | flops 1 | bytes 1 | tf_op jit(solution)/shard_map/place/pallas_call | solution.py:112
  64.4 12.3 %front.1 = (bf16[2048,384]{1,0:T(8,128)(2,1)}, bf16[2048,512]{1,0:T(8,128)(2,1)}, bf16[2048,256]{1,0:T(8,128)(2,1)}, bf16[2048,384]{1,0:T(8,128)(2,1)}) custom-call(s32[2]{0:T(128)} %pad_add_fusion.which, bf16[2,2048,768]{2,1,0:T(8,128)(2,1)} %x_ref.15, bf16[2,2048,768]{2,1,0:T(8,128)(2,1)} %dy_ref.11, bf16[768,1152]{1,0:T(8,128)(2,1)} %get-tuple-element.66.w_ref.refs_9_, ...), custom_call_target="tpu_custom_call" | custom-call | flops 1 | bytes 1 | tf_op jit(solution)/shard_map/front/pallas_call | solution.py:157
  86.0 5.0 place_second.1
  91.0 28.9 %feed.1 = (bf16[2048,768]{1,0:T(8,128)(2,1)}, bf16[2048,768]{1,0:T(8,128)(2,1)}, bf16[2048,1536]{1,0:T(8,128)(2,1)}, bf16[2048,1536]{1,0:T(8,128)(2,1)}) custom-call(s32[2]{0:T(128)} %pad_add_fusion.which, bf16[2,2048,768]{2,1,0:T(8,128)(2,1)} %x_ref.15, bf16[2,2048,768]{2,1,0:T(8,128)(2,1)} %dy_ref.11, bf16[768,1536]{1,0:T(8,128)(2,1)} %get-tuple-element.72.up_ref, ...), custom_call_target="tpu_custom_call" | custom-call | flops 1 | bytes 1 | tf_op jit(solution)/shard_map/feed/pallas_call | solution.py:200
  119.9 5.5 collective-permute-done.8.refs_1_.refs_3_
  126.7 21.5 %attend.4 = (bf16[1024,256]{1,0:T(8,128)(2,1)}, f32[16,1024]{1,0:T(8,128)}, f32[1024,768]{1,0:T(8,128)}) custom-call(s32[3]{0:T(128)} %pad_add_fusion.1.info, s32[4]{0:T(128)} %select_reduce_fusion.slots, bf16[2048,384]{1,0:T(8,128)(2,1)} %get-tuple-element.70.q_ref, bf16[2048,384]{1,0:T(8,128)(2,1)} %get-tuple-element.71.g_ref, ...), custom_call_target="tpu_custom_call" | custom-call | flops 1 | bytes 1 | tf_op jit(solution)/shard_map/attend/pallas_call | solution.py:409
  148.2 28.6 %attend.5 = (bf16[1024,256]{1,0:T(8,128)(2,1)}, f32[16,1024]{1,0:T(8,128)}, f32[1024,768]{1,0:T(8,128)}) custom-call(s32[3]{0:T(128)} %pad_add_fusion.1.info, s32[4]{0:T(128)} %select_reduce_fusion.slots, bf16[2048,384]{1,0:T(8,128)(2,1)} %get-tuple-element.70.q_ref, bf16[2048,384]{1,0:T(8,128)(2,1)} %get-tuple-element.71.g_ref, ...), custom_call_target="tpu_custom_call" | custom-call | flops 1 | bytes 1 | tf_op jit(solution)/shard_map/attend/pallas_call | solution.py:409
  177.8 13.6 %attend.6 = (bf16[1024,128]{1,0:T(8,128)(2,1)}, f32[8,1024]{1,0:T(8,128)}, bf16[512,768]{1,0:T(8,128)(2,1)}, f32[512,768]{1,0:T(8,128)}) custom-call(s32[3]{0:T(128)} %pad_add_fusion.1.info, s32[4]{0:T(128)} %select_reduce_fusion.slots, bf16[2048,384]{1,0:T(8,128)(2,1)} %get-tuple-element.70.q_ref, bf16[2048,384]{1,0:T(8,128)(2,1)} %get-tuple-element.71.g_ref, ...), custom_call_target="tpu_custom_call" | custom-call | flops 1 | bytes 1 | tf_op jit(solution)/shard_map/attend/pallas_call | solution.py:409
  194.9 16.9 %attend.7 = (bf16[1024,128]{1,0:T(8,128)(2,1)}, f32[8,1024]{1,0:T(8,128)}, bf16[512,768]{1,0:T(8,128)(2,1)}, f32[512,768]{1,0:T(8,128)}) custom-call(s32[3]{0:T(128)} %pad_add_fusion.1.info, s32[4]{0:T(128)} %select_reduce_fusion.slots, bf16[2048,384]{1,0:T(8,128)(2,1)} %get-tuple-element.70.q_ref, bf16[2048,384]{1,0:T(8,128)(2,1)} %get-tuple-element.71.g_ref, ...), custom_call_target="tpu_custom_call" | custom-call | flops 1 | bytes 1 | tf_op jit(solution)/shard_map/attend/pallas_call | solution.py:409
  217.1 33.6 %attend_back.3 = (bf16[2048,128]{1,0:T(8,128)(2,1)}, f32[2048,128]{1,0:T(8,128)}, f32[2048,128]{1,0:T(8,128)}, bf16[2048,256]{1,0:T(8,128)(2,1)}) custom-call(s32[3]{0:T(128)} %pad_add_fusion.1.info, s32[4]{0:T(128)} %select_reduce_fusion.slots, bf16[2048,384]{1,0:T(8,128)(2,1)} %get-tuple-element.70.q_ref, bf16[2048,384]{1,0:T(8,128)(2,1)} %get-tuple-element.71.g_ref, ...), custom_call_target="tpu_custom_call" | custom-call | flops 8589934592 | bytes 16777216 | tf_op jit(solution)/shard_map/attend_back/pallas_call | solution.py:541
  252.1 33.9 %attend_back.4 = (bf16[2048,128]{1,0:T(8,128)(2,1)}, f32[2048,128]{1,0:T(8,128)}, f32[2048,128]{1,0:T(8,128)}, bf16[2048,256]{1,0:T(8,128)(2,1)}) custom-call(s32[3]{0:T(128)} %pad_add_fusion.1.info, s32[4]{0:T(128)} %select_reduce_fusion.slots, bf16[2048,384]{1,0:T(8,128)(2,1)} %get-tuple-element.70.q_ref, bf16[2048,384]{1,0:T(8,128)(2,1)} %get-tuple-element.71.g_ref, ...), custom_call_target="tpu_custom_call" | custom-call | flops 8589934592 | bytes 16777216 | tf_op jit(solution)/shard_map/attend_back/pallas_call | solution.py:541
  286.1 10.8 %collective-permute-done.11.got_ref = bf16[512,768]{1,0:T(8,128)(2,1)S(1)} collective-permute-done((bf16[512,768]{1,0:T(8,128)(2,1)S(1)}, bf16[512,768]{1,0:T(8,128)(2,1)S(1)}, u32[]{:S(2)}, u32[]{:S(2)}) %collective-permute-start.11) | collective-permute-done | bytes 786464 | tf_op jit(solution)/shard_map/ppermute | solution.py:822
  307.3 33.7 %attend_back.5 = (bf16[2048,128]{1,0:T(8,128)(2,1)}, f32[2048,128]{1,0:T(8,128)}, f32[2048,128]{1,0:T(8,128)}, bf16[2048,256]{1,0:T(8,128)(2,1)}) custom-call(s32[3]{0:T(128)} %pad_add_fusion.1.info, s32[4]{0:T(128)} %select_reduce_fusion.slots, bf16[2048,384]{1,0:T(8,128)(2,1)} %get-tuple-element.70.q_ref, bf16[2048,384]{1,0:T(8,128)(2,1)} %get-tuple-element.71.g_ref, ...), custom_call_target="tpu_custom_call" | custom-call | flops 8589934592 | bytes 16777216 | tf_op jit(solution)/shard_map/attend_back/pallas_call | solution.py:541
  344.9 21.8 %feed_grads.1 = (bf16[768,3072]{1,0:T(8,128)(2,1)}, f32[768,128]{1,0:T(8,128)}, f32[1,1536]{1,0:T(1,128)}) custom-call(s32[2]{0:T(128)} %pad_add_fusion.which, bf16[2,2048,768]{2,1,0:T(8,128)(2,1)} %x_ref.15, bf16[2,2048,768]{2,1,0:T(8,128)(2,1)} %dy_ref.11, bf16[2048,1536]{1,0:T(8,128)(2,1)} %get-tuple-element.104.act_ref, ...), custom_call_target="tpu_custom_call" | custom-call | flops 8589934592 | bytes 16777216 | tf_op jit(solution)/shard_map/feed_grads/pallas_call | solution.py:265
  367.8 14.6 %back.1 = (bf16[2048,1152]{1,0:T(8,128)(2,1)}, bf16[1024,768]{1,0:T(8,128)(2,1)}, f32[1024,768]{1,0:T(8,128)}) custom-call(s32[2]{0:T(128)} %pad_add_fusion.which, bf16[2048,384]{1,0:T(8,128)(2,1)} %pad_maximum_fusion.dq_ref, f32[2048,128]{1,0:T(8,128)} %get-tuple-element.95.refs_0_, f32[2048,128]{1,0:T(8,128)} %get-tuple-element.96.refs_1_, ...), custom_call_target="tpu_custom_call" | custom-call | flops 1 | bytes 1 | tf_op jit(solution)/shard_map/back/pallas_call | solution.py:599
  386.1 15.3 %weight_grads.1 = (bf16[768,1152]{1,0:T(8,128)(2,1)}, bf16[768,384]{1,0:T(8,128)(2,1)}, f32[768,128]{1,0:T(8,128)}, f32[1,1152]{1,0:T(1,128)}) custom-call(s32[2]{0:T(128)} %pad_add_fusion.which, bf16[2,2048,768]{2,1,0:T(8,128)(2,1)} %x_ref.15, bf16[2,2048,768]{2,1,0:T(8,128)(2,1)} %dy_ref.11, bf16[2048,1152]{1,0:T(8,128)(2,1)} %get-tuple-element.107.refs_0_.dproj_ref, ...), custom_call_target="tpu_custom_call" | custom-call | flops 8589934592 | bytes 16777216 | tf_op jit(solution)/shard_map/weight_grads/pallas_call | solution.py:656
  404.6 6.5 %join.1 = bf16[768,4736]{1,0:T(8,128)(2,1)} custom-call(bf16[768,1152]{1,0:T(8,128)(2,1)} %get-tuple-element.111.refs_0_, bf16[768,384]{1,0:T(8,128)(2,1)} %get-tuple-element.112.refs_1_, bf16[768,128]{1,0:T(8,128)(2,1)} %copy.151.refs_2_, bf16[768,3072]{1,0:T(8,128)(2,1)} %get-tuple-element.115.refs_3_), custom_call_target="tpu_custom_call" | custom-call | flops 1 | bytes 1 | tf_op jit(solution)/shard_map/join/pallas_call | solution.py:692
  420.3 16.9 %collective-permute-done.15.got_ref = bf16[512,768]{1,0:T(8,128)(2,1)S(1)} collective-permute-done((bf16[512,768]{1,0:T(8,128)(2,1)S(1)}, bf16[512,768]{1,0:T(8,128)(2,1)S(1)}, u32[]{:S(2)}, u32[]{:S(2)}) %collective-permute-start.15) | collective-permute-done | bytes 786464 | tf_op jit(solution)/shard_map/ppermute | solution.py:822
  446.1 31.9 %reduce-scatter.2.cloned.1.call-done = bf16[96,4736]{1,0:T(8,128)(2,1)} async-done(((bf16[768,4736]{1,0:T(8,128)(2,1)}), bf16[96,4736]{1,0:T(8,128)(2,1)}) %reduce-scatter.2.cloned.1.call-update) | async-done | bytes 909328 | tf_op jit(solution)/shard_map/reduce_scatter | solution.py:1011
  485.2 6.8 %lay_gathered.1 = bf16[2,2048,768]{2,1,0:T(8,128)(2,1)} custom-call(bf16[2048,768]{1,0:T(8,128)(2,1)} %all-gather.6.cloned.1.call-done.refs_2_.early_ref, bf16[2048,768]{1,0:T(8,128)(2,1)} %all-gather.8.cloned.1.call-done.late_ref.refs_0_, bf16[2048,1152]{1,0:T(8,128)(2,1)} %get-tuple-element.107.refs_0_.dproj_ref), custom_call_target="tpu_custom_call" | custom-call | flops 1 | bytes 1 | tf_op jit(solution)/shard_map/lay_gathered/pallas_call | solution.py:781
  492.0 56.4 %collective-permute-done.17.refs_2_ = bf16[512,768]{1,0:T(8,128)(2,1)} collective-permute-done((bf16[512,768]{1,0:T(8,128)(2,1)}, bf16[512,768]{1,0:T(8,128)(2,1)}, u32[]{:S(2)}, u32[]{:S(2)}) %collective-permute-start.17) | collective-permute-done | bytes 786464 | tf_op jit(solution)/shard_map/ppermute | solution.py:840
  548.4 6.9 %lay_round.1 = bf16[2,2048,768]{2,1,0:T(8,128)(2,1)} custom-call(s32[1]{0:T(128)} %bitcast.31.index, bf16[512,768]{1,0:T(8,128)(2,1)} %norm_back.2.refs_0_, bf16[512,768]{1,0:T(8,128)(2,1)} %collective-permute-done.16.refs_1_, bf16[512,768]{1,0:T(8,128)(2,1)} %collective-permute-done.17.refs_2_, bf16[512,768]{1,0:T(8,128)(2,1)} %collective-permute-done.18.refs_3_, ...), custom_call_target="tpu_custom_call" | custom-call | flops 1 | bytes 1 | tf_op jit(solution)/shard_map/lay_round/pallas_call | solution.py:806
  555.8 18.3 %collective-permute-done.23 = bf16[96,2368]{1,0:T(8,128)(2,1)} collective-permute-done((bf16[96,2368]{1,0:T(8,128)(2,1)}, bf16[96,2368]{1,0:T(8,128)(2,1)}, u32[]{:S(2)}, u32[]{:S(2)}) %collective-permute-start.23) | collective-permute-done | bytes 454688 | tf_op jit(solution)/shard_map/ppermute | solution.py:822
  (249 shorter events, 117.8 us)
Async XLA Ops:
  7.2 78.8 %all-gather.4.cloned.1.call-start = ((), (), s32[]{:S(2)}) async-start(), calls=%async_computation.1 | async-start | bytes 5013504 | tf_op jit(solution)/shard_map/all_gather | solution.py:895
  9.0 335.0 %all-gather.6.cloned.1.call-start = ((), (), s32[]{:S(2)}) async-start(), calls=%async_computation.2 | async-start | bytes 3932160 | tf_op jit(solution)/shard_map/all_gather | solution.py:970
  14.8 17.2 %collective-permute-start.4 = (bf16[96,512]{1,0:T(8,128)(2,1)S(1)}, bf16[96,512]{1,0:T(8,128)(2,1)S(1)}, u32[]{:S(2)}, u32[]{:S(2)}) collective-permute-start(bf16[96,512]{1,0:T(8,128)(2,1)S(1)} %get-tuple-element.187), channel_id=1, source_target_pairs={{0,2},{2,0},{1,3},{3,1},{4,6},{6,4},{5,7},{7,5},{8,10},{10,8},{9,1... | collective-permute-start | bytes 294920 | tf_op jit(solution)/shard_map/ppermute | solution.py:822
  20.0 10.2 %collective-permute-start = (bf16[96,384]{1,0:T(8,128)(2,1)S(1)}, bf16[96,384]{1,0:T(8,128)(2,1)S(1)}, u32[]{:S(2)}, u32[]{:S(2)}) collective-permute-start(bf16[96,384]{1,0:T(8,128)(2,1)S(1)} %reshape.124), channel_id=1, source_target_pairs={{0,2},{2,0},{1,3},{3,1},{4,6},{6,4},{5,7},{7,5},{8,10},{10,8},{9,1... | collective-permute-start | bytes 221192 | tf_op jit(solution)/shard_map/ppermute | solution.py:822
  32.1 8.4 %collective-permute-start.5 = (bf16[2,96,512]{2,1,0:T(8,128)(2,1)S(1)}, bf16[2,96,512]{2,1,0:T(8,128)(2,1)S(1)}, u32[]{:S(2)}, u32[]{:S(2)}) collective-permute-start(bf16[2,96,512]{2,1,0:T(8,128)(2,1)S(1)} %pad_maximum_fusion.6), channel_id=1, source_target_pairs={{0,16},{8,24},{16,0},{24,8},{1,17},{9,25},{17,1},{25,9},{2,18},{10... | collective-permute-start | bytes 589832 | tf_op jit(solution)/shard_map/ppermute | solution.py:826
  36.2 10.9 %collective-permute-start.2 = (bf16[4,96,384]{2,1,0:T(8,128)(2,1)}, bf16[4,96,384]{2,1,0:T(8,128)(2,1)S(1)}, u32[]{:S(2)}, u32[]{:S(2)}) collective-permute-start(bf16[4,96,384]{2,1,0:T(8,128)(2,1)} %pad_maximum_fusion.4), channel_id=1, source_target_pairs={{0,16},{8,24},{16,0},{24,8},{1,17},{9,25},{17,1},{25,9},{2,18},{10... | collective-permute-start | bytes 884744 | tf_op jit(solution)/shard_map/ppermute | solution.py:826
  76.7 48.8 %collective-permute-start.8 = (bf16[2048,512]{1,0:T(8,128)(2,1)}, bf16[2048,512]{1,0:T(8,128)(2,1)S(1)}, u32[]{:S(2)}, u32[]{:S(2)}) collective-permute-start(bf16[2048,512]{1,0:T(8,128)(2,1)} %get-tuple-element.75.refs_0_.refs_2_), channel_id=1, source_target_pairs={{0,4},{4,0},{1,5},{5,1},{2,6},{6,2},{3,7},{7,3},{8,12},{12,8},{9,1... | collective-permute-start | bytes 6291464 | tf_op jit(solution)/shard_map/ppermute | solution.py:822
  77.4 99.4 %collective-permute-start.9 = (bf16[2048,256]{1,0:T(8,128)(2,1)}, bf16[2048,256]{1,0:T(8,128)(2,1)S(1)}, u32[]{:S(2)}, u32[]{:S(2)}) collective-permute-start(bf16[2048,256]{1,0:T(8,128)(2,1)} %get-tuple-element.77.refs_0_.refs_2_), channel_id=1, source_target_pairs={{0,4},{4,0},{1,5},{5,1},{2,6},{6,2},{3,7},{7,3},{8,12},{12,8},{9,1... | collective-permute-start | bytes 3145736 | tf_op jit(solution)/shard_map/ppermute | solution.py:822
  191.5 20.3 %collective-permute-start.10 = (bf16[512,768]{1,0:T(8,128)(2,1)}, bf16[512,768]{1,0:T(8,128)(2,1)S(1)}, u32[]{:S(2)}, u32[]{:S(2)}) collective-permute-start(bf16[512,768]{1,0:T(8,128)(2,1)} %get-tuple-element.81), channel_id=1, source_target_pairs={{0,1},{1,0},{2,3},{3,2},{4,5},{5,4},{6,7},{7,6},{8,9},{9,8},{10,11... | collective-permute-start | bytes 2359304 | tf_op jit(solution)/shard_map/ppermute | solution.py:822
  216.3 169.9 %all-gather.8.cloned.1.call-start = ((), (), s32[]{:S(2)}) async-start(), calls=%async_computation.3 | async-start | bytes 3932160 | tf_op jit(solution)/shard_map/all_gather | solution.py:991
  250.7 46.2 %collective-permute-start.12 = (bf16[2048,256]{1,0:T(8,128)(2,1)}, bf16[2048,256]{1,0:T(8,128)(2,1)S(1)}, u32[]{:S(2)}, u32[]{:S(2)}) collective-permute-start(bf16[2048,256]{1,0:T(8,128)(2,1)} %get-tuple-element.93), channel_id=1, source_target_pairs={{0,4},{4,0},{1,5},{5,1},{2,6},{6,2},{3,7},{7,3},{8,12},{12,8},{9,1... | collective-permute-start | bytes 3145736 | tf_op jit(solution)/shard_map/ppermute | solution.py:822
  250.7 46.2 %collective-permute-start.11 = (bf16[512,768]{1,0:T(8,128)(2,1)S(1)}, bf16[512,768]{1,0:T(8,128)(2,1)S(1)}, u32[]{:S(2)}, u32[]{:S(2)}) collective-permute-start(bf16[512,768]{1,0:T(8,128)(2,1)S(1)} %copy-done.30), channel_id=1, source_target_pairs={{0,1},{1,0},{2,3},{3,2},{4,5},{5,4},{6,7},{7,6},{8,9},{9,8},{10,11... | collective-permute-start | bytes 2359304 | tf_op jit(solution)/shard_map/ppermute | solution.py:822
  301.8 176.2 %reduce-scatter.2.cloned.1.call-start = ((), (), s32[]{:S(2)}) async-start(), calls=%async_computation.4 | async-start | bytes 8183808 | tf_op jit(solution)/shard_map/reduce_scatter | solution.py:1011
  305.9 38.1 %collective-permute-start.13 = (bf16[2048,256]{1,0:T(8,128)(2,1)}, bf16[2048,256]{1,0:T(8,128)(2,1)S(1)}, u32[]{:S(2)}, u32[]{:S(2)}) collective-permute-start(bf16[2048,256]{1,0:T(8,128)(2,1)} %get-tuple-element.101), channel_id=1, source_target_pairs={{0,4},{4,0},{1,5},{5,1},{2,6},{6,2},{3,7},{7,3},{8,12},{12,8},{9,1... | collective-permute-start | bytes 3145736 | tf_op jit(solution)/shard_map/ppermute | solution.py:822
  341.0 25.7 %collective-permute-start.14 = (bf16[2048,256]{1,0:T(8,128)(2,1)}, bf16[2048,256]{1,0:T(8,128)(2,1)S(1)}, u32[]{:S(2)}, u32[]{:S(2)}) collective-permute-start(bf16[2048,256]{1,0:T(8,128)(2,1)} %get-tuple-element.102), channel_id=1, source_target_pairs={{0,4},{4,0},{1,5},{5,1},{2,6},{6,2},{3,7},{7,3},{8,12},{12,8},{9,1... | collective-permute-start | bytes 3145736 | tf_op jit(solution)/shard_map/ppermute | solution.py:822
  384.0 27.0 %collective-permute-start.19 = (bf16[512,768]{1,0:T(8,128)(2,1)S(1)}, bf16[512,768]{1,0:T(8,128)(2,1)S(1)}, u32[]{:S(2)}, u32[]{:S(2)}) collective-permute-start(bf16[512,768]{1,0:T(8,128)(2,1)S(1)} %get-tuple-element.190), channel_id=1, source_target_pairs={{0,1},{1,0},{2,3},{3,2},{4,5},{5,4},{6,7},{7,6},{8,9},{9,8},{10,11... | collective-permute-start | bytes 2359304 | tf_op jit(solution)/shard_map/ppermute | solution.py:822
  384.1 53.1 %collective-permute-start.15 = (bf16[512,768]{1,0:T(8,128)(2,1)S(1)}, bf16[512,768]{1,0:T(8,128)(2,1)S(1)}, u32[]{:S(2)}, u32[]{:S(2)}) collective-permute-start(bf16[512,768]{1,0:T(8,128)(2,1)S(1)} %get-tuple-element.191), channel_id=1, source_target_pairs={{0,1},{1,0},{2,3},{3,2},{4,5},{5,4},{6,7},{7,6},{8,9},{9,8},{10,11... | collective-permute-start | bytes 2359304 | tf_op jit(solution)/shard_map/ppermute | solution.py:822
  416.3 26.0 %collective-permute-start.20 = (bf16[512,768]{1,0:T(8,128)(2,1)}, bf16[512,768]{1,0:T(8,128)(2,1)}, u32[]{:S(2)}, u32[]{:S(2)}) collective-permute-start(bf16[512,768]{1,0:T(8,128)(2,1)} %norm_back.3.refs_4_), channel_id=1, source_target_pairs={{0,1},{1,2},{2,3},{3,0},{4,5},{5,6},{6,7},{7,4},{8,9},{9,10},{10,1... | collective-permute-start | bytes 2359304 | tf_op jit(solution)/shard_map/ppermute | solution.py:840
  416.4 66.5 %collective-permute-start.21 = (bf16[512,768]{1,0:T(8,128)(2,1)}, bf16[512,768]{1,0:T(8,128)(2,1)}, u32[]{:S(2)}, u32[]{:S(2)}) collective-permute-start(bf16[512,768]{1,0:T(8,128)(2,1)} %norm_back.3.refs_4_), channel_id=1, source_target_pairs={{0,2},{1,3},{2,0},{3,1},{4,6},{5,7},{6,4},{7,5},{8,10},{9,11},{10,... | collective-permute-start | bytes 2359304 | tf_op jit(solution)/shard_map/ppermute | solution.py:840
  419.3 72.7 %collective-permute-start.22 = (bf16[512,768]{1,0:T(8,128)(2,1)}, bf16[512,768]{1,0:T(8,128)(2,1)}, u32[]{:S(2)}, u32[]{:S(2)}) collective-permute-start(bf16[512,768]{1,0:T(8,128)(2,1)} %norm_back.3.refs_4_), channel_id=1, source_target_pairs={{0,3},{1,0},{2,1},{3,2},{4,7},{5,4},{6,5},{7,6},{8,11},{9,8},{10,9... | collective-permute-start | bytes 2359304 | tf_op jit(solution)/shard_map/ppermute | solution.py:840
  442.2 49.8 %collective-permute-start.16 = (bf16[512,768]{1,0:T(8,128)(2,1)}, bf16[512,768]{1,0:T(8,128)(2,1)}, u32[]{:S(2)}, u32[]{:S(2)}) collective-permute-start(bf16[512,768]{1,0:T(8,128)(2,1)} %norm_back.2.refs_0_), channel_id=1, source_target_pairs={{0,1},{1,2},{2,3},{3,0},{4,5},{5,6},{6,7},{7,4},{8,9},{9,10},{10,1... | collective-permute-start | bytes 2359304 | tf_op jit(solution)/shard_map/ppermute | solution.py:840
  442.2 106.2 %collective-permute-start.17 = (bf16[512,768]{1,0:T(8,128)(2,1)}, bf16[512,768]{1,0:T(8,128)(2,1)}, u32[]{:S(2)}, u32[]{:S(2)}) collective-permute-start(bf16[512,768]{1,0:T(8,128)(2,1)} %norm_back.2.refs_0_), channel_id=1, source_target_pairs={{0,2},{1,3},{2,0},{3,1},{4,6},{5,7},{6,4},{7,5},{8,10},{9,11},{10,... | collective-permute-start | bytes 2359304 | tf_op jit(solution)/shard_map/ppermute | solution.py:840
  442.3 106.2 %collective-permute-start.18 = (bf16[512,768]{1,0:T(8,128)(2,1)}, bf16[512,768]{1,0:T(8,128)(2,1)}, u32[]{:S(2)}, u32[]{:S(2)}) collective-permute-start(bf16[512,768]{1,0:T(8,128)(2,1)} %norm_back.2.refs_0_), channel_id=1, source_target_pairs={{0,3},{1,0},{2,1},{3,2},{4,7},{5,4},{6,5},{7,6},{8,11},{9,8},{10,9... | collective-permute-start | bytes 2359304 | tf_op jit(solution)/shard_map/ppermute | solution.py:840
  482.8 91.2 %collective-permute-start.23 = (bf16[96,2368]{1,0:T(8,128)(2,1)}, bf16[96,2368]{1,0:T(8,128)(2,1)}, u32[]{:S(2)}, u32[]{:S(2)}) collective-permute-start(bf16[96,2368]{1,0:T(8,128)(2,1)} %fusion), channel_id=1, source_target_pairs={{0,2},{2,0},{1,3},{3,1},{4,6},{6,4},{5,7},{7,5},{8,10},{10,8},{9,1... | collective-permute-start | bytes 1363976 | tf_op jit(solution)/shard_map/ppermute | solution.py:822
  (40 other events, 235.2 us)
Sparse Core Ops, SparseCore 0:
  10.9 63.2 all-gather.3
  216.4 78.6 all-gather.5
  301.8 63.4 all-gather.7
  411.2 66.7 reduce-scatter.1

commit v7 on v6

--- a/solution.py
+++ b/solution.py
@@ -61,16 +61,21 @@
 
 def place_first_kernel(where, one_ref, two_ref, qkv_ref, dense_ref, small_ref):
     cols = one_ref.shape[-1] // 2
+    share = one_ref.shape[2]
     near = where[0] == 0
-    one = [one_ref[0, j] for j in range(2)]
-    two = [two_ref[0, j] for j in range(2)]
-    one = (jnp.where(near, one[0], one[1]), jnp.where(near, one[1], one[0]))
-    two = (jnp.where(near, two[0], two[1]), jnp.where(near, two[1], two[0]))
-    pieces = [one[j][:, i * cols : (i + 1) * cols] for i in range(2) for j in range(2)]
-    pieces += [two[j][:, :cols] for j in range(2)]
-    qkv_ref[...] = jnp.concatenate(pieces, axis=1)
-    dense_ref[...] = jnp.concatenate([two[j][:, cols : 2 * cols] for j in range(2)], axis=1)
-    small_ref[...] = jnp.concatenate([two[j][:, 2 * cols :] for j in range(2)], axis=1).astype(F32)
+    for i in range(4):
+        bits = (pl.program_id(0) * 4 + i) ^ where[1]
+        upper, lower, across = bits // 4, (bits // 2) % 2, bits % 2
+        one = [one_ref[lower * 4 + upper * 2 + across, j] for j in range(2)]
+        two = [two_ref[lower * 4 + across * 2 + upper, j] for j in range(2)]
+        one = (jnp.where(near, one[0], one[1]), jnp.where(near, one[1], one[0]))
+        two = (jnp.where(near, two[0], two[1]), jnp.where(near, two[1], two[0]))
+        pieces = [one[j][:, at * cols : (at + 1) * cols] for at in range(2) for j in range(2)]
+        pieces += [two[j][:, :cols] for j in range(2)]
+        rows = slice(i * share, (i + 1) * share)
+        qkv_ref[rows, :] = jnp.concatenate(pieces, axis=1)
+        dense_ref[rows, :] = jnp.concatenate([two[j][:, cols : 2 * cols] for j in range(2)], axis=1)
+        small_ref[rows, :] = jnp.concatenate([two[j][:, 2 * cols :] for j in range(2)], axis=1).astype(F32)
 
 
 def place_second_kernel(pack_ref, up_ref, down_ref):
@@ -97,30 +102,20 @@
     )(pack)
 
 
-def place(kernel, where, one, two, widths, types):
+def place_first(where, one, two, widths, types):
     owners, _, share, _ = one.shape
-
-    def spec(array, low, high):
-        def index(i, where):
-            bits = i ^ where[1]
-            upper, lower, across = bits // 4, (bits // 2) % 2, bits % 2
-            near, far = (across, upper) if low == "seq" else (upper, across)
-            return (lower * 4 + far * 2 + near, 0, 0, 0)
-
-        return pl.BlockSpec((1,) + array.shape[1:], index)
-
-    return pl.pallas_call(
-        kernel,
+    return pl.pallas_call(
+        place_first_kernel,
         grid_spec=pltpu.PrefetchScalarGridSpec(
             num_scalar_prefetch=1,
-            grid=(owners,),
-            in_specs=[spec(one, "seq", "dp"), spec(two, "dp", "seq")],
-            out_specs=[pl.BlockSpec((share, width), lambda i, *_: (i, 0)) for width in widths],
+            grid=(owners // 4,),
+            in_specs=[whole(one.shape), whole(two.shape)],
+            out_specs=[pl.BlockSpec((4 * share, width), lambda i, *_: (i, 0)) for width in widths],
         ),
         out_shape=[jax.ShapeDtypeStruct((owners * share, width), kind) for width, kind in zip(widths, types)],
         compiler_params=params(),
         cost_estimate=brief,
-        name="place",
+        name="place_first",
     )(where, one, two)
 
 
@@ -295,7 +290,29 @@
     return [jnp.where(mine, both, jnp.zeros_like(both)) for mine in heads]
 
 
-def attend_kernel(info, slots, q_ref, g_ref, dense_ref, prior_ref, *refs, block, run_rows, parts, run, ties, split):
+def head_lanes(rows):
+    lane = lax.broadcasted_iota(jnp.int32, (rows, LANES), 1)
+    return lane < HD, lane >= HD
+
+
+def tiles(block, last):
+    half = block // 2
+    if last and block >= 512:
+        return (0, 0, half), (half, half, half)
+    return ((0, 0, block),)
+
+
+def visible(shape):
+    return lax.broadcasted_iota(jnp.int32, shape, 1) <= lax.broadcasted_iota(jnp.int32, shape, 0)
+
+
+def merge(whole_rows, row, part, combine):
+    if row == 0:
+        return combine(whole_rows, part)
+    return jnp.concatenate([whole_rows[:row], combine(whole_rows[row:], part)], axis=0)
+
+
+def attend_kernel(info, slots, q_ref, g_ref, dense_ref, prior_ref, *refs, block, parts, run, ties, split):
     k_parts, v_parts, refs = refs[:parts], refs[parts : 2 * parts], refs[2 * parts + ties :]
     o_ref, stat_ref, refs = refs[0], refs[1], refs[2:]
     if split:
@@ -303,86 +320,77 @@
     else:
         sum_ref, refs = refs[0], refs[1:]
     k_ref, v_ref, score_ref, acc_ref, branch_ref = refs
-    per_run = run_rows // block
-    pair, place_in_run = pl.program_id(0), pl.program_id(1)
+    pair = pl.program_id(0)
     full = info[run]
 
-    @pl.when((pair == 0) & (place_in_run == 0))
+    @pl.when(pair == 0)
     def _():
         branch_ref[...] = prior_ref[...].astype(F32)
 
-    @pl.when(place_in_run == 0)
-    def _():
-        at = 0
-        for j in range(parts):
-            there = pl.ds(at, k_parts[j].shape[0])
-            k_ref[there, :] = k_parts[j][...]
-            v_ref[there, :] = v_parts[j][...]
-            at += k_parts[j].shape[0]
-
+    at = 0
+    for j in range(parts):
+        there = pl.ds(at, k_parts[j].shape[0])
+        k_ref[there, :] = k_parts[j][...]
+        v_ref[there, :] = v_parts[j][...]
+        at += k_parts[j].shape[0]
+
+    heads = head_lanes(block)
+    queries = pick_heads(q_ref[...], heads)
+
+    def rows_of(at, col, count):
+        return pl.ds(pl.multiple_of(slots[at] * block + col, count), count)
+
+    def score(at, tops, last):
+        out = []
+        for h in range(2):
+            top = tops[h]
+            for row, col, count in tiles(block, last):
+                scores = dot(queries[h][row:], k_ref[rows_of(at, col, count), :], NT)
+                if last:
+                    scores = jnp.where(visible(scores.shape), scores, masked_value)
+                score_ref[h, at, row:, col : col + count] = scores
+                top = merge(top, row, lane_fold(scores, jnp.maximum), jnp.maximum)
+            out.append(top)
+        return tuple(out)
+
+    least = jnp.full((block, LANES), masked_value, F32)
+    tops = lax.fori_loop(0, full, lambda at, carry: score(at, carry, False), (least, least))
+    tops = score(full, tops, True)
+    tops = [jnp.max(top, axis=1, keepdims=True) * F32(LOG2E) for top in tops]
+
+    acc_ref[...] = jnp.zeros_like(acc_ref)
+
+    def weigh(at, totals, last):
+        out = []
+        for h in range(2):
+            total = totals[h]
+            for row, col, count in tiles(block, last):
+                values = v_ref[rows_of(at, col, count), :]
+                soft = jnp.exp2(score_ref[h, at, row:, col : col + count] * F32(LOG2E) - tops[h][row:])
+                total = merge(total, row, lane_fold(soft, jnp.add), jnp.add)
+                acc_ref[h, row:, :] += dot(soft.astype(BF16), values, NN)
+            out.append(total)
+        return tuple(out)
+
+    nought = jnp.zeros((block, LANES), F32)
+    totals = lax.fori_loop(0, full, lambda at, carry: weigh(at, carry, False), (nought, nought))
+    totals = weigh(full, totals, True)
+    totals = [jnp.sum(total, axis=1, keepdims=True) for total in totals]
+    attended = jnp.where(heads[0], acc_ref[0] / totals[0], acc_ref[1] / totals[1])
+    o_ref[...] = attended.astype(o_ref.dtype)
+    branch_ref[...] += dot(attended.astype(BF16), dense_ref[...], NT)
+    product = attended * g_ref[...].astype(F32)
+    row_terms = [jnp.sum(jnp.where(mine, product, 0.0), axis=1, keepdims=True) for mine in heads]
+    logs = [tops[h] + jnp.log2(totals[h]) for h in range(2)]
     lane = lax.broadcasted_iota(jnp.int32, (block, LANES), 1)
-    heads = (lane < HD, lane >= HD)
-
-    def rows_of(at, count):
-        return pl.ds(pl.multiple_of(slots[at] * run_rows, run_rows), count)
-
-    def one_block(within):
-        queries = pick_heads(q_ref[...], heads)
-        seen = (within + 1) * block
-
-        def score(at, tops, last):
-            count = seen if last else run_rows
-            keys = k_ref[rows_of(at, count), :]
-            out = []
-            for h in range(2):
-                scores = dot(queries[h], keys, NT)
-                if last:
-                    row = lax.broadcasted_iota(jnp.int32, (block, count), 0)
-                    col = lax.broadcasted_iota(jnp.int32, (block, count), 1)
-                    scores = jnp.where(col <= row + within * block, scores, masked_value)
-                score_ref[h, at, :, :count] = scores
-                out.append(jnp.maximum(tops[h], lane_fold(scores, jnp.maximum)))
-            return tuple(out)
-
-        least = jnp.full((block, LANES), masked_value, F32)
-        tops = lax.fori_loop(0, full, lambda at, carry: score(at, carry, False), (least, least))
-        tops = score(full, tops, True)
-        tops = [jnp.max(top, axis=1, keepdims=True) * F32(LOG2E) for top in tops]
-
-        acc_ref[...] = jnp.zeros_like(acc_ref)
-
-        def weigh(at, totals, last):
-            count = seen if last else run_rows
-            values = v_ref[rows_of(at, count), :]
-            out = []
-            for h in range(2):
-                soft = jnp.exp2(score_ref[h, at, :, :count] * F32(LOG2E) - tops[h])
-                out.append(totals[h] + lane_fold(soft, jnp.add))
-                acc_ref[h] += dot(soft.astype(BF16), values, NN)
-            return tuple(out)
-
-        nought = jnp.zeros((block, LANES), F32)
-        totals = lax.fori_loop(0, full, lambda at, carry: weigh(at, carry, False), (nought, nought))
-        totals = weigh(full, totals, True)
-        totals = [jnp.sum(total, axis=1, keepdims=True) for total in totals]
-        attended = jnp.where(heads[0], acc_ref[0] / totals[0], acc_ref[1] / totals[1])
-        o_ref[...] = attended.astype(o_ref.dtype)
-        mine = pl.ds(within * block, block)
-        branch_ref[mine, :] += dot(attended.astype(BF16), dense_ref[...], NT)
-        product = attended * g_ref[...].astype(F32)
-        row_terms = [jnp.sum(jnp.where(mine, product, 0.0), axis=1, keepdims=True) for mine in heads]
-        logs = [tops[h] + jnp.log2(totals[h]) for h in range(2)]
-        stats = jnp.where(lane == 0, logs[0], jnp.where(lane == 1, logs[1], 0.0))
-        stats = jnp.where(lane == 2, row_terms[0], jnp.where(lane == 3, row_terms[1], stats))
-        stat_ref[...] = jnp.transpose(stats)[:8]
-
-    for within in range(per_run):
-        pl.when(place_in_run == within)(functools.partial(one_block, within))
-
-    @pl.when((pair == pl.num_programs(0) - 1) & (place_in_run == per_run - 1))
+    stats = jnp.where(lane == 0, logs[0], jnp.where(lane == 1, logs[1], 0.0))
+    stats = jnp.where(lane == 2, row_terms[0], jnp.where(lane == 3, row_terms[1], stats))
+    stat_ref[...] = jnp.transpose(stats)[:8]
+
+    @pl.when(pair == pl.num_programs(0) - 1)
     def _():
         if split:
-            half = run_rows // 2
+            half = block // 2
             send_ref[...] = branch_ref[pl.ds(pl.multiple_of((1 - info[2]) * half, half), half), :].astype(BF16)
             keep_ref[...] = branch_ref[pl.ds(pl.multiple_of(info[2] * half, half), half), :]
         else:
@@ -394,32 +402,31 @@
     model = dense.shape[0]
     keys = sum(kv.shape[0] for kv in kv_parts)
     run_rows = rows // 2
-    block = min(512, run_rows)
-    per_run = run_rows // block
+    block = run_rows
     pairs = kv_parts[0].shape[1] // (2 * LANES)
     split = (base + pairs) * LANES == width
     prior_row = run if prior.shape[0] == rows else 0
-    by_query = pl.BlockSpec((block, LANES), lambda p, i, *_: (run * per_run + i, base + p))
-    by_key = [pl.BlockSpec((kv.shape[0], LANES), lambda p, i, *_: (0, p)) for kv in kv_parts]
-    by_value = [pl.BlockSpec((kv.shape[0], LANES), lambda p, i, *_: (0, pairs + p)) for kv in kv_parts]
+    by_query = pl.BlockSpec((block, LANES), lambda p, *_: (run, base + p))
+    by_key = [pl.BlockSpec((kv.shape[0], LANES), lambda p, *_: (0, p)) for kv in kv_parts]
+    by_value = [pl.BlockSpec((kv.shape[0], LANES), lambda p, *_: (0, pairs + p)) for kv in kv_parts]
     kernel = functools.partial(
-        attend_kernel, block=block, run_rows=run_rows, parts=len(kv_parts), run=run,
+        attend_kernel, block=block, parts=len(kv_parts), run=run,
         ties=len(after), split=split,
     )
     return pl.pallas_call(
         kernel,
         grid_spec=pltpu.PrefetchScalarGridSpec(
             num_scalar_prefetch=2,
-            grid=(pairs, per_run),
+            grid=(pairs,),
             in_specs=[
                 by_query, by_query,
-                pl.BlockSpec((model, LANES), lambda p, i, *_: (0, base + p)),
-                pl.BlockSpec((run_rows, model), lambda p, i, *_: (prior_row, 0)),
+                pl.BlockSpec((model, LANES), lambda p, *_: (0, base + p)),
+                pl.BlockSpec((run_rows, model), lambda p, *_: (prior_row, 0)),
                 *by_key, *by_value,
             ] + [anywhere] * len(after),
             out_specs=[
-                pl.BlockSpec((block, LANES), lambda p, i, *_: (i, p)),
-                pl.BlockSpec((8, block), lambda p, i, *_: (p, i)),
+                pl.BlockSpec((block, LANES), lambda p, *_: (0, p)),
+                pl.BlockSpec((8, block), lambda p, *_: (p, 0)),
             ] + ([whole((run_rows // 2, model))] * 2 if split else [whole((run_rows, model))]),
             scratch_shapes=[
                 pltpu.VMEM((keys, LANES), BF16),
@@ -442,15 +449,14 @@
     )(info, slots, q, g, dense, prior, *kv_parts, *kv_parts, *after)
 
 
-def attend_back_kernel(info, slots, q_ref, g_ref, stat_ref, *refs, block, run_rows, parts, home, ties):
+def attend_back_kernel(info, slots, q_ref, g_ref, stat_ref, *refs, block, parts, home, ties):
     k_parts, v_parts, refs = refs[:parts], refs[parts : 2 * parts], refs[2 * parts + ties :]
     dq_ref, dk_out, dv_out, refs = refs[0], refs[1], refs[2], refs[3:]
     if home:
         back_ref, refs = refs[0], refs[1:]
     k_ref, v_ref, dk_ref, dv_ref, acc_ref = refs
-    per_run = run_rows // block
     step = pl.program_id(0)
-    full = info[step // per_run]
+    full = info[step]
 
     @pl.when(step == 0)
     def _():
@@ -463,48 +469,37 @@
         dk_ref[...] = jnp.zeros_like(dk_ref)
         dv_ref[...] = jnp.zeros_like(dv_ref)
 
-    lane = lax.broadcasted_iota(jnp.int32, (block, LANES), 1)
-    heads = (lane < HD, lane >= HD)
-
-    def rows_of(at, count):
-        return pl.ds(pl.multiple_of(slots[at] * run_rows, run_rows), count)
-
-    def one_block(within):
-        queries, grads = pick_heads(q_ref[...], heads), pick_heads(g_ref[...], heads)
-        stats = jnp.transpose(stat_ref[...])
-        logs, row_terms = [stats[:, h : h + 1] for h in range(2)], [stats[:, 2 + h : 3 + h] for h in range(2)]
-        seen = (within + 1) * block
-        acc_ref[...] = jnp.zeros_like(acc_ref)
-
-        def back(at, last):
-            count = seen if last else run_rows
-            there = rows_of(at, count)
+    heads = head_lanes(block)
+    queries, grads = pick_heads(q_ref[...], heads), pick_heads(g_ref[...], heads)
+    stats = jnp.transpose(stat_ref[...])
+    logs, row_terms = [stats[:, h : h + 1] for h in range(2)], [stats[:, 2 + h : 3 + h] for h in range(2)]
+    acc_ref[...] = jnp.zeros_like(acc_ref)
+
+    def back(at, last):
+        for row, col, count in tiles(block, last):
+            there = pl.ds(pl.multiple_of(slots[at] * block + col, count), count)
             keys, values = k_ref[there, :], v_ref[there, :]
             key_terms, value_terms = [], []
             for h in range(2):
-                soft = jnp.exp2(dot(queries[h], keys, NT) * F32(LOG2E) - logs[h])
+                query, grad = queries[h][row:], grads[h][row:]
+                soft = jnp.exp2(dot(query, keys, NT) * F32(LOG2E) - logs[h][row:])
                 if last:
-                    row = lax.broadcasted_iota(jnp.int32, (block, count), 0)
-                    col = lax.broadcasted_iota(jnp.int32, (block, count), 1)
-                    soft = jnp.where(col <= row + within * block, soft, 0.0)
-                grad_soft = dot(grads[h], values, NT)
-                grad_score = (soft * (grad_soft - row_terms[h])).astype(BF16)
-                acc_ref[h] += dot(grad_score, keys, NN)
-                key_terms.append(dot(grad_score, queries[h], TN))
-                value_terms.append(dot(soft.astype(BF16), grads[h], TN))
+                    soft = jnp.where(visible(soft.shape), soft, 0.0)
+                grad_soft = dot(grad, values, NT)
+                grad_score = (soft * (grad_soft - row_terms[h][row:])).astype(BF16)
+                acc_ref[h, row:, :] += dot(grad_score, keys, NN)
+                key_terms.append(dot(grad_score, query, TN))
+                value_terms.append(dot(soft.astype(BF16), grad, TN))
             dk_ref[there, :] += key_terms[0] + key_terms[1]
             dv_ref[there, :] += value_terms[0] + value_terms[1]
 
-        def back_whole(at, carry):
-            back(at, False)
-            return carry
-
-        lax.fori_loop(0, full, back_whole, 0)
-        back(full, True)
-        dq_ref[...] = (jnp.where(heads[0], acc_ref[0], acc_ref[1]) * F32(HD**-0.5)).astype(dq_ref.dtype)
-
-    for within in range(per_run):
-        pl.when(step % per_run == within)(functools.partial(one_block, within))
+    def back_whole(at, carry):
+        back(at, False)
+        return carry
+
+    lax.fori_loop(0, full, back_whole, 0)
+    back(full, True)
+    dq_ref[...] = (jnp.where(heads[0], acc_ref[0], acc_ref[1]) * F32(HD**-0.5)).astype(dq_ref.dtype)
 
     @pl.when(step == pl.num_programs(0) - 1)
     def _():
@@ -520,14 +515,14 @@
     rows, width = q.shape
     keys = sum(kv.shape[0] for kv in kv_parts)
     run_rows = rows // 2
-    block = min(512, run_rows)
+    block = run_rows
     pairs = kv_parts[0].shape[1] // (2 * LANES)
     own = home or keys
     by_query = pl.BlockSpec((block, LANES), lambda i, *_: (i, pair))
     by_key = [pl.BlockSpec((kv.shape[0], LANES), lambda i, *_: (0, at)) for kv in kv_parts]
     by_value = [pl.BlockSpec((kv.shape[0], LANES), lambda i, *_: (0, pairs + at)) for kv in kv_parts]
     kernel = functools.partial(
-        attend_back_kernel, block=block, run_rows=run_rows, parts=len(kv_parts), home=home, ties=len(after)
+        attend_back_kernel, block=block, parts=len(kv_parts), home=home, ties=len(after)
     )
     out_specs = [pl.BlockSpec((block, LANES), lambda i, *_: (i, 0)), whole((own, LANES)), whole((own, LANES))]
     out_shape = [
@@ -790,32 +785,63 @@
     )(early, late, *after)
 
 
-def lay_round_kernel(index, *refs):
+STEPS = (0, 1, 2, 3, -1, -2, -3)
+
+
+def lay_line_kernel(index, *refs):
     out = refs[-1]
     run, slot = pl.program_id(0) // 4, pl.program_id(0) % 4
-    back = (index[0] + 4 - slot) % 4
-    for j in range(8):
-
-        @pl.when((run == j // 4) & (back == j % 4))
+    for j in range(2 * len(STEPS)):
+
+        @pl.when((run == j // len(STEPS)) & (index[0] - slot == STEPS[j % len(STEPS)]))
         def _(j=j):
             out[0] = refs[j][...]
 
 
-def lay_round(index, early, late):
+def lay_line(index, early, late):
     half, width = early[0].shape
     return pl.pallas_call(
-        lay_round_kernel,
+        lay_line_kernel,
         grid_spec=pltpu.PrefetchScalarGridSpec(
             num_scalar_prefetch=1,
             grid=(8,),
-            in_specs=[whole((half, width))] * 8,
+            in_specs=[whole((half, width))] * 14,
             out_specs=pl.BlockSpec((1, half, width), lambda i, *_: ((i % 4) // 2, 2 * (i // 4) + i % 2, 0)),
         ),
         out_shape=jax.ShapeDtypeStruct((2, 4 * half, width), BF16),
         compiler_params=params(),
         cost_estimate=brief,
-        name="lay_round",
+        name="lay_line",
     )(index[None], *early, *late)
+
+
+def sides_kernel(which, sums_ref, *refs, segments):
+    keep_ref, send_ref = refs[-2:]
+    near = which[0] == 0
+    at = out = 0
+    for cols in segments:
+        one, two = sums_ref[:, at : at + cols], sums_ref[:, at + cols : at + 2 * cols]
+        keep_ref[:, out : out + cols] = jnp.where(near, one, two)
+        send_ref[:, out : out + cols] = jnp.where(near, two, one)
+        at, out = at + 2 * cols, out + cols
+
+
+def sides(which, sums, segments, after):
+    rows = sums.shape[0]
+    half = sum(segments)
+    return pl.pallas_call(
+        functools.partial(sides_kernel, segments=segments),
+        grid_spec=pltpu.PrefetchScalarGridSpec(
+            num_scalar_prefetch=1,
+            grid=(1,),
+            in_specs=[whole(sums.shape)] + [anywhere] * len(after),
+            out_specs=[whole((rows, half))] * 2,
+        ),
+        out_shape=[jax.ShapeDtypeStruct((rows, half), BF16)] * 2,
+        compiler_params=params(),
+        cost_estimate=brief,
+        name="sides",
+    )(which, sums, *after)
 
 
 def swap(values, axis):
@@ -835,9 +861,13 @@
     return values.reshape(8, 2, *values.shape[1:])
 
 
-def round_mp(mine):
+def line_mp(mine):
     axes = ("mh", "ml")
-    return [mine] + [lax.ppermute(mine, axes, [(i, (i + k) % 4) for i in range(4)]) for k in (1, 2, 3)]
+    before, behind = [mine], [mine]
+    for _ in range(3):
+        before.append(lax.ppermute(before[-1], axes, [(i, i + 1) for i in range(3)]))
+        behind.append(lax.ppermute(behind[-1], axes, [(i + 1, i) for i in range(3)]))
+    return before + behind[1:]
 
 
 def rotation_tables(positions):
@@ -891,7 +921,7 @@
     first_widths = (6 * cols, 2 * cols, 2 * LANES)
     if owners == 8 and seq_size == 2:
         one, two = gather_half(one, True), gather_half(two, False)
-        qkv_w, dense_w, small = place(place_first_kernel, where, one, two, first_widths, (BF16, BF16, F32))
+        qkv_w, dense_w, small = place_first(where, one, two, first_widths, (BF16, BF16, F32))
         pack = lax.all_gather(jnp.concatenate([three, four], axis=1), ("dp", "seq", "mh"), axis=0, tiled=True)
         up_w, down_w = place_second(pack.reshape(owners, 2, share, 2 * units))
     else:
@@ -1005,16 +1035,11 @@
     )
     ties = ((grad_qkv_b,), (grad_qkv_b,))
     input_grad = [norm_back(which, tokens, out_grad, keep, got[run], run, ties[run]) for run in range(2)]
-    input_grad = lay_round(index, *[round_mp(rows_done) for rows_done in input_grad])
+    travelled = [line_mp(rows_done) for rows_done in input_grad]
+    input_grad = lay_line(index, *travelled)
 
     def scatter(grads):
         return lax.psum_scatter(grads, ("dp", "seq"), scatter_dimension=0, tiled=True)
-
-    def settle(sums):
-        sums = sums.astype(F32)
-        mine = lax.dynamic_index_in_dim(sums, side, 1, keepdims=False)
-        other = lax.dynamic_index_in_dim(sums, 1 - side, 1, keepdims=False)
-        return mine + swap(other.astype(BF16), "mh").astype(F32)
 
     vector_grads = (mlp_vectors + qkv_vectors)[:, None, :5]
     vector_grads = jnp.broadcast_to(vector_grads, (width, 2, 5))
@@ -1025,13 +1050,10 @@
     tail = jnp.concatenate([vector_grads, bias_qkv, bias_up], axis=2)
     tail = jnp.pad(tail, ((0, 0), (0, 0), (0, LANES // 2 - 7))).astype(BF16).reshape(width, LANES)
     packed = scatter(join((grad_qkv, grad_dense, tail, feed_weights)))
-    first, owned_feed = packed[:, : 8 * cols + LANES], packed[:, 8 * cols + LANES :]
-    owned_feed = owned_feed.reshape(share, 2, 2, units).transpose(0, 2, 1, 3).reshape(share, 2, 2 * units)
-    owned_qkv = first[:, : 6 * cols].reshape(share, 3, 2, cols).transpose(0, 2, 1, 3).reshape(share, 2, 3 * cols)
-    owned_dense = first[:, 6 * cols : 8 * cols].reshape(share, 2, cols)
-    owned_tail = first[:, 8 * cols :].reshape(share, 2, LANES // 2)
-    owned = settle(jnp.concatenate([owned_feed, owned_qkv, owned_dense, owned_tail], axis=2))
-    owned_feed, owned = owned[:, : 2 * units], owned[:, 2 * units :]
+    segments = (cols,) * 4 + (LANES // 2, units, units)
+    kept, sent = sides(which, packed, segments, [steps[at] for steps in travelled for at in (2, 5)])
+    owned = kept.astype(F32) + swap(sent, "mh").astype(F32)
+    owned, owned_feed = owned[:, : 4 * cols + LANES // 2], owned[:, 4 * cols + LANES // 2 :]
     vectors = owned[:, 4 * cols :]
     norms = vectors[:, :5]
     norms = norms + swap(norms, "ml")

time: 598 us -> 564 us (0.943)
  waiting for transfers between devices: 156 us -> 102 us
  starting transfers between devices: 31.6 us -> 56.5 us
    reduce_scatter x1, waiting for transfers between devices: 31.9 us -> 0.02 us  [scatter(): lax.psum_scatter(grads, ('dp', 'seq'), scatter_dimension=0, tiled=True)]
    ppermute x6 -> x12, starting transfers between devices: 7.81 us -> 34.3 us  [the longest x6 26.6 us: line_mp(): lax.ppermute(before[-1], axes, [(i, i + 1) for i in range(3)])]
    ppermute x15, waiting for transfers between devices: 63.4 us -> 42 us  [swap(): return lax.ppermute(values, axis, [(0, 1), (1, 0)])]
    pallas_call x2 -> x3, Pallas kernels: 14.1 us -> 16.2 us  [the longest x1 8.52 us: lay_line(): pl.pallas_call(lay_line_kernel, grid_spec=pltpu.PrefetchScalarGridSpec(nu...]
    ppermute x6 -> x12, waiting for transfers between devices: 56.4 us -> 55.1 us  [the longest x6 47.1 us: line_mp(): lax.ppermute(before[-1], axes, [(i, i + 1) for i in range(3)])]
    unnamed x77 -> x96, local copies, waits for them, and re-layouts: 17.8 us -> 17.6 us
  transfers between devices with their start and end apart: 29 -> 35, of which waited for: 11 -> 19; matrix products, arithmetic and copies ran while one was open for 8% -> 8% of each run, Pallas kernels for 52% -> 55%
where the time goes in v7:
time: 564 us; the launch traced here: 554 us
  Pallas kernels  320 us (57%)
  waiting for transfers between devices  102 us (18%)
  starting transfers between devices  56.5 us (10%)
  local copies, waits for them, and re-layouts  43.4 us (8%)
  other arithmetic  17.1 us (3%)
  between operations  15 us (3%)
    pallas_call x3, Pallas kernels, attend_back(): pl.pallas_call(kernel, grid_spec=pltpu.PrefetchScalarGridSpec(num_scalar_...  100 us
    pallas_call x4, Pallas kernels, attend(): pl.pallas_call(kernel, grid_spec=pltpu.PrefetchScalarGridSpec(num_scalar_...  76.4 us
    ppermute x6, waiting for transfers between devices, line_mp(): lax.ppermute(before[-1], axes, [(i, i + 1) for i in range(3)])  47.1 us
    ppermute x15, waiting for transfers between devices, swap(): return lax.ppermute(values, axis, [(0, 1), (1, 0)])  42 us
    pallas_call x1, Pallas kernels, feed(): pl.pallas_call(feed_kernel, grid_spec=pltpu.PrefetchScalarGridSpec(num_sc...  28.9 us
    ppermute x6, starting transfers between devices, line_mp(): lax.ppermute(before[-1], axes, [(i, i + 1) for i in range(3)])  26.6 us
    pallas_call x1, Pallas kernels, feed_grads(): pl.pallas_call(feed_grads_kernel, grid_spec=pltpu.PrefetchScalarGridSpec(...  21.8 us
    ppermute x15, starting transfers between devices, swap(): return lax.ppermute(values, axis, [(0, 1), (1, 0)])  18.5 us
  transfers between devices with their start and end apart: 35, of which 19 were waited for; matrix products, arithmetic and copies ran while one was open for 8% of the time, Pallas kernels for 55%

profile of v7, /device:TPU:0, one launch (start us, length us, event | category | flops | bytes accessed | tf_op | source)
XLA Modules:
  0.0 554.3 jit_solution(7103321386047255917)
XLA Ops:
  22.1 9.0 %collective-permute-done = bf16[96,384]{1,0:T(8,128)(2,1)S(1)} collective-permute-done((bf16[96,384]{1,0:T(8,128)(2,1)S(1)}, bf16[96,384]{1,0:T(8,128)(2,1)S(1)}, u32[]{:S(2)}, u32[]{:S(2)}) %collective-permute-start) | collective-permute-done | bytes 73760 | tf_op jit(solution)/shard_map/ppermute | solution.py:848
  64.0 12.4 %front.1 = (bf16[2048,384]{1,0:T(8,128)(2,1)}, bf16[2048,512]{1,0:T(8,128)(2,1)}, bf16[2048,256]{1,0:T(8,128)(2,1)}, bf16[2048,384]{1,0:T(8,128)(2,1)}) custom-call(s32[2]{0:T(128)} %pad_add_fusion.which, bf16[2,2048,768]{2,1,0:T(8,128)(2,1)} %x_ref.15, bf16[2,2048,768]{2,1,0:T(8,128)(2,1)} %dy_ref.11, bf16[768,1152]{1,0:T(8,128)(2,1)} %get-tuple-element.68.w_ref.refs_9_, ...), custom_call_target="tpu_custom_call" | custom-call | flops 1 | bytes 1 | tf_op jit(solution)/shard_map/front/pallas_call | solution.py:152
  90.7 28.9 %feed.1 = (bf16[2048,768]{1,0:T(8,128)(2,1)}, bf16[2048,768]{1,0:T(8,128)(2,1)}, bf16[2048,1536]{1,0:T(8,128)(2,1)}, bf16[2048,1536]{1,0:T(8,128)(2,1)}) custom-call(s32[2]{0:T(128)} %pad_add_fusion.which, bf16[2,2048,768]{2,1,0:T(8,128)(2,1)} %x_ref.15, bf16[2,2048,768]{2,1,0:T(8,128)(2,1)} %dy_ref.11, bf16[768,1536]{1,0:T(8,128)(2,1)} %get-tuple-element.74.up_ref, ...), custom_call_target="tpu_custom_call" | custom-call | flops 1 | bytes 1 | tf_op jit(solution)/shard_map/feed/pallas_call | solution.py:195
  119.6 5.5 collective-permute-done.8.refs_1_.refs_3_
  126.4 20.7 %attend.4 = (bf16[1024,256]{1,0:T(8,128)(2,1)}, f32[16,1024]{1,0:T(8,128)}, f32[1024,768]{1,0:T(8,128)}) custom-call(s32[3]{0:T(128)} %pad_add_fusion.1.info, s32[4]{0:T(128)} %select_reduce_fusion.slots, bf16[2048,384]{1,0:T(8,128)(2,1)} %get-tuple-element.72.q_ref, bf16[2048,384]{1,0:T(8,128)(2,1)} %get-tuple-element.73.g_ref, ...), custom_call_target="tpu_custom_call" | custom-call | flops 1 | bytes 1 | tf_op jit(solution)/shard_map/attend/pallas_call | solution.py:416
  147.1 27.4 %attend.5 = (bf16[1024,256]{1,0:T(8,128)(2,1)}, f32[16,1024]{1,0:T(8,128)}, f32[1024,768]{1,0:T(8,128)}) custom-call(s32[3]{0:T(128)} %pad_add_fusion.1.info, s32[4]{0:T(128)} %select_reduce_fusion.slots, bf16[2048,384]{1,0:T(8,128)(2,1)} %get-tuple-element.72.q_ref, bf16[2048,384]{1,0:T(8,128)(2,1)} %get-tuple-element.73.g_ref, ...), custom_call_target="tpu_custom_call" | custom-call | flops 1 | bytes 1 | tf_op jit(solution)/shard_map/attend/pallas_call | solution.py:416
  175.6 12.6 %attend.6 = (bf16[1024,128]{1,0:T(8,128)(2,1)}, f32[8,1024]{1,0:T(8,128)}, bf16[512,768]{1,0:T(8,128)(2,1)}, f32[512,768]{1,0:T(8,128)}) custom-call(s32[3]{0:T(128)} %pad_add_fusion.1.info, s32[4]{0:T(128)} %select_reduce_fusion.slots, bf16[2048,384]{1,0:T(8,128)(2,1)} %get-tuple-element.72.q_ref, bf16[2048,384]{1,0:T(8,128)(2,1)} %get-tuple-element.73.g_ref, ...), custom_call_target="tpu_custom_call" | custom-call | flops 1 | bytes 1 | tf_op jit(solution)/shard_map/attend/pallas_call | solution.py:416
  189.7 15.8 %attend.7 = (bf16[1024,128]{1,0:T(8,128)(2,1)}, f32[8,1024]{1,0:T(8,128)}, bf16[512,768]{1,0:T(8,128)(2,1)}, f32[512,768]{1,0:T(8,128)}) custom-call(s32[3]{0:T(128)} %pad_add_fusion.1.info, s32[4]{0:T(128)} %select_reduce_fusion.slots, bf16[2048,384]{1,0:T(8,128)(2,1)} %get-tuple-element.72.q_ref, bf16[2048,384]{1,0:T(8,128)(2,1)} %get-tuple-element.73.g_ref, ...), custom_call_target="tpu_custom_call" | custom-call | flops 1 | bytes 1 | tf_op jit(solution)/shard_map/attend/pallas_call | solution.py:416
  212.3 33.3 %attend_back.3 = (bf16[2048,128]{1,0:T(8,128)(2,1)}, f32[2048,128]{1,0:T(8,128)}, f32[2048,128]{1,0:T(8,128)}, bf16[2048,256]{1,0:T(8,128)(2,1)}) custom-call(s32[3]{0:T(128)} %pad_add_fusion.1.info, s32[4]{0:T(128)} %select_reduce_fusion.slots, bf16[2048,384]{1,0:T(8,128)(2,1)} %get-tuple-element.72.q_ref, bf16[2048,384]{1,0:T(8,128)(2,1)} %get-tuple-element.73.g_ref, ...), custom_call_target="tpu_custom_call" | custom-call | flops 8589934592 | bytes 16777216 | tf_op jit(solution)/shard_map/attend_back/pallas_call | solution.py:536
  246.8 33.4 %attend_back.4 = (bf16[2048,128]{1,0:T(8,128)(2,1)}, f32[2048,128]{1,0:T(8,128)}, f32[2048,128]{1,0:T(8,128)}, bf16[2048,256]{1,0:T(8,128)(2,1)}) custom-call(s32[3]{0:T(128)} %pad_add_fusion.1.info, s32[4]{0:T(128)} %select_reduce_fusion.slots, bf16[2048,384]{1,0:T(8,128)(2,1)} %get-tuple-element.72.q_ref, bf16[2048,384]{1,0:T(8,128)(2,1)} %get-tuple-element.73.g_ref, ...), custom_call_target="tpu_custom_call" | custom-call | flops 8589934592 | bytes 16777216 | tf_op jit(solution)/shard_map/attend_back/pallas_call | solution.py:536
  280.2 11.9 %collective-permute-done.11.got_ref = bf16[512,768]{1,0:T(8,128)(2,1)S(1)} collective-permute-done((bf16[512,768]{1,0:T(8,128)(2,1)S(1)}, bf16[512,768]{1,0:T(8,128)(2,1)S(1)}, u32[]{:S(2)}, u32[]{:S(2)}) %collective-permute-start.11) | collective-permute-done | bytes 786464 | tf_op jit(solution)/shard_map/ppermute | solution.py:848
  302.6 33.4 %attend_back.5 = (bf16[2048,128]{1,0:T(8,128)(2,1)}, f32[2048,128]{1,0:T(8,128)}, f32[2048,128]{1,0:T(8,128)}, bf16[2048,256]{1,0:T(8,128)(2,1)}) custom-call(s32[3]{0:T(128)} %pad_add_fusion.1.info, s32[4]{0:T(128)} %select_reduce_fusion.slots, bf16[2048,384]{1,0:T(8,128)(2,1)} %get-tuple-element.72.q_ref, bf16[2048,384]{1,0:T(8,128)(2,1)} %get-tuple-element.73.g_ref, ...), custom_call_target="tpu_custom_call" | custom-call | flops 8589934592 | bytes 16777216 | tf_op jit(solution)/shard_map/attend_back/pallas_call | solution.py:536
  339.9 21.8 %feed_grads.1 = (bf16[768,3072]{1,0:T(8,128)(2,1)}, f32[768,128]{1,0:T(8,128)}, f32[1,1536]{1,0:T(1,128)}) custom-call(s32[2]{0:T(128)} %pad_add_fusion.which, bf16[2,2048,768]{2,1,0:T(8,128)(2,1)} %x_ref.15, bf16[2,2048,768]{2,1,0:T(8,128)(2,1)} %dy_ref.11, bf16[2048,1536]{1,0:T(8,128)(2,1)} %get-tuple-element.106.act_ref, ...), custom_call_target="tpu_custom_call" | custom-call | flops 8589934592 | bytes 16777216 | tf_op jit(solution)/shard_map/feed_grads/pallas_call | solution.py:260
  362.7 14.6 %back.1 = (bf16[2048,1152]{1,0:T(8,128)(2,1)}, bf16[1024,768]{1,0:T(8,128)(2,1)}, f32[1024,768]{1,0:T(8,128)}) custom-call(s32[2]{0:T(128)} %pad_add_fusion.which, bf16[2048,384]{1,0:T(8,128)(2,1)} %pad_maximum_fusion.dq_ref, f32[2048,128]{1,0:T(8,128)} %get-tuple-element.97.refs_0_, f32[2048,128]{1,0:T(8,128)} %get-tuple-element.98.refs_1_, ...), custom_call_target="tpu_custom_call" | custom-call | flops 1 | bytes 1 | tf_op jit(solution)/shard_map/back/pallas_call | solution.py:594
  381.1 15.4 %weight_grads.1 = (bf16[768,1152]{1,0:T(8,128)(2,1)}, bf16[768,384]{1,0:T(8,128)(2,1)}, f32[768,128]{1,0:T(8,128)}, f32[1,1152]{1,0:T(1,128)}) custom-call(s32[2]{0:T(128)} %pad_add_fusion.which, bf16[2,2048,768]{2,1,0:T(8,128)(2,1)} %x_ref.15, bf16[2,2048,768]{2,1,0:T(8,128)(2,1)} %dy_ref.11, bf16[2048,1152]{1,0:T(8,128)(2,1)} %get-tuple-element.109.refs_0_.dproj_ref, ...), custom_call_target="tpu_custom_call" | custom-call | flops 8589934592 | bytes 16777216 | tf_op jit(solution)/shard_map/weight_grads/pallas_call | solution.py:651
  399.6 6.5 %join.1 = bf16[768,4736]{1,0:T(8,128)(2,1)} custom-call(bf16[768,1152]{1,0:T(8,128)(2,1)} %get-tuple-element.113.refs_0_, bf16[768,384]{1,0:T(8,128)(2,1)} %get-tuple-element.114.refs_1_, bf16[768,128]{1,0:T(8,128)(2,1)} %copy.127.refs_2_, bf16[768,3072]{1,0:T(8,128)(2,1)} %get-tuple-element.117.refs_3_), custom_call_target="tpu_custom_call" | custom-call | flops 1 | bytes 1 | tf_op jit(solution)/shard_map/join/pallas_call | solution.py:687
  438.1 10.3 %collective-permute-done.16.refs_1_ = bf16[512,768]{1,0:T(8,128)(2,1)S(1)} collective-permute-done((bf16[512,768]{1,0:T(8,128)(2,1)}, bf16[512,768]{1,0:T(8,128)(2,1)S(1)}, u32[]{:S(2)}, u32[]{:S(2)}) %collective-permute-start.16) | collective-permute-done | bytes 786464 | tf_op jit(solution)/shard_map/ppermute | solution.py:868
  454.9 10.4 %collective-permute-done.24.refs_9_.refs_2_ = bf16[512,768]{1,0:T(8,128)(2,1)S(1)} collective-permute-done((bf16[512,768]{1,0:T(8,128)(2,1)}, bf16[512,768]{1,0:T(8,128)(2,1)S(1)}, u32[]{:S(2)}, u32[]{:S(2)}) %collective-permute-start.24) | collective-permute-done | bytes 786464 | tf_op jit(solution)/shard_map/ppermute | solution.py:868
  471.8 10.2 %collective-permute-done.17.refs_2_.refs_0_ = bf16[512,768]{1,0:T(8,128)(2,1)S(1)} collective-permute-done((bf16[512,768]{1,0:T(8,128)(2,1)S(1)}, bf16[512,768]{1,0:T(8,128)(2,1)S(1)}, u32[]{:S(2)}, u32[]{:S(2)}) %collective-permute-start.17) | collective-permute-done | bytes 786464 | tf_op jit(solution)/shard_map/ppermute | solution.py:868
  482.0 5.3 collective-permute-start.18
  494.7 6.8 %lay_gathered.1 = bf16[2,2048,768]{2,1,0:T(8,128)(2,1)} custom-call(bf16[2048,768]{1,0:T(8,128)(2,1)} %all-gather.6.cloned.1.call-done.refs_2_.early_ref, bf16[2048,768]{1,0:T(8,128)(2,1)} %all-gather.8.cloned.1.call-done.late_ref.refs_0_, bf16[2048,1152]{1,0:T(8,128)(2,1)} %get-tuple-element.109.refs_0_.dproj_ref), custom_call_target="tpu_custom_call" | custom-call | flops 1 | bytes 1 | tf_op jit(solution)/shard_map/lay_gathered/pallas_call | solution.py:776
  504.2 11.5 %collective-permute-done.18.refs_3_ = bf16[512,768]{1,0:T(8,128)(2,1)} collective-permute-done((bf16[512,768]{1,0:T(8,128)(2,1)S(1)}, bf16[512,768]{1,0:T(8,128)(2,1)}, u32[]{:S(2)}, u32[]{:S(2)}) %collective-permute-start.18) | collective-permute-done | bytes 786464 | tf_op jit(solution)/shard_map/ppermute | solution.py:868
  519.3 8.5 %lay_line.1 = bf16[2,2048,768]{2,1,0:T(8,128)(2,1)} custom-call(s32[1]{0:T(128)} %bitcast.31.index, bf16[512,768]{1,0:T(8,128)(2,1)} %norm_back.2.refs_0_, bf16[512,768]{1,0:T(8,128)(2,1)} %copy-done.23, bf16[512,768]{1,0:T(8,128)(2,1)} %copy-done.9, bf16[512,768]{1,0:T(8,128)(2,1)} %collective-permute-done.18.refs_3_, bf16[512,768]{1,0:T(8,128)(2,1)} %copy-done.24, ...), custom_call_target="tpu_custom_call" | custom-call | flops 1 | bytes 1 | tf_op jit(solution)/shard_map/lay_line/pallas_call | solution.py:803
  527.8 11.5 %collective-permute-done.29 = bf16[96,2368]{1,0:T(8,128)(2,1)} collective-permute-done((bf16[96,2368]{1,0:T(8,128)(2,1)}, bf16[96,2368]{1,0:T(8,128)(2,1)}, u32[]{:S(2)}, u32[]{:S(2)}) %collective-permute-start.29) | collective-permute-done | bytes 454688 | tf_op jit(solution)/shard_map/ppermute | solution.py:848
  (258 shorter events, 162.5 us)
Async XLA Ops:
  7.2 78.6 %all-gather.4.cloned.1.call-start = ((), (), s32[]{:S(2)}) async-start(), calls=%async_computation.1 | async-start | bytes 5013504 | tf_op jit(solution)/shard_map/all_gather | solution.py:925
  9.0 329.9 %all-gather.6.cloned.1.call-start = ((), (), s32[]{:S(2)}) async-start(), calls=%async_computation.2 | async-start | bytes 3932160 | tf_op jit(solution)/shard_map/all_gather | solution.py:1000
  76.4 48.7 %collective-permute-start.8 = (bf16[2048,512]{1,0:T(8,128)(2,1)}, bf16[2048,512]{1,0:T(8,128)(2,1)S(1)}, u32[]{:S(2)}, u32[]{:S(2)}) collective-permute-start(bf16[2048,512]{1,0:T(8,128)(2,1)} %get-tuple-element.77.refs_0_.refs_2_), channel_id=1, source_target_pairs={{0,4},{4,0},{1,5},{5,1},{2,6},{6,2},{3,7},{7,3},{8,12},{12,8},{9,1... | collective-permute-start | bytes 6291464 | tf_op jit(solution)/shard_map/ppermute | solution.py:848
  77.1 97.5 %collective-permute-start.9 = (bf16[2048,256]{1,0:T(8,128)(2,1)}, bf16[2048,256]{1,0:T(8,128)(2,1)S(1)}, u32[]{:S(2)}, u32[]{:S(2)}) collective-permute-start(bf16[2048,256]{1,0:T(8,128)(2,1)} %get-tuple-element.79.refs_0_.refs_2_), channel_id=1, source_target_pairs={{0,4},{4,0},{1,5},{5,1},{2,6},{6,2},{3,7},{7,3},{8,12},{12,8},{9,1... | collective-permute-start | bytes 3145736 | tf_op jit(solution)/shard_map/ppermute | solution.py:848
  211.5 169.6 %all-gather.8.cloned.1.call-start = ((), (), s32[]{:S(2)}) async-start(), calls=%async_computation.3 | async-start | bytes 3932160 | tf_op jit(solution)/shard_map/all_gather | solution.py:1021
  245.6 46.6 %collective-permute-start.12 = (bf16[2048,256]{1,0:T(8,128)(2,1)}, bf16[2048,256]{1,0:T(8,128)(2,1)S(1)}, u32[]{:S(2)}, u32[]{:S(2)}) collective-permute-start(bf16[2048,256]{1,0:T(8,128)(2,1)} %get-tuple-element.95), channel_id=1, source_target_pairs={{0,4},{4,0},{1,5},{5,1},{2,6},{6,2},{3,7},{7,3},{8,12},{12,8},{9,1... | collective-permute-start | bytes 3145736 | tf_op jit(solution)/shard_map/ppermute | solution.py:848
  245.6 46.6 %collective-permute-start.11 = (bf16[512,768]{1,0:T(8,128)(2,1)S(1)}, bf16[512,768]{1,0:T(8,128)(2,1)S(1)}, u32[]{:S(2)}, u32[]{:S(2)}) collective-permute-start(bf16[512,768]{1,0:T(8,128)(2,1)S(1)} %copy-done.40), channel_id=1, source_target_pairs={{0,1},{1,0},{2,3},{3,2},{4,5},{5,4},{6,7},{7,6},{8,9},{9,8},{10,11... | collective-permute-start | bytes 2359304 | tf_op jit(solution)/shard_map/ppermute | solution.py:848
  297.1 191.5 %reduce-scatter.2.cloned.1.call-start = ((), (), s32[]{:S(2)}) async-start(), calls=%async_computation.4 | async-start | bytes 8183808 | tf_op jit(solution)/shard_map/reduce_scatter | solution.py:1042
  301.2 37.8 %collective-permute-start.13 = (bf16[2048,256]{1,0:T(8,128)(2,1)}, bf16[2048,256]{1,0:T(8,128)(2,1)S(1)}, u32[]{:S(2)}, u32[]{:S(2)}) collective-permute-start(bf16[2048,256]{1,0:T(8,128)(2,1)} %get-tuple-element.103), channel_id=1, source_target_pairs={{0,4},{4,0},{1,5},{5,1},{2,6},{6,2},{3,7},{7,3},{8,12},{12,8},{9,1... | collective-permute-start | bytes 3145736 | tf_op jit(solution)/shard_map/ppermute | solution.py:848
  336.0 25.7 %collective-permute-start.14 = (bf16[2048,256]{1,0:T(8,128)(2,1)}, bf16[2048,256]{1,0:T(8,128)(2,1)S(1)}, u32[]{:S(2)}, u32[]{:S(2)}) collective-permute-start(bf16[2048,256]{1,0:T(8,128)(2,1)} %get-tuple-element.104), channel_id=1, source_target_pairs={{0,4},{4,0},{1,5},{5,1},{2,6},{6,2},{3,7},{7,3},{8,12},{12,8},{9,1... | collective-permute-start | bytes 3145736 | tf_op jit(solution)/shard_map/ppermute | solution.py:848
  379.0 27.1 %collective-permute-start.22 = (bf16[512,768]{1,0:T(8,128)(2,1)S(1)}, bf16[512,768]{1,0:T(8,128)(2,1)S(1)}, u32[]{:S(2)}, u32[]{:S(2)}) collective-permute-start(bf16[512,768]{1,0:T(8,128)(2,1)S(1)} %get-tuple-element.199), channel_id=1, source_target_pairs={{0,1},{1,0},{2,3},{3,2},{4,5},{5,4},{6,7},{7,6},{8,9},{9,8},{10,11... | collective-permute-start | bytes 2359304 | tf_op jit(solution)/shard_map/ppermute | solution.py:848
  379.1 36.4 %collective-permute-start.15 = (bf16[512,768]{1,0:T(8,128)(2,1)S(1)}, bf16[512,768]{1,0:T(8,128)(2,1)S(1)}, u32[]{:S(2)}, u32[]{:S(2)}) collective-permute-start(bf16[512,768]{1,0:T(8,128)(2,1)S(1)} %get-tuple-element.200), channel_id=1, source_target_pairs={{0,1},{1,0},{2,3},{3,2},{4,5},{5,4},{6,7},{7,6},{8,9},{9,8},{10,11... | collective-permute-start | bytes 2359304 | tf_op jit(solution)/shard_map/ppermute | solution.py:848
  414.1 22.7 %collective-permute-start.26 = (bf16[512,768]{1,0:T(8,128)(2,1)}, bf16[512,768]{1,0:T(8,128)(2,1)}, u32[]{:S(2)}, u32[]{:S(2)}) collective-permute-start(bf16[512,768]{1,0:T(8,128)(2,1)} %norm_back.3.refs_7_), channel_id=1, source_target_pairs={{1,0},{2,1},{3,2},{5,4},{6,5},{7,6},{9,8},{10,9},{11,10},{13,12},{... | collective-permute-start | bytes 2359304 | tf_op jit(solution)/shard_map/ppermute | solution.py:869
  421.0 27.4 %collective-permute-start.16 = (bf16[512,768]{1,0:T(8,128)(2,1)}, bf16[512,768]{1,0:T(8,128)(2,1)S(1)}, u32[]{:S(2)}, u32[]{:S(2)}) collective-permute-start(bf16[512,768]{1,0:T(8,128)(2,1)} %norm_back.2.refs_0_), channel_id=1, source_target_pairs={{0,1},{1,2},{2,3},{4,5},{5,6},{6,7},{8,9},{9,10},{10,11},{12,13},{... | collective-permute-start | bytes 2359304 | tf_op jit(solution)/shard_map/ppermute | solution.py:868
  425.5 28.0 %collective-permute-start.19 = (bf16[512,768]{1,0:T(8,128)(2,1)}, bf16[512,768]{1,0:T(8,128)(2,1)S(1)}, u32[]{:S(2)}, u32[]{:S(2)}) collective-permute-start(bf16[512,768]{1,0:T(8,128)(2,1)} %norm_back.2.refs_0_), channel_id=1, source_target_pairs={{1,0},{2,1},{3,2},{5,4},{6,5},{7,6},{9,8},{10,9},{11,10},{13,12},{... | collective-permute-start | bytes 2359304 | tf_op jit(solution)/shard_map/ppermute | solution.py:869
  431.5 33.7 %collective-permute-start.24 = (bf16[512,768]{1,0:T(8,128)(2,1)}, bf16[512,768]{1,0:T(8,128)(2,1)S(1)}, u32[]{:S(2)}, u32[]{:S(2)}) collective-permute-start(bf16[512,768]{1,0:T(8,128)(2,1)} %collective-permute-done.23.refs_8_), channel_id=1, source_target_pairs={{0,1},{1,2},{2,3},{4,5},{5,6},{6,7},{8,9},{9,10},{10,11},{12,13},{... | collective-permute-start | bytes 2359304 | tf_op jit(solution)/shard_map/ppermute | solution.py:868
  436.8 33.7 %collective-permute-start.27 = (bf16[512,768]{1,0:T(8,128)(2,1)}, bf16[512,768]{1,0:T(8,128)(2,1)S(1)}, u32[]{:S(2)}, u32[]{:S(2)}) collective-permute-start(bf16[512,768]{1,0:T(8,128)(2,1)} %collective-permute-done.26.refs_11_), channel_id=1, source_target_pairs={{1,0},{2,1},{3,2},{5,4},{6,5},{7,6},{9,8},{10,9},{11,10},{13,12},{... | collective-permute-start | bytes 2359304 | tf_op jit(solution)/shard_map/ppermute | solution.py:869
  448.4 33.6 %collective-permute-start.17 = (bf16[512,768]{1,0:T(8,128)(2,1)S(1)}, bf16[512,768]{1,0:T(8,128)(2,1)S(1)}, u32[]{:S(2)}, u32[]{:S(2)}) collective-permute-start(bf16[512,768]{1,0:T(8,128)(2,1)S(1)} %collective-permute-done.16.refs_1_), channel_id=1, source_target_pairs={{0,1},{1,2},{2,3},{4,5},{5,6},{6,7},{8,9},{9,10},{10,11},{12,13},{... | collective-permute-start | bytes 2359304 | tf_op jit(solution)/shard_map/ppermute | solution.py:868
  453.6 33.7 %collective-permute-start.20 = (bf16[512,768]{1,0:T(8,128)(2,1)S(1)}, bf16[512,768]{1,0:T(8,128)(2,1)S(1)}, u32[]{:S(2)}, u32[]{:S(2)}) collective-permute-start(bf16[512,768]{1,0:T(8,128)(2,1)S(1)} %collective-permute-done.19.refs_4_), channel_id=1, source_target_pairs={{1,0},{2,1},{3,2},{5,4},{6,5},{7,6},{9,8},{10,9},{11,10},{13,12},{... | collective-permute-start | bytes 2359304 | tf_op jit(solution)/shard_map/ppermute | solution.py:869
  465.3 36.3 %collective-permute-start.25 = (bf16[512,768]{1,0:T(8,128)(2,1)S(1)}, bf16[512,768]{1,0:T(8,128)(2,1)}, u32[]{:S(2)}, u32[]{:S(2)}) collective-permute-start(bf16[512,768]{1,0:T(8,128)(2,1)S(1)} %collective-permute-done.24.refs_9_.refs_2_), channel_id=1, source_target_pairs={{0,1},{1,2},{2,3},{4,5},{5,6},{6,7},{8,9},{9,10},{10,11},{12,13},{... | collective-permute-start | bytes 2359304 | tf_op jit(solution)/shard_map/ppermute | solution.py:868
  470.5 33.8 %collective-permute-start.28 = (bf16[512,768]{1,0:T(8,128)(2,1)S(1)}, bf16[512,768]{1,0:T(8,128)(2,1)}, u32[]{:S(2)}, u32[]{:S(2)}) collective-permute-start(bf16[512,768]{1,0:T(8,128)(2,1)S(1)} %collective-permute-done.27.refs_12_.refs_3_), channel_id=1, source_target_pairs={{1,0},{2,1},{3,2},{5,4},{6,5},{7,6},{9,8},{10,9},{11,10},{13,12},{... | collective-permute-start | bytes 2359304 | tf_op jit(solution)/shard_map/ppermute | solution.py:869
  482.0 33.7 %collective-permute-start.18 = (bf16[512,768]{1,0:T(8,128)(2,1)S(1)}, bf16[512,768]{1,0:T(8,128)(2,1)}, u32[]{:S(2)}, u32[]{:S(2)}) collective-permute-start(bf16[512,768]{1,0:T(8,128)(2,1)S(1)} %collective-permute-done.17.refs_2_.refs_0_), channel_id=1, source_target_pairs={{0,1},{1,2},{2,3},{4,5},{5,6},{6,7},{8,9},{9,10},{10,11},{12,13},{... | collective-permute-start | bytes 2359304 | tf_op jit(solution)/shard_map/ppermute | solution.py:868
  487.3 32.0 %collective-permute-start.21 = (bf16[512,768]{1,0:T(8,128)(2,1)S(1)}, bf16[512,768]{1,0:T(8,128)(2,1)}, u32[]{:S(2)}, u32[]{:S(2)}) collective-permute-start(bf16[512,768]{1,0:T(8,128)(2,1)S(1)} %collective-permute-done.20.refs_5_.refs_1_), channel_id=1, source_target_pairs={{1,0},{2,1},{3,2},{5,4},{6,5},{7,6},{9,8},{10,9},{11,10},{13,12},{... | collective-permute-start | bytes 2359304 | tf_op jit(solution)/shard_map/ppermute | solution.py:869
  492.0 47.2 %collective-permute-start.29 = (bf16[96,2368]{1,0:T(8,128)(2,1)}, bf16[96,2368]{1,0:T(8,128)(2,1)}, u32[]{:S(2)}, u32[]{:S(2)}) collective-permute-start(bf16[96,2368]{1,0:T(8,128)(2,1)} %get-tuple-element.119), channel_id=1, source_target_pairs={{0,2},{2,0},{1,3},{3,1},{4,6},{6,4},{5,7},{7,5},{8,10},{10,8},{9,1... | collective-permute-start | bytes 1363976 | tf_op jit(solution)/shard_map/ppermute | solution.py:848
  (52 other events, 488.7 us)
Sparse Core Ops, SparseCore 0:
  10.9 63.8 all-gather.3
  211.7 78.6 all-gather.5
  297.2 63.4 all-gather.7
  406.2 66.6 reduce-scatter.1

commit v8 on v7

--- a/solution.py
+++ b/solution.py
@@ -789,13 +789,15 @@
 
 
 def lay_line_kernel(index, *refs):
-    out = refs[-1]
+    out, sem = refs[-2:]
     run, slot = pl.program_id(0) // 4, pl.program_id(0) % 4
     for j in range(2 * len(STEPS)):
 
         @pl.when((run == j // len(STEPS)) & (index[0] - slot == STEPS[j % len(STEPS)]))
         def _(j=j):
-            out[0] = refs[j][...]
+            copy = pltpu.make_async_copy(refs[j], out.at[0], sem)
+            copy.start()
+            copy.wait()
 
 
 def lay_line(index, early, late):
@@ -805,8 +807,9 @@
         grid_spec=pltpu.PrefetchScalarGridSpec(
             num_scalar_prefetch=1,
             grid=(8,),
-            in_specs=[whole((half, width))] * 14,
+            in_specs=[anywhere] * 14,
             out_specs=pl.BlockSpec((1, half, width), lambda i, *_: ((i % 4) // 2, 2 * (i // 4) + i % 2, 0)),
+            scratch_shapes=[pltpu.SemaphoreType.DMA],
         ),
         out_shape=jax.ShapeDtypeStruct((2, 4 * half, width), BF16),
         compiler_params=params(),
@@ -1051,7 +1054,7 @@
     tail = jnp.pad(tail, ((0, 0), (0, 0), (0, LANES // 2 - 7))).astype(BF16).reshape(width, LANES)
     packed = scatter(join((grad_qkv, grad_dense, tail, feed_weights)))
     segments = (cols,) * 4 + (LANES // 2, units, units)
-    kept, sent = sides(which, packed, segments, [steps[at] for steps in travelled for at in (2, 5)])
+    kept, sent = sides(which, packed, segments, [travelled[1][at] for at in (2, 5)])
     owned = kept.astype(F32) + swap(sent, "mh").astype(F32)
     owned, owned_feed = owned[:, : 4 * cols + LANES // 2], owned[:, 4 * cols + LANES // 2 :]
     vectors = owned[:, 4 * cols :]

time: 564 us -> 568 us (level)
    unnamed x96 -> x94, local copies, waits for them, and re-layouts: 17.6 us -> 16.8 us
  transfers between devices with their start and end apart: 35 -> 35, of which waited for: 19 -> 17; matrix products, arithmetic and copies ran while one was open for 8% -> 8% of each run, Pallas kernels for 55% -> 55%
where the time goes in v8:
time: 568 us; the launch traced here: 558 us
  Pallas kernels  324 us (57%)
  waiting for transfers between devices  99 us (17%)
  starting transfers between devices  60.4 us (11%)
  local copies, waits for them, and re-layouts  42.6 us (8%)
  other arithmetic  17.1 us (3%)
  between operations  15 us (3%)
    pallas_call x3, Pallas kernels, attend_back(): pl.pallas_call(kernel, grid_spec=pltpu.PrefetchScalarGridSpec(num_scalar_...  100 us
    pallas_call x4, Pallas kernels, attend(): pl.pallas_call(kernel, grid_spec=pltpu.PrefetchScalarGridSpec(num_scalar_...  76.7 us
    ppermute x6, waiting for transfers between devices, line_mp(): lax.ppermute(before[-1], axes, [(i, i + 1) for i in range(3)])  50.5 us
    ppermute x15, waiting for transfers between devices, swap(): return lax.ppermute(values, axis, [(0, 1), (1, 0)])  38.8 us
    pallas_call x1, Pallas kernels, feed(): pl.pallas_call(feed_kernel, grid_spec=pltpu.PrefetchScalarGridSpec(num_sc...  28.9 us
    ppermute x6, starting transfers between devices, line_mp(): lax.ppermute(before[-1], axes, [(i, i + 1) for i in range(3)])  26.9 us
    ppermute x15, starting transfers between devices, swap(): return lax.ppermute(values, axis, [(0, 1), (1, 0)])  22.1 us
    pallas_call x1, Pallas kernels, feed_grads(): pl.pallas_call(feed_grads_kernel, grid_spec=pltpu.PrefetchScalarGridSpec(...  21.8 us
  transfers between devices with their start and end apart: 35, of which 17 were waited for; matrix products, arithmetic and copies ran while one was open for 8% of the time, Pallas kernels for 55%

profile of v8, /device:TPU:0, one launch (start us, length us, event | category | flops | bytes accessed | tf_op | source)
XLA Modules:
  0.0 557.9 jit_solution(1992222160009409390)
XLA Ops:
  22.2 9.0 %collective-permute-done = bf16[96,384]{1,0:T(8,128)(2,1)S(1)} collective-permute-done((bf16[96,384]{1,0:T(8,128)(2,1)S(1)}, bf16[96,384]{1,0:T(8,128)(2,1)S(1)}, u32[]{:S(2)}, u32[]{:S(2)}) %collective-permute-start) | collective-permute-done | bytes 73760 | tf_op jit(solution)/shard_map/ppermute | solution.py:851
  64.1 12.4 %front.1 = (bf16[2048,384]{1,0:T(8,128)(2,1)}, bf16[2048,512]{1,0:T(8,128)(2,1)}, bf16[2048,256]{1,0:T(8,128)(2,1)}, bf16[2048,384]{1,0:T(8,128)(2,1)}) custom-call(s32[2]{0:T(128)} %pad_add_fusion.which, bf16[2,2048,768]{2,1,0:T(8,128)(2,1)} %x_ref.15, bf16[2,2048,768]{2,1,0:T(8,128)(2,1)} %dy_ref.11, bf16[768,1152]{1,0:T(8,128)(2,1)} %get-tuple-element.68.w_ref.refs_9_, ...), custom_call_target="tpu_custom_call" | custom-call | flops 1 | bytes 1 | tf_op jit(solution)/shard_map/front/pallas_call | solution.py:152
  90.8 28.9 %feed.1 = (bf16[2048,768]{1,0:T(8,128)(2,1)}, bf16[2048,768]{1,0:T(8,128)(2,1)}, bf16[2048,1536]{1,0:T(8,128)(2,1)}, bf16[2048,1536]{1,0:T(8,128)(2,1)}) custom-call(s32[2]{0:T(128)} %pad_add_fusion.which, bf16[2,2048,768]{2,1,0:T(8,128)(2,1)} %x_ref.15, bf16[2,2048,768]{2,1,0:T(8,128)(2,1)} %dy_ref.11, bf16[768,1536]{1,0:T(8,128)(2,1)} %get-tuple-element.74.up_ref, ...), custom_call_target="tpu_custom_call" | custom-call | flops 1 | bytes 1 | tf_op jit(solution)/shard_map/feed/pallas_call | solution.py:195
  119.7 5.5 collective-permute-done.8.refs_1_.refs_3_
  126.5 20.7 %attend.4 = (bf16[1024,256]{1,0:T(8,128)(2,1)}, f32[16,1024]{1,0:T(8,128)}, f32[1024,768]{1,0:T(8,128)}) custom-call(s32[3]{0:T(128)} %pad_add_fusion.1.info, s32[4]{0:T(128)} %select_reduce_fusion.slots, bf16[2048,384]{1,0:T(8,128)(2,1)} %get-tuple-element.72.q_ref, bf16[2048,384]{1,0:T(8,128)(2,1)} %get-tuple-element.73.g_ref, ...), custom_call_target="tpu_custom_call" | custom-call | flops 1 | bytes 1 | tf_op jit(solution)/shard_map/attend/pallas_call | solution.py:416
  147.1 27.4 %attend.5 = (bf16[1024,256]{1,0:T(8,128)(2,1)}, f32[16,1024]{1,0:T(8,128)}, f32[1024,768]{1,0:T(8,128)}) custom-call(s32[3]{0:T(128)} %pad_add_fusion.1.info, s32[4]{0:T(128)} %select_reduce_fusion.slots, bf16[2048,384]{1,0:T(8,128)(2,1)} %get-tuple-element.72.q_ref, bf16[2048,384]{1,0:T(8,128)(2,1)} %get-tuple-element.73.g_ref, ...), custom_call_target="tpu_custom_call" | custom-call | flops 1 | bytes 1 | tf_op jit(solution)/shard_map/attend/pallas_call | solution.py:416
  175.6 12.7 %attend.6 = (bf16[1024,128]{1,0:T(8,128)(2,1)}, f32[8,1024]{1,0:T(8,128)}, bf16[512,768]{1,0:T(8,128)(2,1)}, f32[512,768]{1,0:T(8,128)}) custom-call(s32[3]{0:T(128)} %pad_add_fusion.1.info, s32[4]{0:T(128)} %select_reduce_fusion.slots, bf16[2048,384]{1,0:T(8,128)(2,1)} %get-tuple-element.72.q_ref, bf16[2048,384]{1,0:T(8,128)(2,1)} %get-tuple-element.73.g_ref, ...), custom_call_target="tpu_custom_call" | custom-call | flops 1 | bytes 1 | tf_op jit(solution)/shard_map/attend/pallas_call | solution.py:416
  189.8 16.0 %attend.7 = (bf16[1024,128]{1,0:T(8,128)(2,1)}, f32[8,1024]{1,0:T(8,128)}, bf16[512,768]{1,0:T(8,128)(2,1)}, f32[512,768]{1,0:T(8,128)}) custom-call(s32[3]{0:T(128)} %pad_add_fusion.1.info, s32[4]{0:T(128)} %select_reduce_fusion.slots, bf16[2048,384]{1,0:T(8,128)(2,1)} %get-tuple-element.72.q_ref, bf16[2048,384]{1,0:T(8,128)(2,1)} %get-tuple-element.73.g_ref, ...), custom_call_target="tpu_custom_call" | custom-call | flops 1 | bytes 1 | tf_op jit(solution)/shard_map/attend/pallas_call | solution.py:416
  212.5 33.3 %attend_back.3 = (bf16[2048,128]{1,0:T(8,128)(2,1)}, f32[2048,128]{1,0:T(8,128)}, f32[2048,128]{1,0:T(8,128)}, bf16[2048,256]{1,0:T(8,128)(2,1)}) custom-call(s32[3]{0:T(128)} %pad_add_fusion.1.info, s32[4]{0:T(128)} %select_reduce_fusion.slots, bf16[2048,384]{1,0:T(8,128)(2,1)} %get-tuple-element.72.q_ref, bf16[2048,384]{1,0:T(8,128)(2,1)} %get-tuple-element.73.g_ref, ...), custom_call_target="tpu_custom_call" | custom-call | flops 8589934592 | bytes 16777216 | tf_op jit(solution)/shard_map/attend_back/pallas_call | solution.py:536
  247.0 33.5 %attend_back.4 = (bf16[2048,128]{1,0:T(8,128)(2,1)}, f32[2048,128]{1,0:T(8,128)}, f32[2048,128]{1,0:T(8,128)}, bf16[2048,256]{1,0:T(8,128)(2,1)}) custom-call(s32[3]{0:T(128)} %pad_add_fusion.1.info, s32[4]{0:T(128)} %select_reduce_fusion.slots, bf16[2048,384]{1,0:T(8,128)(2,1)} %get-tuple-element.72.q_ref, bf16[2048,384]{1,0:T(8,128)(2,1)} %get-tuple-element.73.g_ref, ...), custom_call_target="tpu_custom_call" | custom-call | flops 8589934592 | bytes 16777216 | tf_op jit(solution)/shard_map/attend_back/pallas_call | solution.py:536
  280.4 11.8 %collective-permute-done.11.got_ref = bf16[512,768]{1,0:T(8,128)(2,1)S(1)} collective-permute-done((bf16[512,768]{1,0:T(8,128)(2,1)S(1)}, bf16[512,768]{1,0:T(8,128)(2,1)S(1)}, u32[]{:S(2)}, u32[]{:S(2)}) %collective-permute-start.11) | collective-permute-done | bytes 786464 | tf_op jit(solution)/shard_map/ppermute | solution.py:851
  302.7 33.3 %attend_back.5 = (bf16[2048,128]{1,0:T(8,128)(2,1)}, f32[2048,128]{1,0:T(8,128)}, f32[2048,128]{1,0:T(8,128)}, bf16[2048,256]{1,0:T(8,128)(2,1)}) custom-call(s32[3]{0:T(128)} %pad_add_fusion.1.info, s32[4]{0:T(128)} %select_reduce_fusion.slots, bf16[2048,384]{1,0:T(8,128)(2,1)} %get-tuple-element.72.q_ref, bf16[2048,384]{1,0:T(8,128)(2,1)} %get-tuple-element.73.g_ref, ...), custom_call_target="tpu_custom_call" | custom-call | flops 8589934592 | bytes 16777216 | tf_op jit(solution)/shard_map/attend_back/pallas_call | solution.py:536
  340.0 21.8 %feed_grads.1 = (bf16[768,3072]{1,0:T(8,128)(2,1)}, f32[768,128]{1,0:T(8,128)}, f32[1,1536]{1,0:T(1,128)}) custom-call(s32[2]{0:T(128)} %pad_add_fusion.which, bf16[2,2048,768]{2,1,0:T(8,128)(2,1)} %x_ref.15, bf16[2,2048,768]{2,1,0:T(8,128)(2,1)} %dy_ref.11, bf16[2048,1536]{1,0:T(8,128)(2,1)} %get-tuple-element.106.act_ref, ...), custom_call_target="tpu_custom_call" | custom-call | flops 8589934592 | bytes 16777216 | tf_op jit(solution)/shard_map/feed_grads/pallas_call | solution.py:260
  362.8 14.6 %back.1 = (bf16[2048,1152]{1,0:T(8,128)(2,1)}, bf16[1024,768]{1,0:T(8,128)(2,1)}, f32[1024,768]{1,0:T(8,128)}) custom-call(s32[2]{0:T(128)} %pad_add_fusion.which, bf16[2048,384]{1,0:T(8,128)(2,1)} %pad_maximum_fusion.dq_ref, f32[2048,128]{1,0:T(8,128)} %get-tuple-element.97.refs_0_, f32[2048,128]{1,0:T(8,128)} %get-tuple-element.98.refs_1_, ...), custom_call_target="tpu_custom_call" | custom-call | flops 1 | bytes 1 | tf_op jit(solution)/shard_map/back/pallas_call | solution.py:594
  381.1 15.4 %weight_grads.1 = (bf16[768,1152]{1,0:T(8,128)(2,1)}, bf16[768,384]{1,0:T(8,128)(2,1)}, f32[768,128]{1,0:T(8,128)}, f32[1,1152]{1,0:T(1,128)}) custom-call(s32[2]{0:T(128)} %pad_add_fusion.which, bf16[2,2048,768]{2,1,0:T(8,128)(2,1)} %x_ref.15, bf16[2,2048,768]{2,1,0:T(8,128)(2,1)} %dy_ref.11, bf16[2048,1152]{1,0:T(8,128)(2,1)} %get-tuple-element.109.refs_0_.dproj_ref, ...), custom_call_target="tpu_custom_call" | custom-call | flops 8589934592 | bytes 16777216 | tf_op jit(solution)/shard_map/weight_grads/pallas_call | solution.py:651
  399.7 6.5 %join.1 = bf16[768,4736]{1,0:T(8,128)(2,1)} custom-call(bf16[768,1152]{1,0:T(8,128)(2,1)} %get-tuple-element.113.refs_0_, bf16[768,384]{1,0:T(8,128)(2,1)} %get-tuple-element.114.refs_1_, bf16[768,128]{1,0:T(8,128)(2,1)} %copy.127.refs_2_, bf16[768,3072]{1,0:T(8,128)(2,1)} %get-tuple-element.117.refs_3_), custom_call_target="tpu_custom_call" | custom-call | flops 1 | bytes 1 | tf_op jit(solution)/shard_map/join/pallas_call | solution.py:687
  425.2 6.4 %collective-permute-done.23.refs_8_ = bf16[512,768]{1,0:T(8,128)(2,1)S(1)} collective-permute-done((bf16[512,768]{1,0:T(8,128)(2,1)}, bf16[512,768]{1,0:T(8,128)(2,1)S(1)}, u32[]{:S(2)}, u32[]{:S(2)}) %collective-permute-start.23) | collective-permute-done | bytes 786464 | tf_op jit(solution)/shard_map/ppermute | solution.py:871
  437.3 11.2 %collective-permute-done.16.refs_1_ = bf16[512,768]{1,0:T(8,128)(2,1)S(1)} collective-permute-done((bf16[512,768]{1,0:T(8,128)(2,1)}, bf16[512,768]{1,0:T(8,128)(2,1)S(1)}, u32[]{:S(2)}, u32[]{:S(2)}) %collective-permute-start.16) | collective-permute-done | bytes 786464 | tf_op jit(solution)/shard_map/ppermute | solution.py:871
  455.0 10.2 %collective-permute-done.24.refs_9_.refs_0_ = bf16[512,768]{1,0:T(8,128)(2,1)S(1)} collective-permute-done((bf16[512,768]{1,0:T(8,128)(2,1)S(1)}, bf16[512,768]{1,0:T(8,128)(2,1)S(1)}, u32[]{:S(2)}, u32[]{:S(2)}) %collective-permute-start.24) | collective-permute-done | bytes 786464 | tf_op jit(solution)/shard_map/ppermute | solution.py:871
  471.8 10.3 %collective-permute-done.17.refs_2_ = bf16[512,768]{1,0:T(8,128)(2,1)} collective-permute-done((bf16[512,768]{1,0:T(8,128)(2,1)S(1)}, bf16[512,768]{1,0:T(8,128)(2,1)}, u32[]{:S(2)}, u32[]{:S(2)}) %collective-permute-start.17) | collective-permute-done | bytes 786464 | tf_op jit(solution)/shard_map/ppermute | solution.py:871
  494.9 6.8 %lay_gathered.1 = bf16[2,2048,768]{2,1,0:T(8,128)(2,1)} custom-call(bf16[2048,768]{1,0:T(8,128)(2,1)} %all-gather.6.cloned.1.call-done.refs_2_.early_ref, bf16[2048,768]{1,0:T(8,128)(2,1)} %all-gather.8.cloned.1.call-done.late_ref.refs_0_, bf16[2048,1152]{1,0:T(8,128)(2,1)} %get-tuple-element.109.refs_0_.dproj_ref), custom_call_target="tpu_custom_call" | custom-call | flops 1 | bytes 1 | tf_op jit(solution)/shard_map/lay_gathered/pallas_call | solution.py:776
  503.5 12.4 %collective-permute-done.18.refs_3_ = bf16[512,768]{1,0:T(8,128)(2,1)} collective-permute-done((bf16[512,768]{1,0:T(8,128)(2,1)}, bf16[512,768]{1,0:T(8,128)(2,1)}, u32[]{:S(2)}, u32[]{:S(2)}) %collective-permute-start.18) | collective-permute-done | bytes 786464 | tf_op jit(solution)/shard_map/ppermute | solution.py:871
  518.6 12.0 %lay_line.1 = bf16[2,2048,768]{2,1,0:T(8,128)(2,1)} custom-call(s32[1]{0:T(128)} %bitcast.31.index, bf16[512,768]{1,0:T(8,128)(2,1)} %norm_back.2.refs_0_, bf16[512,768]{1,0:T(8,128)(2,1)} %copy-done.23, bf16[512,768]{1,0:T(8,128)(2,1)} %collective-permute-done.17.refs_2_, bf16[512,768]{1,0:T(8,128)(2,1)} %collective-permute-done.18.refs_3_, ...), custom_call_target="tpu_custom_call" | custom-call | flops 1 | bytes 1 | tf_op jit(solution)/shard_map/lay_line/pallas_call | solution.py:805
  530.6 8.6 %collective-permute-done.29 = bf16[96,2368]{1,0:T(8,128)(2,1)} collective-permute-done((bf16[96,2368]{1,0:T(8,128)(2,1)}, bf16[96,2368]{1,0:T(8,128)(2,1)}, u32[]{:S(2)}, u32[]{:S(2)}) %collective-permute-start.29) | collective-permute-done | bytes 454688 | tf_op jit(solution)/shard_map/ppermute | solution.py:851
  (256 shorter events, 162.5 us)
Async XLA Ops:
  7.2 78.6 %all-gather.4.cloned.1.call-start = ((), (), s32[]{:S(2)}) async-start(), calls=%async_computation.1 | async-start | bytes 5013504 | tf_op jit(solution)/shard_map/all_gather | solution.py:928
  9.0 330.0 %all-gather.6.cloned.1.call-start = ((), (), s32[]{:S(2)}) async-start(), calls=%async_computation.2 | async-start | bytes 3932160 | tf_op jit(solution)/shard_map/all_gather | solution.py:1003
  76.4 48.7 %collective-permute-start.8 = (bf16[2048,512]{1,0:T(8,128)(2,1)}, bf16[2048,512]{1,0:T(8,128)(2,1)S(1)}, u32[]{:S(2)}, u32[]{:S(2)}) collective-permute-start(bf16[2048,512]{1,0:T(8,128)(2,1)} %get-tuple-element.77.refs_0_.refs_2_), channel_id=1, source_target_pairs={{0,4},{4,0},{1,5},{5,1},{2,6},{6,2},{3,7},{7,3},{8,12},{12,8},{9,1... | collective-permute-start | bytes 6291464 | tf_op jit(solution)/shard_map/ppermute | solution.py:851
  77.1 97.5 %collective-permute-start.9 = (bf16[2048,256]{1,0:T(8,128)(2,1)}, bf16[2048,256]{1,0:T(8,128)(2,1)S(1)}, u32[]{:S(2)}, u32[]{:S(2)}) collective-permute-start(bf16[2048,256]{1,0:T(8,128)(2,1)} %get-tuple-element.79.refs_0_.refs_2_), channel_id=1, source_target_pairs={{0,4},{4,0},{1,5},{5,1},{2,6},{6,2},{3,7},{7,3},{8,12},{12,8},{9,1... | collective-permute-start | bytes 3145736 | tf_op jit(solution)/shard_map/ppermute | solution.py:851
  211.8 169.4 %all-gather.8.cloned.1.call-start = ((), (), s32[]{:S(2)}) async-start(), calls=%async_computation.3 | async-start | bytes 3932160 | tf_op jit(solution)/shard_map/all_gather | solution.py:1024
  245.8 46.4 %collective-permute-start.12 = (bf16[2048,256]{1,0:T(8,128)(2,1)}, bf16[2048,256]{1,0:T(8,128)(2,1)S(1)}, u32[]{:S(2)}, u32[]{:S(2)}) collective-permute-start(bf16[2048,256]{1,0:T(8,128)(2,1)} %get-tuple-element.95), channel_id=1, source_target_pairs={{0,4},{4,0},{1,5},{5,1},{2,6},{6,2},{3,7},{7,3},{8,12},{12,8},{9,1... | collective-permute-start | bytes 3145736 | tf_op jit(solution)/shard_map/ppermute | solution.py:851
  245.8 46.4 %collective-permute-start.11 = (bf16[512,768]{1,0:T(8,128)(2,1)S(1)}, bf16[512,768]{1,0:T(8,128)(2,1)S(1)}, u32[]{:S(2)}, u32[]{:S(2)}) collective-permute-start(bf16[512,768]{1,0:T(8,128)(2,1)S(1)} %copy-done.39), channel_id=1, source_target_pairs={{0,1},{1,0},{2,3},{3,2},{4,5},{5,4},{6,7},{7,6},{8,9},{9,8},{10,11... | collective-permute-start | bytes 2359304 | tf_op jit(solution)/shard_map/ppermute | solution.py:851
  297.2 191.6 %reduce-scatter.2.cloned.1.call-start = ((), (), s32[]{:S(2)}) async-start(), calls=%async_computation.4 | async-start | bytes 8183808 | tf_op jit(solution)/shard_map/reduce_scatter | solution.py:1045
  301.2 37.7 %collective-permute-start.13 = (bf16[2048,256]{1,0:T(8,128)(2,1)}, bf16[2048,256]{1,0:T(8,128)(2,1)S(1)}, u32[]{:S(2)}, u32[]{:S(2)}) collective-permute-start(bf16[2048,256]{1,0:T(8,128)(2,1)} %get-tuple-element.103), channel_id=1, source_target_pairs={{0,4},{4,0},{1,5},{5,1},{2,6},{6,2},{3,7},{7,3},{8,12},{12,8},{9,1... | collective-permute-start | bytes 3145736 | tf_op jit(solution)/shard_map/ppermute | solution.py:851
  336.0 25.7 %collective-permute-start.14 = (bf16[2048,256]{1,0:T(8,128)(2,1)}, bf16[2048,256]{1,0:T(8,128)(2,1)S(1)}, u32[]{:S(2)}, u32[]{:S(2)}) collective-permute-start(bf16[2048,256]{1,0:T(8,128)(2,1)} %get-tuple-element.104), channel_id=1, source_target_pairs={{0,4},{4,0},{1,5},{5,1},{2,6},{6,2},{3,7},{7,3},{8,12},{12,8},{9,1... | collective-permute-start | bytes 3145736 | tf_op jit(solution)/shard_map/ppermute | solution.py:851
  379.0 27.1 %collective-permute-start.22 = (bf16[512,768]{1,0:T(8,128)(2,1)S(1)}, bf16[512,768]{1,0:T(8,128)(2,1)S(1)}, u32[]{:S(2)}, u32[]{:S(2)}) collective-permute-start(bf16[512,768]{1,0:T(8,128)(2,1)S(1)} %get-tuple-element.199), channel_id=1, source_target_pairs={{0,1},{1,0},{2,3},{3,2},{4,5},{5,4},{6,7},{7,6},{8,9},{9,8},{10,11... | collective-permute-start | bytes 2359304 | tf_op jit(solution)/shard_map/ppermute | solution.py:851
  379.1 35.5 %collective-permute-start.15 = (bf16[512,768]{1,0:T(8,128)(2,1)S(1)}, bf16[512,768]{1,0:T(8,128)(2,1)}, u32[]{:S(2)}, u32[]{:S(2)}) collective-permute-start(bf16[512,768]{1,0:T(8,128)(2,1)S(1)} %get-tuple-element.200), channel_id=1, source_target_pairs={{0,1},{1,0},{2,3},{3,2},{4,5},{5,4},{6,7},{7,6},{8,9},{9,8},{10,11... | collective-permute-start | bytes 2359304 | tf_op jit(solution)/shard_map/ppermute | solution.py:851
  413.4 22.6 %collective-permute-start.26 = (bf16[512,768]{1,0:T(8,128)(2,1)}, bf16[512,768]{1,0:T(8,128)(2,1)S(1)}, u32[]{:S(2)}, u32[]{:S(2)}) collective-permute-start(bf16[512,768]{1,0:T(8,128)(2,1)} %norm_back.3.refs_7_), channel_id=1, source_target_pairs={{1,0},{2,1},{3,2},{5,4},{6,5},{7,6},{9,8},{10,9},{11,10},{13,12},{... | collective-permute-start | bytes 2359304 | tf_op jit(solution)/shard_map/ppermute | solution.py:872
  419.3 29.2 %collective-permute-start.16 = (bf16[512,768]{1,0:T(8,128)(2,1)}, bf16[512,768]{1,0:T(8,128)(2,1)S(1)}, u32[]{:S(2)}, u32[]{:S(2)}) collective-permute-start(bf16[512,768]{1,0:T(8,128)(2,1)} %norm_back.2.refs_0_), channel_id=1, source_target_pairs={{0,1},{1,2},{2,3},{4,5},{5,6},{6,7},{8,9},{9,10},{10,11},{12,13},{... | collective-permute-start | bytes 2359304 | tf_op jit(solution)/shard_map/ppermute | solution.py:871
  423.9 29.7 %collective-permute-start.19 = (bf16[512,768]{1,0:T(8,128)(2,1)}, bf16[512,768]{1,0:T(8,128)(2,1)S(1)}, u32[]{:S(2)}, u32[]{:S(2)}) collective-permute-start(bf16[512,768]{1,0:T(8,128)(2,1)} %norm_back.2.refs_0_), channel_id=1, source_target_pairs={{1,0},{2,1},{3,2},{5,4},{6,5},{7,6},{9,8},{10,9},{11,10},{13,12},{... | collective-permute-start | bytes 2359304 | tf_op jit(solution)/shard_map/ppermute | solution.py:872
  431.6 33.6 %collective-permute-start.24 = (bf16[512,768]{1,0:T(8,128)(2,1)S(1)}, bf16[512,768]{1,0:T(8,128)(2,1)S(1)}, u32[]{:S(2)}, u32[]{:S(2)}) collective-permute-start(bf16[512,768]{1,0:T(8,128)(2,1)S(1)} %collective-permute-done.23.refs_8_), channel_id=1, source_target_pairs={{0,1},{1,2},{2,3},{4,5},{5,6},{6,7},{8,9},{9,10},{10,11},{12,13},{... | collective-permute-start | bytes 2359304 | tf_op jit(solution)/shard_map/ppermute | solution.py:871
  436.0 34.5 %collective-permute-start.27 = (bf16[512,768]{1,0:T(8,128)(2,1)S(1)}, bf16[512,768]{1,0:T(8,128)(2,1)S(1)}, u32[]{:S(2)}, u32[]{:S(2)}) collective-permute-start(bf16[512,768]{1,0:T(8,128)(2,1)S(1)} %collective-permute-done.26.refs_11_), channel_id=1, source_target_pairs={{1,0},{2,1},{3,2},{5,4},{6,5},{7,6},{9,8},{10,9},{11,10},{13,12},{... | collective-permute-start | bytes 2359304 | tf_op jit(solution)/shard_map/ppermute | solution.py:872
  448.5 33.6 %collective-permute-start.17 = (bf16[512,768]{1,0:T(8,128)(2,1)S(1)}, bf16[512,768]{1,0:T(8,128)(2,1)}, u32[]{:S(2)}, u32[]{:S(2)}) collective-permute-start(bf16[512,768]{1,0:T(8,128)(2,1)S(1)} %collective-permute-done.16.refs_1_), channel_id=1, source_target_pairs={{0,1},{1,2},{2,3},{4,5},{5,6},{6,7},{8,9},{9,10},{10,11},{12,13},{... | collective-permute-start | bytes 2359304 | tf_op jit(solution)/shard_map/ppermute | solution.py:871
  453.7 33.8 %collective-permute-start.20 = (bf16[512,768]{1,0:T(8,128)(2,1)S(1)}, bf16[512,768]{1,0:T(8,128)(2,1)}, u32[]{:S(2)}, u32[]{:S(2)}) collective-permute-start(bf16[512,768]{1,0:T(8,128)(2,1)S(1)} %collective-permute-done.19.refs_4_), channel_id=1, source_target_pairs={{1,0},{2,1},{3,2},{5,4},{6,5},{7,6},{9,8},{10,9},{11,10},{13,12},{... | collective-permute-start | bytes 2359304 | tf_op jit(solution)/shard_map/ppermute | solution.py:872
  465.2 36.4 %collective-permute-start.25 = (bf16[512,768]{1,0:T(8,128)(2,1)S(1)}, bf16[512,768]{1,0:T(8,128)(2,1)}, u32[]{:S(2)}, u32[]{:S(2)}) collective-permute-start(bf16[512,768]{1,0:T(8,128)(2,1)S(1)} %collective-permute-done.24.refs_9_.refs_0_), channel_id=1, source_target_pairs={{0,1},{1,2},{2,3},{4,5},{5,6},{6,7},{8,9},{9,10},{10,11},{12,13},{... | collective-permute-start | bytes 2359304 | tf_op jit(solution)/shard_map/ppermute | solution.py:871
  470.5 33.0 %collective-permute-start.28 = (bf16[512,768]{1,0:T(8,128)(2,1)S(1)}, bf16[512,768]{1,0:T(8,128)(2,1)}, u32[]{:S(2)}, u32[]{:S(2)}) collective-permute-start(bf16[512,768]{1,0:T(8,128)(2,1)S(1)} %collective-permute-done.27.refs_12_.refs_1_), channel_id=1, source_target_pairs={{1,0},{2,1},{3,2},{5,4},{6,5},{7,6},{9,8},{10,9},{11,10},{13,12},{... | collective-permute-start | bytes 2359304 | tf_op jit(solution)/shard_map/ppermute | solution.py:872
  482.1 33.8 %collective-permute-start.18 = (bf16[512,768]{1,0:T(8,128)(2,1)}, bf16[512,768]{1,0:T(8,128)(2,1)}, u32[]{:S(2)}, u32[]{:S(2)}) collective-permute-start(bf16[512,768]{1,0:T(8,128)(2,1)} %collective-permute-done.17.refs_2_), channel_id=1, source_target_pairs={{0,1},{1,2},{2,3},{4,5},{5,6},{6,7},{8,9},{9,10},{10,11},{12,13},{... | collective-permute-start | bytes 2359304 | tf_op jit(solution)/shard_map/ppermute | solution.py:871
  487.4 31.1 %collective-permute-start.21 = (bf16[512,768]{1,0:T(8,128)(2,1)}, bf16[512,768]{1,0:T(8,128)(2,1)}, u32[]{:S(2)}, u32[]{:S(2)}) collective-permute-start(bf16[512,768]{1,0:T(8,128)(2,1)} %collective-permute-done.20.refs_5_), channel_id=1, source_target_pairs={{1,0},{2,1},{3,2},{5,4},{6,5},{7,6},{9,8},{10,9},{11,10},{13,12},{... | collective-permute-start | bytes 2359304 | tf_op jit(solution)/shard_map/ppermute | solution.py:872
  492.1 47.1 %collective-permute-start.29 = (bf16[96,2368]{1,0:T(8,128)(2,1)}, bf16[96,2368]{1,0:T(8,128)(2,1)}, u32[]{:S(2)}, u32[]{:S(2)}) collective-permute-start(bf16[96,2368]{1,0:T(8,128)(2,1)} %get-tuple-element.119), channel_id=1, source_target_pairs={{0,2},{2,0},{1,3},{3,1},{4,6},{6,4},{5,7},{7,5},{8,10},{10,8},{9,1... | collective-permute-start | bytes 1363976 | tf_op jit(solution)/shard_map/ppermute | solution.py:851
  (51 other events, 598.0 us)
Sparse Core Ops, SparseCore 0:
  10.9 63.7 all-gather.3
  211.9 78.4 all-gather.5
  297.2 63.4 all-gather.7
  406.3 66.7 reduce-scatter.1
